TPU v7x, 32 devices: a whole 2x2x4 slice. The times are simulated.
32 devices in a mesh: comp: 4 (over z), tile: 8 (over y, x, core).
Axes of the slice: x: 2, y: 2, z: 4, core: 2. Of those that a mesh axis runs over, the one named last changes fastest.
Arguments:
- state: float32 [4, 16, 32, 3072], P('comp', None, 'tile'), may hold values from -6 to 6
- coupling: float32 [4, 32, 3072], P('comp', 'tile'), may hold values from -6 to 6
- land_mask: int32 [4, 32, 3072], P('comp', 'tile'), may hold values 0 or 1
- codes: int32 [4, 32, 3072], P('comp', 'tile'), may hold values from 0 to 3
- mixing: float32 [4, 16], P('comp'), may hold values from 0.1 to 0.19
- courant: float32 [4, 16], P('comp'), may hold values from 0.05 to 0.24
- matrices: float32 [4, 4, 16, 16], P('comp'), may hold values from -1.5 to 1.5
- weights: bfloat16 [4, 2304, 8, 128], P('comp', 'tile'), may hold values from 0 to 0.25
- sources: int32 [4, 2304], P('comp', 'tile'), may hold values from 0 to 95, as said below
- targets: int32 [4, 2304], P('comp', 'tile'), may hold values from 0 to 383, as said below
Outputs:
- new_state: float32 [4, 16, 32, 3072], P('comp', None, 'tile')
- new_coupling: float32 [4, 32, 3072], P('comp', 'tile')
Inputs may be any that keep to these rules, and one draw needn't show every extreme that they name: `sources`: on every tile each of its 96 blocks is the source of exactly 3 of its margin blocks. An atmosphere tile of group a targets only blocks of group 3 * 4 / 4 + a // 3, each of them exactly 3 times; an ocean tile of group o targets every block of the groups 3 (o - 3 * 4 / 4) + j, j < 3, exactly once.
All inputs are finite; a program needn't handle non-finite values. No bound on the sum of `land_mask` on one device may be relied on, other than what follows from the above.
Results may differ from a plain program's by a relative error of at most 0.0011.
Values sent between devices are 32-bit elements; how exact they have to be, the bound alone decides.
No kernel may reach another device: no remote copies, remote signals or barrier semaphores. Data moves between devices by JAX's collectives and lax.ppermute only.
A program may use at most 64 MiB of HBM per device.

v0:
```python
import jax
import jax.numpy as jnp
from jax import lax
from jax.sharding import PartitionSpec as P

SUBSTEPS = 2
INTERVALS = 2


EXCHANGE = 0.5
OCEAN_SHARE = 0.3


def shifted_2(value, axis, steps):
    count = lax.axis_size(axis)
    pairs = [(source, (source + steps) % count) for source in range(count)]
    return lax.ppermute(value, axis, pairs)


def with_halo(cells, sides, width):
    for axis, dim in sides:
        count = lax.axis_size(axis)
        head = lax.slice_in_dim(cells, 0, width, axis=dim)
        tail = lax.slice_in_dim(cells, cells.shape[dim] - width, cells.shape[dim], axis=dim)
        cells = jnp.concatenate(
            [
                lax.ppermute(tail, axis, [(i, (i + 1) % count) for i in range(count)]),
                cells,
                lax.ppermute(head, axis, [((i + 1) % count, i) for i in range(count)]),
            ],
            axis=dim,
        )
    return cells


def advance_rows(padded, mixing_rate, courant_rate):
    center = padded[:, 1:-1]
    row_above = padded[:, :-2]
    row_below = padded[:, 2:]
    col_left = jnp.roll(center, 1, axis=2)
    col_right = jnp.roll(center, -1, axis=2)
    return (
        center
        + mixing_rate * (row_above + row_below + col_left + col_right - 4.0 * center)
        + courant_rate * (row_above - center)
    )


def remap_local(handed, weight_blocks, source_list, target_list, groups):
    block_width = weight_blocks.shape[-1]
    band_count = weight_blocks.shape[1]
    blocks = handed.reshape(-1, block_width).astype(jnp.bfloat16)
    picked = jnp.take(blocks, source_list, axis=0).astype(jnp.float32)
    shifted = jnp.stack([jnp.roll(picked, -offset, axis=1) for offset in range(band_count)], axis=1)
    contrib = jnp.sum(weight_blocks.astype(jnp.float32) * shifted, axis=1)
    slot_count = groups * blocks.shape[0]
    selector = (target_list[:, None] == jnp.arange(slot_count, dtype=jnp.int32)[None, :]).astype(
        jnp.float32
    )
    payload = jnp.dot(selector.T, contrib, precision=lax.Precision.HIGHEST)
    return payload.reshape(groups, -1)


def partner_offsets(groups):
    air_count = 3 * groups // 4
    upward = [(air_count + member // 3 - member) % groups for member in range(air_count)]
    downward = [
        (3 * member + offset - air_count - member) % groups
        for member in range(groups - air_count)
        for offset in range(3)
    ]
    return sorted(set(upward + downward))


def on_device(
    state, coupling, land_mask, codes, mixing, courant, matrices, weights, sources, targets
):
    groups = lax.axis_size("comp")
    own_index = lax.axis_index("comp")
    air_group = own_index < 3 * groups // 4
    evolved = state[0]
    handed = coupling[0]
    wet_cells = land_mask[0].astype(jnp.float32)
    mixing_rate = mixing[0][:, None, None]
    courant_rate = courant[0][:, None, None]
    physics_table = matrices[0]
    branch_index = jnp.arange(physics_table.shape[0], dtype=jnp.int32)[:, None, None]
    code_select = (codes[0][None] == branch_index).astype(jnp.float32)
    for interval in range(INTERVALS):
        payload = remap_local(handed, weights[0], sources[0], targets[0], groups)
        received = jnp.zeros(payload.shape[1:], jnp.float32)
        for distance in partner_offsets(groups):
            outgoing = lax.dynamic_index_in_dim(
                payload, (own_index + distance) % groups, 0, keepdims=False
            )
            received = received + shifted_2(outgoing, "comp", distance)
        received = received.reshape(handed.shape)
        surface = evolved[0]
        surface_flux = wet_cells * EXCHANGE * (received - surface)
        diffused = evolved.at[0].set(
            jnp.where(air_group, surface + surface_flux, surface - OCEAN_SHARE * received)
        )
        for substep in range(SUBSTEPS):
            padded = with_halo(diffused, (("tile", 1),), 1)
            diffused = advance_rows(padded, mixing_rate, courant_rate)
        branch_terms = jnp.einsum(
            "bij,jrw->birw", physics_table, jnp.tanh(diffused), precision=lax.Precision.HIGHEST
        )
        evolved = diffused + jnp.einsum(
            "birw,brw->irw", branch_terms, code_select, precision=lax.Precision.HIGHEST
        )
        evolved = jnp.where(air_group, evolved, evolved * wet_cells[None])
        handed = jnp.where(air_group, surface_flux, evolved[0])
    return (evolved[None], handed[None])


def solution(mesh):
    placed = (
        P("comp", None, "tile", None),
        P("comp", "tile", None),
        P("comp", "tile", None),
        P("comp", "tile", None),
        P("comp", None),
        P("comp", None),
        P("comp", None, None, None),
        P("comp", "tile", None, None),
        P("comp", "tile"),
        P("comp", "tile"),
    )
    return jax.shard_map(
        on_device,
        mesh=mesh,
        in_specs=placed,
        out_specs=(P("comp", None, "tile", None), P("comp", "tile", None)),
        check_vma=False,
    )
```

profile of v0, /device:TPU:0, one launch (start us, length us, event | category | flops | bytes accessed | tf_op | source)
XLA Modules:
  0.0 71.4 jit_solution(15581298252337993904)
XLA Ops:
  0.6 0.7 reduce.7
  1.4 0.8 %convert_element_type.37 = bf16[1,4,3072]{2,1,0:T(4,128)(2,1)S(1)} convert(f32[1,4,3072]{2,1,0:T(4,128)} %param.17) | non-fusion elementwise | flops 12288 | bytes 73728 | tf_op jit(solution)/shard_map/convert_element_type | solution.py:52
  2.2 1.4 %gather_fusion = bf16[288,128]{1,0:T(8,128)(2,1)S(1)} fusion(bf16[96,128]{1,0:T(8,128)(2,1)S(1)} %convert_element_type.38, s32[1024]{0:T(1024)S(1)} %pad_clamp_fusion), kind=kCustom, calls=%fused_computation.clone | custom fusion | bytes 148608 | tf_op jit(solution)/shard_map/jit(_take)/gather | solution.py:53
  5.5 0.5 copy-done.1
  6.1 0.8 %fusion.45 = f32[384,128]{1,0:T(8,128)S(1)} fusion(f32[288,128]{1,0:T(8,128)S(1)} %fusion.2, s32[288]{0:T(512)S(1)} %reduce.6), kind=kOutput, calls=%fused_computation.65 | convolution fusion | flops 169979904 | bytes 345216 | tf_op jit(solution)/shard_map/dot_general | solution.py:60
  7.1 3.1 %collective-permute-start = (f32[12288]{0:T(1024)S(1)}, f32[12288]{0:T(1024)S(1)}, u32[]{:S(2)}, u32[]{:S(2)}) collective-permute-start(f32[12288]{0:T(1024)S(1)} %bitcast.182), channel_id=1, source_target_pairs={{0,8},{8,16},{16,24},{24,0},{1,9},{9,17},{17,25},{25,1},{2,10},{10... | collective-permute-start | bytes 147464 | tf_op jit(solution)/shard_map/ppermute | solution.py:17
  10.2 2.6 %collective-permute-start.1 = (f32[12288]{0:T(1024)S(1)}, f32[12288]{0:T(1024)S(1)}, u32[]{:S(2)}, u32[]{:S(2)}) collective-permute-start(f32[12288]{0:T(1024)S(1)} %bitcast.181), channel_id=1, source_target_pairs={{0,16},{8,24},{16,0},{24,8},{1,17},{9,25},{17,1},{25,9},{2,18},{10... | collective-permute-start | bytes 147464 | tf_op jit(solution)/shard_map/ppermute | solution.py:17
  12.8 1.4 %collective-permute-start.2 = (f32[12288]{0:T(1024)S(1)}, f32[12288]{0:T(1024)S(1)}, u32[]{:S(2)}, u32[]{:S(2)}) collective-permute-start(f32[12288]{0:T(1024)S(1)} %bitcast.180), channel_id=1, source_target_pairs={{0,24},{8,0},{16,8},{24,16},{1,25},{9,1},{17,9},{25,17},{2,26},{10... | collective-permute-start | bytes 147464 | tf_op jit(solution)/shard_map/ppermute | solution.py:17
  15.0 1.4 %collective-permute-done.1 = f32[12288]{0:T(1024)S(1)} collective-permute-done((f32[12288]{0:T(1024)S(1)}, f32[12288]{0:T(1024)S(1)}, u32[]{:S(2)}, u32[]{:S(2)}) %collective-permute-start.1) | collective-permute-done | bytes 49184 | tf_op jit(solution)/shard_map/ppermute | solution.py:17
  16.4 0.5 collective-permute-done.2
  17.1 0.5 scatter.6
  17.9 2.6 %collective-permute-start.4 = (f32[16,1,3072]{2,0,1:T(8,128)S(1)}, f32[16,1,3072]{2,0,1:T(8,128)S(1)}, u32[]{:S(2)}, u32[]{:S(2)}) collective-permute-start(f32[16,1,3072]{2,0,1:T(8,128)S(1)} %get-tuple-element.54), channel_id=1, source_target_pairs={{1,0},{2,1},{3,2},{4,3},{5,4},{6,5},{7,6},{0,7},{9,8},{10,9},{11,1... | collective-permute-start | bytes 589832 | tf_op jit(solution)/shard_map/ppermute | solution.py:29
  20.6 3.4 %collective-permute-done.3 = f32[16,1,3072]{2,0,1:T(8,128)S(1)} collective-permute-done((f32[16,1,3072]{2,0,1:T(8,128)S(1)}, f32[16,1,3072]{2,0,1:T(8,128)S(1)}, u32[]{:S(2)}, u32[]{:S(2)}) %collective-permute-start.3) | collective-permute-done | bytes 196640 | tf_op jit(solution)/shard_map/ppermute | solution.py:27
  25.0 1.8 %collective-permute-start.5 = (f32[16,1,3072]{2,0,1:T(8,128)S(1)}, f32[16,1,3072]{2,0,1:T(8,128)S(1)}, u32[]{:S(2)}, u32[]{:S(2)}) collective-permute-start(f32[16,1,3072]{2,0,1:T(8,128)S(1)} %get-tuple-element.47), channel_id=1, source_target_pairs={{0,1},{1,2},{2,3},{3,4},{4,5},{5,6},{6,7},{7,0},{8,9},{9,10},{10,1... | collective-permute-start | bytes 589832 | tf_op jit(solution)/shard_map/ppermute | solution.py:27
  26.9 1.1 %collective-permute-start.6 = (f32[16,1,3072]{2,0,1:T(8,128)S(1)}, f32[16,1,3072]{2,0,1:T(8,128)S(1)}, u32[]{:S(2)}, u32[]{:S(2)}) collective-permute-start(f32[16,1,3072]{2,0,1:T(8,128)S(1)} %get-tuple-element.48), channel_id=1, source_target_pairs={{1,0},{2,1},{3,2},{4,3},{5,4},{6,5},{7,6},{0,7},{9,8},{10,9},{11,1... | collective-permute-start | bytes 589832 | tf_op jit(solution)/shard_map/ppermute | solution.py:29
  28.0 4.2 %collective-permute-done.5 = f32[16,1,3072]{2,0,1:T(8,128)S(1)} collective-permute-done((f32[16,1,3072]{2,0,1:T(8,128)S(1)}, f32[16,1,3072]{2,0,1:T(8,128)S(1)}, u32[]{:S(2)}, u32[]{:S(2)}) %collective-permute-start.5) | collective-permute-done | bytes 196640 | tf_op jit(solution)/shard_map/ppermute | solution.py:27
  32.8 2.6 %fusion = f32[4,3072,16]{1,2,0:T(8,128)S(1)} fusion(f32[4,3072,4]{1,2,0:T(4,128)S(1)} %copy.43, f32[16,4,3072]{2,0,1:T(8,128)S(1)} %fusion.28, f32[1,4,16,16]{3,2,1,0:T(8,128)S(1)} %copy-done), kind=kOutput, calls=%fused_computation.4 | convolution fusion | flops 152371200 | bytes 1773568 | tf_op jit(solution)/shard_map/bij,jrw->birw/dot_general | solution.py:106
  35.6 1.4 %gather_fusion.1 = bf16[288,128]{1,0:T(8,128)(2,1)S(1)} fusion(bf16[96,128]{1,0:T(8,128)(2,1)S(1)} %fusion.66, s32[1024]{0:T(1024)S(1)} %pad_clamp_fusion), kind=kCustom, calls=%fused_computation.1.clone | custom fusion | bytes 148608 | tf_op jit(solution)/shard_map/jit(_take)/gather | solution.py:53
  38.9 0.8 %fusion.44 = f32[384,128]{1,0:T(8,128)S(1)} fusion(f32[288,128]{1,0:T(8,128)S(1)} %fusion.3, s32[288]{0:T(512)S(1)} %reduce.6), kind=kOutput, calls=%fused_computation.64 | convolution fusion | flops 169979904 | bytes 345216 | tf_op jit(solution)/shard_map/dot_general | solution.py:60
  39.9 0.6 collective-permute-start.7
  40.5 2.9 %collective-permute-start.8 = (f32[12288]{0:T(1024)S(1)}, f32[12288]{0:T(1024)S(1)}, u32[]{:S(2)}, u32[]{:S(2)}) collective-permute-start(f32[12288]{0:T(1024)S(1)} %bitcast.184), channel_id=1, source_target_pairs={{0,16},{8,24},{16,0},{24,8},{1,17},{9,25},{17,1},{25,9},{2,18},{10... | collective-permute-start | bytes 147464 | tf_op jit(solution)/shard_map/ppermute | solution.py:17
  43.8 2.1 %collective-permute-done.7 = f32[12288]{0:T(1024)S(1)} collective-permute-done((f32[12288]{0:T(1024)S(1)}, f32[12288]{0:T(1024)S(1)}, u32[]{:S(2)}, u32[]{:S(2)}) %collective-permute-start.7) | collective-permute-done | bytes 49184 | tf_op jit(solution)/shard_map/ppermute | solution.py:17
  45.9 1.3 %collective-permute-done.8 = f32[12288]{0:T(1024)S(1)} collective-permute-done((f32[12288]{0:T(1024)S(1)}, f32[12288]{0:T(1024)S(1)}, u32[]{:S(2)}, u32[]{:S(2)}) %collective-permute-start.8) | collective-permute-done | bytes 49184 | tf_op jit(solution)/shard_map/ppermute | solution.py:17
  47.2 1.3 %collective-permute-done.9 = f32[12288]{0:T(1024)S(1)} collective-permute-done((f32[12288]{0:T(1024)S(1)}, f32[12288]{0:T(1024)S(1)}, u32[]{:S(2)}, u32[]{:S(2)}) %collective-permute-start.9) | collective-permute-done | bytes 49184 | tf_op jit(solution)/shard_map/ppermute | solution.py:17
  49.7 2.5 %collective-permute-start.11 = (f32[16,1,3072]{2,0,1:T(8,128)S(1)}, f32[16,1,3072]{2,0,1:T(8,128)S(1)}, u32[]{:S(2)}, u32[]{:S(2)}) collective-permute-start(f32[16,1,3072]{2,0,1:T(8,128)S(1)} %get-tuple-element.42), channel_id=1, source_target_pairs={{1,0},{2,1},{3,2},{4,3},{5,4},{6,5},{7,6},{0,7},{9,8},{10,9},{11,1... | collective-permute-start | bytes 589832 | tf_op jit(solution)/shard_map/ppermute | solution.py:29
  52.3 5.2 %collective-permute-done.10 = f32[16,1,3072]{2,0,1:T(8,128)S(1)} collective-permute-done((f32[16,1,3072]{2,0,1:T(8,128)S(1)}, f32[16,1,3072]{2,0,1:T(8,128)S(1)}, u32[]{:S(2)}, u32[]{:S(2)}) %collective-permute-start.10) | collective-permute-done | bytes 196640 | tf_op jit(solution)/shard_map/ppermute | solution.py:27
  58.3 1.0 %collective-permute-start.12 = (f32[16,1,3072]{2,0,1:T(8,128)S(1)}, f32[16,1,3072]{2,0,1:T(8,128)S(1)}, u32[]{:S(2)}, u32[]{:S(2)}) collective-permute-start(f32[16,1,3072]{2,0,1:T(8,128)S(1)} %get-tuple-element.35), channel_id=1, source_target_pairs={{0,1},{1,2},{2,3},{3,4},{4,5},{5,6},{6,7},{7,0},{8,9},{9,10},{10,1... | collective-permute-start | bytes 589832 | tf_op jit(solution)/shard_map/ppermute | solution.py:27
  59.3 1.7 %collective-permute-start.13 = (f32[16,1,3072]{2,0,1:T(8,128)S(1)}, f32[16,1,3072]{2,0,1:T(8,128)S(1)}, u32[]{:S(2)}, u32[]{:S(2)}) collective-permute-start(f32[16,1,3072]{2,0,1:T(8,128)S(1)} %get-tuple-element.36), channel_id=1, source_target_pairs={{1,0},{2,1},{3,2},{4,3},{5,4},{6,5},{7,6},{0,7},{9,8},{10,9},{11,1... | collective-permute-start | bytes 589832 | tf_op jit(solution)/shard_map/ppermute | solution.py:29
  61.1 5.0 %collective-permute-done.12 = f32[16,1,3072]{2,0,1:T(8,128)S(1)} collective-permute-done((f32[16,1,3072]{2,0,1:T(8,128)S(1)}, f32[16,1,3072]{2,0,1:T(8,128)S(1)}, u32[]{:S(2)}, u32[]{:S(2)}) %collective-permute-start.12) | collective-permute-done | bytes 196640 | tf_op jit(solution)/shard_map/ppermute | solution.py:27
  66.5 2.6 %fusion.1 = f32[4,3072,16]{1,2,0:T(8,128)S(1)} fusion(f32[4,3072,4]{1,2,0:T(4,128)S(1)} %copy.43, f32[16,4,3072]{2,0,1:T(8,128)S(1)} %fusion.10, f32[1,4,16,16]{3,2,1,0:T(8,128)S(1)} %copy-done), kind=kOutput, calls=%fused_computation.5 | convolution fusion | flops 152371200 | bytes 1773568 | tf_op jit(solution)/shard_map/bij,jrw->birw/dot_general | solution.py:106
  69.4 0.6 copy.24
  70.0 1.4 %copy.23 = f32[1,16,4,3072]{3,2,1,0:T(4,128)} copy(f32[1,16,4,3072]{3,1,2,0:T(8,128)S(1)} %bitcast.171) | data formatting | bytes 1572864
  (100 shorter events, 10.2 us)
Async XLA Ops:
  0.6 32.1 %copy-start = (f32[1,4,16,16]{3,2,1,0:T(8,128)S(1)}, f32[1,4,16,16]{3,2,1,0:T(8,128)}, u32[]{:S(2)}) copy-start(f32[1,4,16,16]{3,2,1,0:T(8,128)} %param.22) | copy-start | bytes 12292
  3.7 0.9 %copy-start.7 = (s32[1,288]{1,0:T(1,128)S(1)}, s32[1,288]{1,0:T(1,128)}, u32[]{:S(2)}) copy-start(s32[1,288]{1,0:T(1,128)} %param.25) | copy-start | bytes 3460
  4.9 1.1 %copy-start.1 = (bf16[1,288,8,128]{3,2,1,0:T(8,128)(2,1)S(1)}, bf16[1,288,8,128]{3,2,1,0:T(8,128)(2,1)}, u32[]{:S(2)}) copy-start(bf16[1,288,8,128]{3,2,1,0:T(8,128)(2,1)} %param.23) | copy-start | bytes 1769476
  6.0 8.2 %copy-start.4 = (s32[1,4,3072]{2,1,0:T(4,128)S(1)}, s32[1,4,3072]{2,1,0:T(4,128)}, u32[]{:S(2)}) copy-start(s32[1,4,3072]{2,1,0:T(4,128)} %param.19) | copy-start | bytes 147460
  6.0 8.2 %copy-start.3 = (s32[1,4,3072]{2,1,0:T(4,128)S(1)}, s32[1,4,3072]{2,1,0:T(4,128)}, u32[]{:S(2)}) copy-start(s32[1,4,3072]{2,1,0:T(4,128)} %param.18) | copy-start | bytes 147460
  6.1 8.2 %copy-start.2 = (f32[1,16,4,3072]{3,2,1,0:T(4,128)S(1)}, f32[1,16,4,3072]{3,2,1,0:T(4,128)}, u32[]{:S(2)}) copy-start(f32[1,16,4,3072]{3,2,1,0:T(4,128)} %param.16) | copy-start | bytes 2359300
  7.1 7.8 %collective-permute-start = (f32[12288]{0:T(1024)S(1)}, f32[12288]{0:T(1024)S(1)}, u32[]{:S(2)}, u32[]{:S(2)}) collective-permute-start(f32[12288]{0:T(1024)S(1)} %bitcast.182), channel_id=1, source_target_pairs={{0,8},{8,16},{16,24},{24,0},{1,9},{9,17},{17,25},{25,1},{2,10},{10... | collective-permute-start | bytes 147464 | tf_op jit(solution)/shard_map/ppermute | solution.py:17
  10.2 6.2 %collective-permute-start.1 = (f32[12288]{0:T(1024)S(1)}, f32[12288]{0:T(1024)S(1)}, u32[]{:S(2)}, u32[]{:S(2)}) collective-permute-start(f32[12288]{0:T(1024)S(1)} %bitcast.181), channel_id=1, source_target_pairs={{0,16},{8,24},{16,0},{24,8},{1,17},{9,25},{17,1},{25,9},{2,18},{10... | collective-permute-start | bytes 147464 | tf_op jit(solution)/shard_map/ppermute | solution.py:17
  12.8 4.1 %collective-permute-start.2 = (f32[12288]{0:T(1024)S(1)}, f32[12288]{0:T(1024)S(1)}, u32[]{:S(2)}, u32[]{:S(2)}) collective-permute-start(f32[12288]{0:T(1024)S(1)} %bitcast.180), channel_id=1, source_target_pairs={{0,24},{8,0},{16,8},{24,16},{1,25},{9,1},{17,9},{25,17},{2,26},{10... | collective-permute-start | bytes 147464 | tf_op jit(solution)/shard_map/ppermute | solution.py:17
  17.5 6.7 %copy-start.5 = (f32[1,16]{1,0:T(1,128)S(1)}, f32[1,16]{1,0:T(1,128)}, u32[]{:S(2)}) copy-start(f32[1,16]{1,0:T(1,128)} %param.21) | copy-start | bytes 196
  17.5 6.7 %copy-start.6 = (f32[1,16]{1,0:T(1,128)S(1)}, f32[1,16]{1,0:T(1,128)}, u32[]{:S(2)}) copy-start(f32[1,16]{1,0:T(1,128)} %param.20) | copy-start | bytes 196
  17.9 6.1 %collective-permute-start.3 = (f32[16,1,3072]{2,0,1:T(8,128)S(1)}, f32[16,1,3072]{2,0,1:T(8,128)S(1)}, u32[]{:S(2)}, u32[]{:S(2)}) collective-permute-start(f32[16,1,3072]{2,0,1:T(8,128)S(1)} %get-tuple-element.53), channel_id=1, source_target_pairs={{0,1},{1,2},{2,3},{3,4},{4,5},{5,6},{6,7},{7,0},{8,9},{9,10},{10,1... | collective-permute-start | bytes 589832 | tf_op jit(solution)/shard_map/ppermute | solution.py:27
  17.9 6.3 %collective-permute-start.4 = (f32[16,1,3072]{2,0,1:T(8,128)S(1)}, f32[16,1,3072]{2,0,1:T(8,128)S(1)}, u32[]{:S(2)}, u32[]{:S(2)}) collective-permute-start(f32[16,1,3072]{2,0,1:T(8,128)S(1)} %get-tuple-element.54), channel_id=1, source_target_pairs={{1,0},{2,1},{3,2},{4,3},{5,4},{6,5},{7,6},{0,7},{9,8},{10,9},{11,1... | collective-permute-start | bytes 589832 | tf_op jit(solution)/shard_map/ppermute | solution.py:29
  25.0 7.2 %collective-permute-start.5 = (f32[16,1,3072]{2,0,1:T(8,128)S(1)}, f32[16,1,3072]{2,0,1:T(8,128)S(1)}, u32[]{:S(2)}, u32[]{:S(2)}) collective-permute-start(f32[16,1,3072]{2,0,1:T(8,128)S(1)} %get-tuple-element.47), channel_id=1, source_target_pairs={{0,1},{1,2},{2,3},{3,4},{4,5},{5,6},{6,7},{7,0},{8,9},{9,10},{10,1... | collective-permute-start | bytes 589832 | tf_op jit(solution)/shard_map/ppermute | solution.py:27
  26.9 5.4 %collective-permute-start.6 = (f32[16,1,3072]{2,0,1:T(8,128)S(1)}, f32[16,1,3072]{2,0,1:T(8,128)S(1)}, u32[]{:S(2)}, u32[]{:S(2)}) collective-permute-start(f32[16,1,3072]{2,0,1:T(8,128)S(1)} %get-tuple-element.48), channel_id=1, source_target_pairs={{1,0},{2,1},{3,2},{4,3},{5,4},{6,5},{7,6},{0,7},{9,8},{10,9},{11,1... | collective-permute-start | bytes 589832 | tf_op jit(solution)/shard_map/ppermute | solution.py:29
  39.9 6.0 %collective-permute-start.7 = (f32[12288]{0:T(1024)S(1)}, f32[12288]{0:T(1024)S(1)}, u32[]{:S(2)}, u32[]{:S(2)}) collective-permute-start(f32[12288]{0:T(1024)S(1)} %bitcast.185), channel_id=1, source_target_pairs={{0,8},{8,16},{16,24},{24,0},{1,9},{9,17},{17,25},{25,1},{2,10},{10... | collective-permute-start | bytes 147464 | tf_op jit(solution)/shard_map/ppermute | solution.py:17
  40.5 6.7 %collective-permute-start.8 = (f32[12288]{0:T(1024)S(1)}, f32[12288]{0:T(1024)S(1)}, u32[]{:S(2)}, u32[]{:S(2)}) collective-permute-start(f32[12288]{0:T(1024)S(1)} %bitcast.184), channel_id=1, source_target_pairs={{0,16},{8,24},{16,0},{24,8},{1,17},{9,25},{17,1},{25,9},{2,18},{10... | collective-permute-start | bytes 147464 | tf_op jit(solution)/shard_map/ppermute | solution.py:17
  43.4 5.2 %collective-permute-start.9 = (f32[12288]{0:T(1024)S(1)}, f32[12288]{0:T(1024)S(1)}, u32[]{:S(2)}, u32[]{:S(2)}) collective-permute-start(f32[12288]{0:T(1024)S(1)} %bitcast.183), channel_id=1, source_target_pairs={{0,24},{8,0},{16,8},{24,16},{1,25},{9,1},{17,9},{25,17},{2,26},{10... | collective-permute-start | bytes 147464 | tf_op jit(solution)/shard_map/ppermute | solution.py:17
  49.5 8.0 %collective-permute-start.10 = (f32[16,1,3072]{2,0,1:T(8,128)S(1)}, f32[16,1,3072]{2,0,1:T(8,128)S(1)}, u32[]{:S(2)}, u32[]{:S(2)}) collective-permute-start(f32[16,1,3072]{2,0,1:T(8,128)S(1)} %get-tuple-element.41), channel_id=1, source_target_pairs={{0,1},{1,2},{2,3},{3,4},{4,5},{5,6},{6,7},{7,0},{8,9},{9,10},{10,1... | collective-permute-start | bytes 589832 | tf_op jit(solution)/shard_map/ppermute | solution.py:27
  49.7 7.9 %collective-permute-start.11 = (f32[16,1,3072]{2,0,1:T(8,128)S(1)}, f32[16,1,3072]{2,0,1:T(8,128)S(1)}, u32[]{:S(2)}, u32[]{:S(2)}) collective-permute-start(f32[16,1,3072]{2,0,1:T(8,128)S(1)} %get-tuple-element.42), channel_id=1, source_target_pairs={{1,0},{2,1},{3,2},{4,3},{5,4},{6,5},{7,6},{0,7},{9,8},{10,9},{11,1... | collective-permute-start | bytes 589832 | tf_op jit(solution)/shard_map/ppermute | solution.py:29
  58.3 7.7 %collective-permute-start.12 = (f32[16,1,3072]{2,0,1:T(8,128)S(1)}, f32[16,1,3072]{2,0,1:T(8,128)S(1)}, u32[]{:S(2)}, u32[]{:S(2)}) collective-permute-start(f32[16,1,3072]{2,0,1:T(8,128)S(1)} %get-tuple-element.35), channel_id=1, source_target_pairs={{0,1},{1,2},{2,3},{3,4},{4,5},{5,6},{6,7},{7,0},{8,9},{9,10},{10,1... | collective-permute-start | bytes 589832 | tf_op jit(solution)/shard_map/ppermute | solution.py:27
  59.3 6.7 %collective-permute-start.13 = (f32[16,1,3072]{2,0,1:T(8,128)S(1)}, f32[16,1,3072]{2,0,1:T(8,128)S(1)}, u32[]{:S(2)}, u32[]{:S(2)}) collective-permute-start(f32[16,1,3072]{2,0,1:T(8,128)S(1)} %get-tuple-element.36), channel_id=1, source_target_pairs={{1,0},{2,1},{3,2},{4,3},{5,4},{6,5},{7,6},{0,7},{9,8},{10,9},{11,1... | collective-permute-start | bytes 589832 | tf_op jit(solution)/shard_map/ppermute | solution.py:29
where the time goes:
time: 71.7 us; the launch traced here: 71.4 us
  waiting for transfers between devices  24.8 us (35%)
  starting transfers between devices  21.9 us (31%)
  local copies, waits for them, and re-layouts  10.4 us (15%)
  matrix products  6.8 us (9%)
  other arithmetic  6.29 us (9%)
  between operations  1.3 us (2%)
    ppermute x4, waiting for transfers between devices, with_halo(): lax.ppermute(tail, axis, [(i, (i + 1) % count) for i in range(count)])  17.8 us
    ppermute x6, starting transfers between devices, shifted_2(): return lax.ppermute(value, axis, pairs)  10.9 us
    ppermute x4, starting transfers between devices, with_halo(): lax.ppermute(head, axis, [((i + 1) % count, i) for i in range(count)])  7.91 us
    ppermute x6, waiting for transfers between devices, shifted_2(): return lax.ppermute(value, axis, pairs)  6.69 us
    dot_general x2, matrix products, on_device(): jnp.einsum('bij,jrw->birw', physics_table, jnp.tanh(diffused), precision=...  5.28 us
    unnamed x23, local copies, waits for them, and re-layouts  3.27 us
    ppermute x4, starting transfers between devices, with_halo(): lax.ppermute(tail, axis, [(i, (i + 1) % count) for i in range(count)])  3.09 us
    gather x2, local copies, waits for them, and re-layouts, remap_local(): picked = jnp.take(blocks, source_list, axis=0).astype(jnp.float32)  2.77 us
  transfers between devices with their start and end apart: 14, of which 10 were waited for; matrix products, arithmetic and copies ran while one was open for 2% of the time, Pallas kernels for 0%

commit v1 on v0

v1 whole, which is shorter than its diff:
```python
import functools

import jax
import jax.numpy as jnp
from jax import lax
from jax.experimental import pallas as pl
from jax.experimental.pallas import tpu as pltpu
from jax.sharding import PartitionSpec as P

SUBSTEPS = 2
INTERVALS = 2
EXCHANGE = 0.5
OCEAN_SHARE = 0.3

F32 = jnp.float32
BF16 = jnp.bfloat16
VMEM = pl.BlockSpec(memory_space=pltpu.VMEM)
PARAMS = pltpu.CompilerParams(vmem_limit_bytes=40 * 1024 * 1024)


def partner_offsets(groups):
    air_count = 3 * groups // 4
    upward = [(air_count + member // 3 - member) % groups for member in range(air_count)]
    downward = [
        (3 * member + offset - air_count - member) % groups
        for member in range(groups - air_count)
        for offset in range(3)
    ]
    return sorted(set(upward + downward))


def ring_pairs(count, steps):
    return [(source, (source + steps) % count) for source in range(count)]


def inner_pairs(count):
    return [(tile, tile ^ 1) for tile in range(count)]


def outer_pairs(count):
    return [(tile, (tile + 1) % count if tile % 2 else (tile - 1) % count) for tile in range(count)]


def split_high_low(value):
    high = value.astype(BF16)
    low = (value - high.astype(F32)).astype(BF16)
    return high, low


def remap(handed, w_ref, src_ref, tgt_ref, out_refs, offsets, groups, blk_ref, wide_ref):
    rows, width = handed.shape
    block = w_ref.shape[-1]
    per_row = width // block
    count = rows * per_row
    margins, band = w_ref.shape[1], w_ref.shape[2]
    for c in range(per_row):
        blk_ref[pl.ds(c, rows, stride=per_row), :] = handed[:, c * block : (c + 1) * block]
    blocks = blk_ref[...].astype(BF16)
    pick = (lax.broadcasted_iota(jnp.int32, (count, margins), 0) == src_ref[...]).astype(F32).astype(BF16)
    picked = lax.dot_general(pick, blocks, (((0,), (0,)), ((), ())), preferred_element_type=F32)
    wide_ref[...] = w_ref[0].reshape(margins * band, block).astype(F32)
    contrib = wide_ref[pl.ds(0, margins, stride=band), :] * picked
    for j in range(1, band):
        turned = pltpu.roll(picked, block - j, 1)
        contrib = contrib + wide_ref[pl.ds(j, margins, stride=band), :] * turned
    high, low = split_high_low(contrib)
    both = jnp.concatenate([high, low], axis=0)
    me = lax.axis_index("comp")
    slot = lax.broadcasted_iota(jnp.int32, (count, margins), 0)
    targets = tgt_ref[...]
    for out_ref, offset in zip(out_refs, offsets):
        base = lax.rem(me + offset, groups) * count
        chosen = (targets == slot + base).astype(F32).astype(BF16)
        out_ref[...] = jnp.dot(
            jnp.concatenate([chosen, chosen], axis=1), both, preferred_element_type=F32
        )


def open_kernel(offsets, groups, state, coupling, w, src, tgt, x1, x2, *rest):
    outs, (blk, wide) = rest[: len(offsets)], rest[len(offsets) :]
    odd = lax.rem(lax.axis_index("tile"), 2) == 1
    half = x1.shape[0]
    for i in range(half):
        head, tail = state[0, :, i, :], state[0, :, half + i, :]
        x1[i] = jnp.where(odd, head, tail)
        x2[i] = jnp.where(odd, tail, head)
    remap(coupling[0], w, src, tgt, outs, offsets, groups, blk, wide)


def surface_kernel(groups, n_rec, *refs):
    recs, (surface_ref, mask_ref, ns_ref, flux_ref, d1, d2, blk) = refs[:n_rec], refs[n_rec:]
    odd = lax.rem(lax.axis_index("tile"), 2) == 1
    air = lax.axis_index("comp") < 3 * groups // 4
    rows, width = ns_ref.shape
    block = blk.shape[-1]
    per_row = width // block
    total = recs[0][...]
    for rec in recs[1:]:
        total = total + rec[...]
    blk[...] = total
    received = jnp.concatenate(
        [blk[pl.ds(c, rows, stride=per_row), :] for c in range(per_row)], axis=1
    )
    surface = surface_ref[...].reshape(rows, width)
    flux = mask_ref[0].astype(F32) * EXCHANGE * (received - surface)
    new = surface + jnp.where(air, flux, -OCEAN_SHARE * received)
    ns_ref[...] = new
    flux_ref[...] = flux
    half = rows // 2
    head, tail = new[:half], new[half:]
    d1[...] = jnp.where(odd, head, tail)
    d2[...] = jnp.where(odd, tail, head)


def substep(f, up, down, c0, cu, m):
    width = f.shape[1]
    sides = pltpu.roll(f, 1, 1) + pltpu.roll(f, width - 1, 1)
    return c0 * f + cu * up + m * (down + sides)


def fields_kernel(x1, x2, y1, y2, coef, table, codes, part, grid_ref):
    odd = lax.rem(lax.axis_index("tile"), 2) == 1
    half, fields, width = x1.shape
    c0, cu, m = coef[0], coef[1], coef[2]
    branches = table.shape[0] // fields

    def row(i):
        group, at = divmod(i, half)
        first, second = ((y2, y1), (x2, x1), (x1, x2), (y1, y2))[group]
        return jnp.where(odd, second[at], first[at])

    above, here = row(0), row(1)
    for i in range(1, 4 * half - 1):
        below = row(i + 1)
        grid_ref[i - 1] = substep(here, above, below, c0, cu, m)
        above, here = here, below
    keep = lax.broadcasted_iota(jnp.int32, (fields, width), 0) > 0
    for r in range(2 * half):
        f = substep(grid_ref[r + 1], grid_ref[r], grid_ref[r + 2], c0, cu, m)
        high, low = split_high_low(jnp.tanh(f))
        terms = jnp.dot(
            table[...], jnp.concatenate([high, low, high], axis=0), preferred_element_type=F32
        )
        code = codes[0, r : r + 1, :]
        tendency = terms[:fields]
        for b in range(1, branches):
            tendency = jnp.where(code == b, terms[b * fields : (b + 1) * fields], tendency)
        part[r] = jnp.where(keep, f, 0.0) + tendency


def field0(ns, e1, e2, coef0, odd):
    half = e1.shape[0]
    first, last = e1[...], e2[...]
    f = jnp.concatenate(
        [jnp.where(odd, first, last), ns[...], jnp.where(odd, last, first)], axis=0
    )
    rows = f.shape[0]
    for _ in range(SUBSTEPS):
        f = substep(f, pltpu.roll(f, 1, 0), pltpu.roll(f, rows - 1, 0), coef0[0], coef0[1], coef0[2])
    return f[half : rows - half]


def evolve_rows(part, f0, codes, col0, mask, sea):
    rows, fields, width = part.shape
    branches = col0.shape[0]
    squashed = jnp.tanh(f0)
    top = lax.broadcasted_iota(jnp.int32, (fields, width), 0) == 0
    done = []
    for r in range(rows):
        code = codes[0, r : r + 1, :]
        gain = jnp.broadcast_to(col0[0], (fields, width))
        for b in range(1, branches):
            gain = jnp.where(code == b, col0[b], gain)
        value = part[r] + gain * squashed[r : r + 1, :] + jnp.where(top, f0[r : r + 1, :], 0.0)
        wet = jnp.where(sea, mask[0, r : r + 1, :].astype(F32), 1.0)
        done.append(value * wet)
    return done


def middle_kernel(
    offsets, groups, part, ns, flux, e1, e2, coef0, codes, col0, mask, w, src, tgt, x1, x2, surf, *rest
):
    outs, (blk, wide) = rest[: len(offsets)], rest[len(offsets) :]
    odd = lax.rem(lax.axis_index("tile"), 2) == 1
    sea = lax.axis_index("comp") >= 3 * groups // 4
    f0 = field0(ns, e1, e2, coef0, odd)
    rows = evolve_rows(part, f0, codes, col0, mask, sea)
    half = x1.shape[0]
    for i in range(half):
        x1[i] = jnp.where(odd, rows[i], rows[half + i])
        x2[i] = jnp.where(odd, rows[half + i], rows[i])
    for r, value in enumerate(rows):
        surf[r : r + 1, :] = value[:1]
    handed = jnp.where(sea, surf[...], flux[...])
    remap(handed, w, src, tgt, outs, offsets, groups, blk, wide)


def close_kernel(groups, part, ns, flux, e1, e2, coef0, codes, col0, mask, new_state, new_coupling):
    odd = lax.rem(lax.axis_index("tile"), 2) == 1
    sea = lax.axis_index("comp") >= 3 * groups // 4
    f0 = field0(ns, e1, e2, coef0, odd)
    rows = evolve_rows(part, f0, codes, col0, mask, sea)
    for r, value in enumerate(rows):
        new_state[0, :, r, :] = value
        new_coupling[0, r : r + 1, :] = jnp.where(sea, value[:1], flux[r : r + 1, :])


def call(kernel, name, outs, args, scratch=(), in_specs=None, flops=0, grid=()):
    moved = sum(a.size * a.dtype.itemsize for a in list(args) + list(outs))
    return pl.pallas_call(
        kernel,
        name=name,
        grid=grid,
        out_shape=outs,
        in_specs=in_specs or [VMEM] * len(args),
        out_specs=[VMEM] * len(outs),
        scratch_shapes=list(scratch),
        compiler_params=PARAMS,
        cost_estimate=pl.CostEstimate(flops=flops, bytes_accessed=moved, transcendentals=0),
    )(*args)


def on_device(
    state, coupling, land_mask, codes, mixing, courant, matrices, weights, sources, targets
):
    groups = lax.axis_size("comp")
    tiles = lax.axis_size("tile")
    offsets = partner_offsets(groups)
    _, fields, rows, width = state.shape
    _, margins, band, block = weights.shape
    count = rows * width // block
    half = rows // 2
    branches = matrices.shape[1]
    shape = jax.ShapeDtypeStruct

    m, c = mixing[0][:, None], courant[0][:, None]
    coef = jnp.stack([1.0 - 4.0 * m - c, m + c, m])
    coef0 = coef[:, :1]
    flat = matrices[0].reshape(branches * fields, fields)
    col0 = matrices[0][:, :, :1]
    flat = jnp.where(jnp.arange(fields)[None] == 0, 0.0, flat)
    high = lax.reduce_precision(flat, 8, 7)
    table = jnp.concatenate([high, high, flat - high], axis=1).astype(BF16)

    halves = [shape((half, fields, width), F32)] * 2
    payloads = [shape((count, block), F32)] * len(offsets)
    remap_scratch = [pltpu.VMEM((count, block), F32), pltpu.VMEM((margins * band, block), F32)]
    x1, x2, *sent = call(
        functools.partial(open_kernel, offsets, groups),
        "open",
        halves + payloads,
        (state, coupling, weights, sources, targets),
        remap_scratch,
    )
    surface, surface_spec = state, pl.BlockSpec((1, 1, rows, width), lambda i: (0, 0, 0, 0))
    for interval in range(INTERVALS):
        y2 = lax.ppermute(x2, "tile", outer_pairs(tiles))
        y1 = lax.ppermute(x1, "tile", inner_pairs(tiles))
        recs = [
            lax.ppermute(value, "comp", ring_pairs(groups, offset))
            for value, offset in zip(sent, offsets)
        ]
        ns, flux, d1, d2 = call(
            functools.partial(surface_kernel, groups, len(recs)),
            "surface",
            [shape((rows, width), F32)] * 2 + [shape((half, width), F32)] * 2,
            (*recs, surface, land_mask),
            [pltpu.VMEM((count, block), F32)],
            [VMEM] * len(recs) + [surface_spec, VMEM],
            grid=(1,),
        )
        e2 = lax.ppermute(d2, "tile", outer_pairs(tiles))
        e1 = lax.ppermute(d1, "tile", inner_pairs(tiles))
        (part,) = call(
            fields_kernel,
            "fields",
            [shape((rows, fields, width), F32)],
            (x1, x2, y1, y2, coef, table, codes),
            [pltpu.VMEM((rows + 2, fields, width), F32)],
            flops=4_000_000_000,
        )
        common = (part, ns, flux, e1, e2, coef0, codes, col0, land_mask)
        if interval < INTERVALS - 1:
            x1, x2, surface, *sent = call(
                functools.partial(middle_kernel, offsets, groups),
                "middle",
                halves + [shape((rows, width), F32)] + payloads,
                common + (weights, sources, targets),
                remap_scratch,
            )
            surface_spec = VMEM
        else:
            new_state, new_coupling = call(
                functools.partial(close_kernel, groups),
                "close",
                [shape(state.shape, F32), shape(coupling.shape, F32)],
                common,
            )
    return new_state, new_coupling


def solution(mesh):
    placed = (
        P("comp", None, "tile", None),
        P("comp", "tile", None),
        P("comp", "tile", None),
        P("comp", "tile", None),
        P("comp", None),
        P("comp", None),
        P("comp", None, None, None),
        P("comp", "tile", None, None),
        P("comp", "tile"),
        P("comp", "tile"),
    )
    return jax.shard_map(
        on_device,
        mesh=mesh,
        in_specs=placed,
        out_specs=(P("comp", None, "tile", None), P("comp", "tile", None)),
        check_vma=False,
    )
```

time: 71.7 us -> 45.1 us (0.63)
  waiting for transfers between devices: 24.8 us -> 11.9 us
  Pallas kernels: 0 us -> 7.68 us
  matrix products: 6.8 us -> 0 us
  other arithmetic: 6.29 us -> 0.11 us
  local copies, waits for them, and re-layouts: 10.4 us -> 5.73 us
  starting transfers between devices: 21.9 us -> 18.4 us
    ppermute x14, waiting for transfers between devices: 24.8 us -> 11.9 us  [the longest x2 6.57 us: on_device(): y2 = lax.ppermute(x2, 'tile', outer_pairs(tiles))]
    pallas_call x0 -> x7, Pallas kernels: none -> 7.68 us  [call(): pl.pallas_call(kernel, name=name, grid=grid, out_shape=outs, in_specs=in_...]
    dot_general x4 -> x0, matrix products: 6.8 us -> none  [the longest x2 5.28 us: on_device(): jnp.einsum('bij,jrw->birw', physics_table, jnp.tanh(diffused), precision=...]
    ppermute x14, starting transfers between devices: 21.9 us -> 18.4 us  [the longest x6 10.8 us: on_device(): lax.ppermute(value, 'comp', ring_pairs(groups, offset))]
    slice x28 -> x1, local copies, waits for them, and re-layouts: 2.94 us -> 0.01 us  [on_device(): coef0 = coef[:, :1]]
    gather x2 -> x0, local copies, waits for them, and re-layouts: 2.77 us -> none  [remap_local(): picked = jnp.take(blocks, source_list, axis=0).astype(jnp.float32)]
    unnamed x23 -> x28, local copies, waits for them, and re-layouts: 3.27 us -> 5.63 us
    unnamed x17 -> x0, other arithmetic: 2.26 us -> none
  transfers between devices with their start and end apart: 14 -> 14, of which waited for: 10 -> 5; matrix products, arithmetic and copies ran while one was open for 2% -> 0% of each run, Pallas kernels for 0% -> 8%
where the time goes in v1:
time: 45.1 us; the launch traced here: 44.7 us
  starting transfers between devices  18.4 us (41%)
  waiting for transfers between devices  11.9 us (26%)
  Pallas kernels  7.68 us (17%)
  local copies, waits for them, and re-layouts  5.73 us (13%)
  between operations  0.84 us (2%)
    ppermute x6, starting transfers between devices, on_device(): lax.ppermute(value, 'comp', ring_pairs(groups, offset))  10.8 us
    pallas_call x7, Pallas kernels, call(): pl.pallas_call(kernel, name=name, grid=grid, out_shape=outs, in_specs=in_...  7.68 us
    ppermute x2, waiting for transfers between devices, on_device(): y2 = lax.ppermute(x2, 'tile', outer_pairs(tiles))  6.57 us
    unnamed x28, local copies, waits for them, and re-layouts  5.63 us
    ppermute x2, starting transfers between devices, on_device(): y2 = lax.ppermute(x2, 'tile', outer_pairs(tiles))  4.19 us
    ppermute x6, waiting for transfers between devices, on_device(): lax.ppermute(value, 'comp', ring_pairs(groups, offset))  4.17 us
    ppermute x2, starting transfers between devices, on_device(): e2 = lax.ppermute(d2, 'tile', outer_pairs(tiles))  2.87 us
    ppermute x2, waiting for transfers between devices, on_device(): e2 = lax.ppermute(d2, 'tile', outer_pairs(tiles))  1.18 us
  transfers between devices with their start and end apart: 14, of which 5 were waited for; matrix products, arithmetic and copies ran while one was open for 0% of the time, Pallas kernels for 8%

profile of v1, /device:TPU:0, one launch (start us, length us, event | category | flops | bytes accessed | tf_op | source)
XLA Modules:
  0.0 44.7 jit_solution(3944076127947218553)
XLA Ops:
  0.6 1.1 %copy-done = f32[1,16,4,3072]{3,2,1,0:T(4,128)S(1)} copy-done((f32[1,16,4,3072]{3,2,1,0:T(4,128)S(1)}, f32[1,16,4,3072]{3,2,1,0:T(4,128)}, u32[]{:S(2)}) %copy-start) | copy-done | bytes 786456
  1.8 1.1 %copy-done.2 = bf16[1,288,8,128]{3,2,1,0:T(8,128)(2,1)S(1)} copy-done((bf16[1,288,8,128]{3,2,1,0:T(8,128)(2,1)S(1)}, bf16[1,288,8,128]{3,2,1,0:T(8,128)(2,1)}, u32[]{:S(2)}) %copy-start.2) | copy-done | bytes 589848
  2.8 0.8 %copy-done.7 = f32[1,4,3072]{2,1,0:T(4,128)S(1)} copy-done((f32[1,4,3072]{2,1,0:T(4,128)S(1)}, f32[1,4,3072]{2,1,0:T(4,128)}, u32[]{:S(2)}) %copy-start.7) | copy-done | bytes 49176
  3.6 0.7 %copy-done.8 = s32[1,288]{1,0:T(1,128)S(1)} copy-done((s32[1,288]{1,0:T(1,128)S(1)}, s32[1,288]{1,0:T(1,128)}, u32[]{:S(2)}) %copy-start.8) | copy-done | bytes 1176
  4.3 0.7 %copy-done.10 = s32[1,288]{1,0:T(1,128)S(1)} copy-done((s32[1,288]{1,0:T(1,128)S(1)}, s32[1,288]{1,0:T(1,128)}, u32[]{:S(2)}) %copy-start.10) | copy-done | bytes 1176
  5.0 1.0 %open.1 = (f32[2,16,3072]{2,1,0:T(8,128)S(1)}, f32[2,16,3072]{2,1,0:T(8,128)S(1)}, f32[96,128]{1,0:T(8,128)S(1)}, f32[96,128]{1,0:T(8,128)S(1)}, f32[96,128]{1,0:T(8,128)S(1)}) custom-call(f32[1,16,4,3072]{3,2,1,0:T(4,128)S(1)} %copy-done, f32[1,4,3072]{2,1,0:T(4,128)S(1)} %copy-done.7, bf16[1,288,8,128]{3,2,1,0:T(8,128)(2,1)S(1)} %copy-done.2, ...), custom_call_target="tpu_custom_call" | custom-call | bytes 2361600 | tf_op jit(solution)/shard_map/open/pallas_call | solution.py:210
  6.0 3.1 %collective-permute-start.2 = (f32[96,128]{1,0:T(8,128)S(1)}, f32[96,128]{1,0:T(8,128)S(1)}, u32[]{:S(2)}, u32[]{:S(2)}) collective-permute-start(f32[96,128]{1,0:T(8,128)S(1)} %get-tuple-element.23), channel_id=1, source_target_pairs={{0,8},{8,16},{16,24},{24,0},{1,9},{9,17},{17,25},{25,1},{2,10},{10... | collective-permute-start | bytes 147464 | tf_op jit(solution)/shard_map/ppermute | solution.py:260
  9.1 2.6 %collective-permute-start.3 = (f32[96,128]{1,0:T(8,128)S(1)}, f32[96,128]{1,0:T(8,128)S(1)}, u32[]{:S(2)}, u32[]{:S(2)}) collective-permute-start(f32[96,128]{1,0:T(8,128)S(1)} %get-tuple-element.24), channel_id=1, source_target_pairs={{0,16},{8,24},{16,0},{24,8},{1,17},{9,25},{17,1},{25,9},{2,18},{10... | collective-permute-start | bytes 147464 | tf_op jit(solution)/shard_map/ppermute | solution.py:260
  11.7 1.3 %collective-permute-start.4 = (f32[96,128]{1,0:T(8,128)S(1)}, f32[96,128]{1,0:T(8,128)S(1)}, u32[]{:S(2)}, u32[]{:S(2)}) collective-permute-start(f32[96,128]{1,0:T(8,128)S(1)} %get-tuple-element.25), channel_id=1, source_target_pairs={{0,24},{8,0},{16,8},{24,16},{1,25},{9,1},{17,9},{25,17},{2,26},{10... | collective-permute-start | bytes 147464 | tf_op jit(solution)/shard_map/ppermute | solution.py:260
  13.1 2.6 %collective-permute-start.1 = (f32[2,16,3072]{2,1,0:T(8,128)S(1)}, f32[2,16,3072]{2,1,0:T(8,128)S(1)}, u32[]{:S(2)}, u32[]{:S(2)}) collective-permute-start(f32[2,16,3072]{2,1,0:T(8,128)S(1)} %get-tuple-element.22.x2), channel_id=1, source_target_pairs={{0,7},{1,2},{2,1},{3,4},{4,3},{5,6},{6,5},{7,0},{8,15},{9,10},{10,... | collective-permute-start | bytes 1179656 | tf_op jit(solution)/shard_map/ppermute | solution.py:257
  15.7 0.1 pad_maximum_fusion.table
  15.8 0.6 %copy-done.12 = f32[1,16]{1,0:T(1,128)S(1)} copy-done((f32[1,16]{1,0:T(1,128)S(1)}, f32[1,16]{1,0:T(1,128)}, u32[]{:S(2)}) %copy-start.12) | copy-done | bytes 88
  16.3 0.1 copy.20.coef
  16.6 0.1 collective-permute-start.5
  16.6 2.0 %collective-permute-start.6 = (f32[2,3072]{1,0:T(2,128)S(1)}, f32[2,3072]{1,0:T(2,128)S(1)}, u32[]{:S(2)}, u32[]{:S(2)}) collective-permute-start(f32[2,3072]{1,0:T(2,128)S(1)} %get-tuple-element.29), channel_id=1, source_target_pairs={{0,7},{1,2},{2,1},{3,4},{4,3},{5,6},{6,5},{7,0},{8,15},{9,10},{10,... | collective-permute-start | bytes 73736 | tf_op jit(solution)/shard_map/ppermute | solution.py:272
  18.6 6.0 %collective-permute-done.1.y2 = f32[2,16,3072]{2,1,0:T(8,128)S(1)} collective-permute-done((f32[2,16,3072]{2,1,0:T(8,128)S(1)}, f32[2,16,3072]{2,1,0:T(8,128)S(1)}, u32[]{:S(2)}, u32[]{:S(2)}) %collective-permute-start.1) | collective-permute-done | bytes 393248 | tf_op jit(solution)/shard_map/ppermute | solution.py:257
  24.7 1.7 %fields.2.part = f32[4,16,3072]{2,1,0:T(8,128)S(1)} custom-call(f32[2,16,3072]{2,1,0:T(8,128)S(1)} %get-tuple-element.21.x1, f32[2,16,3072]{2,1,0:T(8,128)S(1)} %get-tuple-element.22.x2, f32[2,16,3072]{2,1,0:T(8,128)S(1)} %collective-permute-done.y1, f32[2,16,3072]{2,1,0:T(8,128)S(1)} %collective-permute-done.1.y2, f32[3,16,1]{2,1,0:T(8,128)S(1)} %copy.20.coef, ...), custom_call_target="tpu_custom_call" | custom-call | flops 4000000000 | bytes 2414784 | tf_op jit(solution)/shard_map/fields/pallas_call | solution.py:210
  26.4 0.6 %copy-done.9 = s32[1,288]{1,0:T(1,128)S(1)} copy-done((s32[1,288]{1,0:T(1,128)S(1)}, s32[1,288]{1,0:T(1,128)}, u32[]{:S(2)}) %copy-start.9) | copy-done | bytes 1176
  27.1 1.5 %middle.1 = (f32[2,16,3072]{2,1,0:T(8,128)S(1)}, f32[2,16,3072]{2,1,0:T(8,128)S(1)}, f32[4,3072]{1,0:T(4,128)S(1)}, f32[96,128]{1,0:T(8,128)S(1)}, f32[96,128]{1,0:T(8,128)S(1)}, /*index=5*/f32[96,128]{1,0:T(8,128)S(1)}) custom-call(f32[4,16,3072]{2,1,0:T(8,128)S(1)} %fields.2.part, f32[4,3072]{1,0:T(4,128)S(1)} %get-tuple-element.26.ns, ...), custom_call_target="tpu_custom_call" | custom-call | bytes 2607628 | tf_op jit(solution)/shard_map/middle/pallas_call | solution.py:210
  28.5 0.4 collective-permute-start.7
  28.9 1.6 %collective-permute-start.8 = (f32[2,16,3072]{2,1,0:T(8,128)S(1)}, f32[2,16,3072]{2,1,0:T(8,128)S(1)}, u32[]{:S(2)}, u32[]{:S(2)}) collective-permute-start(f32[2,16,3072]{2,1,0:T(8,128)S(1)} %get-tuple-element.31.x2), channel_id=1, source_target_pairs={{0,7},{1,2},{2,1},{3,4},{4,3},{5,6},{6,5},{7,0},{8,15},{9,10},{10,... | collective-permute-start | bytes 1179656 | tf_op jit(solution)/shard_map/ppermute | solution.py:257
  30.6 0.7 %collective-permute-start.9 = (f32[96,128]{1,0:T(8,128)S(1)}, f32[96,128]{1,0:T(8,128)S(1)}, u32[]{:S(2)}, u32[]{:S(2)}) collective-permute-start(f32[96,128]{1,0:T(8,128)S(1)} %get-tuple-element.32), channel_id=1, source_target_pairs={{0,8},{8,16},{16,24},{24,0},{1,9},{9,17},{17,25},{25,1},{2,10},{10... | collective-permute-start | bytes 147464 | tf_op jit(solution)/shard_map/ppermute | solution.py:260
  31.3 0.3 collective-permute-start.10
  31.6 2.8 %collective-permute-start.11 = (f32[96,128]{1,0:T(8,128)S(1)}, f32[96,128]{1,0:T(8,128)S(1)}, u32[]{:S(2)}, u32[]{:S(2)}) collective-permute-start(f32[96,128]{1,0:T(8,128)S(1)} %get-tuple-element.34), channel_id=1, source_target_pairs={{0,24},{8,0},{16,8},{24,16},{1,25},{9,1},{17,9},{25,17},{2,26},{10... | collective-permute-start | bytes 147464 | tf_op jit(solution)/shard_map/ppermute | solution.py:260
  34.4 2.6 %collective-permute-done.9.refs_0_ = f32[96,128]{1,0:T(8,128)S(1)} collective-permute-done((f32[96,128]{1,0:T(8,128)S(1)}, f32[96,128]{1,0:T(8,128)S(1)}, u32[]{:S(2)}, u32[]{:S(2)}) %collective-permute-start.9) | collective-permute-done | bytes 49184 | tf_op jit(solution)/shard_map/ppermute | solution.py:260
  37.0 1.6 %collective-permute-done.10.refs_1_ = f32[96,128]{1,0:T(8,128)S(1)} collective-permute-done((f32[96,128]{1,0:T(8,128)S(1)}, f32[96,128]{1,0:T(8,128)S(1)}, u32[]{:S(2)}, u32[]{:S(2)}) %collective-permute-start.10) | collective-permute-done | bytes 49184 | tf_op jit(solution)/shard_map/ppermute | solution.py:260
  38.6 0.1 collective-permute-start.12
  38.7 0.9 %collective-permute-start.13 = (f32[2,3072]{1,0:T(2,128)S(1)}, f32[2,3072]{1,0:T(2,128)S(1)}, u32[]{:S(2)}, u32[]{:S(2)}) collective-permute-start(f32[2,3072]{1,0:T(2,128)S(1)} %get-tuple-element.39), channel_id=1, source_target_pairs={{0,7},{1,2},{2,1},{3,4},{4,3},{5,6},{6,5},{7,0},{8,15},{9,10},{10,... | collective-permute-start | bytes 73736 | tf_op jit(solution)/shard_map/ppermute | solution.py:272
  39.6 0.5 %collective-permute-done.8.y2 = f32[2,16,3072]{2,1,0:T(8,128)S(1)} collective-permute-done((f32[2,16,3072]{2,1,0:T(8,128)S(1)}, f32[2,16,3072]{2,1,0:T(8,128)S(1)}, u32[]{:S(2)}, u32[]{:S(2)}) %collective-permute-start.8) | collective-permute-done | bytes 393248 | tf_op jit(solution)/shard_map/ppermute | solution.py:257
  40.1 1.6 %fields.3.part = f32[4,16,3072]{2,1,0:T(8,128)S(1)} custom-call(f32[2,16,3072]{2,1,0:T(8,128)S(1)} %get-tuple-element.30.x1, f32[2,16,3072]{2,1,0:T(8,128)S(1)} %get-tuple-element.31.x2, f32[2,16,3072]{2,1,0:T(8,128)S(1)} %collective-permute-done.7.y1, f32[2,16,3072]{2,1,0:T(8,128)S(1)} %collective-permute-done.8.y2, f32[3,16,1]{2,1,0:T(8,128)S(1)} %copy.20.coef, ...), custom_call_target="tpu_custom_call" | custom-call | flops 4000000000 | bytes 2414784 | tf_op jit(solution)/shard_map/fields/pallas_call | solution.py:210
  41.7 1.2 %collective-permute-done.13.e2 = f32[2,3072]{1,0:T(2,128)S(1)} collective-permute-done((f32[2,3072]{1,0:T(2,128)S(1)}, f32[2,3072]{1,0:T(2,128)S(1)}, u32[]{:S(2)}, u32[]{:S(2)}) %collective-permute-start.13) | collective-permute-done | bytes 24608 | tf_op jit(solution)/shard_map/ppermute | solution.py:272
  42.9 1.8 %close.1 = (f32[1,16,4,3072]{3,2,1,0:T(4,128)}, f32[1,4,3072]{2,1,0:T(4,128)}) custom-call(f32[4,16,3072]{2,1,0:T(8,128)S(1)} %fields.3.part, f32[4,3072]{1,0:T(4,128)S(1)} %get-tuple-element.36.ns, f32[4,3072]{1,0:T(4,128)S(1)} %get-tuple-element.37.flux, f32[2,3072]{1,0:T(2,128)S(1)} %collective-permute-done.12.e1, ...), custom_call_target="tpu_custom_call" | custom-call | bytes 1868044 | tf_op jit(solution)/shard_map/close/pallas_call | solution.py:210
  (38 shorter events, 0.2 us)
Async XLA Ops:
  0.6 1.1 %copy-start = (f32[1,16,4,3072]{3,2,1,0:T(4,128)S(1)}, f32[1,16,4,3072]{3,2,1,0:T(4,128)}, u32[]{:S(2)}) copy-start(f32[1,16,4,3072]{3,2,1,0:T(4,128)} %refs_3_.1) | copy-start | bytes 2359300
  1.8 1.1 %copy-start.2 = (bf16[1,288,8,128]{3,2,1,0:T(8,128)(2,1)S(1)}, bf16[1,288,8,128]{3,2,1,0:T(8,128)(2,1)}, u32[]{:S(2)}) copy-start(bf16[1,288,8,128]{3,2,1,0:T(8,128)(2,1)} %w.3) | copy-start | bytes 1769476
  2.8 0.8 %copy-start.7 = (f32[1,4,3072]{2,1,0:T(4,128)S(1)}, f32[1,4,3072]{2,1,0:T(4,128)}, u32[]{:S(2)}) copy-start(f32[1,4,3072]{2,1,0:T(4,128)} %coupling.1) | copy-start | bytes 147460
  3.6 0.7 %copy-start.8 = (s32[1,288]{1,0:T(1,128)S(1)}, s32[1,288]{1,0:T(1,128)}, u32[]{:S(2)}) copy-start(s32[1,288]{1,0:T(1,128)} %src.3) | copy-start | bytes 3460
  4.3 0.7 %copy-start.10 = (s32[1,288]{1,0:T(1,128)S(1)}, s32[1,288]{1,0:T(1,128)}, u32[]{:S(2)}) copy-start(s32[1,288]{1,0:T(1,128)} %tgt.3) | copy-start | bytes 3460
  5.0 10.6 %copy-start.5 = (f32[1,4,16,16]{3,2,1,0:T(8,128)S(1)}, f32[1,4,16,16]{3,2,1,0:T(8,128)}, u32[]{:S(2)}) copy-start(f32[1,4,16,16]{3,2,1,0:T(8,128)} %param.16) | copy-start | bytes 12292
  5.0 11.5 %copy-start.1 = (f32[1,16,4,3072]{3,2,1,0:T(4,128)S(1)}, f32[1,16,4,3072]{3,2,1,0:T(4,128)}, u32[]{:S(2)}) copy-start(f32[1,16,4,3072]{3,2,1,0:T(4,128)} %refs_3_.1) | copy-start | bytes 2359300
  6.0 10.4 %collective-permute-start.2 = (f32[96,128]{1,0:T(8,128)S(1)}, f32[96,128]{1,0:T(8,128)S(1)}, u32[]{:S(2)}, u32[]{:S(2)}) collective-permute-start(f32[96,128]{1,0:T(8,128)S(1)} %get-tuple-element.23), channel_id=1, source_target_pairs={{0,8},{8,16},{16,24},{24,0},{1,9},{9,17},{17,25},{25,1},{2,10},{10... | collective-permute-start | bytes 147464 | tf_op jit(solution)/shard_map/ppermute | solution.py:260
  9.1 7.3 %collective-permute-start.3 = (f32[96,128]{1,0:T(8,128)S(1)}, f32[96,128]{1,0:T(8,128)S(1)}, u32[]{:S(2)}, u32[]{:S(2)}) collective-permute-start(f32[96,128]{1,0:T(8,128)S(1)} %get-tuple-element.24), channel_id=1, source_target_pairs={{0,16},{8,24},{16,0},{24,8},{1,17},{9,25},{17,1},{25,9},{2,18},{10... | collective-permute-start | bytes 147464 | tf_op jit(solution)/shard_map/ppermute | solution.py:260
  11.7 4.8 %collective-permute-start.4 = (f32[96,128]{1,0:T(8,128)S(1)}, f32[96,128]{1,0:T(8,128)S(1)}, u32[]{:S(2)}, u32[]{:S(2)}) collective-permute-start(f32[96,128]{1,0:T(8,128)S(1)} %get-tuple-element.25), channel_id=1, source_target_pairs={{0,24},{8,0},{16,8},{24,16},{1,25},{9,1},{17,9},{25,17},{2,26},{10... | collective-permute-start | bytes 147464 | tf_op jit(solution)/shard_map/ppermute | solution.py:260
  13.1 5.6 %collective-permute-start = (f32[2,16,3072]{2,1,0:T(8,128)S(1)}, f32[2,16,3072]{2,1,0:T(8,128)S(1)}, u32[]{:S(2)}, u32[]{:S(2)}) collective-permute-start(f32[2,16,3072]{2,1,0:T(8,128)S(1)} %get-tuple-element.21.x1), channel_id=1, source_target_pairs={{0,1},{1,0},{2,3},{3,2},{4,5},{5,4},{6,7},{7,6},{8,9},{9,8},{10,11... | collective-permute-start | bytes 1179656 | tf_op jit(solution)/shard_map/ppermute | solution.py:258
  13.1 11.6 %collective-permute-start.1 = (f32[2,16,3072]{2,1,0:T(8,128)S(1)}, f32[2,16,3072]{2,1,0:T(8,128)S(1)}, u32[]{:S(2)}, u32[]{:S(2)}) collective-permute-start(f32[2,16,3072]{2,1,0:T(8,128)S(1)} %get-tuple-element.22.x2), channel_id=1, source_target_pairs={{0,7},{1,2},{2,1},{3,4},{4,3},{5,6},{6,5},{7,0},{8,15},{9,10},{10,... | collective-permute-start | bytes 1179656 | tf_op jit(solution)/shard_map/ppermute | solution.py:257
  15.6 0.9 %copy-start.4 = (s32[1,4,3072]{2,1,0:T(4,128)S(1)}, s32[1,4,3072]{2,1,0:T(4,128)}, u32[]{:S(2)}) copy-start(s32[1,4,3072]{2,1,0:T(4,128)} %mask.3) | copy-start | bytes 147460
  15.6 0.7 %copy-start.12 = (f32[1,16]{1,0:T(1,128)S(1)}, f32[1,16]{1,0:T(1,128)}, u32[]{:S(2)}) copy-start(f32[1,16]{1,0:T(1,128)} %param.14) | copy-start | bytes 196
  15.7 0.7 %copy-start.13 = (f32[1,16]{1,0:T(1,128)S(1)}, f32[1,16]{1,0:T(1,128)}, u32[]{:S(2)}) copy-start(f32[1,16]{1,0:T(1,128)} %param.15) | copy-start | bytes 196
  16.5 8.2 %copy-start.6 = (s32[1,4,3072]{2,1,0:T(4,128)S(1)}, s32[1,4,3072]{2,1,0:T(4,128)}, u32[]{:S(2)}) copy-start(s32[1,4,3072]{2,1,0:T(4,128)} %codes.7) | copy-start | bytes 147460
  16.6 9.8 %collective-permute-start.5 = (f32[2,3072]{1,0:T(2,128)S(1)}, f32[2,3072]{1,0:T(2,128)S(1)}, u32[]{:S(2)}, u32[]{:S(2)}) collective-permute-start(f32[2,3072]{1,0:T(2,128)S(1)} %get-tuple-element.28), channel_id=1, source_target_pairs={{0,1},{1,0},{2,3},{3,2},{4,5},{5,4},{6,7},{7,6},{8,9},{9,8},{10,11... | collective-permute-start | bytes 73736 | tf_op jit(solution)/shard_map/ppermute | solution.py:273
  16.6 9.8 %copy-start.3 = (bf16[1,288,8,128]{3,2,1,0:T(8,128)(2,1)S(1)}, bf16[1,288,8,128]{3,2,1,0:T(8,128)(2,1)}, u32[]{:S(2)}) copy-start(bf16[1,288,8,128]{3,2,1,0:T(8,128)(2,1)} %w.3) | copy-start | bytes 1769476
  16.6 9.7 %collective-permute-start.6 = (f32[2,3072]{1,0:T(2,128)S(1)}, f32[2,3072]{1,0:T(2,128)S(1)}, u32[]{:S(2)}, u32[]{:S(2)}) collective-permute-start(f32[2,3072]{1,0:T(2,128)S(1)} %get-tuple-element.29), channel_id=1, source_target_pairs={{0,7},{1,2},{2,1},{3,4},{4,3},{5,6},{6,5},{7,0},{8,15},{9,10},{10,... | collective-permute-start | bytes 73736 | tf_op jit(solution)/shard_map/ppermute | solution.py:272
  26.4 0.7 %copy-start.9 = (s32[1,288]{1,0:T(1,128)S(1)}, s32[1,288]{1,0:T(1,128)}, u32[]{:S(2)}) copy-start(s32[1,288]{1,0:T(1,128)} %src.3) | copy-start | bytes 3460
  26.4 0.7 %copy-start.11 = (s32[1,288]{1,0:T(1,128)S(1)}, s32[1,288]{1,0:T(1,128)}, u32[]{:S(2)}) copy-start(s32[1,288]{1,0:T(1,128)} %tgt.3) | copy-start | bytes 3460
  28.5 11.1 %collective-permute-start.7 = (f32[2,16,3072]{2,1,0:T(8,128)S(1)}, f32[2,16,3072]{2,1,0:T(8,128)S(1)}, u32[]{:S(2)}, u32[]{:S(2)}) collective-permute-start(f32[2,16,3072]{2,1,0:T(8,128)S(1)} %get-tuple-element.30.x1), channel_id=1, source_target_pairs={{0,1},{1,0},{2,3},{3,2},{4,5},{5,4},{6,7},{7,6},{8,9},{9,8},{10,11... | collective-permute-start | bytes 1179656 | tf_op jit(solution)/shard_map/ppermute | solution.py:258
  28.9 11.2 %collective-permute-start.8 = (f32[2,16,3072]{2,1,0:T(8,128)S(1)}, f32[2,16,3072]{2,1,0:T(8,128)S(1)}, u32[]{:S(2)}, u32[]{:S(2)}) collective-permute-start(f32[2,16,3072]{2,1,0:T(8,128)S(1)} %get-tuple-element.31.x2), channel_id=1, source_target_pairs={{0,7},{1,2},{2,1},{3,4},{4,3},{5,6},{6,5},{7,0},{8,15},{9,10},{10,... | collective-permute-start | bytes 1179656 | tf_op jit(solution)/shard_map/ppermute | solution.py:257
  30.6 6.4 %collective-permute-start.9 = (f32[96,128]{1,0:T(8,128)S(1)}, f32[96,128]{1,0:T(8,128)S(1)}, u32[]{:S(2)}, u32[]{:S(2)}) collective-permute-start(f32[96,128]{1,0:T(8,128)S(1)} %get-tuple-element.32), channel_id=1, source_target_pairs={{0,8},{8,16},{16,24},{24,0},{1,9},{9,17},{17,25},{25,1},{2,10},{10... | collective-permute-start | bytes 147464 | tf_op jit(solution)/shard_map/ppermute | solution.py:260
  31.3 7.3 %collective-permute-start.10 = (f32[96,128]{1,0:T(8,128)S(1)}, f32[96,128]{1,0:T(8,128)S(1)}, u32[]{:S(2)}, u32[]{:S(2)}) collective-permute-start(f32[96,128]{1,0:T(8,128)S(1)} %get-tuple-element.33), channel_id=1, source_target_pairs={{0,16},{8,24},{16,0},{24,8},{1,17},{9,25},{17,1},{25,9},{2,18},{10... | collective-permute-start | bytes 147464 | tf_op jit(solution)/shard_map/ppermute | solution.py:260
  31.6 7.0 %collective-permute-start.11 = (f32[96,128]{1,0:T(8,128)S(1)}, f32[96,128]{1,0:T(8,128)S(1)}, u32[]{:S(2)}, u32[]{:S(2)}) collective-permute-start(f32[96,128]{1,0:T(8,128)S(1)} %get-tuple-element.34), channel_id=1, source_target_pairs={{0,24},{8,0},{16,8},{24,16},{1,25},{9,1},{17,9},{25,17},{2,26},{10... | collective-permute-start | bytes 147464 | tf_op jit(solution)/shard_map/ppermute | solution.py:260
  38.6 3.1 %collective-permute-start.12 = (f32[2,3072]{1,0:T(2,128)S(1)}, f32[2,3072]{1,0:T(2,128)S(1)}, u32[]{:S(2)}, u32[]{:S(2)}) collective-permute-start(f32[2,3072]{1,0:T(2,128)S(1)} %get-tuple-element.38), channel_id=1, source_target_pairs={{0,1},{1,0},{2,3},{3,2},{4,5},{5,4},{6,7},{7,6},{8,9},{9,8},{10,11... | collective-permute-start | bytes 73736 | tf_op jit(solution)/shard_map/ppermute | solution.py:273
  38.7 4.2 %collective-permute-start.13 = (f32[2,3072]{1,0:T(2,128)S(1)}, f32[2,3072]{1,0:T(2,128)S(1)}, u32[]{:S(2)}, u32[]{:S(2)}) collective-permute-start(f32[2,3072]{1,0:T(2,128)S(1)} %get-tuple-element.39), channel_id=1, source_target_pairs={{0,7},{1,2},{2,1},{3,4},{4,3},{5,6},{6,5},{7,0},{8,15},{9,10},{10,... | collective-permute-start | bytes 73736 | tf_op jit(solution)/shard_map/ppermute | solution.py:272

commit v2 on v1

--- a/solution.py
+++ b/solution.py
@@ -47,44 +47,84 @@
     return high, low
 
 
-def remap(handed, w_ref, src_ref, tgt_ref, out_refs, offsets, groups, blk_ref, wide_ref):
+def payload(handed, wide_ref, pick_ref, chosen_ref, out_refs, blk_ref):
     rows, width = handed.shape
-    block = w_ref.shape[-1]
+    count, block = blk_ref.shape
     per_row = width // block
-    count = rows * per_row
-    margins, band = w_ref.shape[1], w_ref.shape[2]
+    margins = pick_ref.shape[1]
+    band = wide_ref.shape[0] // margins
     for c in range(per_row):
         blk_ref[pl.ds(c, rows, stride=per_row), :] = handed[:, c * block : (c + 1) * block]
-    blocks = blk_ref[...].astype(BF16)
-    pick = (lax.broadcasted_iota(jnp.int32, (count, margins), 0) == src_ref[...]).astype(F32).astype(BF16)
-    picked = lax.dot_general(pick, blocks, (((0,), (0,)), ((), ())), preferred_element_type=F32)
-    wide_ref[...] = w_ref[0].reshape(margins * band, block).astype(F32)
+    picked = lax.dot_general(
+        pick_ref[...], blk_ref[...].astype(BF16), (((0,), (0,)), ((), ())), preferred_element_type=F32
+    )
     contrib = wide_ref[pl.ds(0, margins, stride=band), :] * picked
     for j in range(1, band):
         turned = pltpu.roll(picked, block - j, 1)
         contrib = contrib + wide_ref[pl.ds(j, margins, stride=band), :] * turned
     high, low = split_high_low(contrib)
     both = jnp.concatenate([high, low], axis=0)
+    for n, out_ref in enumerate(out_refs):
+        out_ref[...] = jnp.dot(chosen_ref[n], both, preferred_element_type=F32)
+
+
+def column(row):
+    n = row.shape[1]
+    diagonal = lax.broadcasted_iota(jnp.int32, (n, n), 0) == lax.broadcasted_iota(jnp.int32, (n, n), 1)
+    return jnp.sum(jnp.where(diagonal, row, 0.0), axis=1, keepdims=True)
+
+
+def open_kernel(offsets, groups, *refs):
+    args, refs = refs[:10], refs[10:]
+    state, coupling, mask, codes, mixing, courant, matrices, weights, sources, targets = args
+    x1, x2, surface, mask_out, codes_out, coef, table, col0, wide, pick, chosen, *refs = refs
+    outs, refs = refs[: len(offsets)], refs[len(offsets) :]
+    state_v, coupling_v, weights_v, mixing_v, courant_v, matrices_v, sources_v, targets_v, blk, sems = refs
+    pairs = (
+        (coupling, coupling_v),
+        (sources, sources_v),
+        (targets, targets_v),
+        (weights, weights_v),
+        (state, state_v),
+        (mixing, mixing_v),
+        (courant, courant_v),
+        (matrices, matrices_v),
+        (mask, mask_out),
+        (codes, codes_out),
+    )
+    copies = [pltpu.make_async_copy(src, dst, sems.at[n]) for n, (src, dst) in enumerate(pairs)]
+    for copy in copies:
+        copy.start()
+    for copy in copies[:4]:
+        copy.wait()
+    count, margins = pick.shape
+    block = blk.shape[1]
+    slot = lax.broadcasted_iota(jnp.int32, (count, margins), 0)
+    pick[...] = (slot == sources_v[...]).astype(F32).astype(BF16)
     me = lax.axis_index("comp")
-    slot = lax.broadcasted_iota(jnp.int32, (count, margins), 0)
-    targets = tgt_ref[...]
-    for out_ref, offset in zip(out_refs, offsets):
+    for n, offset in enumerate(offsets):
         base = lax.rem(me + offset, groups) * count
-        chosen = (targets == slot + base).astype(F32).astype(BF16)
-        out_ref[...] = jnp.dot(
-            jnp.concatenate([chosen, chosen], axis=1), both, preferred_element_type=F32
-        )
-
-
-def open_kernel(offsets, groups, state, coupling, w, src, tgt, x1, x2, *rest):
-    outs, (blk, wide) = rest[: len(offsets)], rest[len(offsets) :]
+        hit = (targets_v[...] == slot + base).astype(F32).astype(BF16)
+        chosen[n] = jnp.concatenate([hit, hit], axis=1)
+    wide[...] = weights_v[0].reshape(wide.shape).astype(F32)
+    payload(coupling_v[0], wide, pick, chosen, outs, blk)
+    for copy in copies[4:]:
+        copy.wait()
     odd = lax.rem(lax.axis_index("tile"), 2) == 1
     half = x1.shape[0]
     for i in range(half):
-        head, tail = state[0, :, i, :], state[0, :, half + i, :]
+        head, tail = state_v[0, :, i, :], state_v[0, :, half + i, :]
         x1[i] = jnp.where(odd, head, tail)
         x2[i] = jnp.where(odd, tail, head)
-    remap(coupling[0], w, src, tgt, outs, offsets, groups, blk, wide)
+    surface[...] = state_v[0, 0]
+    m, c = column(mixing_v[...]), column(courant_v[...])
+    coef[0], coef[1], coef[2] = 1.0 - 4.0 * m - c, m + c, m
+    branches, fields = matrices_v.shape[1:3]
+    flat = matrices_v[0].reshape(branches * fields, fields)
+    col0[...] = flat[:, :1].reshape(branches, fields, 1)
+    flat = jnp.where(lax.broadcasted_iota(jnp.int32, flat.shape, 1) == 0, 0.0, flat)
+    high, low = split_high_low(flat)
+    table[...] = jnp.concatenate([high, high, low], axis=1)
 
 
 def surface_kernel(groups, n_rec, *refs):
@@ -101,7 +141,7 @@
     received = jnp.concatenate(
         [blk[pl.ds(c, rows, stride=per_row), :] for c in range(per_row)], axis=1
     )
-    surface = surface_ref[...].reshape(rows, width)
+    surface = surface_ref[...]
     flux = mask_ref[0].astype(F32) * EXCHANGE * (received - surface)
     new = surface + jnp.where(air, flux, -OCEAN_SHARE * received)
     ns_ref[...] = new
@@ -148,7 +188,8 @@
         part[r] = jnp.where(keep, f, 0.0) + tendency
 
 
-def field0(ns, e1, e2, coef0, odd):
+def field0(ns, e1, e2, coef, odd):
+    c0, cu, m = coef[0, :1], coef[1, :1], coef[2, :1]
     half = e1.shape[0]
     first, last = e1[...], e2[...]
     f = jnp.concatenate(
@@ -156,7 +197,7 @@
     )
     rows = f.shape[0]
     for _ in range(SUBSTEPS):
-        f = substep(f, pltpu.roll(f, 1, 0), pltpu.roll(f, rows - 1, 0), coef0[0], coef0[1], coef0[2])
+        f = substep(f, pltpu.roll(f, 1, 0), pltpu.roll(f, rows - 1, 0), c0, cu, m)
     return f[half : rows - half]
 
 
@@ -178,12 +219,12 @@
 
 
 def middle_kernel(
-    offsets, groups, part, ns, flux, e1, e2, coef0, codes, col0, mask, w, src, tgt, x1, x2, surf, *rest
+    groups, part, ns, flux, e1, e2, coef, codes, col0, mask, wide, pick, chosen, x1, x2, surf, *rest
 ):
-    outs, (blk, wide) = rest[: len(offsets)], rest[len(offsets) :]
+    outs, blk = rest[:-1], rest[-1]
     odd = lax.rem(lax.axis_index("tile"), 2) == 1
     sea = lax.axis_index("comp") >= 3 * groups // 4
-    f0 = field0(ns, e1, e2, coef0, odd)
+    f0 = field0(ns, e1, e2, coef, odd)
     rows = evolve_rows(part, f0, codes, col0, mask, sea)
     half = x1.shape[0]
     for i in range(half):
@@ -192,25 +233,24 @@
     for r, value in enumerate(rows):
         surf[r : r + 1, :] = value[:1]
     handed = jnp.where(sea, surf[...], flux[...])
-    remap(handed, w, src, tgt, outs, offsets, groups, blk, wide)
-
-
-def close_kernel(groups, part, ns, flux, e1, e2, coef0, codes, col0, mask, new_state, new_coupling):
+    payload(handed, wide, pick, chosen, outs, blk)
+
+
+def close_kernel(groups, part, ns, flux, e1, e2, coef, codes, col0, mask, new_state, new_coupling):
     odd = lax.rem(lax.axis_index("tile"), 2) == 1
     sea = lax.axis_index("comp") >= 3 * groups // 4
-    f0 = field0(ns, e1, e2, coef0, odd)
+    f0 = field0(ns, e1, e2, coef, odd)
     rows = evolve_rows(part, f0, codes, col0, mask, sea)
     for r, value in enumerate(rows):
         new_state[0, :, r, :] = value
         new_coupling[0, r : r + 1, :] = jnp.where(sea, value[:1], flux[r : r + 1, :])
 
 
-def call(kernel, name, outs, args, scratch=(), in_specs=None, flops=0, grid=()):
+def call(kernel, name, outs, args, scratch=(), in_specs=None, flops=0):
     moved = sum(a.size * a.dtype.itemsize for a in list(args) + list(outs))
     return pl.pallas_call(
         kernel,
         name=name,
-        grid=grid,
         out_shape=outs,
         in_specs=in_specs or [VMEM] * len(args),
         out_specs=[VMEM] * len(outs),
@@ -233,26 +273,31 @@
     branches = matrices.shape[1]
     shape = jax.ShapeDtypeStruct
 
-    m, c = mixing[0][:, None], courant[0][:, None]
-    coef = jnp.stack([1.0 - 4.0 * m - c, m + c, m])
-    coef0 = coef[:, :1]
-    flat = matrices[0].reshape(branches * fields, fields)
-    col0 = matrices[0][:, :, :1]
-    flat = jnp.where(jnp.arange(fields)[None] == 0, 0.0, flat)
-    high = lax.reduce_precision(flat, 8, 7)
-    table = jnp.concatenate([high, high, flat - high], axis=1).astype(BF16)
-
     halves = [shape((half, fields, width), F32)] * 2
     payloads = [shape((count, block), F32)] * len(offsets)
-    remap_scratch = [pltpu.VMEM((count, block), F32), pltpu.VMEM((margins * band, block), F32)]
-    x1, x2, *sent = call(
+    blocks = pltpu.VMEM((count, block), F32)
+    tables = [
+        shape(land_mask.shape, jnp.int32),
+        shape(codes.shape, jnp.int32),
+        shape((3, fields, 1), F32),
+        shape((branches * fields, 3 * fields), BF16),
+        shape((branches, fields, 1), F32),
+        shape((margins * band, block), F32),
+        shape((count, margins), BF16),
+        shape((len(offsets), count, 2 * margins), BF16),
+    ]
+    args = (
+        state, coupling, land_mask, codes, mixing, courant, matrices, weights, sources, targets
+    )
+    staged = (state, coupling, weights, mixing, courant, matrices, sources, targets)
+    x1, x2, surface, mask, codes, coef, table, col0, wide, pick, chosen, *sent = call(
         functools.partial(open_kernel, offsets, groups),
         "open",
-        halves + payloads,
-        (state, coupling, weights, sources, targets),
-        remap_scratch,
-    )
-    surface, surface_spec = state, pl.BlockSpec((1, 1, rows, width), lambda i: (0, 0, 0, 0))
+        halves + [shape((rows, width), F32)] + tables + payloads,
+        [pltpu.with_memory_space_constraint(a, pltpu.HBM) for a in args],
+        [pltpu.VMEM(a.shape, a.dtype) for a in staged] + [blocks, pltpu.SemaphoreType.DMA((10,))],
+        [pl.BlockSpec(memory_space=pltpu.HBM)] * len(args),
+    )
     for interval in range(INTERVALS):
         y2 = lax.ppermute(x2, "tile", outer_pairs(tiles))
         y1 = lax.ppermute(x1, "tile", inner_pairs(tiles))
@@ -264,10 +309,8 @@
             functools.partial(surface_kernel, groups, len(recs)),
             "surface",
             [shape((rows, width), F32)] * 2 + [shape((half, width), F32)] * 2,
-            (*recs, surface, land_mask),
-            [pltpu.VMEM((count, block), F32)],
-            [VMEM] * len(recs) + [surface_spec, VMEM],
-            grid=(1,),
+            (*recs, surface, mask),
+            [blocks],
         )
         e2 = lax.ppermute(d2, "tile", outer_pairs(tiles))
         e1 = lax.ppermute(d1, "tile", inner_pairs(tiles))
@@ -279,16 +322,15 @@
             [pltpu.VMEM((rows + 2, fields, width), F32)],
             flops=4_000_000_000,
         )
-        common = (part, ns, flux, e1, e2, coef0, codes, col0, land_mask)
+        common = (part, ns, flux, e1, e2, coef, codes, col0, mask)
         if interval < INTERVALS - 1:
             x1, x2, surface, *sent = call(
-                functools.partial(middle_kernel, offsets, groups),
+                functools.partial(middle_kernel, groups),
                 "middle",
                 halves + [shape((rows, width), F32)] + payloads,
-                common + (weights, sources, targets),
-                remap_scratch,
+                common + (wide, pick, chosen),
+                [blocks],
             )
-            surface_spec = VMEM
         else:
             new_state, new_coupling = call(
                 functools.partial(close_kernel, groups),

time: 45.1 us -> 36.9 us (0.82)
  local copies, waits for them, and re-layouts: 5.73 us -> 0 us
  waiting for transfers between devices: 11.9 us -> 8.75 us
  Pallas kernels: 7.68 us -> 8.81 us
    unnamed x28 -> x0, local copies, waits for them, and re-layouts: 5.63 us -> none
    ppermute x2, waiting for transfers between devices: 6.57 us -> 1.13 us  [on_device(): y2 = lax.ppermute(x2, 'tile', outer_pairs(tiles))]
    ppermute x6, waiting for transfers between devices: 4.17 us -> 5.78 us  [on_device(): lax.ppermute(value, 'comp', ring_pairs(groups, offset))]
    pallas_call x7, Pallas kernels: 7.68 us -> 8.81 us  [call(): pl.pallas_call(kernel, name=name, out_shape=outs, in_specs=in_specs or [V...]
    ppermute x2, waiting for transfers between devices: 1.18 us -> 1.84 us  [on_device(): e2 = lax.ppermute(d2, 'tile', outer_pairs(tiles))]
  transfers between devices with their start and end apart: 14 -> 14, of which waited for: 5 -> 8; matrix products, arithmetic and copies ran while one was open for 0% -> 0% of each run, Pallas kernels for 8% -> 9%
where the time goes in v2:
time: 36.9 us; the launch traced here: 36.7 us
  starting transfers between devices  18.4 us (50%)
  Pallas kernels  8.81 us (24%)
  waiting for transfers between devices  8.75 us (24%)
  between operations  0.73 us (2%)
    ppermute x6, starting transfers between devices, on_device(): lax.ppermute(value, 'comp', ring_pairs(groups, offset))  10.4 us
    pallas_call x7, Pallas kernels, call(): pl.pallas_call(kernel, name=name, out_shape=outs, in_specs=in_specs or [V...  8.81 us
    ppermute x6, waiting for transfers between devices, on_device(): lax.ppermute(value, 'comp', ring_pairs(groups, offset))  5.78 us
    ppermute x2, starting transfers between devices, on_device(): y2 = lax.ppermute(x2, 'tile', outer_pairs(tiles))  4.26 us
    ppermute x2, starting transfers between devices, on_device(): e2 = lax.ppermute(d2, 'tile', outer_pairs(tiles))  3.01 us
    ppermute x2, waiting for transfers between devices, on_device(): e2 = lax.ppermute(d2, 'tile', outer_pairs(tiles))  1.84 us
    ppermute x2, waiting for transfers between devices, on_device(): y2 = lax.ppermute(x2, 'tile', outer_pairs(tiles))  1.13 us
  transfers between devices with their start and end apart: 14, of which 8 were waited for; matrix products, arithmetic and copies ran while one was open for 0% of the time, Pallas kernels for 9%

profile of v2, /device:TPU:0, one launch (start us, length us, event | category | flops | bytes accessed | tf_op | source)
XLA Modules:
  0.0 36.7 jit_solution(8417653339520233845)
XLA Ops:
  0.6 2.2 %open.1 = (f32[2,16,3072]{2,1,0:T(8,128)S(1)}, f32[2,16,3072]{2,1,0:T(8,128)S(1)}, f32[4,3072]{1,0:T(4,128)S(1)}, s32[1,4,3072]{2,1,0:T(4,128)S(1)}, s32[1,4,307...) custom-call(f32[1,16,4,3072]{3,2,1,0:T(4,128)} %refs_0_.1, ...), custom_call_target="tpu_custom_call" | custom-call | bytes 4184896 | tf_op jit(solution)/shard_map/open/pallas_call | solution.py:251
  2.8 0.5 %collective-permute-start = (f32[2,16,3072]{2,1,0:T(8,128)S(1)}, f32[2,16,3072]{2,1,0:T(8,128)S(1)}, u32[]{:S(2)}, u32[]{:S(2)}) collective-permute-start(f32[2,16,3072]{2,1,0:T(8,128)S(1)} %get-tuple-element.30.x1), channel_id=1, source_target_pairs={{0,1},{1,0},{2,3},{3,2},{4,5},{5,4},{6,7},{7,6},{8,9},{9,8},{10,11... | collective-permute-start | bytes 1179656 | tf_op jit(solution)/shard_map/ppermute | solution.py:303
  3.4 3.6 %collective-permute-start.1 = (f32[2,16,3072]{2,1,0:T(8,128)S(1)}, f32[2,16,3072]{2,1,0:T(8,128)S(1)}, u32[]{:S(2)}, u32[]{:S(2)}) collective-permute-start(f32[2,16,3072]{2,1,0:T(8,128)S(1)} %get-tuple-element.31.x2), channel_id=1, source_target_pairs={{0,7},{1,2},{2,1},{3,4},{4,3},{5,6},{6,5},{7,0},{8,15},{9,10},{10,... | collective-permute-start | bytes 1179656 | tf_op jit(solution)/shard_map/ppermute | solution.py:302
  6.9 1.6 %collective-permute-start.2 = (f32[96,128]{1,0:T(8,128)S(1)}, f32[96,128]{1,0:T(8,128)S(1)}, u32[]{:S(2)}, u32[]{:S(2)}) collective-permute-start(f32[96,128]{1,0:T(8,128)S(1)} %get-tuple-element.35), channel_id=1, source_target_pairs={{0,8},{8,16},{16,24},{24,0},{1,9},{9,17},{17,25},{25,1},{2,10},{10... | collective-permute-start | bytes 147464 | tf_op jit(solution)/shard_map/ppermute | solution.py:305
  8.5 2.6 %collective-permute-start.3 = (f32[96,128]{1,0:T(8,128)S(1)}, f32[96,128]{1,0:T(8,128)S(1)}, u32[]{:S(2)}, u32[]{:S(2)}) collective-permute-start(f32[96,128]{1,0:T(8,128)S(1)} %get-tuple-element.36), channel_id=1, source_target_pairs={{0,16},{8,24},{16,0},{24,8},{1,17},{9,25},{17,1},{25,9},{2,18},{10... | collective-permute-start | bytes 147464 | tf_op jit(solution)/shard_map/ppermute | solution.py:305
  11.1 1.3 %collective-permute-start.4 = (f32[96,128]{1,0:T(8,128)S(1)}, f32[96,128]{1,0:T(8,128)S(1)}, u32[]{:S(2)}, u32[]{:S(2)}) collective-permute-start(f32[96,128]{1,0:T(8,128)S(1)} %get-tuple-element.37), channel_id=1, source_target_pairs={{0,24},{8,0},{16,8},{24,16},{1,25},{9,1},{17,9},{25,17},{2,26},{10... | collective-permute-start | bytes 147464 | tf_op jit(solution)/shard_map/ppermute | solution.py:305
  12.4 0.8 %collective-permute-done.2.refs_0_ = f32[96,128]{1,0:T(8,128)S(1)} collective-permute-done((f32[96,128]{1,0:T(8,128)S(1)}, f32[96,128]{1,0:T(8,128)S(1)}, u32[]{:S(2)}, u32[]{:S(2)}) %collective-permute-start.2) | collective-permute-done | bytes 49184 | tf_op jit(solution)/shard_map/ppermute | solution.py:305
  13.3 0.7 %collective-permute-done.3.refs_1_ = f32[96,128]{1,0:T(8,128)S(1)} collective-permute-done((f32[96,128]{1,0:T(8,128)S(1)}, f32[96,128]{1,0:T(8,128)S(1)}, u32[]{:S(2)}, u32[]{:S(2)}) %collective-permute-start.3) | collective-permute-done | bytes 49184 | tf_op jit(solution)/shard_map/ppermute | solution.py:305
  14.0 1.2 %collective-permute-done.4.refs_2_ = f32[96,128]{1,0:T(8,128)S(1)} collective-permute-done((f32[96,128]{1,0:T(8,128)S(1)}, f32[96,128]{1,0:T(8,128)S(1)}, u32[]{:S(2)}, u32[]{:S(2)}) %collective-permute-start.4) | collective-permute-done | bytes 49184 | tf_op jit(solution)/shard_map/ppermute | solution.py:305
  15.2 0.1 collective-permute-start.5
  15.3 0.8 %collective-permute-start.6 = (f32[2,3072]{1,0:T(2,128)S(1)}, f32[2,3072]{1,0:T(2,128)S(1)}, u32[]{:S(2)}, u32[]{:S(2)}) collective-permute-start(f32[2,3072]{1,0:T(2,128)S(1)} %get-tuple-element.43), channel_id=1, source_target_pairs={{0,7},{1,2},{2,1},{3,4},{4,3},{5,6},{6,5},{7,0},{8,15},{9,10},{10,... | collective-permute-start | bytes 73736 | tf_op jit(solution)/shard_map/ppermute | solution.py:315
  16.1 0.0 collective-permute-done.y1
  16.1 0.0 collective-permute-done.1.y2
  16.1 1.6 %fields.2.part = f32[4,16,3072]{2,1,0:T(8,128)S(1)} custom-call(f32[2,16,3072]{2,1,0:T(8,128)S(1)} %get-tuple-element.30.x1, f32[2,16,3072]{2,1,0:T(8,128)S(1)} %get-tuple-element.31.x2, f32[2,16,3072]{2,1,0:T(8,128)S(1)} %collective-permute-done.y1, f32[2,16,3072]{2,1,0:T(8,128)S(1)} %collective-permute-done.1.y2, f32[3,16,1]{2,1,0:T(8,128)S(1)} %get-tuple-element.32.coef, ...), custom_call_target="tpu_custom_call" | custom-call | flops 4000000000 | bytes 2414784 | tf_op jit(solution)/shard_map/fields/pallas_call | solution.py:251
  17.8 0.0 collective-permute-done.5.e1
  17.8 1.8 %collective-permute-done.6.e2 = f32[2,3072]{1,0:T(2,128)S(1)} collective-permute-done((f32[2,3072]{1,0:T(2,128)S(1)}, f32[2,3072]{1,0:T(2,128)S(1)}, u32[]{:S(2)}, u32[]{:S(2)}) %collective-permute-start.6) | collective-permute-done | bytes 24608 | tf_op jit(solution)/shard_map/ppermute | solution.py:315
  19.6 1.5 %middle.1 = (f32[2,16,3072]{2,1,0:T(8,128)S(1)}, f32[2,16,3072]{2,1,0:T(8,128)S(1)}, f32[4,3072]{1,0:T(4,128)S(1)}, f32[96,128]{1,0:T(8,128)S(1)}, f32[96,128]{1,0:T(8,128)S(1)}, /*index=5*/f32[96,128]{1,0:T(8,128)S(1)}) custom-call(f32[4,16,3072]{2,1,0:T(8,128)S(1)} %fields.2.part, f32[4,3072]{1,0:T(4,128)S(1)} %get-tuple-element.40.ns, ...), custom_call_target="tpu_custom_call" | custom-call | bytes 3582400 | tf_op jit(solution)/shard_map/middle/pallas_call | solution.py:251
  21.1 0.1 collective-permute-start.7
  21.2 0.7 %collective-permute-start.8 = (f32[2,16,3072]{2,1,0:T(8,128)S(1)}, f32[2,16,3072]{2,1,0:T(8,128)S(1)}, u32[]{:S(2)}, u32[]{:S(2)}) collective-permute-start(f32[2,16,3072]{2,1,0:T(8,128)S(1)} %get-tuple-element.49.x2), channel_id=1, source_target_pairs={{0,7},{1,2},{2,1},{3,4},{4,3},{5,6},{6,5},{7,0},{8,15},{9,10},{10,... | collective-permute-start | bytes 1179656 | tf_op jit(solution)/shard_map/ppermute | solution.py:302
  21.9 0.9 %collective-permute-start.9 = (f32[96,128]{1,0:T(8,128)S(1)}, f32[96,128]{1,0:T(8,128)S(1)}, u32[]{:S(2)}, u32[]{:S(2)}) collective-permute-start(f32[96,128]{1,0:T(8,128)S(1)} %get-tuple-element.50), channel_id=1, source_target_pairs={{0,8},{8,16},{16,24},{24,0},{1,9},{9,17},{17,25},{25,1},{2,10},{10... | collective-permute-start | bytes 147464 | tf_op jit(solution)/shard_map/ppermute | solution.py:305
  22.7 2.7 %collective-permute-start.10 = (f32[96,128]{1,0:T(8,128)S(1)}, f32[96,128]{1,0:T(8,128)S(1)}, u32[]{:S(2)}, u32[]{:S(2)}) collective-permute-start(f32[96,128]{1,0:T(8,128)S(1)} %get-tuple-element.51), channel_id=1, source_target_pairs={{0,16},{8,24},{16,0},{24,8},{1,17},{9,25},{17,1},{25,9},{2,18},{10... | collective-permute-start | bytes 147464 | tf_op jit(solution)/shard_map/ppermute | solution.py:305
  25.4 1.3 %collective-permute-start.11 = (f32[96,128]{1,0:T(8,128)S(1)}, f32[96,128]{1,0:T(8,128)S(1)}, u32[]{:S(2)}, u32[]{:S(2)}) collective-permute-start(f32[96,128]{1,0:T(8,128)S(1)} %get-tuple-element.52), channel_id=1, source_target_pairs={{0,24},{8,0},{16,8},{24,16},{1,25},{9,1},{17,9},{25,17},{2,26},{10... | collective-permute-start | bytes 147464 | tf_op jit(solution)/shard_map/ppermute | solution.py:305
  26.8 1.3 %collective-permute-done.9.refs_0_ = f32[96,128]{1,0:T(8,128)S(1)} collective-permute-done((f32[96,128]{1,0:T(8,128)S(1)}, f32[96,128]{1,0:T(8,128)S(1)}, u32[]{:S(2)}, u32[]{:S(2)}) %collective-permute-start.9) | collective-permute-done | bytes 49184 | tf_op jit(solution)/shard_map/ppermute | solution.py:305
  28.1 1.6 %collective-permute-done.10.refs_1_ = f32[96,128]{1,0:T(8,128)S(1)} collective-permute-done((f32[96,128]{1,0:T(8,128)S(1)}, f32[96,128]{1,0:T(8,128)S(1)}, u32[]{:S(2)}, u32[]{:S(2)}) %collective-permute-start.10) | collective-permute-done | bytes 49184 | tf_op jit(solution)/shard_map/ppermute | solution.py:305
  29.7 0.1 collective-permute-done.11.refs_2_
  29.9 0.1 collective-permute-start.12
  29.9 2.2 %collective-permute-start.13 = (f32[2,3072]{1,0:T(2,128)S(1)}, f32[2,3072]{1,0:T(2,128)S(1)}, u32[]{:S(2)}, u32[]{:S(2)}) collective-permute-start(f32[2,3072]{1,0:T(2,128)S(1)} %get-tuple-element.57), channel_id=1, source_target_pairs={{0,7},{1,2},{2,1},{3,4},{4,3},{5,6},{6,5},{7,0},{8,15},{9,10},{10,... | collective-permute-start | bytes 73736 | tf_op jit(solution)/shard_map/ppermute | solution.py:315
  32.2 0.0 collective-permute-done.7.y1
  32.2 1.1 %collective-permute-done.8.y2 = f32[2,16,3072]{2,1,0:T(8,128)S(1)} collective-permute-done((f32[2,16,3072]{2,1,0:T(8,128)S(1)}, f32[2,16,3072]{2,1,0:T(8,128)S(1)}, u32[]{:S(2)}, u32[]{:S(2)}) %collective-permute-start.8) | collective-permute-done | bytes 393248 | tf_op jit(solution)/shard_map/ppermute | solution.py:302
  33.3 1.6 %fields.3.part = f32[4,16,3072]{2,1,0:T(8,128)S(1)} custom-call(f32[2,16,3072]{2,1,0:T(8,128)S(1)} %get-tuple-element.48.x1, f32[2,16,3072]{2,1,0:T(8,128)S(1)} %get-tuple-element.49.x2, f32[2,16,3072]{2,1,0:T(8,128)S(1)} %collective-permute-done.7.y1, f32[2,16,3072]{2,1,0:T(8,128)S(1)} %collective-permute-done.8.y2, ...), custom_call_target="tpu_custom_call" | custom-call | flops 4000000000 | bytes 2414784 | tf_op jit(solution)/shard_map/fields/pallas_call | solution.py:251
  34.9 0.0 collective-permute-done.13.e2
  34.9 1.8 %close.1 = (f32[1,16,4,3072]{3,2,1,0:T(4,128)}, f32[1,4,3072]{2,1,0:T(4,128)}) custom-call(f32[4,16,3072]{2,1,0:T(8,128)S(1)} %fields.3.part, f32[4,3072]{1,0:T(4,128)S(1)} %get-tuple-element.54.ns, f32[4,3072]{1,0:T(4,128)S(1)} %get-tuple-element.55.flux, f32[2,3072]{1,0:T(2,128)S(1)} %collective-permute-done.12.e1, ...), custom_call_target="tpu_custom_call" | custom-call | bytes 1868224 | tf_op jit(solution)/shard_map/close/pallas_call | solution.py:251
  (3 shorter events, 0.1 us)
Async XLA Ops:
  2.8 13.3 %collective-permute-start = (f32[2,16,3072]{2,1,0:T(8,128)S(1)}, f32[2,16,3072]{2,1,0:T(8,128)S(1)}, u32[]{:S(2)}, u32[]{:S(2)}) collective-permute-start(f32[2,16,3072]{2,1,0:T(8,128)S(1)} %get-tuple-element.30.x1), channel_id=1, source_target_pairs={{0,1},{1,0},{2,3},{3,2},{4,5},{5,4},{6,7},{7,6},{8,9},{9,8},{10,11... | collective-permute-start | bytes 1179656 | tf_op jit(solution)/shard_map/ppermute | solution.py:303
  3.4 12.7 %collective-permute-start.1 = (f32[2,16,3072]{2,1,0:T(8,128)S(1)}, f32[2,16,3072]{2,1,0:T(8,128)S(1)}, u32[]{:S(2)}, u32[]{:S(2)}) collective-permute-start(f32[2,16,3072]{2,1,0:T(8,128)S(1)} %get-tuple-element.31.x2), channel_id=1, source_target_pairs={{0,7},{1,2},{2,1},{3,4},{4,3},{5,6},{6,5},{7,0},{8,15},{9,10},{10,... | collective-permute-start | bytes 1179656 | tf_op jit(solution)/shard_map/ppermute | solution.py:302
  6.9 6.3 %collective-permute-start.2 = (f32[96,128]{1,0:T(8,128)S(1)}, f32[96,128]{1,0:T(8,128)S(1)}, u32[]{:S(2)}, u32[]{:S(2)}) collective-permute-start(f32[96,128]{1,0:T(8,128)S(1)} %get-tuple-element.35), channel_id=1, source_target_pairs={{0,8},{8,16},{16,24},{24,0},{1,9},{9,17},{17,25},{25,1},{2,10},{10... | collective-permute-start | bytes 147464 | tf_op jit(solution)/shard_map/ppermute | solution.py:305
  8.5 5.5 %collective-permute-start.3 = (f32[96,128]{1,0:T(8,128)S(1)}, f32[96,128]{1,0:T(8,128)S(1)}, u32[]{:S(2)}, u32[]{:S(2)}) collective-permute-start(f32[96,128]{1,0:T(8,128)S(1)} %get-tuple-element.36), channel_id=1, source_target_pairs={{0,16},{8,24},{16,0},{24,8},{1,17},{9,25},{17,1},{25,9},{2,18},{10... | collective-permute-start | bytes 147464 | tf_op jit(solution)/shard_map/ppermute | solution.py:305
  11.1 4.1 %collective-permute-start.4 = (f32[96,128]{1,0:T(8,128)S(1)}, f32[96,128]{1,0:T(8,128)S(1)}, u32[]{:S(2)}, u32[]{:S(2)}) collective-permute-start(f32[96,128]{1,0:T(8,128)S(1)} %get-tuple-element.37), channel_id=1, source_target_pairs={{0,24},{8,0},{16,8},{24,16},{1,25},{9,1},{17,9},{25,17},{2,26},{10... | collective-permute-start | bytes 147464 | tf_op jit(solution)/shard_map/ppermute | solution.py:305
  15.2 2.5 %collective-permute-start.5 = (f32[2,3072]{1,0:T(2,128)S(1)}, f32[2,3072]{1,0:T(2,128)S(1)}, u32[]{:S(2)}, u32[]{:S(2)}) collective-permute-start(f32[2,3072]{1,0:T(2,128)S(1)} %get-tuple-element.42), channel_id=1, source_target_pairs={{0,1},{1,0},{2,3},{3,2},{4,5},{5,4},{6,7},{7,6},{8,9},{9,8},{10,11... | collective-permute-start | bytes 73736 | tf_op jit(solution)/shard_map/ppermute | solution.py:316
  15.3 4.3 %collective-permute-start.6 = (f32[2,3072]{1,0:T(2,128)S(1)}, f32[2,3072]{1,0:T(2,128)S(1)}, u32[]{:S(2)}, u32[]{:S(2)}) collective-permute-start(f32[2,3072]{1,0:T(2,128)S(1)} %get-tuple-element.43), channel_id=1, source_target_pairs={{0,7},{1,2},{2,1},{3,4},{4,3},{5,6},{6,5},{7,0},{8,15},{9,10},{10,... | collective-permute-start | bytes 73736 | tf_op jit(solution)/shard_map/ppermute | solution.py:315
  21.1 11.1 %collective-permute-start.7 = (f32[2,16,3072]{2,1,0:T(8,128)S(1)}, f32[2,16,3072]{2,1,0:T(8,128)S(1)}, u32[]{:S(2)}, u32[]{:S(2)}) collective-permute-start(f32[2,16,3072]{2,1,0:T(8,128)S(1)} %get-tuple-element.48.x1), channel_id=1, source_target_pairs={{0,1},{1,0},{2,3},{3,2},{4,5},{5,4},{6,7},{7,6},{8,9},{9,8},{10,11... | collective-permute-start | bytes 1179656 | tf_op jit(solution)/shard_map/ppermute | solution.py:303
  21.2 12.1 %collective-permute-start.8 = (f32[2,16,3072]{2,1,0:T(8,128)S(1)}, f32[2,16,3072]{2,1,0:T(8,128)S(1)}, u32[]{:S(2)}, u32[]{:S(2)}) collective-permute-start(f32[2,16,3072]{2,1,0:T(8,128)S(1)} %get-tuple-element.49.x2), channel_id=1, source_target_pairs={{0,7},{1,2},{2,1},{3,4},{4,3},{5,6},{6,5},{7,0},{8,15},{9,10},{10,... | collective-permute-start | bytes 1179656 | tf_op jit(solution)/shard_map/ppermute | solution.py:302
  21.9 6.2 %collective-permute-start.9 = (f32[96,128]{1,0:T(8,128)S(1)}, f32[96,128]{1,0:T(8,128)S(1)}, u32[]{:S(2)}, u32[]{:S(2)}) collective-permute-start(f32[96,128]{1,0:T(8,128)S(1)} %get-tuple-element.50), channel_id=1, source_target_pairs={{0,8},{8,16},{16,24},{24,0},{1,9},{9,17},{17,25},{25,1},{2,10},{10... | collective-permute-start | bytes 147464 | tf_op jit(solution)/shard_map/ppermute | solution.py:305
  22.7 7.0 %collective-permute-start.10 = (f32[96,128]{1,0:T(8,128)S(1)}, f32[96,128]{1,0:T(8,128)S(1)}, u32[]{:S(2)}, u32[]{:S(2)}) collective-permute-start(f32[96,128]{1,0:T(8,128)S(1)} %get-tuple-element.51), channel_id=1, source_target_pairs={{0,16},{8,24},{16,0},{24,8},{1,17},{9,25},{17,1},{25,9},{2,18},{10... | collective-permute-start | bytes 147464 | tf_op jit(solution)/shard_map/ppermute | solution.py:305
  25.4 4.4 %collective-permute-start.11 = (f32[96,128]{1,0:T(8,128)S(1)}, f32[96,128]{1,0:T(8,128)S(1)}, u32[]{:S(2)}, u32[]{:S(2)}) collective-permute-start(f32[96,128]{1,0:T(8,128)S(1)} %get-tuple-element.52), channel_id=1, source_target_pairs={{0,24},{8,0},{16,8},{24,16},{1,25},{9,1},{17,9},{25,17},{2,26},{10... | collective-permute-start | bytes 147464 | tf_op jit(solution)/shard_map/ppermute | solution.py:305
  29.9 5.0 %collective-permute-start.12 = (f32[2,3072]{1,0:T(2,128)S(1)}, f32[2,3072]{1,0:T(2,128)S(1)}, u32[]{:S(2)}, u32[]{:S(2)}) collective-permute-start(f32[2,3072]{1,0:T(2,128)S(1)} %get-tuple-element.56), channel_id=1, source_target_pairs={{0,1},{1,0},{2,3},{3,2},{4,5},{5,4},{6,7},{7,6},{8,9},{9,8},{10,11... | collective-permute-start | bytes 73736 | tf_op jit(solution)/shard_map/ppermute | solution.py:316
  29.9 5.0 %collective-permute-start.13 = (f32[2,3072]{1,0:T(2,128)S(1)}, f32[2,3072]{1,0:T(2,128)S(1)}, u32[]{:S(2)}, u32[]{:S(2)}) collective-permute-start(f32[2,3072]{1,0:T(2,128)S(1)} %get-tuple-element.57), channel_id=1, source_target_pairs={{0,7},{1,2},{2,1},{3,4},{4,3},{5,6},{6,5},{7,0},{8,15},{9,10},{10,... | collective-permute-start | bytes 73736 | tf_op jit(solution)/shard_map/ppermute | solution.py:315

commit v3 on v2

--- a/solution.py
+++ b/solution.py
@@ -64,8 +64,9 @@
         contrib = contrib + wide_ref[pl.ds(j, margins, stride=band), :] * turned
     high, low = split_high_low(contrib)
     both = jnp.concatenate([high, low], axis=0)
+    blocks = jnp.dot(chosen_ref[...], both, preferred_element_type=F32)
     for n, out_ref in enumerate(out_refs):
-        out_ref[...] = jnp.dot(chosen_ref[n], both, preferred_element_type=F32)
+        out_ref[...] = blocks[n * count : (n + 1) * count]
 
 
 def column(row):
@@ -81,21 +82,22 @@
     outs, refs = refs[: len(offsets)], refs[len(offsets) :]
     state_v, coupling_v, weights_v, mixing_v, courant_v, matrices_v, sources_v, targets_v, blk, sems = refs
     pairs = (
-        (coupling, coupling_v),
         (sources, sources_v),
         (targets, targets_v),
-        (weights, weights_v),
-        (state, state_v),
         (mixing, mixing_v),
         (courant, courant_v),
         (matrices, matrices_v),
+        (coupling, coupling_v),
         (mask, mask_out),
         (codes, codes_out),
+        (weights, weights_v),
+        (state, state_v),
     )
     copies = [pltpu.make_async_copy(src, dst, sems.at[n]) for n, (src, dst) in enumerate(pairs)]
     for copy in copies:
         copy.start()
-    for copy in copies[:4]:
+    small = 8
+    for copy in copies[:small]:
         copy.wait()
     count, margins = pick.shape
     block = blk.shape[1]
@@ -105,18 +107,7 @@
     for n, offset in enumerate(offsets):
         base = lax.rem(me + offset, groups) * count
         hit = (targets_v[...] == slot + base).astype(F32).astype(BF16)
-        chosen[n] = jnp.concatenate([hit, hit], axis=1)
-    wide[...] = weights_v[0].reshape(wide.shape).astype(F32)
-    payload(coupling_v[0], wide, pick, chosen, outs, blk)
-    for copy in copies[4:]:
-        copy.wait()
-    odd = lax.rem(lax.axis_index("tile"), 2) == 1
-    half = x1.shape[0]
-    for i in range(half):
-        head, tail = state_v[0, :, i, :], state_v[0, :, half + i, :]
-        x1[i] = jnp.where(odd, head, tail)
-        x2[i] = jnp.where(odd, tail, head)
-    surface[...] = state_v[0, 0]
+        chosen[n * count : (n + 1) * count] = jnp.concatenate([hit, hit], axis=1)
     m, c = column(mixing_v[...]), column(courant_v[...])
     coef[0], coef[1], coef[2] = 1.0 - 4.0 * m - c, m + c, m
     branches, fields = matrices_v.shape[1:3]
@@ -125,6 +116,17 @@
     flat = jnp.where(lax.broadcasted_iota(jnp.int32, flat.shape, 1) == 0, 0.0, flat)
     high, low = split_high_low(flat)
     table[...] = jnp.concatenate([high, high, low], axis=1)
+    copies[small].wait()
+    wide[...] = weights_v[0].reshape(wide.shape).astype(F32)
+    payload(coupling_v[0], wide, pick, chosen, outs, blk)
+    copies[small + 1].wait()
+    odd = lax.rem(lax.axis_index("tile"), 2) == 1
+    half = x1.shape[0]
+    for i in range(half):
+        head, tail = state_v[0, :, i, :], state_v[0, :, half + i, :]
+        x1[i] = jnp.where(odd, head, tail)
+        x2[i] = jnp.where(odd, tail, head)
+    surface[...] = state_v[0, 0]
 
 
 def surface_kernel(groups, n_rec, *refs):
@@ -158,34 +160,53 @@
     return c0 * f + cu * up + m * (down + sides)
 
 
-def fields_kernel(x1, x2, y1, y2, coef, table, codes, part, grid_ref):
-    odd = lax.rem(lax.axis_index("tile"), 2) == 1
-    half, fields, width = x1.shape
+def sides(f):
+    return pltpu.roll(f, 1, 1) + pltpu.roll(f, f.shape[1] - 1, 1)
+
+
+def inner_kernel(x1, x2, coef, base):
+    odd = lax.rem(lax.axis_index("tile"), 2) == 1
+    c0, cu, m = coef[0], coef[1], coef[2]
+    f0, f1 = (jnp.where(odd, x1[i], x2[i]) for i in range(2))
+    f2, f3 = (jnp.where(odd, x2[i], x1[i]) for i in range(2))
+    g0 = c0 * f0 + m * (f1 + sides(f0))
+    g1 = substep(f1, f0, f2, c0, cu, m)
+    g2 = substep(f2, f1, f3, c0, cu, m)
+    g3 = c0 * f3 + cu * f2 + m * sides(f3)
+    base[0] = c0 * g0 + m * (g1 + sides(g0)) + (cu * m) * f0
+    base[1] = substep(g1, g0, g2, c0, cu, m)
+    base[2] = substep(g2, g1, g3, c0, cu, m)
+    base[3] = c0 * g3 + cu * g2 + m * sides(g3) + (cu * m) * f3
+
+
+def fields_kernel(groups, base, y1, y2, coef, table, col0, codes, mask, part, gain):
+    odd = lax.rem(lax.axis_index("tile"), 2) == 1
+    sea = lax.axis_index("comp") >= 3 * groups // 4
+    rows, fields, width = base.shape
     c0, cu, m = coef[0], coef[1], coef[2]
     branches = table.shape[0] // fields
-
-    def row(i):
-        group, at = divmod(i, half)
-        first, second = ((y2, y1), (x2, x1), (x1, x2), (y1, y2))[group]
-        return jnp.where(odd, second[at], first[at])
-
-    above, here = row(0), row(1)
-    for i in range(1, 4 * half - 1):
-        below = row(i + 1)
-        grid_ref[i - 1] = substep(here, above, below, c0, cu, m)
-        above, here = here, below
+    near, far = jnp.where(odd, y1[1], y2[1]), jnp.where(odd, y1[0], y2[0])
+    top = (2.0 * cu * c0) * near + (2.0 * cu * m) * sides(near) + (cu * cu) * far
+    top_next = (cu * cu) * near
+    near, far = jnp.where(odd, y2[0], y1[0]), jnp.where(odd, y2[1], y1[1])
+    bottom = (2.0 * m * c0) * near + (2.0 * m * m) * sides(near) + (m * m) * far
+    bottom_next = (m * m) * near
     keep = lax.broadcasted_iota(jnp.int32, (fields, width), 0) > 0
-    for r in range(2 * half):
-        f = substep(grid_ref[r + 1], grid_ref[r], grid_ref[r + 2], c0, cu, m)
+    for r, halo in enumerate((top, top_next, bottom_next, bottom)):
+        f = base[r] + halo
         high, low = split_high_low(jnp.tanh(f))
         terms = jnp.dot(
             table[...], jnp.concatenate([high, low, high], axis=0), preferred_element_type=F32
         )
         code = codes[0, r : r + 1, :]
+        wet = jnp.where(sea, mask[0, r : r + 1, :].astype(F32), 1.0)
         tendency = terms[:fields]
+        factor = jnp.broadcast_to(col0[0], (fields, width))
         for b in range(1, branches):
             tendency = jnp.where(code == b, terms[b * fields : (b + 1) * fields], tendency)
-        part[r] = jnp.where(keep, f, 0.0) + tendency
+            factor = jnp.where(code == b, col0[b], factor)
+        part[r] = (jnp.where(keep, f, 0.0) + tendency) * wet
+        gain[r] = factor * wet
 
 
 def field0(ns, e1, e2, coef, odd):
@@ -201,49 +222,57 @@
     return f[half : rows - half]
 
 
-def evolve_rows(part, f0, codes, col0, mask, sea):
-    rows, fields, width = part.shape
-    branches = col0.shape[0]
-    squashed = jnp.tanh(f0)
-    top = lax.broadcasted_iota(jnp.int32, (fields, width), 0) == 0
-    done = []
-    for r in range(rows):
-        code = codes[0, r : r + 1, :]
-        gain = jnp.broadcast_to(col0[0], (fields, width))
-        for b in range(1, branches):
-            gain = jnp.where(code == b, col0[b], gain)
-        value = part[r] + gain * squashed[r : r + 1, :] + jnp.where(top, f0[r : r + 1, :], 0.0)
-        wet = jnp.where(sea, mask[0, r : r + 1, :].astype(F32), 1.0)
-        done.append(value * wet)
-    return done
-
-
-def middle_kernel(
-    groups, part, ns, flux, e1, e2, coef, codes, col0, mask, wide, pick, chosen, x1, x2, surf, *rest
-):
-    outs, blk = rest[:-1], rest[-1]
+SUBLANES = 8
+
+
+def evolve_rows(groups, part, gain, ns, e1, e2, coef, mask, f0_ref, squashed_ref):
     odd = lax.rem(lax.axis_index("tile"), 2) == 1
     sea = lax.axis_index("comp") >= 3 * groups // 4
     f0 = field0(ns, e1, e2, coef, odd)
-    rows = evolve_rows(part, f0, codes, col0, mask, sea)
-    half = x1.shape[0]
+    squashed_ref[...] = jnp.tanh(f0)
+    f0_ref[...] = f0 * jnp.where(sea, mask[0].astype(F32), 1.0)
+    width = part.shape[2]
+    first = (lax.broadcasted_iota(jnp.int32, (SUBLANES, width), 0) == 0).astype(F32)
+
+    def value(r, h):
+        some = slice(h, h + SUBLANES)
+        total = part[r, some] + gain[r, some] * squashed_ref[r : r + 1, :]
+        return total + first * f0_ref[r : r + 1, :] if h == 0 else total
+
+    return value
+
+
+def evolve_kernel(groups, part, gain, ns, e1, e2, coef, mask, x1, x2, surf, *scratch):
+    odd = lax.rem(lax.axis_index("tile"), 2) == 1
+    value = evolve_rows(groups, part, gain, ns, e1, e2, coef, mask, *scratch)
+    half, fields, _ = x1.shape
     for i in range(half):
-        x1[i] = jnp.where(odd, rows[i], rows[half + i])
-        x2[i] = jnp.where(odd, rows[half + i], rows[i])
-    for r, value in enumerate(rows):
-        surf[r : r + 1, :] = value[:1]
-    handed = jnp.where(sea, surf[...], flux[...])
-    payload(handed, wide, pick, chosen, outs, blk)
-
-
-def close_kernel(groups, part, ns, flux, e1, e2, coef, codes, col0, mask, new_state, new_coupling):
-    odd = lax.rem(lax.axis_index("tile"), 2) == 1
+        for h in range(0, fields, SUBLANES):
+            head, tail = value(i, h), value(half + i, h)
+            x1[i, h : h + SUBLANES] = jnp.where(odd, head, tail)
+            x2[i, h : h + SUBLANES] = jnp.where(odd, tail, head)
+            if h == 0:
+                surf[i : i + 1, :] = head[:1]
+                surf[half + i : half + i + 1, :] = tail[:1]
+
+
+def payload_kernel(groups, surf, flux, wide, pick, chosen, *rest):
     sea = lax.axis_index("comp") >= 3 * groups // 4
-    f0 = field0(ns, e1, e2, coef, odd)
-    rows = evolve_rows(part, f0, codes, col0, mask, sea)
-    for r, value in enumerate(rows):
-        new_state[0, :, r, :] = value
-        new_coupling[0, r : r + 1, :] = jnp.where(sea, value[:1], flux[r : r + 1, :])
+    payload(jnp.where(sea, surf[...], flux[...]), wide, pick, chosen, rest[:-1], rest[-1])
+
+
+def close_kernel(
+    groups, part, gain, ns, flux, e1, e2, coef, mask, new_state, new_coupling, *scratch
+):
+    sea = lax.axis_index("comp") >= 3 * groups // 4
+    value = evolve_rows(groups, part, gain, ns, e1, e2, coef, mask, *scratch)
+    rows, fields, _ = part.shape
+    for h in range(0, fields, SUBLANES):
+        for r in range(rows):
+            done = value(r, h)
+            new_state[0, h : h + SUBLANES, r, :] = done
+            if h == 0:
+                new_coupling[0, r : r + 1, :] = jnp.where(sea, done[:1], flux[r : r + 1, :])
 
 
 def call(kernel, name, outs, args, scratch=(), in_specs=None, flops=0):
@@ -284,7 +313,7 @@
         shape((branches, fields, 1), F32),
         shape((margins * band, block), F32),
         shape((count, margins), BF16),
-        shape((len(offsets), count, 2 * margins), BF16),
+        shape((len(offsets) * count, 2 * margins), BF16),
     ]
     args = (
         state, coupling, land_mask, codes, mixing, courant, matrices, weights, sources, targets
@@ -314,21 +343,30 @@
         )
         e2 = lax.ppermute(d2, "tile", outer_pairs(tiles))
         e1 = lax.ppermute(d1, "tile", inner_pairs(tiles))
-        (part,) = call(
-            fields_kernel,
+        (base,) = call(
+            inner_kernel, "inner", [shape((rows, fields, width), F32)], (x1, x2, coef)
+        )
+        part, gain = call(
+            functools.partial(fields_kernel, groups),
             "fields",
-            [shape((rows, fields, width), F32)],
-            (x1, x2, y1, y2, coef, table, codes),
-            [pltpu.VMEM((rows + 2, fields, width), F32)],
+            [shape((rows, fields, width), F32)] * 2,
+            (base, y1, y2, coef, table, col0, codes, mask),
             flops=4_000_000_000,
         )
-        common = (part, ns, flux, e1, e2, coef, codes, col0, mask)
+        lines = [pltpu.VMEM((rows, width), F32)] * 2
         if interval < INTERVALS - 1:
-            x1, x2, surface, *sent = call(
-                functools.partial(middle_kernel, groups),
-                "middle",
-                halves + [shape((rows, width), F32)] + payloads,
-                common + (wide, pick, chosen),
+            x1, x2, surface = call(
+                functools.partial(evolve_kernel, groups),
+                "evolve",
+                halves + [shape((rows, width), F32)],
+                (part, gain, ns, e1, e2, coef, mask),
+                lines,
+            )
+            sent = call(
+                functools.partial(payload_kernel, groups),
+                "payload",
+                payloads,
+                (surface, flux, wide, pick, chosen),
                 [blocks],
             )
         else:
@@ -336,7 +374,8 @@
                 functools.partial(close_kernel, groups),
                 "close",
                 [shape(state.shape, F32), shape(coupling.shape, F32)],
-                common,
+                (part, gain, ns, flux, e1, e2, coef, mask),
+                lines,
             )
     return new_state, new_coupling
 

time: 36.9 us -> 35.7 us (0.967)
  starting transfers between devices: 18.4 us -> 17.8 us
  waiting for transfers between devices: 8.75 us -> 8.27 us
    ppermute x2, waiting for transfers between devices: 1.84 us -> 3.52 us  [on_device(): e2 = lax.ppermute(d2, 'tile', outer_pairs(tiles))]
    ppermute x6, waiting for transfers between devices: 5.78 us -> 4.41 us  [on_device(): lax.ppermute(value, 'comp', ring_pairs(groups, offset))]
    ppermute x2, waiting for transfers between devices: 1.13 us -> 0.33 us  [on_device(): y2 = lax.ppermute(x2, 'tile', outer_pairs(tiles))]
    ppermute x6, starting transfers between devices: 10.4 us -> 9.69 us  [on_device(): lax.ppermute(value, 'comp', ring_pairs(groups, offset))]
    pallas_call x7 -> x10, Pallas kernels: 8.81 us -> 8.82 us  [call(): pl.pallas_call(kernel, name=name, out_shape=outs, in_specs=in_specs or [V...]
  transfers between devices with their start and end apart: 14 -> 14, of which waited for: 8 -> 8; matrix products, arithmetic and copies ran while one was open for 0% -> 0% of each run, Pallas kernels for 9% -> 13%
where the time goes in v3:
time: 35.7 us; the launch traced here: 35.6 us
  starting transfers between devices  17.8 us (50%)
  Pallas kernels  8.82 us (25%)
  waiting for transfers between devices  8.27 us (23%)
  between operations  0.75 us (2%)
    ppermute x6, starting transfers between devices, on_device(): lax.ppermute(value, 'comp', ring_pairs(groups, offset))  9.69 us
    pallas_call x10, Pallas kernels, call(): pl.pallas_call(kernel, name=name, out_shape=outs, in_specs=in_specs or [V...  8.82 us
    ppermute x6, waiting for transfers between devices, on_device(): lax.ppermute(value, 'comp', ring_pairs(groups, offset))  4.41 us
    ppermute x2, starting transfers between devices, on_device(): y2 = lax.ppermute(x2, 'tile', outer_pairs(tiles))  4.26 us
    ppermute x2, waiting for transfers between devices, on_device(): e2 = lax.ppermute(d2, 'tile', outer_pairs(tiles))  3.52 us
    ppermute x2, starting transfers between devices, on_device(): e2 = lax.ppermute(d2, 'tile', outer_pairs(tiles))  3.07 us
  transfers between devices with their start and end apart: 14, of which 8 were waited for; matrix products, arithmetic and copies ran while one was open for 0% of the time, Pallas kernels for 13%

profile of v3, /device:TPU:0, one launch (start us, length us, event | category | flops | bytes accessed | tf_op | source)
XLA Modules:
  0.0 35.6 jit_solution(8258174576771680812)
XLA Ops:
  0.6 2.3 %open.1 = (f32[2,16,3072]{2,1,0:T(8,128)S(1)}, f32[2,16,3072]{2,1,0:T(8,128)S(1)}, f32[4,3072]{1,0:T(4,128)S(1)}, s32[1,4,3072]{2,1,0:T(4,128)S(1)}, s32[1,4,307...) custom-call(f32[1,16,4,3072]{3,2,1,0:T(4,128)} %refs_0_.1, ...), custom_call_target="tpu_custom_call" | custom-call | bytes 4184896 | tf_op jit(solution)/shard_map/open/pallas_call | solution.py:280
  2.9 0.5 %collective-permute-start = (f32[2,16,3072]{2,1,0:T(8,128)S(1)}, f32[2,16,3072]{2,1,0:T(8,128)S(1)}, u32[]{:S(2)}, u32[]{:S(2)}) collective-permute-start(f32[2,16,3072]{2,1,0:T(8,128)S(1)} %get-tuple-element.34.x1), channel_id=1, source_target_pairs={{0,1},{1,0},{2,3},{3,2},{4,5},{5,4},{6,7},{7,6},{8,9},{9,8},{10,11... | collective-permute-start | bytes 1179656 | tf_op jit(solution)/shard_map/ppermute | solution.py:332
  3.4 3.6 %collective-permute-start.1 = (f32[2,16,3072]{2,1,0:T(8,128)S(1)}, f32[2,16,3072]{2,1,0:T(8,128)S(1)}, u32[]{:S(2)}, u32[]{:S(2)}) collective-permute-start(f32[2,16,3072]{2,1,0:T(8,128)S(1)} %get-tuple-element.35.x2), channel_id=1, source_target_pairs={{0,7},{1,2},{2,1},{3,4},{4,3},{5,6},{6,5},{7,0},{8,15},{9,10},{10,... | collective-permute-start | bytes 1179656 | tf_op jit(solution)/shard_map/ppermute | solution.py:331
  7.0 1.6 %collective-permute-start.2 = (f32[96,128]{1,0:T(8,128)S(1)}, f32[96,128]{1,0:T(8,128)S(1)}, u32[]{:S(2)}, u32[]{:S(2)}) collective-permute-start(f32[96,128]{1,0:T(8,128)S(1)} %get-tuple-element.43), channel_id=1, source_target_pairs={{0,8},{8,16},{16,24},{24,0},{1,9},{9,17},{17,25},{25,1},{2,10},{10... | collective-permute-start | bytes 147464 | tf_op jit(solution)/shard_map/ppermute | solution.py:334
  8.6 2.6 %collective-permute-start.3 = (f32[96,128]{1,0:T(8,128)S(1)}, f32[96,128]{1,0:T(8,128)S(1)}, u32[]{:S(2)}, u32[]{:S(2)}) collective-permute-start(f32[96,128]{1,0:T(8,128)S(1)} %get-tuple-element.44), channel_id=1, source_target_pairs={{0,16},{8,24},{16,0},{24,8},{1,17},{9,25},{17,1},{25,9},{2,18},{10... | collective-permute-start | bytes 147464 | tf_op jit(solution)/shard_map/ppermute | solution.py:334
  11.2 1.4 %collective-permute-start.4 = (f32[96,128]{1,0:T(8,128)S(1)}, f32[96,128]{1,0:T(8,128)S(1)}, u32[]{:S(2)}, u32[]{:S(2)}) collective-permute-start(f32[96,128]{1,0:T(8,128)S(1)} %get-tuple-element.45), channel_id=1, source_target_pairs={{0,24},{8,0},{16,8},{24,16},{1,25},{9,1},{17,9},{25,17},{2,26},{10... | collective-permute-start | bytes 147464 | tf_op jit(solution)/shard_map/ppermute | solution.py:334
  12.5 1.0 %inner.2.base = f32[4,16,3072]{2,1,0:T(8,128)S(1)} custom-call(f32[2,16,3072]{2,1,0:T(8,128)S(1)} %get-tuple-element.34.x1, f32[2,16,3072]{2,1,0:T(8,128)S(1)} %get-tuple-element.35.x2, f32[3,16,1]{2,1,0:T(8,128)S(1)} %get-tuple-element.36.coef), custom_call_target="tpu_custom_call" | custom-call | bytes 1573056 | tf_op jit(solution)/shard_map/inner/pallas_call | solution.py:280
  13.5 0.0 collective-permute-done.2.refs_0_
  13.5 0.5 %collective-permute-done.3.refs_1_ = f32[96,128]{1,0:T(8,128)S(1)} collective-permute-done((f32[96,128]{1,0:T(8,128)S(1)}, f32[96,128]{1,0:T(8,128)S(1)}, u32[]{:S(2)}, u32[]{:S(2)}) %collective-permute-start.3) | collective-permute-done | bytes 49184 | tf_op jit(solution)/shard_map/ppermute | solution.py:334
  14.0 1.2 %collective-permute-done.4.refs_2_ = f32[96,128]{1,0:T(8,128)S(1)} collective-permute-done((f32[96,128]{1,0:T(8,128)S(1)}, f32[96,128]{1,0:T(8,128)S(1)}, u32[]{:S(2)}, u32[]{:S(2)}) %collective-permute-start.4) | collective-permute-done | bytes 49184 | tf_op jit(solution)/shard_map/ppermute | solution.py:334
  15.3 0.1 collective-permute-start.5
  15.4 0.8 %collective-permute-start.6 = (f32[2,3072]{1,0:T(2,128)S(1)}, f32[2,3072]{1,0:T(2,128)S(1)}, u32[]{:S(2)}, u32[]{:S(2)}) collective-permute-start(f32[2,3072]{1,0:T(2,128)S(1)} %get-tuple-element.49), channel_id=1, source_target_pairs={{0,7},{1,2},{2,1},{3,4},{4,3},{5,6},{6,5},{7,0},{8,15},{9,10},{10,... | collective-permute-start | bytes 73736 | tf_op jit(solution)/shard_map/ppermute | solution.py:344
  16.2 0.0 collective-permute-done.1.y2
  16.2 0.9 %fields.2 = (f32[4,16,3072]{2,1,0:T(8,128)S(1)}, f32[4,16,3072]{2,1,0:T(8,128)S(1)}) custom-call(f32[4,16,3072]{2,1,0:T(8,128)S(1)} %inner.2.base, f32[2,16,3072]{2,1,0:T(8,128)S(1)} %collective-permute-done.y1, f32[2,16,3072]{2,1,0:T(8,128)S(1)} %collective-permute-done.1.y2, f32[3,16,1]{2,1,0:T(8,128)S(1)} %get-tuple-element.36.coef, ...), custom_call_target="tpu_custom_call" | custom-call | flops 4000000000 | bytes 3250624 | tf_op jit(solution)/shard_map/fields/pallas_call | solution.py:280
  17.1 2.6 %collective-permute-done.6.e2 = f32[2,3072]{1,0:T(2,128)S(1)} collective-permute-done((f32[2,3072]{1,0:T(2,128)S(1)}, f32[2,3072]{1,0:T(2,128)S(1)}, u32[]{:S(2)}, u32[]{:S(2)}) %collective-permute-start.6) | collective-permute-done | bytes 24608 | tf_op jit(solution)/shard_map/ppermute | solution.py:344
  19.7 0.4 %evolve.1 = (f32[2,16,3072]{2,1,0:T(8,128)S(1)}, f32[2,16,3072]{2,1,0:T(8,128)S(1)}, f32[4,3072]{1,0:T(4,128)S(1)}) custom-call(f32[4,16,3072]{2,1,0:T(8,128)S(1)} %get-tuple-element.41.part, f32[4,16,3072]{2,1,0:T(8,128)S(1)} %get-tuple-element.42.gain, f32[4,3072]{1,0:T(4,128)S(1)} %get-tuple-element.47.ns, f32[2,3072]{1,0:T(2,128)S(1)} %collective-permute-done.5.e1, ...), custom_call_target="tpu_custom_call" | custom-call | bytes 2556096 | tf_op jit(solution)/shard_map/evolve/pallas_call | solution.py:280
  20.1 0.1 collective-permute-start.7
  20.2 0.7 %collective-permute-start.8 = (f32[2,16,3072]{2,1,0:T(8,128)S(1)}, f32[2,16,3072]{2,1,0:T(8,128)S(1)}, u32[]{:S(2)}, u32[]{:S(2)}) collective-permute-start(f32[2,16,3072]{2,1,0:T(8,128)S(1)} %get-tuple-element.51.x2), channel_id=1, source_target_pairs={{0,7},{1,2},{2,1},{3,4},{4,3},{5,6},{6,5},{7,0},{8,15},{9,10},{10,... | collective-permute-start | bytes 1179656 | tf_op jit(solution)/shard_map/ppermute | solution.py:331
  20.9 0.7 %payload.1 = (f32[96,128]{1,0:T(8,128)S(1)}, f32[96,128]{1,0:T(8,128)S(1)}, f32[96,128]{1,0:T(8,128)S(1)}) custom-call(f32[4,3072]{1,0:T(4,128)S(1)} %get-tuple-element.54.surf.refs_3_, f32[4,3072]{1,0:T(4,128)S(1)} %get-tuple-element.55.flux, f32[2304,128]{1,0:T(8,128)S(1)} %get-tuple-element.56.wide, bf16[96,288]{1,0:T(8,128)(2,1)S(1)} %get-tuple-element.57.pick, ...), custom_call_target="tpu_custom_call" | custom-call | bytes 1812480 | tf_op jit(solution)/shard_map/payload/pallas_call | solution.py:280
  21.7 0.9 %collective-permute-start.9 = (f32[96,128]{1,0:T(8,128)S(1)}, f32[96,128]{1,0:T(8,128)S(1)}, u32[]{:S(2)}, u32[]{:S(2)}) collective-permute-start(f32[96,128]{1,0:T(8,128)S(1)} %get-tuple-element.59), channel_id=1, source_target_pairs={{0,8},{8,16},{16,24},{24,0},{1,9},{9,17},{17,25},{25,1},{2,10},{10... | collective-permute-start | bytes 147464 | tf_op jit(solution)/shard_map/ppermute | solution.py:334
  22.6 2.7 %collective-permute-start.10 = (f32[96,128]{1,0:T(8,128)S(1)}, f32[96,128]{1,0:T(8,128)S(1)}, u32[]{:S(2)}, u32[]{:S(2)}) collective-permute-start(f32[96,128]{1,0:T(8,128)S(1)} %get-tuple-element.60), channel_id=1, source_target_pairs={{0,16},{8,24},{16,0},{24,8},{1,17},{9,25},{17,1},{25,9},{2,18},{10... | collective-permute-start | bytes 147464 | tf_op jit(solution)/shard_map/ppermute | solution.py:334
  25.3 0.6 %collective-permute-start.11 = (f32[96,128]{1,0:T(8,128)S(1)}, f32[96,128]{1,0:T(8,128)S(1)}, u32[]{:S(2)}, u32[]{:S(2)}) collective-permute-start(f32[96,128]{1,0:T(8,128)S(1)} %get-tuple-element.61), channel_id=1, source_target_pairs={{0,24},{8,0},{16,8},{24,16},{1,25},{9,1},{17,9},{25,17},{2,26},{10... | collective-permute-start | bytes 147464 | tf_op jit(solution)/shard_map/ppermute | solution.py:334
  25.8 1.0 %inner.3.base = f32[4,16,3072]{2,1,0:T(8,128)S(1)} custom-call(f32[2,16,3072]{2,1,0:T(8,128)S(1)} %get-tuple-element.50.x1, f32[2,16,3072]{2,1,0:T(8,128)S(1)} %get-tuple-element.51.x2, f32[3,16,1]{2,1,0:T(8,128)S(1)} %get-tuple-element.36.coef), custom_call_target="tpu_custom_call" | custom-call | bytes 1573056 | tf_op jit(solution)/shard_map/inner/pallas_call | solution.py:280
  26.9 1.3 %collective-permute-done.9.refs_0_ = f32[96,128]{1,0:T(8,128)S(1)} collective-permute-done((f32[96,128]{1,0:T(8,128)S(1)}, f32[96,128]{1,0:T(8,128)S(1)}, u32[]{:S(2)}, u32[]{:S(2)}) %collective-permute-start.9) | collective-permute-done | bytes 49184 | tf_op jit(solution)/shard_map/ppermute | solution.py:334
  28.2 1.1 %collective-permute-done.10.refs_1_ = f32[96,128]{1,0:T(8,128)S(1)} collective-permute-done((f32[96,128]{1,0:T(8,128)S(1)}, f32[96,128]{1,0:T(8,128)S(1)}, u32[]{:S(2)}, u32[]{:S(2)}) %collective-permute-start.10) | collective-permute-done | bytes 49184 | tf_op jit(solution)/shard_map/ppermute | solution.py:334
  29.2 0.3 collective-permute-done.11.refs_2_
  29.6 0.1 collective-permute-start.12
  29.7 2.3 %collective-permute-start.13 = (f32[2,3072]{1,0:T(2,128)S(1)}, f32[2,3072]{1,0:T(2,128)S(1)}, u32[]{:S(2)}, u32[]{:S(2)}) collective-permute-start(f32[2,3072]{1,0:T(2,128)S(1)} %get-tuple-element.65), channel_id=1, source_target_pairs={{0,7},{1,2},{2,1},{3,4},{4,3},{5,6},{6,5},{7,0},{8,15},{9,10},{10,... | collective-permute-start | bytes 73736 | tf_op jit(solution)/shard_map/ppermute | solution.py:344
  32.0 0.3 collective-permute-done.8.y2
  32.3 0.9 %fields.3 = (f32[4,16,3072]{2,1,0:T(8,128)S(1)}, f32[4,16,3072]{2,1,0:T(8,128)S(1)}) custom-call(f32[4,16,3072]{2,1,0:T(8,128)S(1)} %inner.3.base, f32[2,16,3072]{2,1,0:T(8,128)S(1)} %collective-permute-done.7.y1, f32[2,16,3072]{2,1,0:T(8,128)S(1)} %collective-permute-done.8.y2, f32[3,16,1]{2,1,0:T(8,128)S(1)} %get-tuple-element.36.coef, ...), custom_call_target="tpu_custom_call" | custom-call | flops 4000000000 | bytes 3250624 | tf_op jit(solution)/shard_map/fields/pallas_call | solution.py:280
  33.2 0.9 %collective-permute-done.13.e2 = f32[2,3072]{1,0:T(2,128)S(1)} collective-permute-done((f32[2,3072]{1,0:T(2,128)S(1)}, f32[2,3072]{1,0:T(2,128)S(1)}, u32[]{:S(2)}, u32[]{:S(2)}) %collective-permute-start.13) | collective-permute-done | bytes 24608 | tf_op jit(solution)/shard_map/ppermute | solution.py:344
  34.2 1.4 %close.1 = (f32[1,16,4,3072]{3,2,1,0:T(4,128)}, f32[1,4,3072]{2,1,0:T(4,128)}) custom-call(f32[4,16,3072]{2,1,0:T(8,128)S(1)} %get-tuple-element.52.part, f32[4,16,3072]{2,1,0:T(8,128)S(1)} %get-tuple-element.53.gain, f32[4,3072]{1,0:T(4,128)S(1)} %get-tuple-element.62.ns, f32[4,3072]{1,0:T(4,128)S(1)} %get-tuple-element.63.flux, ...), custom_call_target="tpu_custom_call" | custom-call | bytes 2605248 | tf_op jit(solution)/shard_map/close/pallas_call | solution.py:280
  (6 shorter events, 0.1 us)
Async XLA Ops:
  2.9 13.2 %collective-permute-start = (f32[2,16,3072]{2,1,0:T(8,128)S(1)}, f32[2,16,3072]{2,1,0:T(8,128)S(1)}, u32[]{:S(2)}, u32[]{:S(2)}) collective-permute-start(f32[2,16,3072]{2,1,0:T(8,128)S(1)} %get-tuple-element.34.x1), channel_id=1, source_target_pairs={{0,1},{1,0},{2,3},{3,2},{4,5},{5,4},{6,7},{7,6},{8,9},{9,8},{10,11... | collective-permute-start | bytes 1179656 | tf_op jit(solution)/shard_map/ppermute | solution.py:332
  3.4 12.7 %collective-permute-start.1 = (f32[2,16,3072]{2,1,0:T(8,128)S(1)}, f32[2,16,3072]{2,1,0:T(8,128)S(1)}, u32[]{:S(2)}, u32[]{:S(2)}) collective-permute-start(f32[2,16,3072]{2,1,0:T(8,128)S(1)} %get-tuple-element.35.x2), channel_id=1, source_target_pairs={{0,7},{1,2},{2,1},{3,4},{4,3},{5,6},{6,5},{7,0},{8,15},{9,10},{10,... | collective-permute-start | bytes 1179656 | tf_op jit(solution)/shard_map/ppermute | solution.py:331
  7.0 6.5 %collective-permute-start.2 = (f32[96,128]{1,0:T(8,128)S(1)}, f32[96,128]{1,0:T(8,128)S(1)}, u32[]{:S(2)}, u32[]{:S(2)}) collective-permute-start(f32[96,128]{1,0:T(8,128)S(1)} %get-tuple-element.43), channel_id=1, source_target_pairs={{0,8},{8,16},{16,24},{24,0},{1,9},{9,17},{17,25},{25,1},{2,10},{10... | collective-permute-start | bytes 147464 | tf_op jit(solution)/shard_map/ppermute | solution.py:334
  8.6 5.5 %collective-permute-start.3 = (f32[96,128]{1,0:T(8,128)S(1)}, f32[96,128]{1,0:T(8,128)S(1)}, u32[]{:S(2)}, u32[]{:S(2)}) collective-permute-start(f32[96,128]{1,0:T(8,128)S(1)} %get-tuple-element.44), channel_id=1, source_target_pairs={{0,16},{8,24},{16,0},{24,8},{1,17},{9,25},{17,1},{25,9},{2,18},{10... | collective-permute-start | bytes 147464 | tf_op jit(solution)/shard_map/ppermute | solution.py:334
  11.2 4.1 %collective-permute-start.4 = (f32[96,128]{1,0:T(8,128)S(1)}, f32[96,128]{1,0:T(8,128)S(1)}, u32[]{:S(2)}, u32[]{:S(2)}) collective-permute-start(f32[96,128]{1,0:T(8,128)S(1)} %get-tuple-element.45), channel_id=1, source_target_pairs={{0,24},{8,0},{16,8},{24,16},{1,25},{9,1},{17,9},{25,17},{2,26},{10... | collective-permute-start | bytes 147464 | tf_op jit(solution)/shard_map/ppermute | solution.py:334
  15.3 1.8 %collective-permute-start.5 = (f32[2,3072]{1,0:T(2,128)S(1)}, f32[2,3072]{1,0:T(2,128)S(1)}, u32[]{:S(2)}, u32[]{:S(2)}) collective-permute-start(f32[2,3072]{1,0:T(2,128)S(1)} %get-tuple-element.48), channel_id=1, source_target_pairs={{0,1},{1,0},{2,3},{3,2},{4,5},{5,4},{6,7},{7,6},{8,9},{9,8},{10,11... | collective-permute-start | bytes 73736 | tf_op jit(solution)/shard_map/ppermute | solution.py:345
  15.4 4.3 %collective-permute-start.6 = (f32[2,3072]{1,0:T(2,128)S(1)}, f32[2,3072]{1,0:T(2,128)S(1)}, u32[]{:S(2)}, u32[]{:S(2)}) collective-permute-start(f32[2,3072]{1,0:T(2,128)S(1)} %get-tuple-element.49), channel_id=1, source_target_pairs={{0,7},{1,2},{2,1},{3,4},{4,3},{5,6},{6,5},{7,0},{8,15},{9,10},{10,... | collective-permute-start | bytes 73736 | tf_op jit(solution)/shard_map/ppermute | solution.py:344
  20.1 11.9 %collective-permute-start.7 = (f32[2,16,3072]{2,1,0:T(8,128)S(1)}, f32[2,16,3072]{2,1,0:T(8,128)S(1)}, u32[]{:S(2)}, u32[]{:S(2)}) collective-permute-start(f32[2,16,3072]{2,1,0:T(8,128)S(1)} %get-tuple-element.50.x1), channel_id=1, source_target_pairs={{0,1},{1,0},{2,3},{3,2},{4,5},{5,4},{6,7},{7,6},{8,9},{9,8},{10,11... | collective-permute-start | bytes 1179656 | tf_op jit(solution)/shard_map/ppermute | solution.py:332
  20.2 12.1 %collective-permute-start.8 = (f32[2,16,3072]{2,1,0:T(8,128)S(1)}, f32[2,16,3072]{2,1,0:T(8,128)S(1)}, u32[]{:S(2)}, u32[]{:S(2)}) collective-permute-start(f32[2,16,3072]{2,1,0:T(8,128)S(1)} %get-tuple-element.51.x2), channel_id=1, source_target_pairs={{0,7},{1,2},{2,1},{3,4},{4,3},{5,6},{6,5},{7,0},{8,15},{9,10},{10,... | collective-permute-start | bytes 1179656 | tf_op jit(solution)/shard_map/ppermute | solution.py:331
  21.7 6.5 %collective-permute-start.9 = (f32[96,128]{1,0:T(8,128)S(1)}, f32[96,128]{1,0:T(8,128)S(1)}, u32[]{:S(2)}, u32[]{:S(2)}) collective-permute-start(f32[96,128]{1,0:T(8,128)S(1)} %get-tuple-element.59), channel_id=1, source_target_pairs={{0,8},{8,16},{16,24},{24,0},{1,9},{9,17},{17,25},{25,1},{2,10},{10... | collective-permute-start | bytes 147464 | tf_op jit(solution)/shard_map/ppermute | solution.py:334
  22.6 6.7 %collective-permute-start.10 = (f32[96,128]{1,0:T(8,128)S(1)}, f32[96,128]{1,0:T(8,128)S(1)}, u32[]{:S(2)}, u32[]{:S(2)}) collective-permute-start(f32[96,128]{1,0:T(8,128)S(1)} %get-tuple-element.60), channel_id=1, source_target_pairs={{0,16},{8,24},{16,0},{24,8},{1,17},{9,25},{17,1},{25,9},{2,18},{10... | collective-permute-start | bytes 147464 | tf_op jit(solution)/shard_map/ppermute | solution.py:334
  25.3 4.3 %collective-permute-start.11 = (f32[96,128]{1,0:T(8,128)S(1)}, f32[96,128]{1,0:T(8,128)S(1)}, u32[]{:S(2)}, u32[]{:S(2)}) collective-permute-start(f32[96,128]{1,0:T(8,128)S(1)} %get-tuple-element.61), channel_id=1, source_target_pairs={{0,24},{8,0},{16,8},{24,16},{1,25},{9,1},{17,9},{25,17},{2,26},{10... | collective-permute-start | bytes 147464 | tf_op jit(solution)/shard_map/ppermute | solution.py:334
  29.6 3.6 %collective-permute-start.12 = (f32[2,3072]{1,0:T(2,128)S(1)}, f32[2,3072]{1,0:T(2,128)S(1)}, u32[]{:S(2)}, u32[]{:S(2)}) collective-permute-start(f32[2,3072]{1,0:T(2,128)S(1)} %get-tuple-element.64), channel_id=1, source_target_pairs={{0,1},{1,0},{2,3},{3,2},{4,5},{5,4},{6,7},{7,6},{8,9},{9,8},{10,11... | collective-permute-start | bytes 73736 | tf_op jit(solution)/shard_map/ppermute | solution.py:345
  29.7 4.5 %collective-permute-start.13 = (f32[2,3072]{1,0:T(2,128)S(1)}, f32[2,3072]{1,0:T(2,128)S(1)}, u32[]{:S(2)}, u32[]{:S(2)}) collective-permute-start(f32[2,3072]{1,0:T(2,128)S(1)} %get-tuple-element.65), channel_id=1, source_target_pairs={{0,7},{1,2},{2,1},{3,4},{4,3},{5,6},{6,5},{7,0},{8,15},{9,10},{10,... | collective-permute-start | bytes 73736 | tf_op jit(solution)/shard_map/ppermute | solution.py:344

commit v4 on v3

--- a/solution.py
+++ b/solution.py
@@ -18,19 +18,22 @@
 PARAMS = pltpu.CompilerParams(vmem_limit_bytes=40 * 1024 * 1024)
 
 
-def partner_offsets(groups):
-    air_count = 3 * groups // 4
-    upward = [(air_count + member // 3 - member) % groups for member in range(air_count)]
-    downward = [
-        (3 * member + offset - air_count - member) % groups
-        for member in range(groups - air_count)
-        for offset in range(3)
-    ]
-    return sorted(set(upward + downward))
-
-
-def ring_pairs(count, steps):
-    return [(source, (source + steps) % count) for source in range(count)]
+MEMBERS = 3
+
+
+def partner_pairs(groups, tiles, member):
+    air_count = MEMBERS * groups // 4
+    pairs = []
+    for group in range(groups):
+        ocean = group >= air_count
+        if ocean:
+            partner = MEMBERS * (group - air_count) + member
+        else:
+            partner = air_count + group // MEMBERS if group % MEMBERS == member else group
+        for tile in range(tiles):
+            other = tile ^ 1 if partner == group else tile
+            pairs.append((group * tiles + tile, partner * tiles + other))
+    return pairs
 
 
 def inner_pairs(count):
@@ -75,51 +78,17 @@
     return jnp.sum(jnp.where(diagonal, row, 0.0), axis=1, keepdims=True)
 
 
-def open_kernel(offsets, groups, *refs):
-    args, refs = refs[:10], refs[10:]
-    state, coupling, mask, codes, mixing, courant, matrices, weights, sources, targets = args
-    x1, x2, surface, mask_out, codes_out, coef, table, col0, wide, pick, chosen, *refs = refs
-    outs, refs = refs[: len(offsets)], refs[len(offsets) :]
-    state_v, coupling_v, weights_v, mixing_v, courant_v, matrices_v, sources_v, targets_v, blk, sems = refs
-    pairs = (
-        (sources, sources_v),
-        (targets, targets_v),
-        (mixing, mixing_v),
-        (courant, courant_v),
-        (matrices, matrices_v),
-        (coupling, coupling_v),
-        (mask, mask_out),
-        (codes, codes_out),
-        (weights, weights_v),
-        (state, state_v),
-    )
-    copies = [pltpu.make_async_copy(src, dst, sems.at[n]) for n, (src, dst) in enumerate(pairs)]
+def load_kernel(*refs):
+    state, *args = refs[:10]
+    x1, x2, surface = refs[10:13]
+    outs, (state_v, sems) = refs[13:22], refs[22:]
+    copies = [
+        pltpu.make_async_copy(src, dst, sems.at[n])
+        for n, (src, dst) in enumerate(zip((state, *args), (state_v, *outs)))
+    ]
     for copy in copies:
         copy.start()
-    small = 8
-    for copy in copies[:small]:
-        copy.wait()
-    count, margins = pick.shape
-    block = blk.shape[1]
-    slot = lax.broadcasted_iota(jnp.int32, (count, margins), 0)
-    pick[...] = (slot == sources_v[...]).astype(F32).astype(BF16)
-    me = lax.axis_index("comp")
-    for n, offset in enumerate(offsets):
-        base = lax.rem(me + offset, groups) * count
-        hit = (targets_v[...] == slot + base).astype(F32).astype(BF16)
-        chosen[n * count : (n + 1) * count] = jnp.concatenate([hit, hit], axis=1)
-    m, c = column(mixing_v[...]), column(courant_v[...])
-    coef[0], coef[1], coef[2] = 1.0 - 4.0 * m - c, m + c, m
-    branches, fields = matrices_v.shape[1:3]
-    flat = matrices_v[0].reshape(branches * fields, fields)
-    col0[...] = flat[:, :1].reshape(branches, fields, 1)
-    flat = jnp.where(lax.broadcasted_iota(jnp.int32, flat.shape, 1) == 0, 0.0, flat)
-    high, low = split_high_low(flat)
-    table[...] = jnp.concatenate([high, high, low], axis=1)
-    copies[small].wait()
-    wide[...] = weights_v[0].reshape(wide.shape).astype(F32)
-    payload(coupling_v[0], wide, pick, chosen, outs, blk)
-    copies[small + 1].wait()
+    copies[0].wait()
     odd = lax.rem(lax.axis_index("tile"), 2) == 1
     half = x1.shape[0]
     for i in range(half):
@@ -127,6 +96,32 @@
         x1[i] = jnp.where(odd, head, tail)
         x2[i] = jnp.where(odd, tail, head)
     surface[...] = state_v[0, 0]
+    for copy in copies[1:]:
+        copy.wait()
+
+
+def remap_kernel(groups, coupling, mixing, courant, matrices, weights, sources, targets, *refs):
+    coef, table, col0, wide, pick, chosen, *outs, blk = refs
+    count, margins = pick.shape
+    slot = lax.broadcasted_iota(jnp.int32, (count, margins), 0)
+    pick[...] = (slot == sources[...]).astype(F32).astype(BF16)
+    me = lax.axis_index("comp")
+    air_count = MEMBERS * groups // 4
+    for n in range(MEMBERS):
+        ocean = jnp.where(lax.rem(me, MEMBERS) == n, air_count + lax.div(me, MEMBERS), me)
+        partner = jnp.where(me < air_count, ocean, MEMBERS * (me - air_count) + n)
+        hit = (targets[...] == slot + partner * count).astype(F32).astype(BF16)
+        chosen[n * count : (n + 1) * count] = jnp.concatenate([hit, hit], axis=1)
+    wide[...] = weights[0].reshape(wide.shape).astype(F32)
+    payload(coupling[0], wide, pick, chosen, outs, blk)
+    m, c = column(mixing[...]), column(courant[...])
+    coef[0], coef[1], coef[2] = 1.0 - 4.0 * m - c, m + c, m
+    branches, fields = matrices.shape[1:3]
+    flat = matrices[0].reshape(branches * fields, fields)
+    col0[...] = flat[:, :1].reshape(branches, fields, 1)
+    flat = jnp.where(lax.broadcasted_iota(jnp.int32, flat.shape, 1) == 0, 0.0, flat)
+    high, low = split_high_low(flat)
+    table[...] = jnp.concatenate([high, high, low], axis=1)
 
 
 def surface_kernel(groups, n_rec, *refs):
@@ -294,7 +289,6 @@
 ):
     groups = lax.axis_size("comp")
     tiles = lax.axis_size("tile")
-    offsets = partner_offsets(groups)
     _, fields, rows, width = state.shape
     _, margins, band, block = weights.shape
     count = rows * width // block
@@ -303,36 +297,40 @@
     shape = jax.ShapeDtypeStruct
 
     halves = [shape((half, fields, width), F32)] * 2
-    payloads = [shape((count, block), F32)] * len(offsets)
+    payloads = [shape((count, block), F32)] * MEMBERS
     blocks = pltpu.VMEM((count, block), F32)
+    args = (
+        state, coupling, land_mask, codes, mixing, courant, matrices, weights, sources, targets
+    )
+    x1, x2, surface, handed, mask, codes, *raw = call(
+        load_kernel,
+        "load",
+        halves + [shape((rows, width), F32)] + [shape(a.shape, a.dtype) for a in args[1:]],
+        [pltpu.with_memory_space_constraint(a, pltpu.HBM) for a in args],
+        [pltpu.VMEM(state.shape, F32), pltpu.SemaphoreType.DMA((len(args),))],
+        [pl.BlockSpec(memory_space=pltpu.HBM)] * len(args),
+    )
     tables = [
-        shape(land_mask.shape, jnp.int32),
-        shape(codes.shape, jnp.int32),
         shape((3, fields, 1), F32),
         shape((branches * fields, 3 * fields), BF16),
         shape((branches, fields, 1), F32),
         shape((margins * band, block), F32),
         shape((count, margins), BF16),
-        shape((len(offsets) * count, 2 * margins), BF16),
+        shape((MEMBERS * count, 2 * margins), BF16),
     ]
-    args = (
-        state, coupling, land_mask, codes, mixing, courant, matrices, weights, sources, targets
-    )
-    staged = (state, coupling, weights, mixing, courant, matrices, sources, targets)
-    x1, x2, surface, mask, codes, coef, table, col0, wide, pick, chosen, *sent = call(
-        functools.partial(open_kernel, offsets, groups),
-        "open",
-        halves + [shape((rows, width), F32)] + tables + payloads,
-        [pltpu.with_memory_space_constraint(a, pltpu.HBM) for a in args],
-        [pltpu.VMEM(a.shape, a.dtype) for a in staged] + [blocks, pltpu.SemaphoreType.DMA((10,))],
-        [pl.BlockSpec(memory_space=pltpu.HBM)] * len(args),
+    coef, table, col0, wide, pick, chosen, *sent = call(
+        functools.partial(remap_kernel, groups),
+        "remap",
+        tables + payloads,
+        (handed, *raw),
+        [blocks],
     )
     for interval in range(INTERVALS):
         y2 = lax.ppermute(x2, "tile", outer_pairs(tiles))
         y1 = lax.ppermute(x1, "tile", inner_pairs(tiles))
         recs = [
-            lax.ppermute(value, "comp", ring_pairs(groups, offset))
-            for value, offset in zip(sent, offsets)
+            lax.ppermute(value, ("comp", "tile"), partner_pairs(groups, tiles, member))
+            for member, value in enumerate(sent)
         ]
         ns, flux, d1, d2 = call(
             functools.partial(surface_kernel, groups, len(recs)),

time: 35.7 us -> 33.6 us (0.941)
  starting transfers between devices: 17.8 us -> 16.1 us
  waiting for transfers between devices: 8.27 us -> 7.78 us
    ppermute x6, starting transfers between devices: 9.69 us -> 8.56 us  [on_device(): lax.ppermute(value, ('comp', 'tile'), partner_pairs(groups, tiles, member))]
    ppermute x2, waiting for transfers between devices: 0.33 us -> 1.32 us  [on_device(): y2 = lax.ppermute(x2, 'tile', outer_pairs(tiles))]
    ppermute x2, waiting for transfers between devices: 3.52 us -> 2.62 us  [on_device(): e2 = lax.ppermute(d2, 'tile', outer_pairs(tiles))]
    ppermute x6, waiting for transfers between devices: 4.41 us -> 3.83 us  [on_device(): lax.ppermute(value, ('comp', 'tile'), partner_pairs(groups, tiles, member))]
    ppermute x2, starting transfers between devices: 3.07 us -> 2.65 us  [on_device(): e2 = lax.ppermute(d2, 'tile', outer_pairs(tiles))]
    pallas_call x10 -> x11, Pallas kernels: 8.82 us -> 8.81 us  [call(): pl.pallas_call(kernel, name=name, out_shape=outs, in_specs=in_specs or [V...]
  transfers between devices with their start and end apart: 14 -> 14, of which waited for: 8 -> 6; matrix products, arithmetic and copies ran while one was open for 0% -> 0% of each run, Pallas kernels for 13% -> 16%
where the time goes in v4:
time: 33.6 us; the launch traced here: 33.5 us
  starting transfers between devices  16.1 us (48%)
  Pallas kernels  8.81 us (26%)
  waiting for transfers between devices  7.78 us (23%)
  between operations  0.76 us (2%)
    pallas_call x11, Pallas kernels, call(): pl.pallas_call(kernel, name=name, out_shape=outs, in_specs=in_specs or [V...  8.81 us
    ppermute x6, starting transfers between devices, on_device(): lax.ppermute(value, ('comp', 'tile'), partner_pairs(groups, tiles, member))  8.56 us
    ppermute x2, starting transfers between devices, on_device(): y2 = lax.ppermute(x2, 'tile', outer_pairs(tiles))  4.19 us
    ppermute x6, waiting for transfers between devices, on_device(): lax.ppermute(value, ('comp', 'tile'), partner_pairs(groups, tiles, member))  3.83 us
    ppermute x2, starting transfers between devices, on_device(): e2 = lax.ppermute(d2, 'tile', outer_pairs(tiles))  2.65 us
    ppermute x2, waiting for transfers between devices, on_device(): e2 = lax.ppermute(d2, 'tile', outer_pairs(tiles))  2.62 us
    ppermute x2, waiting for transfers between devices, on_device(): y2 = lax.ppermute(x2, 'tile', outer_pairs(tiles))  1.32 us
  transfers between devices with their start and end apart: 14, of which 6 were waited for; matrix products, arithmetic and copies ran while one was open for 0% of the time, Pallas kernels for 16%

profile of v4, /device:TPU:0, one launch (start us, length us, event | category | flops | bytes accessed | tf_op | source)
XLA Modules:
  0.0 33.5 jit_solution(4588678334367733320)
XLA Ops:
  0.6 1.5 %load.1 = (f32[2,16,3072]{2,1,0:T(8,128)S(1)}, f32[2,16,3072]{2,1,0:T(8,128)S(1)}, f32[4,3072]{1,0:T(4,128)S(1)}, f32[1,4,3072]{2,1,0:T(4,128)S(1)}, s32[1,4,307...) custom-call(f32[1,16,4,3072]{3,2,1,0:T(4,128)} %refs_0_.1, ...), custom_call_target="tpu_custom_call" | custom-call | bytes 3109632 | tf_op jit(solution)/shard_map/load/pallas_call | solution.py:275
  2.1 0.5 %collective-permute-start = (f32[2,16,3072]{2,1,0:T(8,128)S(1)}, f32[2,16,3072]{2,1,0:T(8,128)S(1)}, u32[]{:S(2)}, u32[]{:S(2)}) collective-permute-start(f32[2,16,3072]{2,1,0:T(8,128)S(1)} %get-tuple-element.41.x1), channel_id=1, source_target_pairs={{0,1},{1,0},{2,3},{3,2},{4,5},{5,4},{6,7},{7,6},{8,9},{9,8},{10,11... | collective-permute-start | bytes 1179656 | tf_op jit(solution)/shard_map/ppermute | solution.py:330
  2.7 3.6 %collective-permute-start.1 = (f32[2,16,3072]{2,1,0:T(8,128)S(1)}, f32[2,16,3072]{2,1,0:T(8,128)S(1)}, u32[]{:S(2)}, u32[]{:S(2)}) collective-permute-start(f32[2,16,3072]{2,1,0:T(8,128)S(1)} %get-tuple-element.42.x2), channel_id=1, source_target_pairs={{0,7},{1,2},{2,1},{3,4},{4,3},{5,6},{6,5},{7,0},{8,15},{9,10},{10,... | collective-permute-start | bytes 1179656 | tf_op jit(solution)/shard_map/ppermute | solution.py:329
  6.2 0.8 %remap.1 = (f32[3,16,1]{2,1,0:T(8,128)S(1)}, bf16[64,48]{1,0:T(8,128)(2,1)S(1)}, f32[4,16,1]{2,1,0:T(8,128)S(1)}, f32[2304,128]{1,0:T(8,128)S(1)}, bf16[96,288]{...) custom-call(f32[1,4,3072]{2,1,0:T(4,128)S(1)} %get-tuple-element.43., ...), custom_call_target="tpu_custom_call" | custom-call | bytes 2366272 | tf_op jit(solution)/shard_map/remap/pallas_call | solution.py:275
  7.0 3.7 %collective-permute-start.2 = (f32[96,128]{1,0:T(8,128)S(1)}, f32[96,128]{1,0:T(8,128)S(1)}, u32[]{:S(2)}, u32[]{:S(2)}) collective-permute-start(f32[96,128]{1,0:T(8,128)S(1)} %get-tuple-element.57), channel_id=1, source_target_pairs={{0,24},{1,25},{2,26},{3,27},{4,28},{5,29},{6,30},{7,31},{8,9},{9,8... | collective-permute-start | bytes 147464 | tf_op jit(solution)/shard_map/ppermute | solution.py:332
  10.6 0.0 collective-permute-start.3
  10.6 0.5 %collective-permute-start.4 = (f32[96,128]{1,0:T(8,128)S(1)}, f32[96,128]{1,0:T(8,128)S(1)}, u32[]{:S(2)}, u32[]{:S(2)}) collective-permute-start(f32[96,128]{1,0:T(8,128)S(1)} %get-tuple-element.59), channel_id=1, source_target_pairs={{0,1},{1,0},{2,3},{3,2},{4,5},{5,4},{6,7},{7,6},{8,9},{9,8},{10,11... | collective-permute-start | bytes 147464 | tf_op jit(solution)/shard_map/ppermute | solution.py:332
  11.2 1.0 %inner.2.base = f32[4,16,3072]{2,1,0:T(8,128)S(1)} custom-call(f32[2,16,3072]{2,1,0:T(8,128)S(1)} %get-tuple-element.41.x1, f32[2,16,3072]{2,1,0:T(8,128)S(1)} %get-tuple-element.42.x2, f32[3,16,1]{2,1,0:T(8,128)S(1)} %get-tuple-element.50.coef), custom_call_target="tpu_custom_call" | custom-call | bytes 1573056 | tf_op jit(solution)/shard_map/inner/pallas_call | solution.py:275
  12.2 1.3 %collective-permute-done.2.refs_0_ = f32[96,128]{1,0:T(8,128)S(1)} collective-permute-done((f32[96,128]{1,0:T(8,128)S(1)}, f32[96,128]{1,0:T(8,128)S(1)}, u32[]{:S(2)}, u32[]{:S(2)}) %collective-permute-start.2) | collective-permute-done | bytes 49184 | tf_op jit(solution)/shard_map/ppermute | solution.py:332
  13.5 0.0 collective-permute-done.3.refs_1_
  13.5 0.0 collective-permute-done.4.refs_2_
  13.5 0.1 collective-permute-start.5
  13.6 0.6 %collective-permute-start.6 = (f32[2,3072]{1,0:T(2,128)S(1)}, f32[2,3072]{1,0:T(2,128)S(1)}, u32[]{:S(2)}, u32[]{:S(2)}) collective-permute-start(f32[2,3072]{1,0:T(2,128)S(1)} %get-tuple-element.63), channel_id=1, source_target_pairs={{0,7},{1,2},{2,1},{3,4},{4,3},{5,6},{6,5},{7,0},{8,15},{9,10},{10,... | collective-permute-start | bytes 73736 | tf_op jit(solution)/shard_map/ppermute | solution.py:342
  14.2 0.0 collective-permute-done.y1
  14.2 0.9 %collective-permute-done.1.y2 = f32[2,16,3072]{2,1,0:T(8,128)S(1)} collective-permute-done((f32[2,16,3072]{2,1,0:T(8,128)S(1)}, f32[2,16,3072]{2,1,0:T(8,128)S(1)}, u32[]{:S(2)}, u32[]{:S(2)}) %collective-permute-start.1) | collective-permute-done | bytes 393248 | tf_op jit(solution)/shard_map/ppermute | solution.py:329
  15.1 0.9 %fields.2 = (f32[4,16,3072]{2,1,0:T(8,128)S(1)}, f32[4,16,3072]{2,1,0:T(8,128)S(1)}) custom-call(f32[4,16,3072]{2,1,0:T(8,128)S(1)} %inner.2.base, f32[2,16,3072]{2,1,0:T(8,128)S(1)} %collective-permute-done.y1, f32[2,16,3072]{2,1,0:T(8,128)S(1)} %collective-permute-done.1.y2, f32[3,16,1]{2,1,0:T(8,128)S(1)} %get-tuple-element.50.coef, ...), custom_call_target="tpu_custom_call" | custom-call | flops 4000000000 | bytes 3250624 | tf_op jit(solution)/shard_map/fields/pallas_call | solution.py:275
  16.0 1.8 %collective-permute-done.6.e2 = f32[2,3072]{1,0:T(2,128)S(1)} collective-permute-done((f32[2,3072]{1,0:T(2,128)S(1)}, f32[2,3072]{1,0:T(2,128)S(1)}, u32[]{:S(2)}, u32[]{:S(2)}) %collective-permute-start.6) | collective-permute-done | bytes 24608 | tf_op jit(solution)/shard_map/ppermute | solution.py:342
  17.8 0.4 %evolve.1 = (f32[2,16,3072]{2,1,0:T(8,128)S(1)}, f32[2,16,3072]{2,1,0:T(8,128)S(1)}, f32[4,3072]{1,0:T(4,128)S(1)}) custom-call(f32[4,16,3072]{2,1,0:T(8,128)S(1)} %get-tuple-element.55.part, f32[4,16,3072]{2,1,0:T(8,128)S(1)} %get-tuple-element.56.gain, f32[4,3072]{1,0:T(4,128)S(1)} %get-tuple-element.61.ns, f32[2,3072]{1,0:T(2,128)S(1)} %collective-permute-done.5.e1, ...), custom_call_target="tpu_custom_call" | custom-call | bytes 2556096 | tf_op jit(solution)/shard_map/evolve/pallas_call | solution.py:275
  18.3 0.1 collective-permute-start.7
  18.3 0.6 %collective-permute-start.8 = (f32[2,16,3072]{2,1,0:T(8,128)S(1)}, f32[2,16,3072]{2,1,0:T(8,128)S(1)}, u32[]{:S(2)}, u32[]{:S(2)}) collective-permute-start(f32[2,16,3072]{2,1,0:T(8,128)S(1)} %get-tuple-element.65.x2), channel_id=1, source_target_pairs={{0,7},{1,2},{2,1},{3,4},{4,3},{5,6},{6,5},{7,0},{8,15},{9,10},{10,... | collective-permute-start | bytes 1179656 | tf_op jit(solution)/shard_map/ppermute | solution.py:329
  19.0 0.7 %payload.1 = (f32[96,128]{1,0:T(8,128)S(1)}, f32[96,128]{1,0:T(8,128)S(1)}, f32[96,128]{1,0:T(8,128)S(1)}) custom-call(f32[4,3072]{1,0:T(4,128)S(1)} %get-tuple-element.68.surf.refs_3_, f32[4,3072]{1,0:T(4,128)S(1)} %get-tuple-element.69.flux, f32[2304,128]{1,0:T(8,128)S(1)} %get-tuple-element.70.wide, bf16[96,288]{1,0:T(8,128)(2,1)S(1)} %get-tuple-element.71.pick, ...), custom_call_target="tpu_custom_call" | custom-call | bytes 1812480 | tf_op jit(solution)/shard_map/payload/pallas_call | solution.py:275
  19.7 0.3 collective-permute-start.10
  20.1 0.2 collective-permute-start.11
  20.3 3.8 %collective-permute-start.9 = (f32[96,128]{1,0:T(8,128)S(1)}, f32[96,128]{1,0:T(8,128)S(1)}, u32[]{:S(2)}, u32[]{:S(2)}) collective-permute-start(f32[96,128]{1,0:T(8,128)S(1)} %get-tuple-element.73), channel_id=1, source_target_pairs={{0,24},{1,25},{2,26},{3,27},{4,28},{5,29},{6,30},{7,31},{8,9},{9,8... | collective-permute-start | bytes 147464 | tf_op jit(solution)/shard_map/ppermute | solution.py:332
  24.1 1.0 %inner.3.base = f32[4,16,3072]{2,1,0:T(8,128)S(1)} custom-call(f32[2,16,3072]{2,1,0:T(8,128)S(1)} %get-tuple-element.64.x1, f32[2,16,3072]{2,1,0:T(8,128)S(1)} %get-tuple-element.65.x2, f32[3,16,1]{2,1,0:T(8,128)S(1)} %get-tuple-element.50.coef), custom_call_target="tpu_custom_call" | custom-call | bytes 1573056 | tf_op jit(solution)/shard_map/inner/pallas_call | solution.py:275
  25.2 2.6 %collective-permute-done.9.refs_0_ = f32[96,128]{1,0:T(8,128)S(1)} collective-permute-done((f32[96,128]{1,0:T(8,128)S(1)}, f32[96,128]{1,0:T(8,128)S(1)}, u32[]{:S(2)}, u32[]{:S(2)}) %collective-permute-start.9) | collective-permute-done | bytes 49184 | tf_op jit(solution)/shard_map/ppermute | solution.py:332
  27.8 0.1 collective-permute-start.12
  27.9 2.0 %collective-permute-start.13 = (f32[2,3072]{1,0:T(2,128)S(1)}, f32[2,3072]{1,0:T(2,128)S(1)}, u32[]{:S(2)}, u32[]{:S(2)}) collective-permute-start(f32[2,3072]{1,0:T(2,128)S(1)} %get-tuple-element.79), channel_id=1, source_target_pairs={{0,7},{1,2},{2,1},{3,4},{4,3},{5,6},{6,5},{7,0},{8,15},{9,10},{10,... | collective-permute-start | bytes 73736 | tf_op jit(solution)/shard_map/ppermute | solution.py:342
  29.9 0.5 %collective-permute-done.8.y2 = f32[2,16,3072]{2,1,0:T(8,128)S(1)} collective-permute-done((f32[2,16,3072]{2,1,0:T(8,128)S(1)}, f32[2,16,3072]{2,1,0:T(8,128)S(1)}, u32[]{:S(2)}, u32[]{:S(2)}) %collective-permute-start.8) | collective-permute-done | bytes 393248 | tf_op jit(solution)/shard_map/ppermute | solution.py:329
  30.3 0.9 %fields.3 = (f32[4,16,3072]{2,1,0:T(8,128)S(1)}, f32[4,16,3072]{2,1,0:T(8,128)S(1)}) custom-call(f32[4,16,3072]{2,1,0:T(8,128)S(1)} %inner.3.base, f32[2,16,3072]{2,1,0:T(8,128)S(1)} %collective-permute-done.7.y1, f32[2,16,3072]{2,1,0:T(8,128)S(1)} %collective-permute-done.8.y2, f32[3,16,1]{2,1,0:T(8,128)S(1)} %get-tuple-element.50.coef, ...), custom_call_target="tpu_custom_call" | custom-call | flops 4000000000 | bytes 3250624 | tf_op jit(solution)/shard_map/fields/pallas_call | solution.py:275
  31.3 0.8 %collective-permute-done.13.e2 = f32[2,3072]{1,0:T(2,128)S(1)} collective-permute-done((f32[2,3072]{1,0:T(2,128)S(1)}, f32[2,3072]{1,0:T(2,128)S(1)}, u32[]{:S(2)}, u32[]{:S(2)}) %collective-permute-start.13) | collective-permute-done | bytes 24608 | tf_op jit(solution)/shard_map/ppermute | solution.py:342
  32.1 1.4 %close.1 = (f32[1,16,4,3072]{3,2,1,0:T(4,128)}, f32[1,4,3072]{2,1,0:T(4,128)}) custom-call(f32[4,16,3072]{2,1,0:T(8,128)S(1)} %get-tuple-element.66.part, f32[4,16,3072]{2,1,0:T(8,128)S(1)} %get-tuple-element.67.gain, f32[4,3072]{1,0:T(4,128)S(1)} %get-tuple-element.76.ns, f32[4,3072]{1,0:T(4,128)S(1)} %get-tuple-element.77.flux, ...), custom_call_target="tpu_custom_call" | custom-call | bytes 2605248 | tf_op jit(solution)/shard_map/close/pallas_call | solution.py:275
  (7 shorter events, 0.1 us)
Async XLA Ops:
  2.1 12.1 %collective-permute-start = (f32[2,16,3072]{2,1,0:T(8,128)S(1)}, f32[2,16,3072]{2,1,0:T(8,128)S(1)}, u32[]{:S(2)}, u32[]{:S(2)}) collective-permute-start(f32[2,16,3072]{2,1,0:T(8,128)S(1)} %get-tuple-element.41.x1), channel_id=1, source_target_pairs={{0,1},{1,0},{2,3},{3,2},{4,5},{5,4},{6,7},{7,6},{8,9},{9,8},{10,11... | collective-permute-start | bytes 1179656 | tf_op jit(solution)/shard_map/ppermute | solution.py:330
  2.7 12.4 %collective-permute-start.1 = (f32[2,16,3072]{2,1,0:T(8,128)S(1)}, f32[2,16,3072]{2,1,0:T(8,128)S(1)}, u32[]{:S(2)}, u32[]{:S(2)}) collective-permute-start(f32[2,16,3072]{2,1,0:T(8,128)S(1)} %get-tuple-element.42.x2), channel_id=1, source_target_pairs={{0,7},{1,2},{2,1},{3,4},{4,3},{5,6},{6,5},{7,0},{8,15},{9,10},{10,... | collective-permute-start | bytes 1179656 | tf_op jit(solution)/shard_map/ppermute | solution.py:329
  7.0 6.5 %collective-permute-start.2 = (f32[96,128]{1,0:T(8,128)S(1)}, f32[96,128]{1,0:T(8,128)S(1)}, u32[]{:S(2)}, u32[]{:S(2)}) collective-permute-start(f32[96,128]{1,0:T(8,128)S(1)} %get-tuple-element.57), channel_id=1, source_target_pairs={{0,24},{1,25},{2,26},{3,27},{4,28},{5,29},{6,30},{7,31},{8,9},{9,8... | collective-permute-start | bytes 147464 | tf_op jit(solution)/shard_map/ppermute | solution.py:332
  10.6 2.8 %collective-permute-start.3 = (f32[96,128]{1,0:T(8,128)S(1)}, f32[96,128]{1,0:T(8,128)S(1)}, u32[]{:S(2)}, u32[]{:S(2)}) collective-permute-start(f32[96,128]{1,0:T(8,128)S(1)} %get-tuple-element.58), channel_id=1, source_target_pairs={{0,1},{1,0},{2,3},{3,2},{4,5},{5,4},{6,7},{7,6},{8,24},{9,25},{10,... | collective-permute-start | bytes 147464 | tf_op jit(solution)/shard_map/ppermute | solution.py:332
  10.6 2.8 %collective-permute-start.4 = (f32[96,128]{1,0:T(8,128)S(1)}, f32[96,128]{1,0:T(8,128)S(1)}, u32[]{:S(2)}, u32[]{:S(2)}) collective-permute-start(f32[96,128]{1,0:T(8,128)S(1)} %get-tuple-element.59), channel_id=1, source_target_pairs={{0,1},{1,0},{2,3},{3,2},{4,5},{5,4},{6,7},{7,6},{8,9},{9,8},{10,11... | collective-permute-start | bytes 147464 | tf_op jit(solution)/shard_map/ppermute | solution.py:332
  13.5 2.5 %collective-permute-start.5 = (f32[2,3072]{1,0:T(2,128)S(1)}, f32[2,3072]{1,0:T(2,128)S(1)}, u32[]{:S(2)}, u32[]{:S(2)}) collective-permute-start(f32[2,3072]{1,0:T(2,128)S(1)} %get-tuple-element.62), channel_id=1, source_target_pairs={{0,1},{1,0},{2,3},{3,2},{4,5},{5,4},{6,7},{7,6},{8,9},{9,8},{10,11... | collective-permute-start | bytes 73736 | tf_op jit(solution)/shard_map/ppermute | solution.py:343
  13.6 4.2 %collective-permute-start.6 = (f32[2,3072]{1,0:T(2,128)S(1)}, f32[2,3072]{1,0:T(2,128)S(1)}, u32[]{:S(2)}, u32[]{:S(2)}) collective-permute-start(f32[2,3072]{1,0:T(2,128)S(1)} %get-tuple-element.63), channel_id=1, source_target_pairs={{0,7},{1,2},{2,1},{3,4},{4,3},{5,6},{6,5},{7,0},{8,15},{9,10},{10,... | collective-permute-start | bytes 73736 | tf_op jit(solution)/shard_map/ppermute | solution.py:342
  18.3 11.6 %collective-permute-start.7 = (f32[2,16,3072]{2,1,0:T(8,128)S(1)}, f32[2,16,3072]{2,1,0:T(8,128)S(1)}, u32[]{:S(2)}, u32[]{:S(2)}) collective-permute-start(f32[2,16,3072]{2,1,0:T(8,128)S(1)} %get-tuple-element.64.x1), channel_id=1, source_target_pairs={{0,1},{1,0},{2,3},{3,2},{4,5},{5,4},{6,7},{7,6},{8,9},{9,8},{10,11... | collective-permute-start | bytes 1179656 | tf_op jit(solution)/shard_map/ppermute | solution.py:330
  18.3 12.0 %collective-permute-start.8 = (f32[2,16,3072]{2,1,0:T(8,128)S(1)}, f32[2,16,3072]{2,1,0:T(8,128)S(1)}, u32[]{:S(2)}, u32[]{:S(2)}) collective-permute-start(f32[2,16,3072]{2,1,0:T(8,128)S(1)} %get-tuple-element.65.x2), channel_id=1, source_target_pairs={{0,7},{1,2},{2,1},{3,4},{4,3},{5,6},{6,5},{7,0},{8,15},{9,10},{10,... | collective-permute-start | bytes 1179656 | tf_op jit(solution)/shard_map/ppermute | solution.py:329
  19.7 5.4 %collective-permute-start.10 = (f32[96,128]{1,0:T(8,128)S(1)}, f32[96,128]{1,0:T(8,128)S(1)}, u32[]{:S(2)}, u32[]{:S(2)}) collective-permute-start(f32[96,128]{1,0:T(8,128)S(1)} %get-tuple-element.74), channel_id=1, source_target_pairs={{0,1},{1,0},{2,3},{3,2},{4,5},{5,4},{6,7},{7,6},{8,24},{9,25},{10,... | collective-permute-start | bytes 147464 | tf_op jit(solution)/shard_map/ppermute | solution.py:332
  20.1 5.1 %collective-permute-start.11 = (f32[96,128]{1,0:T(8,128)S(1)}, f32[96,128]{1,0:T(8,128)S(1)}, u32[]{:S(2)}, u32[]{:S(2)}) collective-permute-start(f32[96,128]{1,0:T(8,128)S(1)} %get-tuple-element.75), channel_id=1, source_target_pairs={{0,1},{1,0},{2,3},{3,2},{4,5},{5,4},{6,7},{7,6},{8,9},{9,8},{10,11... | collective-permute-start | bytes 147464 | tf_op jit(solution)/shard_map/ppermute | solution.py:332
  20.3 7.4 %collective-permute-start.9 = (f32[96,128]{1,0:T(8,128)S(1)}, f32[96,128]{1,0:T(8,128)S(1)}, u32[]{:S(2)}, u32[]{:S(2)}) collective-permute-start(f32[96,128]{1,0:T(8,128)S(1)} %get-tuple-element.73), channel_id=1, source_target_pairs={{0,24},{1,25},{2,26},{3,27},{4,28},{5,29},{6,30},{7,31},{8,9},{9,8... | collective-permute-start | bytes 147464 | tf_op jit(solution)/shard_map/ppermute | solution.py:332
  27.8 3.5 %collective-permute-start.12 = (f32[2,3072]{1,0:T(2,128)S(1)}, f32[2,3072]{1,0:T(2,128)S(1)}, u32[]{:S(2)}, u32[]{:S(2)}) collective-permute-start(f32[2,3072]{1,0:T(2,128)S(1)} %get-tuple-element.78), channel_id=1, source_target_pairs={{0,1},{1,0},{2,3},{3,2},{4,5},{5,4},{6,7},{7,6},{8,9},{9,8},{10,11... | collective-permute-start | bytes 73736 | tf_op jit(solution)/shard_map/ppermute | solution.py:343
  27.9 4.2 %collective-permute-start.13 = (f32[2,3072]{1,0:T(2,128)S(1)}, f32[2,3072]{1,0:T(2,128)S(1)}, u32[]{:S(2)}, u32[]{:S(2)}) collective-permute-start(f32[2,3072]{1,0:T(2,128)S(1)} %get-tuple-element.79), channel_id=1, source_target_pairs={{0,7},{1,2},{2,1},{3,4},{4,3},{5,6},{6,5},{7,0},{8,15},{9,10},{10,... | collective-permute-start | bytes 73736 | tf_op jit(solution)/shard_map/ppermute | solution.py:342

commit v5 on v4

v5 whole, which is shorter than its diff:
```python
import functools

import jax
import jax.numpy as jnp
from jax import lax
from jax.experimental import pallas as pl
from jax.experimental.pallas import tpu as pltpu
from jax.sharding import PartitionSpec as P

SUBSTEPS = 2
INTERVALS = 2
EXCHANGE = 0.5
OCEAN_SHARE = 0.3

F32 = jnp.float32
BF16 = jnp.bfloat16
VMEM = pl.BlockSpec(memory_space=pltpu.VMEM)
PARAMS = pltpu.CompilerParams(vmem_limit_bytes=40 * 1024 * 1024)


MEMBERS = 3
SUBLANES = 8


def partner_pairs(groups, tiles, member):
    air_count = MEMBERS * groups // 4
    pairs = []
    for group in range(groups):
        ocean = group >= air_count
        if ocean:
            partner = MEMBERS * (group - air_count) + member
        else:
            partner = air_count + group // MEMBERS if group % MEMBERS == member else group
        for tile in range(tiles):
            other = tile ^ 1 if partner == group else tile
            pairs.append((group * tiles + tile, partner * tiles + other))
    return pairs


def inner_pairs(count):
    return [(tile, tile ^ 1) for tile in range(count)]


def outer_pairs(count):
    return [(tile, (tile + 1) % count if tile % 2 else (tile - 1) % count) for tile in range(count)]


def split_high_low(value):
    high = value.astype(BF16)
    low = (value - high.astype(F32)).astype(BF16)
    return high, low


def payload(handed, wide_ref, pick_ref, chosen_ref, out_refs, blk_ref):
    rows, width = handed.shape
    count, block = blk_ref.shape
    per_row = width // block
    margins = pick_ref.shape[1]
    band = wide_ref.shape[0] // margins
    for c in range(per_row):
        blk_ref[pl.ds(c, rows, stride=per_row), :] = handed[:, c * block : (c + 1) * block]
    picked = lax.dot_general(
        pick_ref[...], blk_ref[...].astype(BF16), (((0,), (0,)), ((), ())), preferred_element_type=F32
    )
    contrib = wide_ref[pl.ds(0, margins, stride=band), :] * picked
    for j in range(1, band):
        turned = pltpu.roll(picked, block - j, 1)
        contrib = contrib + wide_ref[pl.ds(j, margins, stride=band), :] * turned
    high, low = split_high_low(contrib)
    both = jnp.concatenate([high, low], axis=0)
    blocks = jnp.dot(chosen_ref[...], both, preferred_element_type=F32)
    for n, out_ref in enumerate(out_refs):
        out_ref[...] = blocks[n * count : (n + 1) * count]


def column(row):
    n = row.shape[1]
    diagonal = lax.broadcasted_iota(jnp.int32, (n, n), 0) == lax.broadcasted_iota(jnp.int32, (n, n), 1)
    return jnp.sum(jnp.where(diagonal, row, 0.0), axis=1, keepdims=True)


def is_odd():
    return lax.rem(lax.axis_index("tile"), 2) == 1


def is_sea(groups):
    return lax.axis_index("comp") >= MEMBERS * groups // 4


def halves_of(rows):
    half = len(rows) // 2
    head, tail = rows[:half], rows[half:]
    inner = [jnp.where(is_odd(), h, t) for h, t in zip(head, tail)]
    outer = [jnp.where(is_odd(), t, h) for h, t in zip(head, tail)]
    return inner, outer


def rows_of(inner, outer):
    head = [jnp.where(is_odd(), i, o) for i, o in zip(inner, outer)]
    tail = [jnp.where(is_odd(), o, i) for i, o in zip(inner, outer)]
    return head + tail


def lines_of(lines):
    return [lines[r : r + 1] for r in range(lines.shape[0])]


def load_kernel(groups, *refs):
    state, *args = refs[:10]
    x1, x2, surface, wet = refs[10:14]
    outs, (state_v, sems) = refs[14:23], refs[23:]
    copies = [
        pltpu.make_async_copy(src, dst, sems.at[n])
        for n, (src, dst) in enumerate(zip((state, *args), (state_v, *outs)))
    ]
    for copy in copies:
        copy.start()
    copies[0].wait()
    for ref, half in zip((x1, x2), halves_of([state_v[0, :, r, :] for r in range(state_v.shape[2])])):
        for i, value in enumerate(half):
            ref[i] = value
    surface[...] = state_v[0, 0]
    for copy in copies[1:]:
        copy.wait()
    mask, codes = outs[1], outs[2]
    wet[...] = jnp.where(is_sea(groups), mask[0].astype(F32), 1.0)
    for ref, half in zip((x1, x2), halves_of(lines_of(codes[0].astype(F32)))):
        for i, value in enumerate(half):
            ref[i, 0:1, :] = value


def remap_kernel(groups, coupling, mixing, courant, matrices, weights, sources, targets, *refs):
    coef, table, col0, wide, pick, chosen, *outs, blk = refs
    count, margins = pick.shape
    slot = lax.broadcasted_iota(jnp.int32, (count, margins), 0)
    pick[...] = (slot == sources[...]).astype(F32).astype(BF16)
    me = lax.axis_index("comp")
    air_count = MEMBERS * groups // 4
    for n in range(MEMBERS):
        ocean = jnp.where(lax.rem(me, MEMBERS) == n, air_count + lax.div(me, MEMBERS), me)
        partner = jnp.where(me < air_count, ocean, MEMBERS * (me - air_count) + n)
        hit = (targets[...] == slot + partner * count).astype(F32).astype(BF16)
        chosen[n * count : (n + 1) * count] = jnp.concatenate([hit, hit], axis=1)
    wide[...] = weights[0].reshape(wide.shape).astype(F32)
    payload(coupling[0], wide, pick, chosen, outs, blk)
    m, c = column(mixing[...]), column(courant[...])
    coef[0], coef[1], coef[2] = 1.0 - 4.0 * m - c, m + c, m
    branches, fields = matrices.shape[1:3]
    flat = matrices[0].reshape(branches * fields, fields)
    col0[...] = flat[:, :1].reshape(branches, fields, 1)
    flat = jnp.where(lax.broadcasted_iota(jnp.int32, flat.shape, 1) == 0, 0.0, flat)
    high, low = split_high_low(flat)
    table[...] = jnp.concatenate([high, high, low], axis=1)


def surface_kernel(groups, late, *refs):
    recs, (surface_ref, mask_ref, *refs) = refs[:MEMBERS], refs[MEMBERS:]
    ns_ref, flux_ref, *ends, blk = refs if late else refs[1:]
    rows, width = ns_ref.shape
    block = blk.shape[-1]
    per_row = width // block
    total = recs[0][...]
    for rec in recs[1:]:
        total = total + rec[...]
    blk[...] = total
    received = jnp.concatenate(
        [blk[pl.ds(c, rows, stride=per_row), :] for c in range(per_row)], axis=1
    )
    surface = surface_ref[...]
    flux = mask_ref[0].astype(F32) * EXCHANGE * (received - surface)
    new = surface + jnp.where(is_sea(groups), -OCEAN_SHARE * received, flux)
    ns_ref[...] = new
    flux_ref[...] = flux
    for ref, half in zip(ends, halves_of([new[: rows // 2], new[rows // 2 :]])):
        ref[...] = half[0]


def substep(f, up, down, c0, cu, m):
    width = f.shape[1]
    sides = pltpu.roll(f, 1, 1) + pltpu.roll(f, width - 1, 1)
    return c0 * f + cu * up + m * (down + sides)


def sides(f):
    return pltpu.roll(f, 1, 1) + pltpu.roll(f, f.shape[1] - 1, 1)


def own_rows(f0, f1, f2, f3, coef, base1, base2):
    c0, cu, m = coef[0], coef[1], coef[2]
    g0 = c0 * f0 + m * (f1 + sides(f0))
    g1 = substep(f1, f0, f2, c0, cu, m)
    g2 = substep(f2, f1, f3, c0, cu, m)
    g3 = c0 * f3 + cu * f2 + m * sides(f3)
    rows = [
        c0 * g0 + m * (g1 + sides(g0)) + (cu * m) * f0,
        substep(g1, g0, g2, c0, cu, m),
        substep(g2, g1, g3, c0, cu, m),
        c0 * g3 + cu * g2 + m * sides(g3) + (cu * m) * f3,
    ]
    for ref, half in zip((base1, base2), halves_of(rows)):
        for i, value in enumerate(half):
            ref[i] = value


def start_kernel(x1, x2, coef, base1, base2):
    own_rows(*rows_of([x1[0], x1[1]], [x2[0], x2[1]]), coef, base1, base2)


def evolve_kernel(part1, part2, gain1, gain2, squashed, coef, base1, base2):
    half = part1.shape[0]
    lines = [squashed[r : r + 1, :] for r in range(half, 3 * half)]
    line1, line2 = halves_of(lines)
    inner = [part1[i] + gain1[i] * line1[i] for i in range(half)]
    outer = [part2[i] + gain2[i] * line2[i] for i in range(half)]
    own_rows(*rows_of(inner, outer), coef, base1, base2)


def branch_factor(col0, code, shape):
    factor = jnp.broadcast_to(col0[0], shape)
    for b in range(1, col0.shape[0]):
        factor = jnp.where(code == b, col0[b], factor)
    return factor


def fields_kernel(inner, late, base, y, coef, table, col0, codes, wet, after, *refs):
    part, part0, gain = refs[-3:]
    z, squashed = refs[:2] if late else (None, None)
    half, fields, width = base.shape
    at_top = is_odd() if inner else jnp.logical_not(is_odd())
    c0, cu, m = coef[0], coef[1], coef[2]
    q = jnp.where(at_top, cu, m)
    branches = table.shape[0] // fields

    def halo_row(top, bottom):
        value = jnp.where(at_top, y[top], y[bottom])
        if not late:
            return value
        code = jnp.where(at_top, z[top, 0:1], z[bottom, 0:1]).astype(jnp.int32)
        line = jnp.where(
            at_top, squashed[top : top + 1, :], squashed[3 * half + bottom : 3 * half + bottom + 1, :]
        )
        return value + branch_factor(col0, code, (fields, width)) * (value[:1] * line)

    near, far = halo_row(1, 0), halo_row(0, 1)
    edge = (2.0 * q * c0) * near + (2.0 * q * m) * sides(near) + (q * q) * far
    next_to_edge = (q * q) * near
    halos = jnp.where(at_top, edge, next_to_edge), jnp.where(at_top, next_to_edge, edge)
    code_lines = halves_of([codes[0, r : r + 1, :] for r in range(2 * half)])[0 if inner else 1]
    wet_lines = halves_of([wet[r : r + 1, :] for r in range(2 * half)])[0 if inner else 1]
    top_field = lax.broadcasted_iota(jnp.int32, (fields, width), 0) == 0
    for i in range(half):
        f = base[i] + halos[i]
        high, low = split_high_low(jnp.tanh(f))
        terms = jnp.dot(
            table[...], jnp.concatenate([high, low, high], axis=0), preferred_element_type=F32
        )
        tendency = terms[:fields]
        for b in range(1, branches):
            chosen = code_lines[i] == b
            tendency = jnp.where(chosen, terms[b * fields : (b + 1) * fields], tendency)
        part0[i : i + 1, :] = tendency[:1] * wet_lines[i]
        part[i] = jnp.where(top_field, 1.0, f + tendency) * wet_lines[i]
        gain[i] = branch_factor(col0, code_lines[i], (fields, width)) * wet_lines[i]


def field0(ns, e2, e1, coef, wet, part01, part02, gain1, gain2):
    c0, cu, m = coef[0, :1], coef[1, :1], coef[2, :1]
    odd = is_odd()
    first, last = e1[...], e2[...]
    f = jnp.concatenate(
        [jnp.where(odd, first, last), ns[...], jnp.where(odd, last, first)], axis=0
    )
    rows = f.shape[0]
    for _ in range(SUBSTEPS):
        f = substep(f, pltpu.roll(f, 1, 0), pltpu.roll(f, rows - 1, 0), c0, cu, m)
    f = f[SUBSTEPS : rows - SUBSTEPS]
    squashed = jnp.tanh(f)
    extra = (f.shape[0] - ns.shape[0]) // 2
    own = slice(extra, extra + ns.shape[0])
    part = jnp.concatenate(rows_of([part01[...]], [part02[...]]), axis=0)
    gain = jnp.concatenate(rows_of([gain1[:, 0, :]], [gain2[:, 0, :]]), axis=0)
    return part + gain * squashed[own] + f[own] * wet[...], squashed


def hand_kernel(
    groups, ns, e2, e1, coef, wet, part01, part02, gain1, gain2, flux, wide, pick, chosen, *refs
):
    surf, squashed, *outs, blk = refs
    surf[...], squashed[...] = field0(ns, e2, e1, coef, wet, part01, part02, gain1, gain2)
    payload(jnp.where(is_sea(groups), surf[...], flux[...]), wide, pick, chosen, outs, blk)


def close_kernel(
    groups, ns, e2, e1, coef, wet, part01, part02, gain1, gain2, flux, part1, part2, *refs
):
    new_state, new_coupling, surf, squashed = refs
    surf[...], squashed[...] = field0(ns, e2, e1, coef, wet, part01, part02, gain1, gain2)
    new_coupling[0] = jnp.where(is_sea(groups), surf[...], flux[...])
    half, fields, width = part1.shape
    top_field = lax.broadcasted_iota(jnp.int32, (SUBLANES, width), 0) == 0
    line1, line2 = halves_of([squashed[r : r + 1, :] for r in range(2 * half)])
    for h in range(0, fields, SUBLANES):
        some = slice(h, h + SUBLANES)
        for i in range(half):
            inner = part1[i, some] + gain1[i, some] * line1[i]
            outer = part2[i, some] + gain2[i, some] * line2[i]
            for r, done in zip((i, half + i), rows_of([inner], [outer])):
                if h == 0:
                    done = jnp.where(top_field, surf[r : r + 1, :], done)
                new_state[0, some, r, :] = done


def call(kernel, name, outs, args, scratch=(), in_specs=None, flops=0):
    moved = sum(a.size * a.dtype.itemsize for a in list(args) + list(outs))
    return pl.pallas_call(
        kernel,
        name=name,
        out_shape=outs,
        in_specs=in_specs or [VMEM] * len(args),
        out_specs=[VMEM] * len(outs),
        scratch_shapes=list(scratch),
        compiler_params=PARAMS,
        cost_estimate=pl.CostEstimate(flops=flops, bytes_accessed=moved, transcendentals=0),
    )(*args)


def on_device(
    state, coupling, land_mask, codes, mixing, courant, matrices, weights, sources, targets
):
    groups = lax.axis_size("comp")
    tiles = lax.axis_size("tile")
    _, fields, rows, width = state.shape
    _, margins, band, block = weights.shape
    count = rows * width // block
    half = rows // 2
    branches = matrices.shape[1]
    shape = jax.ShapeDtypeStruct

    halves = [shape((half, fields, width), F32)] * 2
    payloads = [shape((count, block), F32)] * MEMBERS
    blocks = pltpu.VMEM((count, block), F32)
    args = (
        state, coupling, land_mask, codes, mixing, courant, matrices, weights, sources, targets
    )
    x1, x2, surface, wet, handed, mask, codes, *raw = call(
        functools.partial(load_kernel, groups),
        "load",
        halves + [shape((rows, width), F32)] * 2 + [shape(a.shape, a.dtype) for a in args[1:]],
        [pltpu.with_memory_space_constraint(a, pltpu.HBM) for a in args],
        [pltpu.VMEM(state.shape, F32), pltpu.SemaphoreType.DMA((len(args),))],
        [pl.BlockSpec(memory_space=pltpu.HBM)] * len(args),
    )
    tables = [
        shape((3, fields, 1), F32),
        shape((branches * fields, 3 * fields), BF16),
        shape((branches, fields, 1), F32),
        shape((margins * band, block), F32),
        shape((count, margins), BF16),
        shape((MEMBERS * count, 2 * margins), BF16),
    ]
    coef, table, col0, wide, pick, chosen, *sent = call(
        functools.partial(remap_kernel, groups),
        "remap",
        tables + payloads,
        (handed, *raw),
        [blocks],
    )
    for interval in range(INTERVALS):
        y1 = lax.ppermute(x1, "tile", inner_pairs(tiles))
        y2 = lax.ppermute(x2, "tile", outer_pairs(tiles))
        recs = [
            lax.ppermute(value, ("comp", "tile"), partner_pairs(groups, tiles, member))
            for member, value in enumerate(sent)
        ]
        late, last = interval > 0, interval == INTERVALS - 1
        line, pair = shape((rows, width), F32), shape((half, width), F32)
        if late:
            base1, base2 = call(
                evolve_kernel, "evolve", halves, (part1, part2, gain1, gain2, squashed, coef)
            )
        else:
            base1, base2 = call(start_kernel, "start", halves, (x1, x2, coef))
        kept = (coef, table, col0, codes, wet)
        part1, part01, gain1 = call(
            functools.partial(fields_kernel, True, late),
            "inner",
            [halves[0], pair, halves[0]],
            (base1, y1, *kept, base1) + ((z1, squashed) if late else ()),
        )
        ns, flux, *edges = call(
            functools.partial(surface_kernel, groups, late),
            "surface",
            [line] * 2 + ([pair] * 2 if last else []),
            (*recs, surface, mask) + (() if late else (part01,)),
            [blocks],
        )
        d1, d2 = edges if last else (ns, ns)
        e1 = lax.ppermute(d1, "tile", inner_pairs(tiles))
        e2 = lax.ppermute(d2, "tile", outer_pairs(tiles))
        part2, part02, gain2 = call(
            functools.partial(fields_kernel, False, late),
            "outer",
            [halves[0], pair, halves[0]],
            (base2, y2, *kept, part01 if late else ns) + ((z2, squashed) if late else ()),
            flops=4_000_000_000,
        )
        z1, z2 = y1, y2
        x1, x2 = part1, part2
        common = (ns, e2, e1, coef, wet, part01, part02, gain1, gain2, flux)
        if not last:
            surface, squashed, *sent = call(
                functools.partial(hand_kernel, groups),
                "hand",
                [line, shape((2 * rows, width), F32)] + payloads,
                (*common, wide, pick, chosen),
                [blocks],
                flops=20_000_000_000,
            )
        else:
            new_state, new_coupling = call(
                functools.partial(close_kernel, groups),
                "close",
                [shape(state.shape, F32), shape(coupling.shape, F32)],
                (*common, part1, part2),
                [pltpu.VMEM((rows, width), F32)] * 2,
            )
    return new_state, new_coupling


def solution(mesh):
    placed = (
        P("comp", None, "tile", None),
        P("comp", "tile", None),
        P("comp", "tile", None),
        P("comp", "tile", None),
        P("comp", None),
        P("comp", None),
        P("comp", None, None, None),
        P("comp", "tile", None, None),
        P("comp", "tile"),
        P("comp", "tile"),
    )
    return jax.shard_map(
        on_device,
        mesh=mesh,
        in_specs=placed,
        out_specs=(P("comp", None, "tile", None), P("comp", "tile", None)),
        check_vma=False,
    )
```

time: 33.6 us -> 31.5 us (0.938)
  waiting for transfers between devices: 7.78 us -> 6.12 us
  starting transfers between devices: 16.1 us -> 15.2 us
  Pallas kernels: 8.81 us -> 9.36 us
    ppermute x2, starting transfers between devices: 2.65 us -> 0.14 us  [on_device(): e2 = lax.ppermute(d2, 'tile', outer_pairs(tiles))]
    ppermute x2, starting transfers between devices: 4.19 us -> 6.03 us  [on_device(): y2 = lax.ppermute(x2, 'tile', outer_pairs(tiles))]
    ppermute x6, waiting for transfers between devices: 3.83 us -> 2.43 us  [on_device(): lax.ppermute(value, ('comp', 'tile'), partner_pairs(groups, tiles, member))]
    ppermute x2, waiting for transfers between devices: 2.62 us -> 1.46 us  [on_device(): e2 = lax.ppermute(d2, 'tile', outer_pairs(tiles))]
    ppermute x2, waiting for transfers between devices: 1.32 us -> 2.21 us  [on_device(): y2 = lax.ppermute(x2, 'tile', outer_pairs(tiles))]
    ppermute x6, starting transfers between devices: 8.56 us -> 7.83 us  [on_device(): lax.ppermute(value, ('comp', 'tile'), partner_pairs(groups, tiles, member))]
    pallas_call x11 -> x12, Pallas kernels: 8.81 us -> 9.36 us  [call(): pl.pallas_call(kernel, name=name, out_shape=outs, in_specs=in_specs or [V...]
    ppermute x2, starting transfers between devices: 0.59 us -> 1.01 us  [on_device(): y1 = lax.ppermute(x1, 'tile', inner_pairs(tiles))]
  transfers between devices with their start and end apart: 14 -> 14, of which waited for: 6 -> 5; matrix products, arithmetic and copies ran while one was open for 0% -> 0% of each run, Pallas kernels for 16% -> 20%
where the time goes in v5:
time: 31.5 us; the launch traced here: 31.4 us
  starting transfers between devices  15.2 us (48%)
  Pallas kernels  9.36 us (30%)
  waiting for transfers between devices  6.12 us (19%)
  between operations  0.77 us (2%)
    pallas_call x12, Pallas kernels, call(): pl.pallas_call(kernel, name=name, out_shape=outs, in_specs=in_specs or [V...  9.36 us
    ppermute x6, starting transfers between devices, on_device(): lax.ppermute(value, ('comp', 'tile'), partner_pairs(groups, tiles, member))  7.83 us
    ppermute x2, starting transfers between devices, on_device(): y2 = lax.ppermute(x2, 'tile', outer_pairs(tiles))  6.03 us
    ppermute x6, waiting for transfers between devices, on_device(): lax.ppermute(value, ('comp', 'tile'), partner_pairs(groups, tiles, member))  2.43 us
    ppermute x2, waiting for transfers between devices, on_device(): y2 = lax.ppermute(x2, 'tile', outer_pairs(tiles))  2.21 us
    ppermute x2, waiting for transfers between devices, on_device(): e2 = lax.ppermute(d2, 'tile', outer_pairs(tiles))  1.46 us
    ppermute x2, starting transfers between devices, on_device(): y1 = lax.ppermute(x1, 'tile', inner_pairs(tiles))  1.01 us
  transfers between devices with their start and end apart: 14, of which 5 were waited for; matrix products, arithmetic and copies ran while one was open for 0% of the time, Pallas kernels for 20%

profile of v5, /device:TPU:0, one launch (start us, length us, event | category | flops | bytes accessed | tf_op | source)
XLA Modules:
  0.0 31.4 jit_solution(13316760746821633213)
XLA Ops:
  0.6 1.5 %load.1 = (f32[2,16,3072]{2,1,0:T(8,128)S(1)}, f32[2,16,3072]{2,1,0:T(8,128)S(1)}, f32[4,3072]{1,0:T(4,128)S(1)}, f32[4,3072]{1,0:T(4,128)S(1)}, f32[1,4,3072]{2...) custom-call(f32[1,16,4,3072]{3,2,1,0:T(4,128)} %refs_0_.1, ...), custom_call_target="tpu_custom_call" | custom-call | bytes 3158784 | tf_op jit(solution)/shard_map/load/pallas_call | solution.py:315
  2.2 0.5 %collective-permute-start.3 = (f32[2,16,3072]{2,1,0:T(8,128)S(1)}, f32[2,16,3072]{2,1,0:T(8,128)S(1)}, u32[]{:S(2)}, u32[]{:S(2)}) collective-permute-start(f32[2,16,3072]{2,1,0:T(8,128)S(1)} %get-tuple-element.63.x1), channel_id=1, source_target_pairs={{0,1},{1,0},{2,3},{3,2},{4,5},{5,4},{6,7},{7,6},{8,9},{9,8},{10,11... | collective-permute-start | bytes 1179656 | tf_op jit(solution)/shard_map/ppermute | solution.py:369
  2.7 3.6 %collective-permute-start.6 = (f32[2,16,3072]{2,1,0:T(8,128)S(1)}, f32[2,16,3072]{2,1,0:T(8,128)S(1)}, u32[]{:S(2)}, u32[]{:S(2)}) collective-permute-start(f32[2,16,3072]{2,1,0:T(8,128)S(1)} %get-tuple-element.64.x2), channel_id=1, source_target_pairs={{0,7},{1,2},{2,1},{3,4},{4,3},{5,6},{6,5},{7,0},{8,15},{9,10},{10,... | collective-permute-start | bytes 1179656 | tf_op jit(solution)/shard_map/ppermute | solution.py:370
  6.2 0.8 %remap.1 = (f32[3,16,1]{2,1,0:T(8,128)S(1)}, bf16[64,48]{1,0:T(8,128)(2,1)S(1)}, f32[4,16,1]{2,1,0:T(8,128)S(1)}, f32[2304,128]{1,0:T(8,128)S(1)}, bf16[96,288]{...) custom-call(f32[1,4,3072]{2,1,0:T(4,128)S(1)} %get-tuple-element.51., ...), custom_call_target="tpu_custom_call" | custom-call | bytes 2366272 | tf_op jit(solution)/shard_map/remap/pallas_call | solution.py:315
  7.0 3.7 %collective-permute-start = (f32[96,128]{1,0:T(8,128)S(1)}, f32[96,128]{1,0:T(8,128)S(1)}, u32[]{:S(2)}, u32[]{:S(2)}) collective-permute-start(f32[96,128]{1,0:T(8,128)S(1)} %get-tuple-element.58), channel_id=1, source_target_pairs={{0,24},{1,25},{2,26},{3,27},{4,28},{5,29},{6,30},{7,31},{8,9},{9,8... | collective-permute-start | bytes 147464 | tf_op jit(solution)/shard_map/ppermute | solution.py:372
  10.7 0.0 collective-permute-start.1
  10.7 0.5 %collective-permute-start.2 = (f32[96,128]{1,0:T(8,128)S(1)}, f32[96,128]{1,0:T(8,128)S(1)}, u32[]{:S(2)}, u32[]{:S(2)}) collective-permute-start(f32[96,128]{1,0:T(8,128)S(1)} %get-tuple-element.60), channel_id=1, source_target_pairs={{0,1},{1,0},{2,3},{3,2},{4,5},{5,4},{6,7},{7,6},{8,9},{9,8},{10,11... | collective-permute-start | bytes 147464 | tf_op jit(solution)/shard_map/ppermute | solution.py:372
  11.2 1.1 %start.1 = (f32[2,16,3072]{2,1,0:T(8,128)S(1)}, f32[2,16,3072]{2,1,0:T(8,128)S(1)}) custom-call(f32[2,16,3072]{2,1,0:T(8,128)S(1)} %get-tuple-element.63.x1, f32[2,16,3072]{2,1,0:T(8,128)S(1)} %get-tuple-element.64.x2, f32[3,16,1]{2,1,0:T(8,128)S(1)} %get-tuple-element.65.coef), custom_call_target="tpu_custom_call" | custom-call | bytes 1573056 | tf_op jit(solution)/shard_map/start/pallas_call | solution.py:315
  12.2 0.0 collective-permute-done.3.y.refs_0_
  12.3 0.5 %inner.2 = (f32[2,16,3072]{2,1,0:T(8,128)S(1)}, f32[2,3072]{1,0:T(2,128)S(1)}, f32[2,16,3072]{2,1,0:T(8,128)S(1)}) custom-call(f32[2,16,3072]{2,1,0:T(8,128)S(1)} %get-tuple-element.66.base.after, f32[2,16,3072]{2,1,0:T(8,128)S(1)} %collective-permute-done.3.y.refs_0_, f32[3,16,1]{2,1,0:T(8,128)S(1)} %get-tuple-element.65.coef, ...), custom_call_target="tpu_custom_call" | custom-call | bytes 2095552 | tf_op jit(solution)/shard_map/inner/pallas_call | solution.py:315
  12.8 0.7 %collective-permute-done.refs_0_ = f32[96,128]{1,0:T(8,128)S(1)} collective-permute-done((f32[96,128]{1,0:T(8,128)S(1)}, f32[96,128]{1,0:T(8,128)S(1)}, u32[]{:S(2)}, u32[]{:S(2)}) %collective-permute-start) | collective-permute-done | bytes 49184 | tf_op jit(solution)/shard_map/ppermute | solution.py:372
  13.5 0.0 collective-permute-done.1.refs_1_
  13.5 0.0 collective-permute-done.2.refs_2_
  13.5 0.1 collective-permute-start.4
  13.6 0.1 collective-permute-start.5
  13.7 0.5 %collective-permute-start.12 = (f32[2,16,3072]{2,1,0:T(8,128)S(1)}, f32[2,16,3072]{2,1,0:T(8,128)S(1)}, u32[]{:S(2)}, u32[]{:S(2)}) collective-permute-start(f32[2,16,3072]{2,1,0:T(8,128)S(1)} %get-tuple-element.88.part1), channel_id=1, source_target_pairs={{0,1},{1,0},{2,3},{3,2},{4,5},{5,4},{6,7},{7,6},{8,9},{9,8},{10,11... | collective-permute-start | bytes 1179656 | tf_op jit(solution)/shard_map/ppermute | solution.py:369
  14.2 0.9 %collective-permute-done.6.y.refs_0_ = f32[2,16,3072]{2,1,0:T(8,128)S(1)} collective-permute-done((f32[2,16,3072]{2,1,0:T(8,128)S(1)}, f32[2,16,3072]{2,1,0:T(8,128)S(1)}, u32[]{:S(2)}, u32[]{:S(2)}) %collective-permute-start.6) | collective-permute-done | bytes 393248 | tf_op jit(solution)/shard_map/ppermute | solution.py:370
  15.1 0.5 %outer.2 = (f32[2,16,3072]{2,1,0:T(8,128)S(1)}, f32[2,3072]{1,0:T(2,128)S(1)}, f32[2,16,3072]{2,1,0:T(8,128)S(1)}) custom-call(f32[2,16,3072]{2,1,0:T(8,128)S(1)} %get-tuple-element.73.base, f32[2,16,3072]{2,1,0:T(8,128)S(1)} %collective-permute-done.6.y.refs_0_, f32[3,16,1]{2,1,0:T(8,128)S(1)} %get-tuple-element.65.coef, ...), custom_call_target="tpu_custom_call" | custom-call | flops 4000000000 | bytes 1751488 | tf_op jit(solution)/shard_map/outer/pallas_call | solution.py:315
  15.6 2.5 %collective-permute-start.13 = (f32[2,16,3072]{2,1,0:T(8,128)S(1)}, f32[2,16,3072]{2,1,0:T(8,128)S(1)}, u32[]{:S(2)}, u32[]{:S(2)}) collective-permute-start(f32[2,16,3072]{2,1,0:T(8,128)S(1)} %get-tuple-element.89.part2), channel_id=1, source_target_pairs={{0,7},{1,2},{2,1},{3,4},{4,3},{5,6},{6,5},{7,0},{8,15},{9,10},{10,... | collective-permute-start | bytes 1179656 | tf_op jit(solution)/shard_map/ppermute | solution.py:370
  18.1 1.1 %hand.1 = (f32[4,3072]{1,0:T(4,128)S(1)}, f32[8,3072]{1,0:T(8,128)S(1)}, f32[96,128]{1,0:T(8,128)S(1)}, f32[96,128]{1,0:T(8,128)S(1)}, f32[96,128]{1,0:T(8,128)S(1)}) custom-call(f32[4,3072]{1,0:T(4,128)S(1)} %get-tuple-element.72.after.ns, f32[4,3072]{1,0:T(4,128)S(1)} %collective-permute-done.4.e2, f32[4,3072]{1,0:T(4,128)S(1)} %collective-permute-done.5.e1, ...), custom_call_target="tpu_custom_call" | custom-call | flops 20000000000 | bytes 2943168 | tf_op jit(solution)/shard_map/hand/pallas_call | solution.py:315
  19.2 3.1 %collective-permute-start.7 = (f32[96,128]{1,0:T(8,128)S(1)}, f32[96,128]{1,0:T(8,128)S(1)}, u32[]{:S(2)}, u32[]{:S(2)}) collective-permute-start(f32[96,128]{1,0:T(8,128)S(1)} %get-tuple-element.81), channel_id=1, source_target_pairs={{0,24},{1,25},{2,26},{3,27},{4,28},{5,29},{6,30},{7,31},{8,9},{9,8... | collective-permute-start | bytes 147464 | tf_op jit(solution)/shard_map/ppermute | solution.py:372
  22.4 0.5 %collective-permute-start.9 = (f32[96,128]{1,0:T(8,128)S(1)}, f32[96,128]{1,0:T(8,128)S(1)}, u32[]{:S(2)}, u32[]{:S(2)}) collective-permute-start(f32[96,128]{1,0:T(8,128)S(1)} %get-tuple-element.83), channel_id=1, source_target_pairs={{0,1},{1,0},{2,3},{3,2},{4,5},{5,4},{6,7},{7,6},{8,9},{9,8},{10,11... | collective-permute-start | bytes 147464 | tf_op jit(solution)/shard_map/ppermute | solution.py:372
  22.9 1.0 %evolve.1 = (f32[2,16,3072]{2,1,0:T(8,128)S(1)}, f32[2,16,3072]{2,1,0:T(8,128)S(1)}) custom-call(f32[2,16,3072]{2,1,0:T(8,128)S(1)} %get-tuple-element.88.part1, f32[2,16,3072]{2,1,0:T(8,128)S(1)} %get-tuple-element.89.part2, f32[2,16,3072]{2,1,0:T(8,128)S(1)} %get-tuple-element.75.gain1, f32[2,16,3072]{2,1,0:T(8,128)S(1)} %get-tuple-element.76.gain2, ...), custom_call_target="tpu_custom_call" | custom-call | bytes 2457792 | tf_op jit(solution)/shard_map/evolve/pallas_call | solution.py:315
  23.9 1.7 %collective-permute-done.7.refs_0_ = f32[96,128]{1,0:T(8,128)S(1)} collective-permute-done((f32[96,128]{1,0:T(8,128)S(1)}, f32[96,128]{1,0:T(8,128)S(1)}, u32[]{:S(2)}, u32[]{:S(2)}) %collective-permute-start.7) | collective-permute-done | bytes 49184 | tf_op jit(solution)/shard_map/ppermute | solution.py:372
  25.7 0.1 surface.3
  25.7 0.1 collective-permute-start.10
  25.8 0.1 collective-permute-start.11
  25.9 0.6 %inner.3 = (f32[2,16,3072]{2,1,0:T(8,128)S(1)}, f32[2,3072]{1,0:T(2,128)S(1)}, f32[2,16,3072]{2,1,0:T(8,128)S(1)}) custom-call(f32[2,16,3072]{2,1,0:T(8,128)S(1)} %get-tuple-element.91.base.after, f32[2,16,3072]{2,1,0:T(8,128)S(1)} %collective-permute-done.12.y, f32[3,16,1]{2,1,0:T(8,128)S(1)} %get-tuple-element.65.coef, ...), custom_call_target="tpu_custom_call" | custom-call | bytes 2587072 | tf_op jit(solution)/shard_map/inner/pallas_call | solution.py:315
  26.5 1.3 %collective-permute-done.13.y = f32[2,16,3072]{2,1,0:T(8,128)S(1)} collective-permute-done((f32[2,16,3072]{2,1,0:T(8,128)S(1)}, f32[2,16,3072]{2,1,0:T(8,128)S(1)}, u32[]{:S(2)}, u32[]{:S(2)}) %collective-permute-start.13) | collective-permute-done | bytes 393248 | tf_op jit(solution)/shard_map/ppermute | solution.py:370
  27.8 0.6 %outer.3 = (f32[2,16,3072]{2,1,0:T(8,128)S(1)}, f32[2,3072]{1,0:T(2,128)S(1)}, f32[2,16,3072]{2,1,0:T(8,128)S(1)}) custom-call(f32[2,16,3072]{2,1,0:T(8,128)S(1)} %get-tuple-element.93.base, f32[2,16,3072]{2,1,0:T(8,128)S(1)} %collective-permute-done.13.y, f32[3,16,1]{2,1,0:T(8,128)S(1)} %get-tuple-element.65.coef, ...), custom_call_target="tpu_custom_call" | custom-call | flops 4000000000 | bytes 2218432 | tf_op jit(solution)/shard_map/outer/pallas_call | solution.py:315
  28.5 1.5 %collective-permute-done.10.e2 = f32[2,3072]{1,0:T(2,128)S(1)} collective-permute-done((f32[2,3072]{1,0:T(2,128)S(1)}, f32[2,3072]{1,0:T(2,128)S(1)}, u32[]{:S(2)}, u32[]{:S(2)}) %collective-permute-start.10) | collective-permute-done | bytes 24608 | tf_op jit(solution)/shard_map/ppermute | solution.py:399
  29.9 1.5 %close.1 = (f32[1,16,4,3072]{3,2,1,0:T(4,128)}, f32[1,4,3072]{2,1,0:T(4,128)}) custom-call(f32[4,3072]{1,0:T(4,128)S(1)} %get-tuple-element.85.ns, f32[2,3072]{1,0:T(2,128)S(1)} %collective-permute-done.10.e2, f32[2,3072]{1,0:T(2,128)S(1)} %collective-permute-done.11.e1, f32[3,16,1]{2,1,0:T(8,128)S(1)} %get-tuple-element.65.coef, ...), custom_call_target="tpu_custom_call" | custom-call | bytes 2654400 | tf_op jit(solution)/shard_map/close/pallas_call | solution.py:315
  (8 shorter events, 0.1 us)
Async XLA Ops:
  2.2 10.1 %collective-permute-start.3 = (f32[2,16,3072]{2,1,0:T(8,128)S(1)}, f32[2,16,3072]{2,1,0:T(8,128)S(1)}, u32[]{:S(2)}, u32[]{:S(2)}) collective-permute-start(f32[2,16,3072]{2,1,0:T(8,128)S(1)} %get-tuple-element.63.x1), channel_id=1, source_target_pairs={{0,1},{1,0},{2,3},{3,2},{4,5},{5,4},{6,7},{7,6},{8,9},{9,8},{10,11... | collective-permute-start | bytes 1179656 | tf_op jit(solution)/shard_map/ppermute | solution.py:369
  2.7 12.4 %collective-permute-start.6 = (f32[2,16,3072]{2,1,0:T(8,128)S(1)}, f32[2,16,3072]{2,1,0:T(8,128)S(1)}, u32[]{:S(2)}, u32[]{:S(2)}) collective-permute-start(f32[2,16,3072]{2,1,0:T(8,128)S(1)} %get-tuple-element.64.x2), channel_id=1, source_target_pairs={{0,7},{1,2},{2,1},{3,4},{4,3},{5,6},{6,5},{7,0},{8,15},{9,10},{10,... | collective-permute-start | bytes 1179656 | tf_op jit(solution)/shard_map/ppermute | solution.py:370
  7.0 6.5 %collective-permute-start = (f32[96,128]{1,0:T(8,128)S(1)}, f32[96,128]{1,0:T(8,128)S(1)}, u32[]{:S(2)}, u32[]{:S(2)}) collective-permute-start(f32[96,128]{1,0:T(8,128)S(1)} %get-tuple-element.58), channel_id=1, source_target_pairs={{0,24},{1,25},{2,26},{3,27},{4,28},{5,29},{6,30},{7,31},{8,9},{9,8... | collective-permute-start | bytes 147464 | tf_op jit(solution)/shard_map/ppermute | solution.py:372
  10.7 2.8 %collective-permute-start.1 = (f32[96,128]{1,0:T(8,128)S(1)}, f32[96,128]{1,0:T(8,128)S(1)}, u32[]{:S(2)}, u32[]{:S(2)}) collective-permute-start(f32[96,128]{1,0:T(8,128)S(1)} %get-tuple-element.59), channel_id=1, source_target_pairs={{0,1},{1,0},{2,3},{3,2},{4,5},{5,4},{6,7},{7,6},{8,24},{9,25},{10,... | collective-permute-start | bytes 147464 | tf_op jit(solution)/shard_map/ppermute | solution.py:372
  10.7 2.8 %collective-permute-start.2 = (f32[96,128]{1,0:T(8,128)S(1)}, f32[96,128]{1,0:T(8,128)S(1)}, u32[]{:S(2)}, u32[]{:S(2)}) collective-permute-start(f32[96,128]{1,0:T(8,128)S(1)} %get-tuple-element.60), channel_id=1, source_target_pairs={{0,1},{1,0},{2,3},{3,2},{4,5},{5,4},{6,7},{7,6},{8,9},{9,8},{10,11... | collective-permute-start | bytes 147464 | tf_op jit(solution)/shard_map/ppermute | solution.py:372
  13.5 4.6 %collective-permute-start.4 = (f32[4,3072]{1,0:T(4,128)S(1)}, f32[4,3072]{1,0:T(4,128)S(1)}, u32[]{:S(2)}, u32[]{:S(2)}) collective-permute-start(f32[4,3072]{1,0:T(4,128)S(1)} %get-tuple-element.72.after.ns), channel_id=1, source_target_pairs={{0,7},{1,2},{2,1},{3,4},{4,3},{5,6},{6,5},{7,0},{8,15},{9,10},{10,... | collective-permute-start | bytes 147464 | tf_op jit(solution)/shard_map/ppermute | solution.py:399
  13.6 4.5 %collective-permute-start.5 = (f32[4,3072]{1,0:T(4,128)S(1)}, f32[4,3072]{1,0:T(4,128)S(1)}, u32[]{:S(2)}, u32[]{:S(2)}) collective-permute-start(f32[4,3072]{1,0:T(4,128)S(1)} %get-tuple-element.72.after.ns), channel_id=1, source_target_pairs={{0,1},{1,0},{2,3},{3,2},{4,5},{5,4},{6,7},{7,6},{8,9},{9,8},{10,11... | collective-permute-start | bytes 147464 | tf_op jit(solution)/shard_map/ppermute | solution.py:398
  13.7 12.2 %collective-permute-start.12 = (f32[2,16,3072]{2,1,0:T(8,128)S(1)}, f32[2,16,3072]{2,1,0:T(8,128)S(1)}, u32[]{:S(2)}, u32[]{:S(2)}) collective-permute-start(f32[2,16,3072]{2,1,0:T(8,128)S(1)} %get-tuple-element.88.part1), channel_id=1, source_target_pairs={{0,1},{1,0},{2,3},{3,2},{4,5},{5,4},{6,7},{7,6},{8,9},{9,8},{10,11... | collective-permute-start | bytes 1179656 | tf_op jit(solution)/shard_map/ppermute | solution.py:369
  15.6 12.2 %collective-permute-start.13 = (f32[2,16,3072]{2,1,0:T(8,128)S(1)}, f32[2,16,3072]{2,1,0:T(8,128)S(1)}, u32[]{:S(2)}, u32[]{:S(2)}) collective-permute-start(f32[2,16,3072]{2,1,0:T(8,128)S(1)} %get-tuple-element.89.part2), channel_id=1, source_target_pairs={{0,7},{1,2},{2,1},{3,4},{4,3},{5,6},{6,5},{7,0},{8,15},{9,10},{10,... | collective-permute-start | bytes 1179656 | tf_op jit(solution)/shard_map/ppermute | solution.py:370
  19.2 6.4 %collective-permute-start.7 = (f32[96,128]{1,0:T(8,128)S(1)}, f32[96,128]{1,0:T(8,128)S(1)}, u32[]{:S(2)}, u32[]{:S(2)}) collective-permute-start(f32[96,128]{1,0:T(8,128)S(1)} %get-tuple-element.81), channel_id=1, source_target_pairs={{0,24},{1,25},{2,26},{3,27},{4,28},{5,29},{6,30},{7,31},{8,9},{9,8... | collective-permute-start | bytes 147464 | tf_op jit(solution)/shard_map/ppermute | solution.py:372
  22.4 3.3 %collective-permute-start.8 = (f32[96,128]{1,0:T(8,128)S(1)}, f32[96,128]{1,0:T(8,128)S(1)}, u32[]{:S(2)}, u32[]{:S(2)}) collective-permute-start(f32[96,128]{1,0:T(8,128)S(1)} %get-tuple-element.82), channel_id=1, source_target_pairs={{0,1},{1,0},{2,3},{3,2},{4,5},{5,4},{6,7},{7,6},{8,24},{9,25},{10,... | collective-permute-start | bytes 147464 | tf_op jit(solution)/shard_map/ppermute | solution.py:372
  22.4 3.3 %collective-permute-start.9 = (f32[96,128]{1,0:T(8,128)S(1)}, f32[96,128]{1,0:T(8,128)S(1)}, u32[]{:S(2)}, u32[]{:S(2)}) collective-permute-start(f32[96,128]{1,0:T(8,128)S(1)} %get-tuple-element.83), channel_id=1, source_target_pairs={{0,1},{1,0},{2,3},{3,2},{4,5},{5,4},{6,7},{7,6},{8,9},{9,8},{10,11... | collective-permute-start | bytes 147464 | tf_op jit(solution)/shard_map/ppermute | solution.py:372
  25.7 4.2 %collective-permute-start.10 = (f32[2,3072]{1,0:T(2,128)S(1)}, f32[2,3072]{1,0:T(2,128)S(1)}, u32[]{:S(2)}, u32[]{:S(2)}) collective-permute-start(f32[2,3072]{1,0:T(2,128)S(1)} %get-tuple-element.86), channel_id=1, source_target_pairs={{0,7},{1,2},{2,1},{3,4},{4,3},{5,6},{6,5},{7,0},{8,15},{9,10},{10,... | collective-permute-start | bytes 73736 | tf_op jit(solution)/shard_map/ppermute | solution.py:399
  25.8 4.1 %collective-permute-start.11 = (f32[2,3072]{1,0:T(2,128)S(1)}, f32[2,3072]{1,0:T(2,128)S(1)}, u32[]{:S(2)}, u32[]{:S(2)}) collective-permute-start(f32[2,3072]{1,0:T(2,128)S(1)} %get-tuple-element.87), channel_id=1, source_target_pairs={{0,1},{1,0},{2,3},{3,2},{4,5},{5,4},{6,7},{7,6},{8,9},{9,8},{10,11... | collective-permute-start | bytes 73736 | tf_op jit(solution)/shard_map/ppermute | solution.py:398

commit v6 on v5

--- a/solution.py
+++ b/solution.py
@@ -20,6 +20,7 @@
 
 MEMBERS = 3
 SUBLANES = 8
+BAND = 8
 
 
 def partner_pairs(groups, tiles, member):
@@ -51,26 +52,17 @@
     return high, low
 
 
-def payload(handed, wide_ref, pick_ref, chosen_ref, out_refs, blk_ref):
+def products(handed, picked_by, weight, blk_ref):
     rows, width = handed.shape
     count, block = blk_ref.shape
     per_row = width // block
-    margins = pick_ref.shape[1]
-    band = wide_ref.shape[0] // margins
     for c in range(per_row):
         blk_ref[pl.ds(c, rows, stride=per_row), :] = handed[:, c * block : (c + 1) * block]
-    picked = lax.dot_general(
-        pick_ref[...], blk_ref[...].astype(BF16), (((0,), (0,)), ((), ())), preferred_element_type=F32
-    )
-    contrib = wide_ref[pl.ds(0, margins, stride=band), :] * picked
-    for j in range(1, band):
-        turned = pltpu.roll(picked, block - j, 1)
-        contrib = contrib + wide_ref[pl.ds(j, margins, stride=band), :] * turned
-    high, low = split_high_low(contrib)
-    both = jnp.concatenate([high, low], axis=0)
-    blocks = jnp.dot(chosen_ref[...], both, preferred_element_type=F32)
-    for n, out_ref in enumerate(out_refs):
-        out_ref[...] = blocks[n * count : (n + 1) * count]
+    picked = picked_by(blk_ref[...].astype(BF16))
+    total = weight(0) * picked
+    for j in range(1, BAND):
+        total = total + weight(j) * pltpu.roll(picked, block - j, 1)
+    return total
 
 
 def column(row):
@@ -116,33 +108,50 @@
     for copy in copies:
         copy.start()
     copies[0].wait()
-    for ref, half in zip((x1, x2), halves_of([state_v[0, :, r, :] for r in range(state_v.shape[2])])):
+    for ref, half in zip((x1, x2), halves_of([state_v[0, 1:, r, :] for r in range(state_v.shape[2])])):
         for i, value in enumerate(half):
-            ref[i] = value
+            ref[:, i, :] = value
     surface[...] = state_v[0, 0]
     for copy in copies[1:]:
         copy.wait()
-    mask, codes = outs[1], outs[2]
-    wet[...] = jnp.where(is_sea(groups), mask[0].astype(F32), 1.0)
-    for ref, half in zip((x1, x2), halves_of(lines_of(codes[0].astype(F32)))):
-        for i, value in enumerate(half):
-            ref[i, 0:1, :] = value
+    wet[...] = jnp.where(is_sea(groups), outs[1][0].astype(F32), 1.0)
+
+
+def all_fields(x, i):
+    width = x.shape[2]
+    if x.shape[0] % SUBLANES:
+        cut = SUBLANES - 1
+        top = jnp.concatenate([jnp.zeros((1, width), F32), x[:cut, i, :]], axis=0)
+        return jnp.concatenate([top, x[cut:, i, :]], axis=0)
+    return x[:, i, :]
 
 
 def remap_kernel(groups, coupling, mixing, courant, matrices, weights, sources, targets, *refs):
-    coef, table, col0, wide, pick, chosen, *outs, blk = refs
+    coef, table, col0, wide, pick, *outs, blk = refs
     count, margins = pick.shape
     slot = lax.broadcasted_iota(jnp.int32, (count, margins), 0)
     pick[...] = (slot == sources[...]).astype(F32).astype(BF16)
     me = lax.axis_index("comp")
     air_count = MEMBERS * groups // 4
+    wide[...] = weights[0].reshape(wide.shape).astype(F32)
+    contrib = products(
+        coupling[0],
+        lambda blocks: lax.dot_general(
+            pick[...], blocks, (((0,), (0,)), ((), ())), preferred_element_type=F32
+        ),
+        lambda j: wide[pl.ds(j, margins, stride=BAND), :],
+        blk,
+    )
+    both = jnp.concatenate(split_high_low(contrib), axis=0)
+    chosen = []
     for n in range(MEMBERS):
         ocean = jnp.where(lax.rem(me, MEMBERS) == n, air_count + lax.div(me, MEMBERS), me)
         partner = jnp.where(me < air_count, ocean, MEMBERS * (me - air_count) + n)
         hit = (targets[...] == slot + partner * count).astype(F32).astype(BF16)
-        chosen[n * count : (n + 1) * count] = jnp.concatenate([hit, hit], axis=1)
-    wide[...] = weights[0].reshape(wide.shape).astype(F32)
-    payload(coupling[0], wide, pick, chosen, outs, blk)
+        chosen.append(jnp.concatenate([hit, hit], axis=1))
+    blocks = jnp.dot(jnp.concatenate(chosen, axis=0), both, preferred_element_type=F32)
+    for n, out in enumerate(outs):
+        out[...] = blocks[n * count : (n + 1) * count]
     m, c = column(mixing[...]), column(courant[...])
     coef[0], coef[1], coef[2] = 1.0 - 4.0 * m - c, m + c, m
     branches, fields = matrices.shape[1:3]
@@ -153,9 +162,30 @@
     table[...] = jnp.concatenate([high, high, low], axis=1)
 
 
-def surface_kernel(groups, late, *refs):
-    recs, (surface_ref, mask_ref, *refs) = refs[:MEMBERS], refs[MEMBERS:]
-    ns_ref, flux_ref, *ends, blk = refs if late else refs[1:]
+def sort_kernel(groups, targets, wide, pick, after, wide_out, pick_out):
+    count, margins = pick.shape
+    me = lax.axis_index("comp")
+    air_count = MEMBERS * groups // 4
+    first = jnp.where(is_sea(groups), MEMBERS * (me - air_count), air_count + lax.div(me, MEMBERS))
+    place = targets[...] - first * count
+    here = lax.broadcasted_iota(jnp.int32, (margins, margins), 0)
+    there = lax.broadcasted_iota(jnp.int32, (margins, margins), 1)
+    level = place.astype(F32)
+    same = jnp.logical_and(column(level) == level, here < there)
+    rank = jnp.sum(jnp.where(same, 1.0, 0.0), axis=0, keepdims=True).astype(jnp.int32)
+    place = place + jnp.where(is_sea(groups), 0, rank * count)
+    order = (here == place).astype(F32).astype(BF16)
+    pick_out[...] = lax.dot_general(
+        order, pick[...], (((1,), (1,)), ((), ())), preferred_element_type=F32
+    ).astype(BF16)
+    for j in range(BAND):
+        band = wide[pl.ds(j, margins, stride=BAND), :].astype(BF16)
+        wide_out[j] = jnp.dot(order, band, preferred_element_type=F32)
+
+
+def surface_kernel(groups, *refs):
+    recs, refs = refs[:MEMBERS], refs[MEMBERS:]
+    surface_ref, mask_ref, _, ns_ref, flux_ref, *ends, blk = refs
     rows, width = ns_ref.shape
     block = blk.shape[-1]
     per_row = width // block
@@ -202,16 +232,25 @@
             ref[i] = value
 
 
-def start_kernel(x1, x2, coef, base1, base2):
-    own_rows(*rows_of([x1[0], x1[1]], [x2[0], x2[1]]), coef, base1, base2)
-
-
-def evolve_kernel(part1, part2, gain1, gain2, squashed, coef, base1, base2):
-    half = part1.shape[0]
-    lines = [squashed[r : r + 1, :] for r in range(half, 3 * half)]
-    line1, line2 = halves_of(lines)
-    inner = [part1[i] + gain1[i] * line1[i] for i in range(half)]
-    outer = [part2[i] + gain2[i] * line2[i] for i in range(half)]
+def start_kernel(x1, x2, coef, col0, codes, wet, base1, base2, gain1, gain2):
+    inner, outer = ([all_fields(x, i) for i in range(x.shape[1])] for x in (x1, x2))
+    own_rows(*rows_of(inner, outer), coef, base1, base2)
+    shape = gain1.shape[1:]
+    rows = [
+        branch_factor(col0, code, shape) * line
+        for code, line in zip(lines_of(codes[0]), lines_of(wet[...]))
+    ]
+    for ref, half in zip((gain1, gain2), halves_of(rows)):
+        for i, value in enumerate(half):
+            ref[i] = value
+
+
+def evolve_kernel(part1, part2, gain1, gain2, ns, e2, e1, coef, base1, base2, squashed):
+    squashed[...] = jnp.tanh(field0_rows(ns, e2[...], e1[...], coef))
+    half, fields, _ = gain1.shape
+    line1, line2 = halves_of([squashed[r : r + 1, :] for r in range(half, 3 * half)])
+    inner = [part1[:fields, i, :] + gain1[i] * line1[i] for i in range(half)]
+    outer = [part2[:fields, i, :] + gain2[i] * line2[i] for i in range(half)]
     own_rows(*rows_of(inner, outer), coef, base1, base2)
 
 
@@ -222,9 +261,9 @@
     return factor
 
 
-def fields_kernel(inner, late, base, y, coef, table, col0, codes, wet, after, *refs):
-    part, part0, gain = refs[-3:]
-    z, squashed = refs[:2] if late else (None, None)
+def fields_kernel(inner, late, base, y, after, coef, table, codes, wet, *refs):
+    part, part0 = refs[-2:]
+    col0, squashed = refs[:2] if late else (None, None)
     half, fields, width = base.shape
     at_top = is_odd() if inner else jnp.logical_not(is_odd())
     c0, cu, m = coef[0], coef[1], coef[2]
@@ -232,10 +271,10 @@
     branches = table.shape[0] // fields
 
     def halo_row(top, bottom):
-        value = jnp.where(at_top, y[top], y[bottom])
         if not late:
-            return value
-        code = jnp.where(at_top, z[top, 0:1], z[bottom, 0:1]).astype(jnp.int32)
+            return jnp.where(at_top, all_fields(y, top), all_fields(y, bottom))
+        value = jnp.where(at_top, y[:fields, top, :], y[:fields, bottom, :])
+        code = jnp.where(at_top, y[fields:, top, :], y[fields:, bottom, :]).astype(jnp.int32)
         line = jnp.where(
             at_top, squashed[top : top + 1, :], squashed[3 * half + bottom : 3 * half + bottom + 1, :]
         )
@@ -259,35 +298,47 @@
             chosen = code_lines[i] == b
             tendency = jnp.where(chosen, terms[b * fields : (b + 1) * fields], tendency)
         part0[i : i + 1, :] = tendency[:1] * wet_lines[i]
-        part[i] = jnp.where(top_field, 1.0, f + tendency) * wet_lines[i]
-        gain[i] = branch_factor(col0, code_lines[i], (fields, width)) * wet_lines[i]
-
-
-def field0(ns, e2, e1, coef, wet, part01, part02, gain1, gain2):
+        part[:fields, i, :] = jnp.where(top_field, 1.0, f + tendency) * wet_lines[i]
+        part[fields:, i, :] = code_lines[i].astype(F32)
+
+
+def field0_rows(ns, e2, e1, coef):
     c0, cu, m = coef[0, :1], coef[1, :1], coef[2, :1]
     odd = is_odd()
-    first, last = e1[...], e2[...]
-    f = jnp.concatenate(
-        [jnp.where(odd, first, last), ns[...], jnp.where(odd, last, first)], axis=0
-    )
+    f = jnp.concatenate([jnp.where(odd, e1, e2), ns[...], jnp.where(odd, e2, e1)], axis=0)
     rows = f.shape[0]
     for _ in range(SUBSTEPS):
         f = substep(f, pltpu.roll(f, 1, 0), pltpu.roll(f, rows - 1, 0), c0, cu, m)
-    f = f[SUBSTEPS : rows - SUBSTEPS]
+    return f[SUBSTEPS : rows - SUBSTEPS]
+
+
+def field0(ns, e2, e1, coef, wet, part01, part02, gain1, gain2):
+    odd = is_odd()
+    above, below = jnp.where(odd, e1[...], e2[...])[-SUBSTEPS:], jnp.where(odd, e2[...], e1[...])[:SUBSTEPS]
+    f = field0_rows(ns, jnp.where(odd, below, above), jnp.where(odd, above, below), coef)
     squashed = jnp.tanh(f)
-    extra = (f.shape[0] - ns.shape[0]) // 2
-    own = slice(extra, extra + ns.shape[0])
     part = jnp.concatenate(rows_of([part01[...]], [part02[...]]), axis=0)
     gain = jnp.concatenate(rows_of([gain1[:, 0, :]], [gain2[:, 0, :]]), axis=0)
-    return part + gain * squashed[own] + f[own] * wet[...], squashed
+    return part + gain * squashed + f * wet[...], squashed
 
 
 def hand_kernel(
-    groups, ns, e2, e1, coef, wet, part01, part02, gain1, gain2, flux, wide, pick, chosen, *refs
+    groups, ns, e1, e2, coef, wet, part01, part02, gain1, gain2, flux, wide, pick, *refs
 ):
-    surf, squashed, *outs, blk = refs
-    surf[...], squashed[...] = field0(ns, e2, e1, coef, wet, part01, part02, gain1, gain2)
-    payload(jnp.where(is_sea(groups), surf[...], flux[...]), wide, pick, chosen, outs, blk)
+    surf, *outs, blk = refs
+    surf[...], _ = field0(ns, e2, e1, coef, wet, part01, part02, gain1, gain2)
+    sea = is_sea(groups)
+    contrib = products(
+        jnp.where(sea, surf[...], flux[...]),
+        lambda blocks: jnp.dot(pick[...], blocks, preferred_element_type=F32),
+        lambda j: wide[j],
+        blk,
+    )
+    count = blk.shape[0]
+    thirds = [contrib[n * count : (n + 1) * count] for n in range(MEMBERS)]
+    member = lax.rem(lax.axis_index("comp"), MEMBERS)
+    for n, (out, third) in enumerate(zip(outs, thirds)):
+        out[...] = jnp.where(sea, third, jnp.where(member == n, sum(thirds), 0.0))
 
 
 def close_kernel(
@@ -296,14 +347,14 @@
     new_state, new_coupling, surf, squashed = refs
     surf[...], squashed[...] = field0(ns, e2, e1, coef, wet, part01, part02, gain1, gain2)
     new_coupling[0] = jnp.where(is_sea(groups), surf[...], flux[...])
-    half, fields, width = part1.shape
+    half, fields, width = gain1.shape
     top_field = lax.broadcasted_iota(jnp.int32, (SUBLANES, width), 0) == 0
     line1, line2 = halves_of([squashed[r : r + 1, :] for r in range(2 * half)])
     for h in range(0, fields, SUBLANES):
         some = slice(h, h + SUBLANES)
         for i in range(half):
-            inner = part1[i, some] + gain1[i, some] * line1[i]
-            outer = part2[i, some] + gain2[i, some] * line2[i]
+            inner = part1[some, i, :] + gain1[i, some] * line1[i]
+            outer = part2[some, i, :] + gain2[i, some] * line2[i]
             for r, done in zip((i, half + i), rows_of([inner], [outer])):
                 if h == 0:
                     done = jnp.where(top_field, surf[r : r + 1, :], done)
@@ -324,6 +375,16 @@
     )(*args)
 
 
+def fields_half(late, parts, kept, inner, base, y, after, *rest):
+    return call(
+        functools.partial(fields_kernel, inner, late),
+        "inner" if inner else "outer",
+        parts,
+        (base, y, after, *kept, *rest),
+        flops=0 if inner else 4_000_000_000,
+    )
+
+
 def on_device(
     state, coupling, land_mask, codes, mixing, courant, matrices, weights, sources, targets
 ):
@@ -345,7 +406,9 @@
     x1, x2, surface, wet, handed, mask, codes, *raw = call(
         functools.partial(load_kernel, groups),
         "load",
-        halves + [shape((rows, width), F32)] * 2 + [shape(a.shape, a.dtype) for a in args[1:]],
+        [shape((fields - 1, half, width), F32)] * 2
+        + [shape((rows, width), F32)] * 2
+        + [shape(a.shape, a.dtype) for a in args[1:]],
         [pltpu.with_memory_space_constraint(a, pltpu.HBM) for a in args],
         [pltpu.VMEM(state.shape, F32), pltpu.SemaphoreType.DMA((len(args),))],
         [pl.BlockSpec(memory_space=pltpu.HBM)] * len(args),
@@ -356,9 +419,8 @@
         shape((branches, fields, 1), F32),
         shape((margins * band, block), F32),
         shape((count, margins), BF16),
-        shape((MEMBERS * count, 2 * margins), BF16),
     ]
-    coef, table, col0, wide, pick, chosen, *sent = call(
+    coef, table, col0, wide, pick, *sent = call(
         functools.partial(remap_kernel, groups),
         "remap",
         tables + payloads,
@@ -375,44 +437,49 @@
         late, last = interval > 0, interval == INTERVALS - 1
         line, pair = shape((rows, width), F32), shape((half, width), F32)
         if late:
-            base1, base2 = call(
-                evolve_kernel, "evolve", halves, (part1, part2, gain1, gain2, squashed, coef)
+            base1, base2, squashed = call(
+                evolve_kernel,
+                "evolve",
+                halves + [shape((2 * rows, width), F32)],
+                (part1, part2, gain1, gain2, ns, e2, e1, coef),
             )
         else:
-            base1, base2 = call(start_kernel, "start", halves, (x1, x2, coef))
-        kept = (coef, table, col0, codes, wet)
-        part1, part01, gain1 = call(
-            functools.partial(fields_kernel, True, late),
-            "inner",
-            [halves[0], pair, halves[0]],
-            (base1, y1, *kept, base1) + ((z1, squashed) if late else ()),
-        )
+            base1, base2, gain1, gain2 = call(
+                start_kernel, "start", halves * 2, (x1, x2, coef, col0, codes, wet)
+            )
+            wide, pick = call(
+                functools.partial(sort_kernel, groups),
+                "sort",
+                [shape((band, margins, block), F32), shape((margins, count), BF16)],
+                (raw[-1], wide, pick, base1),
+            )
+        kept = (coef, table, codes, wet)
+        parts = [shape((fields + 1, half, width), F32), pair]
+        run_fields = functools.partial(fields_half, late, parts, kept)
         ns, flux, *edges = call(
-            functools.partial(surface_kernel, groups, late),
+            functools.partial(surface_kernel, groups),
             "surface",
             [line] * 2 + ([pair] * 2 if last else []),
-            (*recs, surface, mask) + (() if late else (part01,)),
+            (*recs, surface, mask, pick),
             [blocks],
         )
         d1, d2 = edges if last else (ns, ns)
         e1 = lax.ppermute(d1, "tile", inner_pairs(tiles))
         e2 = lax.ppermute(d2, "tile", outer_pairs(tiles))
-        part2, part02, gain2 = call(
-            functools.partial(fields_kernel, False, late),
-            "outer",
-            [halves[0], pair, halves[0]],
-            (base2, y2, *kept, part01 if late else ns) + ((z2, squashed) if late else ()),
-            flops=4_000_000_000,
-        )
-        z1, z2 = y1, y2
+        if late:
+            part2, part02 = run_fields(False, base2, y2, ns, col0, squashed)
+            part1, part01 = run_fields(True, base1, y1, part02, col0, squashed)
+        else:
+            part2, part02 = run_fields(False, base2, y2, ns)
+            part1, part01 = run_fields(True, base1, y1, part02)
         x1, x2 = part1, part2
         common = (ns, e2, e1, coef, wet, part01, part02, gain1, gain2, flux)
         if not last:
-            surface, squashed, *sent = call(
+            surface, *sent = call(
                 functools.partial(hand_kernel, groups),
                 "hand",
-                [line, shape((2 * rows, width), F32)] + payloads,
-                (*common, wide, pick, chosen),
+                [line] + payloads,
+                (ns, e1, e2, *common[3:], wide, pick),
                 [blocks],
                 flops=20_000_000_000,
             )

time: 31.5 us -> 30.9 us (0.981)
  waiting for transfers between devices: 6.12 us -> 3.44 us
  Pallas kernels: 9.36 us -> 10.8 us
  starting transfers between devices: 15.2 us -> 15.8 us
    ppermute x6, waiting for transfers between devices: 2.43 us -> 0.92 us  [on_device(): lax.ppermute(value, ('comp', 'tile'), partner_pairs(groups, tiles, member))]
    pallas_call x12 -> x13, Pallas kernels: 9.36 us -> 10.8 us  [call(): pl.pallas_call(kernel, name=name, out_shape=outs, in_specs=in_specs or [V...]
    ppermute x2, starting transfers between devices: 0.14 us -> 1.31 us  [on_device(): e2 = lax.ppermute(d2, 'tile', outer_pairs(tiles))]
    ppermute x2, starting transfers between devices: 1.01 us -> 0.01 us  [on_device(): y1 = lax.ppermute(x1, 'tile', inner_pairs(tiles))]
    ppermute x2, waiting for transfers between devices: 2.21 us -> 1.3 us  [on_device(): y2 = lax.ppermute(x2, 'tile', outer_pairs(tiles))]
    ppermute x6, starting transfers between devices: 7.83 us -> 8.27 us  [on_device(): lax.ppermute(value, ('comp', 'tile'), partner_pairs(groups, tiles, member))]
  transfers between devices with their start and end apart: 14 -> 14, of which waited for: 5 -> 5; matrix products, arithmetic and copies ran while one was open for 0% -> 0% of each run, Pallas kernels for 20% -> 25%
where the time goes in v6:
time: 30.9 us; the launch traced here: 30.8 us
  starting transfers between devices  15.8 us (51%)
  Pallas kernels  10.8 us (35%)
  waiting for transfers between devices  3.44 us (11%)
  between operations  0.74 us (2%)
    pallas_call x13, Pallas kernels, call(): pl.pallas_call(kernel, name=name, out_shape=outs, in_specs=in_specs or [V...  10.8 us
    ppermute x6, starting transfers between devices, on_device(): lax.ppermute(value, ('comp', 'tile'), partner_pairs(groups, tiles, member))  8.27 us
    ppermute x2, starting transfers between devices, on_device(): y2 = lax.ppermute(x2, 'tile', outer_pairs(tiles))  5.87 us
    ppermute x2, starting transfers between devices, on_device(): e2 = lax.ppermute(d2, 'tile', outer_pairs(tiles))  1.31 us
    ppermute x2, waiting for transfers between devices, on_device(): y2 = lax.ppermute(x2, 'tile', outer_pairs(tiles))  1.3 us
    ppermute x2, waiting for transfers between devices, on_device(): e2 = lax.ppermute(d2, 'tile', outer_pairs(tiles))  1.21 us
    ppermute x6, waiting for transfers between devices, on_device(): lax.ppermute(value, ('comp', 'tile'), partner_pairs(groups, tiles, member))  0.92 us
  transfers between devices with their start and end apart: 14, of which 5 were waited for; matrix products, arithmetic and copies ran while one was open for 0% of the time, Pallas kernels for 25%

profile of v6, /device:TPU:0, one launch (start us, length us, event | category | flops | bytes accessed | tf_op | source)
XLA Modules:
  0.0 30.8 jit_solution(11999016974249771672)
XLA Ops:
  0.6 1.5 %load.1 = (f32[15,2,3072]{2,1,0:T(2,128)S(1)}, f32[15,2,3072]{2,1,0:T(2,128)S(1)}, f32[4,3072]{1,0:T(4,128)S(1)}, f32[4,3072]{1,0:T(4,128)S(1)}, f32[1,4,3072]{2...) custom-call(f32[1,16,4,3072]{3,2,1,0:T(4,128)} %refs_0_.1, ...), custom_call_target="tpu_custom_call" | custom-call | bytes 3109632 | tf_op jit(solution)/shard_map/load/pallas_call | solution.py:366
  2.1 3.4 %collective-permute-start.6 = (f32[15,2,3072]{2,1,0:T(2,128)S(1)}, f32[15,2,3072]{2,1,0:T(2,128)S(1)}, u32[]{:S(2)}, u32[]{:S(2)}) collective-permute-start(f32[15,2,3072]{2,1,0:T(2,128)S(1)} %get-tuple-element.65.x2), channel_id=1, source_target_pairs={{0,7},{1,2},{2,1},{3,4},{4,3},{5,6},{6,5},{7,0},{8,15},{9,10},{10,... | collective-permute-start | bytes 1105928 | tf_op jit(solution)/shard_map/ppermute | solution.py:432
  5.5 0.8 %remap.1 = (f32[3,16,1]{2,1,0:T(8,128)S(1)}, bf16[64,48]{1,0:T(8,128)(2,1)S(1)}, f32[4,16,1]{2,1,0:T(8,128)S(1)}, f32[2304,128]{1,0:T(8,128)S(1)}, bf16[96,288]{...) custom-call(f32[1,4,3072]{2,1,0:T(4,128)S(1)} %get-tuple-element.50.coupling, ...), custom_call_target="tpu_custom_call" | custom-call | bytes 2034496 | tf_op jit(solution)/shard_map/remap/pallas_call | solution.py:366
  6.4 3.7 %collective-permute-start = (f32[96,128]{1,0:T(8,128)S(1)}, f32[96,128]{1,0:T(8,128)S(1)}, u32[]{:S(2)}, u32[]{:S(2)}) collective-permute-start(f32[96,128]{1,0:T(8,128)S(1)} %get-tuple-element.57), channel_id=1, source_target_pairs={{0,24},{1,25},{2,26},{3,27},{4,28},{5,29},{6,30},{7,31},{8,9},{9,8... | collective-permute-start | bytes 147464 | tf_op jit(solution)/shard_map/ppermute | solution.py:434
  10.0 0.0 collective-permute-start.1
  10.0 0.5 %collective-permute-start.2 = (f32[96,128]{1,0:T(8,128)S(1)}, f32[96,128]{1,0:T(8,128)S(1)}, u32[]{:S(2)}, u32[]{:S(2)}) collective-permute-start(f32[96,128]{1,0:T(8,128)S(1)} %get-tuple-element.59), channel_id=1, source_target_pairs={{0,1},{1,0},{2,3},{3,2},{4,5},{5,4},{6,7},{7,6},{8,9},{9,8},{10,11... | collective-permute-start | bytes 147464 | tf_op jit(solution)/shard_map/ppermute | solution.py:434
  10.6 1.4 %start.1 = (f32[2,16,3072]{2,1,0:T(8,128)S(1)}, f32[2,16,3072]{2,1,0:T(8,128)S(1)}, f32[2,16,3072]{2,1,0:T(8,128)S(1)}, f32[2,16,3072]{2,1,0:T(8,128)S(1)}) custom-call(f32[15,2,3072]{2,1,0:T(2,128)S(1)} %get-tuple-element.64.x1, f32[15,2,3072]{2,1,0:T(2,128)S(1)} %get-tuple-element.65.x2, f32[3,16,1]{2,1,0:T(8,128)S(1)} %get-tuple-element.66.coef, ...), custom_call_target="tpu_custom_call" | custom-call | bytes 2408896 | tf_op jit(solution)/shard_map/start/pallas_call | solution.py:366
  11.9 0.8 %sort.1 = (f32[8,288,128]{2,1,0:T(8,128)S(1)}, bf16[288,96]{1,0:T(8,128)(2,1)S(1)}) custom-call(s32[1,288]{1,0:T(1,128)S(1)} %get-tuple-element.56.targets, f32[2304,128]{1,0:T(8,128)S(1)} %get-tuple-element.62.wide, bf16[96,288]{1,0:T(8,128)(2,1)S(1)} %get-tuple-element.63.pick, f32[2,16,3072]{2,1,0:T(8,128)S(1)} %get-tuple-element.70.after.base), custom_call_target="tpu_custom_call" | custom-call | bytes 2864256 | tf_op jit(solution)/shard_map/sort/pallas_call | solution.py:366
  12.8 0.1 collective-permute-done.refs_0_
  12.9 0.0 collective-permute-done.1.refs_1_
  12.9 0.0 collective-permute-done.2.refs_2_
  12.9 0.7 %collective-permute-start.4 = (f32[4,3072]{1,0:T(4,128)S(1)}, f32[4,3072]{1,0:T(4,128)S(1)}, u32[]{:S(2)}, u32[]{:S(2)}) collective-permute-start(f32[4,3072]{1,0:T(4,128)S(1)} %get-tuple-element.72.after.ns), channel_id=1, source_target_pairs={{0,7},{1,2},{2,1},{3,4},{4,3},{5,6},{6,5},{7,0},{8,15},{9,10},{10,... | collective-permute-start | bytes 147464 | tf_op jit(solution)/shard_map/ppermute | solution.py:468
  13.6 0.4 %collective-permute-start.3 = (f32[4,3072]{1,0:T(4,128)S(1)}, f32[4,3072]{1,0:T(4,128)S(1)}, u32[]{:S(2)}, u32[]{:S(2)}) collective-permute-start(f32[4,3072]{1,0:T(4,128)S(1)} %get-tuple-element.72.after.ns), channel_id=1, source_target_pairs={{0,1},{1,0},{2,3},{3,2},{4,5},{5,4},{6,7},{7,6},{8,9},{9,8},{10,11... | collective-permute-start | bytes 147464 | tf_op jit(solution)/shard_map/ppermute | solution.py:467
  13.9 0.0 collective-permute-done.6.y
  14.0 0.5 %outer.2 = (f32[17,2,3072]{2,1,0:T(2,128)S(1)}, f32[2,3072]{1,0:T(2,128)S(1)}) custom-call(f32[2,16,3072]{2,1,0:T(8,128)S(1)} %get-tuple-element.73.base, f32[15,2,3072]{2,1,0:T(2,128)S(1)} %collective-permute-done.6.y, f32[4,3072]{1,0:T(4,128)S(1)} %get-tuple-element.72.after.ns, f32[3,16,1]{2,1,0:T(8,128)S(1)} %get-tuple-element.66.coef, ...), custom_call_target="tpu_custom_call" | custom-call | flops 4000000000 | bytes 1358016 | tf_op jit(solution)/shard_map/outer/pallas_call | solution.py:366
  14.5 2.5 %collective-permute-start.13 = (f32[17,2,3072]{2,1,0:T(2,128)S(1)}, f32[17,2,3072]{2,1,0:T(2,128)S(1)}, u32[]{:S(2)}, u32[]{:S(2)}) collective-permute-start(f32[17,2,3072]{2,1,0:T(2,128)S(1)} %get-tuple-element.89.part2), channel_id=1, source_target_pairs={{0,7},{1,2},{2,1},{3,4},{4,3},{5,6},{6,5},{7,0},{8,15},{9,10},{10,... | collective-permute-start | bytes 1253384 | tf_op jit(solution)/shard_map/ppermute | solution.py:432
  16.9 0.0 collective-permute-done.5.y
  16.9 0.5 %inner.2 = (f32[17,2,3072]{2,1,0:T(2,128)S(1)}, f32[2,3072]{1,0:T(2,128)S(1)}) custom-call(f32[2,16,3072]{2,1,0:T(8,128)S(1)} %get-tuple-element.70.after.base, f32[15,2,3072]{2,1,0:T(2,128)S(1)} %collective-permute-done.5.y, f32[2,3072]{1,0:T(2,128)S(1)} %get-tuple-element.75.after.part02, f32[3,16,1]{2,1,0:T(8,128)S(1)} %get-tuple-element.66.coef, ...), custom_call_target="tpu_custom_call" | custom-call | bytes 1333440 | tf_op jit(solution)/shard_map/inner/pallas_call | solution.py:366
  17.5 0.1 collective-permute-done.4.e2
  17.6 0.8 %hand.1 = (f32[4,3072]{1,0:T(4,128)S(1)}, f32[96,128]{1,0:T(8,128)S(1)}, f32[96,128]{1,0:T(8,128)S(1)}, f32[96,128]{1,0:T(8,128)S(1)}) custom-call(f32[4,3072]{1,0:T(4,128)S(1)} %get-tuple-element.72.after.ns, f32[4,3072]{1,0:T(4,128)S(1)} %collective-permute-done.3.e1, f32[4,3072]{1,0:T(4,128)S(1)} %collective-permute-done.4.e2, ...), custom_call_target="tpu_custom_call" | custom-call | flops 20000000000 | bytes 2513088 | tf_op jit(solution)/shard_map/hand/pallas_call | solution.py:366
  18.4 3.6 %collective-permute-start.7 = (f32[96,128]{1,0:T(8,128)S(1)}, f32[96,128]{1,0:T(8,128)S(1)}, u32[]{:S(2)}, u32[]{:S(2)}) collective-permute-start(f32[96,128]{1,0:T(8,128)S(1)} %get-tuple-element.81), channel_id=1, source_target_pairs={{0,24},{1,25},{2,26},{3,27},{4,28},{5,29},{6,30},{7,31},{8,9},{9,8... | collective-permute-start | bytes 147464 | tf_op jit(solution)/shard_map/ppermute | solution.py:434
  22.0 0.0 collective-permute-start.8
  22.0 0.5 %collective-permute-start.9 = (f32[96,128]{1,0:T(8,128)S(1)}, f32[96,128]{1,0:T(8,128)S(1)}, u32[]{:S(2)}, u32[]{:S(2)}) collective-permute-start(f32[96,128]{1,0:T(8,128)S(1)} %get-tuple-element.83), channel_id=1, source_target_pairs={{0,1},{1,0},{2,3},{3,2},{4,5},{5,4},{6,7},{7,6},{8,9},{9,8},{10,11... | collective-permute-start | bytes 147464 | tf_op jit(solution)/shard_map/ppermute | solution.py:434
  22.5 1.5 %evolve.1 = (f32[2,16,3072]{2,1,0:T(8,128)S(1)}, f32[2,16,3072]{2,1,0:T(8,128)S(1)}, f32[8,3072]{1,0:T(8,128)S(1)}) custom-call(f32[17,2,3072]{2,1,0:T(2,128)S(1)} %get-tuple-element.88.part1, f32[17,2,3072]{2,1,0:T(2,128)S(1)} %get-tuple-element.89.part2, f32[2,16,3072]{2,1,0:T(8,128)S(1)} %get-tuple-element.77.gain1, ...), custom_call_target="tpu_custom_call" | custom-call | bytes 2654400 | tf_op jit(solution)/shard_map/evolve/pallas_call | solution.py:366
  24.0 0.8 %collective-permute-done.7.refs_0_ = f32[96,128]{1,0:T(8,128)S(1)} collective-permute-done((f32[96,128]{1,0:T(8,128)S(1)}, f32[96,128]{1,0:T(8,128)S(1)}, u32[]{:S(2)}, u32[]{:S(2)}) %collective-permute-start.7) | collective-permute-done | bytes 49184 | tf_op jit(solution)/shard_map/ppermute | solution.py:434
  24.8 0.1 surface.3
  24.8 0.6 %collective-permute-start.10 = (f32[2,3072]{1,0:T(2,128)S(1)}, f32[2,3072]{1,0:T(2,128)S(1)}, u32[]{:S(2)}, u32[]{:S(2)}) collective-permute-start(f32[2,3072]{1,0:T(2,128)S(1)} %get-tuple-element.86), channel_id=1, source_target_pairs={{0,7},{1,2},{2,1},{3,4},{4,3},{5,6},{6,5},{7,0},{8,15},{9,10},{10,... | collective-permute-start | bytes 73736 | tf_op jit(solution)/shard_map/ppermute | solution.py:468
  25.5 1.3 %collective-permute-done.13.y = f32[17,2,3072]{2,1,0:T(2,128)S(1)} collective-permute-done((f32[17,2,3072]{2,1,0:T(2,128)S(1)}, f32[17,2,3072]{2,1,0:T(2,128)S(1)}, u32[]{:S(2)}, u32[]{:S(2)}) %collective-permute-start.13) | collective-permute-done | bytes 417824 | tf_op jit(solution)/shard_map/ppermute | solution.py:432
  26.8 0.6 %outer.3 = (f32[17,2,3072]{2,1,0:T(2,128)S(1)}, f32[2,3072]{1,0:T(2,128)S(1)}) custom-call(f32[2,16,3072]{2,1,0:T(8,128)S(1)} %get-tuple-element.91.base, f32[17,2,3072]{2,1,0:T(2,128)S(1)} %collective-permute-done.13.y, f32[4,3072]{1,0:T(4,128)S(1)} %get-tuple-element.85.after.ns, f32[3,16,1]{2,1,0:T(8,128)S(1)} %get-tuple-element.66.coef, ...), custom_call_target="tpu_custom_call" | custom-call | flops 4000000000 | bytes 1505728 | tf_op jit(solution)/shard_map/outer/pallas_call | solution.py:366
  27.4 0.7 %inner.3 = (f32[17,2,3072]{2,1,0:T(2,128)S(1)}, f32[2,3072]{1,0:T(2,128)S(1)}) custom-call(f32[2,16,3072]{2,1,0:T(8,128)S(1)} %get-tuple-element.90.base, f32[17,2,3072]{2,1,0:T(2,128)S(1)} %collective-permute-done.12.y, f32[2,3072]{1,0:T(2,128)S(1)} %get-tuple-element.93.after.part02, f32[3,16,1]{2,1,0:T(8,128)S(1)} %get-tuple-element.66.coef, ...), custom_call_target="tpu_custom_call" | custom-call | bytes 1481152 | tf_op jit(solution)/shard_map/inner/pallas_call | solution.py:366
  28.1 1.1 %collective-permute-done.10.e2 = f32[2,3072]{1,0:T(2,128)S(1)} collective-permute-done((f32[2,3072]{1,0:T(2,128)S(1)}, f32[2,3072]{1,0:T(2,128)S(1)}, u32[]{:S(2)}, u32[]{:S(2)}) %collective-permute-start.10) | collective-permute-done | bytes 24608 | tf_op jit(solution)/shard_map/ppermute | solution.py:468
  29.2 1.6 %close.1 = (f32[1,16,4,3072]{3,2,1,0:T(4,128)}, f32[1,4,3072]{2,1,0:T(4,128)}) custom-call(f32[4,3072]{1,0:T(4,128)S(1)} %get-tuple-element.85.after.ns, f32[2,3072]{1,0:T(2,128)S(1)} %collective-permute-done.10.e2, f32[2,3072]{1,0:T(2,128)S(1)} %collective-permute-done.11.e1, f32[3,16,1]{2,1,0:T(8,128)S(1)} %get-tuple-element.66.coef, ...), custom_call_target="tpu_custom_call" | custom-call | bytes 2703552 | tf_op jit(solution)/shard_map/close/pallas_call | solution.py:366
  (9 shorter events, 0.1 us)
Async XLA Ops:
  2.1 11.8 %collective-permute-start.6 = (f32[15,2,3072]{2,1,0:T(2,128)S(1)}, f32[15,2,3072]{2,1,0:T(2,128)S(1)}, u32[]{:S(2)}, u32[]{:S(2)}) collective-permute-start(f32[15,2,3072]{2,1,0:T(2,128)S(1)} %get-tuple-element.65.x2), channel_id=1, source_target_pairs={{0,7},{1,2},{2,1},{3,4},{4,3},{5,6},{6,5},{7,0},{8,15},{9,10},{10,... | collective-permute-start | bytes 1105928 | tf_op jit(solution)/shard_map/ppermute | solution.py:432
  6.4 6.5 %collective-permute-start = (f32[96,128]{1,0:T(8,128)S(1)}, f32[96,128]{1,0:T(8,128)S(1)}, u32[]{:S(2)}, u32[]{:S(2)}) collective-permute-start(f32[96,128]{1,0:T(8,128)S(1)} %get-tuple-element.57), channel_id=1, source_target_pairs={{0,24},{1,25},{2,26},{3,27},{4,28},{5,29},{6,30},{7,31},{8,9},{9,8... | collective-permute-start | bytes 147464 | tf_op jit(solution)/shard_map/ppermute | solution.py:434
  10.0 2.8 %collective-permute-start.1 = (f32[96,128]{1,0:T(8,128)S(1)}, f32[96,128]{1,0:T(8,128)S(1)}, u32[]{:S(2)}, u32[]{:S(2)}) collective-permute-start(f32[96,128]{1,0:T(8,128)S(1)} %get-tuple-element.58), channel_id=1, source_target_pairs={{0,1},{1,0},{2,3},{3,2},{4,5},{5,4},{6,7},{7,6},{8,24},{9,25},{10,... | collective-permute-start | bytes 147464 | tf_op jit(solution)/shard_map/ppermute | solution.py:434
  10.0 2.8 %collective-permute-start.2 = (f32[96,128]{1,0:T(8,128)S(1)}, f32[96,128]{1,0:T(8,128)S(1)}, u32[]{:S(2)}, u32[]{:S(2)}) collective-permute-start(f32[96,128]{1,0:T(8,128)S(1)} %get-tuple-element.59), channel_id=1, source_target_pairs={{0,1},{1,0},{2,3},{3,2},{4,5},{5,4},{6,7},{7,6},{8,9},{9,8},{10,11... | collective-permute-start | bytes 147464 | tf_op jit(solution)/shard_map/ppermute | solution.py:434
  10.6 6.4 %collective-permute-start.5 = (f32[15,2,3072]{2,1,0:T(2,128)S(1)}, f32[15,2,3072]{2,1,0:T(2,128)S(1)}, u32[]{:S(2)}, u32[]{:S(2)}) collective-permute-start(f32[15,2,3072]{2,1,0:T(2,128)S(1)} %get-tuple-element.64.x1), channel_id=1, source_target_pairs={{0,1},{1,0},{2,3},{3,2},{4,5},{5,4},{6,7},{7,6},{8,9},{9,8},{10,11... | collective-permute-start | bytes 1105928 | tf_op jit(solution)/shard_map/ppermute | solution.py:431
  12.9 4.7 %collective-permute-start.4 = (f32[4,3072]{1,0:T(4,128)S(1)}, f32[4,3072]{1,0:T(4,128)S(1)}, u32[]{:S(2)}, u32[]{:S(2)}) collective-permute-start(f32[4,3072]{1,0:T(4,128)S(1)} %get-tuple-element.72.after.ns), channel_id=1, source_target_pairs={{0,7},{1,2},{2,1},{3,4},{4,3},{5,6},{6,5},{7,0},{8,15},{9,10},{10,... | collective-permute-start | bytes 147464 | tf_op jit(solution)/shard_map/ppermute | solution.py:468
  13.6 4.0 %collective-permute-start.3 = (f32[4,3072]{1,0:T(4,128)S(1)}, f32[4,3072]{1,0:T(4,128)S(1)}, u32[]{:S(2)}, u32[]{:S(2)}) collective-permute-start(f32[4,3072]{1,0:T(4,128)S(1)} %get-tuple-element.72.after.ns), channel_id=1, source_target_pairs={{0,1},{1,0},{2,3},{3,2},{4,5},{5,4},{6,7},{7,6},{8,9},{9,8},{10,11... | collective-permute-start | bytes 147464 | tf_op jit(solution)/shard_map/ppermute | solution.py:467
  14.5 12.3 %collective-permute-start.13 = (f32[17,2,3072]{2,1,0:T(2,128)S(1)}, f32[17,2,3072]{2,1,0:T(2,128)S(1)}, u32[]{:S(2)}, u32[]{:S(2)}) collective-permute-start(f32[17,2,3072]{2,1,0:T(2,128)S(1)} %get-tuple-element.89.part2), channel_id=1, source_target_pairs={{0,7},{1,2},{2,1},{3,4},{4,3},{5,6},{6,5},{7,0},{8,15},{9,10},{10,... | collective-permute-start | bytes 1253384 | tf_op jit(solution)/shard_map/ppermute | solution.py:432
  18.4 6.4 %collective-permute-start.7 = (f32[96,128]{1,0:T(8,128)S(1)}, f32[96,128]{1,0:T(8,128)S(1)}, u32[]{:S(2)}, u32[]{:S(2)}) collective-permute-start(f32[96,128]{1,0:T(8,128)S(1)} %get-tuple-element.81), channel_id=1, source_target_pairs={{0,24},{1,25},{2,26},{3,27},{4,28},{5,29},{6,30},{7,31},{8,9},{9,8... | collective-permute-start | bytes 147464 | tf_op jit(solution)/shard_map/ppermute | solution.py:434
  22.0 2.8 %collective-permute-start.8 = (f32[96,128]{1,0:T(8,128)S(1)}, f32[96,128]{1,0:T(8,128)S(1)}, u32[]{:S(2)}, u32[]{:S(2)}) collective-permute-start(f32[96,128]{1,0:T(8,128)S(1)} %get-tuple-element.82), channel_id=1, source_target_pairs={{0,1},{1,0},{2,3},{3,2},{4,5},{5,4},{6,7},{7,6},{8,24},{9,25},{10,... | collective-permute-start | bytes 147464 | tf_op jit(solution)/shard_map/ppermute | solution.py:434
  22.0 2.8 %collective-permute-start.9 = (f32[96,128]{1,0:T(8,128)S(1)}, f32[96,128]{1,0:T(8,128)S(1)}, u32[]{:S(2)}, u32[]{:S(2)}) collective-permute-start(f32[96,128]{1,0:T(8,128)S(1)} %get-tuple-element.83), channel_id=1, source_target_pairs={{0,1},{1,0},{2,3},{3,2},{4,5},{5,4},{6,7},{7,6},{8,9},{9,8},{10,11... | collective-permute-start | bytes 147464 | tf_op jit(solution)/shard_map/ppermute | solution.py:434
  22.5 5.0 %collective-permute-start.12 = (f32[17,2,3072]{2,1,0:T(2,128)S(1)}, f32[17,2,3072]{2,1,0:T(2,128)S(1)}, u32[]{:S(2)}, u32[]{:S(2)}) collective-permute-start(f32[17,2,3072]{2,1,0:T(2,128)S(1)} %get-tuple-element.88.part1), channel_id=1, source_target_pairs={{0,1},{1,0},{2,3},{3,2},{4,5},{5,4},{6,7},{7,6},{8,9},{9,8},{10,11... | collective-permute-start | bytes 1253384 | tf_op jit(solution)/shard_map/ppermute | solution.py:431
  24.8 4.3 %collective-permute-start.10 = (f32[2,3072]{1,0:T(2,128)S(1)}, f32[2,3072]{1,0:T(2,128)S(1)}, u32[]{:S(2)}, u32[]{:S(2)}) collective-permute-start(f32[2,3072]{1,0:T(2,128)S(1)} %get-tuple-element.86), channel_id=1, source_target_pairs={{0,7},{1,2},{2,1},{3,4},{4,3},{5,6},{6,5},{7,0},{8,15},{9,10},{10,... | collective-permute-start | bytes 73736 | tf_op jit(solution)/shard_map/ppermute | solution.py:468
  25.5 3.7 %collective-permute-start.11 = (f32[2,3072]{1,0:T(2,128)S(1)}, f32[2,3072]{1,0:T(2,128)S(1)}, u32[]{:S(2)}, u32[]{:S(2)}) collective-permute-start(f32[2,3072]{1,0:T(2,128)S(1)} %get-tuple-element.87), channel_id=1, source_target_pairs={{0,1},{1,0},{2,3},{3,2},{4,5},{5,4},{6,7},{7,6},{8,9},{9,8},{10,11... | collective-permute-start | bytes 73736 | tf_op jit(solution)/shard_map/ppermute | solution.py:467

commit v7 on v6

--- a/solution.py
+++ b/solution.py
@@ -15,6 +15,7 @@
 F32 = jnp.float32
 BF16 = jnp.bfloat16
 VMEM = pl.BlockSpec(memory_space=pltpu.VMEM)
+HBM = pl.BlockSpec(memory_space=pltpu.HBM)
 PARAMS = pltpu.CompilerParams(vmem_limit_bytes=40 * 1024 * 1024)
 
 
@@ -97,24 +98,44 @@
     return [lines[r : r + 1] for r in range(lines.shape[0])]
 
 
-def load_kernel(groups, *refs):
-    state, *args = refs[:10]
-    x1, x2, surface, wet = refs[10:14]
-    outs, (state_v, sems) = refs[14:23], refs[23:]
-    copies = [
-        pltpu.make_async_copy(src, dst, sems.at[n])
-        for n, (src, dst) in enumerate(zip((state, *args), (state_v, *outs)))
-    ]
+def copy_all(pairs, sems):
+    copies = [pltpu.make_async_copy(src, dst, sems.at[n]) for n, (src, dst) in enumerate(pairs)]
     for copy in copies:
         copy.start()
+    return copies
+
+
+def load_kernel(groups, state, sources, targets, coupling, weights, *refs):
+    x1, x2, surface, pick, chosen, targets_v, coupling_v, weights_v, state_v, sources_v, sems = refs
+    copies = copy_all(
+        (
+            (state, state_v),
+            (sources, sources_v),
+            (targets, targets_v),
+            (coupling, coupling_v),
+            (weights, weights_v),
+        ),
+        sems,
+    )
+    copies[1].wait()
+    copies[2].wait()
+    count, margins = pick.shape
+    slot = lax.broadcasted_iota(jnp.int32, (count, margins), 0)
+    pick[...] = (slot == sources_v[...]).astype(F32).astype(BF16)
+    me = lax.axis_index("comp")
+    air_count = MEMBERS * groups // 4
+    for n in range(MEMBERS):
+        ocean = jnp.where(lax.rem(me, MEMBERS) == n, air_count + lax.div(me, MEMBERS), me)
+        partner = jnp.where(me < air_count, ocean, MEMBERS * (me - air_count) + n)
+        hit = (targets_v[...] == slot + partner * count).astype(F32).astype(BF16)
+        chosen[n * count : (n + 1) * count] = jnp.concatenate([hit, hit], axis=1)
     copies[0].wait()
     for ref, half in zip((x1, x2), halves_of([state_v[0, 1:, r, :] for r in range(state_v.shape[2])])):
         for i, value in enumerate(half):
             ref[:, i, :] = value
     surface[...] = state_v[0, 0]
-    for copy in copies[1:]:
+    for copy in copies[3:]:
         copy.wait()
-    wet[...] = jnp.where(is_sea(groups), outs[1][0].astype(F32), 1.0)
 
 
 def all_fields(x, i):
@@ -126,13 +147,9 @@
     return x[:, i, :]
 
 
-def remap_kernel(groups, coupling, mixing, courant, matrices, weights, sources, targets, *refs):
-    coef, table, col0, wide, pick, *outs, blk = refs
+def remap_kernel(coupling, weights, pick, chosen, wide, *refs):
+    outs, blk = refs[:-1], refs[-1]
     count, margins = pick.shape
-    slot = lax.broadcasted_iota(jnp.int32, (count, margins), 0)
-    pick[...] = (slot == sources[...]).astype(F32).astype(BF16)
-    me = lax.axis_index("comp")
-    air_count = MEMBERS * groups // 4
     wide[...] = weights[0].reshape(wide.shape).astype(F32)
     contrib = products(
         coupling[0],
@@ -143,26 +160,15 @@
         blk,
     )
     both = jnp.concatenate(split_high_low(contrib), axis=0)
-    chosen = []
-    for n in range(MEMBERS):
-        ocean = jnp.where(lax.rem(me, MEMBERS) == n, air_count + lax.div(me, MEMBERS), me)
-        partner = jnp.where(me < air_count, ocean, MEMBERS * (me - air_count) + n)
-        hit = (targets[...] == slot + partner * count).astype(F32).astype(BF16)
-        chosen.append(jnp.concatenate([hit, hit], axis=1))
-    blocks = jnp.dot(jnp.concatenate(chosen, axis=0), both, preferred_element_type=F32)
+    blocks = jnp.dot(chosen[...], both, preferred_element_type=F32)
     for n, out in enumerate(outs):
         out[...] = blocks[n * count : (n + 1) * count]
-    m, c = column(mixing[...]), column(courant[...])
-    coef[0], coef[1], coef[2] = 1.0 - 4.0 * m - c, m + c, m
-    branches, fields = matrices.shape[1:3]
-    flat = matrices[0].reshape(branches * fields, fields)
-    col0[...] = flat[:, :1].reshape(branches, fields, 1)
-    flat = jnp.where(lax.broadcasted_iota(jnp.int32, flat.shape, 1) == 0, 0.0, flat)
-    high, low = split_high_low(flat)
-    table[...] = jnp.concatenate([high, high, low], axis=1)
-
-
-def sort_kernel(groups, targets, wide, pick, after, wide_out, pick_out):
+
+
+def sort_kernel(groups, targets, wide, pick, *refs):
+    args, refs = refs[:5], refs[5:]
+    wide_out, pick_out, mask, codes, wet, coef, table, col0, mixing, courant, matrices, sems = refs
+    copies = copy_all(tuple(zip(args, (mask, codes, mixing, courant, matrices))), sems)
     count, margins = pick.shape
     me = lax.axis_index("comp")
     air_count = MEMBERS * groups // 4
@@ -181,6 +187,17 @@
     for j in range(BAND):
         band = wide[pl.ds(j, margins, stride=BAND), :].astype(BF16)
         wide_out[j] = jnp.dot(order, band, preferred_element_type=F32)
+    for copy in copies:
+        copy.wait()
+    wet[...] = jnp.where(is_sea(groups), mask[0].astype(F32), 1.0)
+    m, c = column(mixing[...]), column(courant[...])
+    coef[0], coef[1], coef[2] = 1.0 - 4.0 * m - c, m + c, m
+    branches, fields = matrices.shape[1:3]
+    flat = matrices[0].reshape(branches * fields, fields)
+    col0[...] = flat[:, :1].reshape(branches, fields, 1)
+    flat = jnp.where(lax.broadcasted_iota(jnp.int32, flat.shape, 1) == 0, 0.0, flat)
+    high, low = split_high_low(flat)
+    table[...] = jnp.concatenate([high, high, low], axis=1)
 
 
 def surface_kernel(groups, *refs):
@@ -232,7 +249,7 @@
             ref[i] = value
 
 
-def start_kernel(x1, x2, coef, col0, codes, wet, base1, base2, gain1, gain2):
+def start_kernel(x1, x2, coef, col0, codes, wet, base1, base2, gain1, gain2, gain0):
     inner, outer = ([all_fields(x, i) for i in range(x.shape[1])] for x in (x1, x2))
     own_rows(*rows_of(inner, outer), coef, base1, base2)
     shape = gain1.shape[1:]
@@ -243,6 +260,8 @@
     for ref, half in zip((gain1, gain2), halves_of(rows)):
         for i, value in enumerate(half):
             ref[i] = value
+    for r, value in enumerate(rows):
+        gain0[r : r + 1, :] = value[:1]
 
 
 def evolve_kernel(part1, part2, gain1, gain2, ns, e2, e1, coef, base1, base2, squashed):
@@ -262,7 +281,10 @@
 
 
 def fields_kernel(inner, late, base, y, after, coef, table, codes, wet, *refs):
-    part, part0 = refs[-2:]
+    part, part0 = refs[-2:] if inner else refs[-3:-1]
+    if not inner:
+        none = jnp.zeros((SUBSTEPS, base.shape[2]), F32)
+        refs[-1][...] = field0_rows(after, none, none, coef)
     col0, squashed = refs[:2] if late else (None, None)
     half, fields, width = base.shape
     at_top = is_odd() if inner else jnp.logical_not(is_odd())
@@ -298,8 +320,11 @@
             chosen = code_lines[i] == b
             tendency = jnp.where(chosen, terms[b * fields : (b + 1) * fields], tendency)
         part0[i : i + 1, :] = tendency[:1] * wet_lines[i]
-        part[:fields, i, :] = jnp.where(top_field, 1.0, f + tendency) * wet_lines[i]
-        part[fields:, i, :] = code_lines[i].astype(F32)
+        if late:
+            part[i] = (f + tendency) * wet_lines[i]
+        else:
+            part[:fields, i, :] = jnp.where(top_field, 1.0, f + tendency) * wet_lines[i]
+            part[fields:, i, :] = code_lines[i].astype(F32)
 
 
 def field0_rows(ns, e2, e1, coef):
@@ -312,21 +337,28 @@
     return f[SUBSTEPS : rows - SUBSTEPS]
 
 
-def field0(ns, e2, e1, coef, wet, part01, part02, gain1, gain2):
+def field0(own, e2, e1, coef, wet, part01, part02, gain0):
     odd = is_odd()
-    above, below = jnp.where(odd, e1[...], e2[...])[-SUBSTEPS:], jnp.where(odd, e2[...], e1[...])[:SUBSTEPS]
-    f = field0_rows(ns, jnp.where(odd, below, above), jnp.where(odd, above, below), coef)
+    rows = own.shape[0]
+    end = e1.shape[0]
+    pick = lambda even, other, at: jnp.where(odd, other[at : at + 1, :], even[at : at + 1, :])
+    near = jnp.concatenate([pick(e2, e1, end - 1), pick(e1, e2, 0)], axis=0)
+    far = jnp.concatenate([pick(e2, e1, end - 2), pick(e1, e2, 1)], axis=0)
+    c0, cu, m = coef[0, :1], coef[1, :1], coef[2, :1]
+    q = jnp.concatenate([cu, m], axis=0)
+    edge = (2.0 * q * c0) * near + (2.0 * q * m) * sides(near) + (q * q) * far
+    inside = (q * q) * near
+    f = own[...] + jnp.concatenate([edge[:1], inside, edge[1:]], axis=0)
     squashed = jnp.tanh(f)
     part = jnp.concatenate(rows_of([part01[...]], [part02[...]]), axis=0)
-    gain = jnp.concatenate(rows_of([gain1[:, 0, :]], [gain2[:, 0, :]]), axis=0)
-    return part + gain * squashed + f * wet[...], squashed
+    return part + gain0[...] * squashed + f * wet[...], squashed
 
 
 def hand_kernel(
-    groups, ns, e1, e2, coef, wet, part01, part02, gain1, gain2, flux, wide, pick, *refs
+    groups, own, e2, e1, coef, wet, part01, part02, gain0, flux, wide, pick, *refs
 ):
     surf, *outs, blk = refs
-    surf[...], _ = field0(ns, e2, e1, coef, wet, part01, part02, gain1, gain2)
+    surf[...], _ = field0(own, e2, e1, coef, wet, part01, part02, gain0)
     sea = is_sea(groups)
     contrib = products(
         jnp.where(sea, surf[...], flux[...]),
@@ -342,33 +374,44 @@
 
 
 def close_kernel(
-    groups, ns, e2, e1, coef, wet, part01, part02, gain1, gain2, flux, part1, part2, *refs
+    groups, own, e2, e1, coef, wet, part01, part02, gain0, flux, gain1, gain2, part1, part2, *refs
 ):
-    new_state, new_coupling, surf, squashed = refs
-    surf[...], squashed[...] = field0(ns, e2, e1, coef, wet, part01, part02, gain1, gain2)
-    new_coupling[0] = jnp.where(is_sea(groups), surf[...], flux[...])
+    new_state, new_coupling, surf, squashed, stage, handed, sems = refs
+    surf[...], squashed[...] = field0(own, e2, e1, coef, wet, part01, part02, gain0)
+    handed[0] = jnp.where(is_sea(groups), surf[...], flux[...])
+    copies = [pltpu.make_async_copy(handed, new_coupling, sems.at[0])]
+    copies[0].start()
     half, fields, width = gain1.shape
     top_field = lax.broadcasted_iota(jnp.int32, (SUBLANES, width), 0) == 0
     line1, line2 = halves_of([squashed[r : r + 1, :] for r in range(2 * half)])
     for h in range(0, fields, SUBLANES):
         some = slice(h, h + SUBLANES)
         for i in range(half):
-            inner = part1[some, i, :] + gain1[i, some] * line1[i]
-            outer = part2[some, i, :] + gain2[i, some] * line2[i]
+            inner = part1[i, some] + gain1[i, some] * line1[i]
+            outer = part2[i, some] + gain2[i, some] * line2[i]
             for r, done in zip((i, half + i), rows_of([inner], [outer])):
                 if h == 0:
                     done = jnp.where(top_field, surf[r : r + 1, :], done)
-                new_state[0, some, r, :] = done
-
-
-def call(kernel, name, outs, args, scratch=(), in_specs=None, flops=0):
+                stage[0, some, r, :] = done
+        window = pl.ds(h, SUBLANES)
+        copies.append(
+            pltpu.make_async_copy(
+                stage.at[:, window], new_state.at[:, window], sems.at[len(copies)]
+            )
+        )
+        copies[-1].start()
+    for copy in copies:
+        copy.wait()
+
+
+def call(kernel, name, outs, args, scratch=(), in_specs=None, out_specs=None, flops=0):
     moved = sum(a.size * a.dtype.itemsize for a in list(args) + list(outs))
     return pl.pallas_call(
         kernel,
         name=name,
         out_shape=outs,
         in_specs=in_specs or [VMEM] * len(args),
-        out_specs=[VMEM] * len(outs),
+        out_specs=out_specs or [VMEM] * len(outs),
         scratch_shapes=list(scratch),
         compiler_params=PARAMS,
         cost_estimate=pl.CostEstimate(flops=flops, bytes_accessed=moved, transcendentals=0),
@@ -379,7 +422,7 @@
     return call(
         functools.partial(fields_kernel, inner, late),
         "inner" if inner else "outer",
-        parts,
+        parts[:2] if inner else parts,
         (base, y, after, *kept, *rest),
         flops=0 if inner else 4_000_000_000,
     )
@@ -400,32 +443,41 @@
     halves = [shape((half, fields, width), F32)] * 2
     payloads = [shape((count, block), F32)] * MEMBERS
     blocks = pltpu.VMEM((count, block), F32)
-    args = (
-        state, coupling, land_mask, codes, mixing, courant, matrices, weights, sources, targets
-    )
-    x1, x2, surface, wet, handed, mask, codes, *raw = call(
+    line, pair = shape((rows, width), F32), shape((half, width), F32)
+    far = lambda args: [pltpu.with_memory_space_constraint(a, pltpu.HBM) for a in args]
+    like = lambda args: [shape(a.shape, a.dtype) for a in args]
+    room = lambda args: [pltpu.VMEM(a.shape, a.dtype) for a in args]
+    x1, x2, surface, pick, chosen, targets, handed, raw = call(
         functools.partial(load_kernel, groups),
         "load",
         [shape((fields - 1, half, width), F32)] * 2
-        + [shape((rows, width), F32)] * 2
-        + [shape(a.shape, a.dtype) for a in args[1:]],
-        [pltpu.with_memory_space_constraint(a, pltpu.HBM) for a in args],
-        [pltpu.VMEM(state.shape, F32), pltpu.SemaphoreType.DMA((len(args),))],
-        [pl.BlockSpec(memory_space=pltpu.HBM)] * len(args),
-    )
-    tables = [
-        shape((3, fields, 1), F32),
-        shape((branches * fields, 3 * fields), BF16),
-        shape((branches, fields, 1), F32),
-        shape((margins * band, block), F32),
-        shape((count, margins), BF16),
-    ]
-    coef, table, col0, wide, pick, *sent = call(
-        functools.partial(remap_kernel, groups),
+        + [line, shape((count, margins), BF16), shape((MEMBERS * count, 2 * margins), BF16)]
+        + like((targets, coupling, weights)),
+        far((state, sources, targets, coupling, weights)),
+        room((state, sources)) + [pltpu.SemaphoreType.DMA((5,))],
+        [HBM] * 5,
+    )
+    wide, *sent = call(
+        remap_kernel,
         "remap",
-        tables + payloads,
-        (handed, *raw),
+        [shape((margins * band, block), F32)] + payloads,
+        (handed, raw, pick, chosen),
         [blocks],
+    )
+    wide, pick, mask, codes, wet, coef, table, col0 = call(
+        functools.partial(sort_kernel, groups),
+        "sort",
+        [shape((band, margins, block), F32), shape((margins, count), BF16)]
+        + like((land_mask, codes))
+        + [
+            line,
+            shape((3, fields, 1), F32),
+            shape((branches * fields, 3 * fields), BF16),
+            shape((branches, fields, 1), F32),
+        ],
+        (targets, wide, pick, *far((land_mask, codes, mixing, courant, matrices))),
+        room((mixing, courant, matrices)) + [pltpu.SemaphoreType.DMA((5,))],
+        [VMEM] * 3 + [HBM] * 5,
     )
     for interval in range(INTERVALS):
         y1 = lax.ppermute(x1, "tile", inner_pairs(tiles))
@@ -435,7 +487,6 @@
             for member, value in enumerate(sent)
         ]
         late, last = interval > 0, interval == INTERVALS - 1
-        line, pair = shape((rows, width), F32), shape((half, width), F32)
         if late:
             base1, base2, squashed = call(
                 evolve_kernel,
@@ -444,42 +495,36 @@
                 (part1, part2, gain1, gain2, ns, e2, e1, coef),
             )
         else:
-            base1, base2, gain1, gain2 = call(
-                start_kernel, "start", halves * 2, (x1, x2, coef, col0, codes, wet)
-            )
-            wide, pick = call(
-                functools.partial(sort_kernel, groups),
-                "sort",
-                [shape((band, margins, block), F32), shape((margins, count), BF16)],
-                (raw[-1], wide, pick, base1),
+            base1, base2, gain1, gain2, gain0 = call(
+                start_kernel, "start", halves * 2 + [line], (x1, x2, coef, col0, codes, wet)
             )
         kept = (coef, table, codes, wet)
-        parts = [shape((fields + 1, half, width), F32), pair]
+        parts = [halves[0] if late else shape((fields + 1, half, width), F32), pair, line]
         run_fields = functools.partial(fields_half, late, parts, kept)
         ns, flux, *edges = call(
             functools.partial(surface_kernel, groups),
             "surface",
             [line] * 2 + ([pair] * 2 if last else []),
-            (*recs, surface, mask, pick),
+            (*(recs[1:] + recs[:1] if last else recs), surface, mask, pick),
             [blocks],
         )
         d1, d2 = edges if last else (ns, ns)
         e1 = lax.ppermute(d1, "tile", inner_pairs(tiles))
         e2 = lax.ppermute(d2, "tile", outer_pairs(tiles))
         if late:
-            part2, part02 = run_fields(False, base2, y2, ns, col0, squashed)
+            part2, part02, own = run_fields(False, base2, y2, ns, col0, squashed)
             part1, part01 = run_fields(True, base1, y1, part02, col0, squashed)
         else:
-            part2, part02 = run_fields(False, base2, y2, ns)
+            part2, part02, own = run_fields(False, base2, y2, ns)
             part1, part01 = run_fields(True, base1, y1, part02)
         x1, x2 = part1, part2
-        common = (ns, e2, e1, coef, wet, part01, part02, gain1, gain2, flux)
+        common = (own, e2, e1, coef, wet, part01, part02, gain0, flux)
         if not last:
             surface, *sent = call(
                 functools.partial(hand_kernel, groups),
                 "hand",
                 [line] + payloads,
-                (ns, e1, e2, *common[3:], wide, pick),
+                (*common, wide, pick),
                 [blocks],
                 flops=20_000_000_000,
             )
@@ -488,8 +533,14 @@
                 functools.partial(close_kernel, groups),
                 "close",
                 [shape(state.shape, F32), shape(coupling.shape, F32)],
-                (*common, part1, part2),
-                [pltpu.VMEM((rows, width), F32)] * 2,
+                (*common, gain1, gain2, part1, part2),
+                [pltpu.VMEM((rows, width), F32)] * 2
+                + [
+                    pltpu.VMEM(state.shape, F32),
+                    pltpu.VMEM(coupling.shape, F32),
+                    pltpu.SemaphoreType.DMA((1 + fields // SUBLANES,)),
+                ],
+                out_specs=[HBM] * 2,
             )
     return new_state, new_coupling
 

time: 30.9 us -> 30.5 us (0.987)
    ppermute x2, waiting for transfers between devices: 1.3 us -> 1.68 us  [on_device(): y2 = lax.ppermute(x2, 'tile', outer_pairs(tiles))]
    ppermute x2, waiting for transfers between devices: 1.21 us -> 0.89 us  [on_device(): e2 = lax.ppermute(d2, 'tile', outer_pairs(tiles))]
  transfers between devices with their start and end apart: 14 -> 14, of which waited for: 5 -> 4; matrix products, arithmetic and copies ran while one was open for 0% -> 0% of each run, Pallas kernels for 25% -> 26%
where the time goes in v7:
time: 30.5 us; the launch traced here: 30.3 us
  starting transfers between devices  15.6 us (51%)
  Pallas kernels  10.5 us (34%)
  waiting for transfers between devices  3.47 us (11%)
  between operations  0.76 us (2%)
    pallas_call x13, Pallas kernels, call(): pl.pallas_call(kernel, name=name, out_shape=outs, in_specs=in_specs or [V...  10.5 us
    ppermute x6, starting transfers between devices, on_device(): lax.ppermute(value, ('comp', 'tile'), partner_pairs(groups, tiles, member))  8.21 us
    ppermute x2, starting transfers between devices, on_device(): y2 = lax.ppermute(x2, 'tile', outer_pairs(tiles))  5.74 us
    ppermute x2, waiting for transfers between devices, on_device(): y2 = lax.ppermute(x2, 'tile', outer_pairs(tiles))  1.68 us
    ppermute x2, starting transfers between devices, on_device(): e2 = lax.ppermute(d2, 'tile', outer_pairs(tiles))  1.31 us
    ppermute x2, waiting for transfers between devices, on_device(): e2 = lax.ppermute(d2, 'tile', outer_pairs(tiles))  0.89 us
    ppermute x6, waiting for transfers between devices, on_device(): lax.ppermute(value, ('comp', 'tile'), partner_pairs(groups, tiles, member))  0.89 us
  transfers between devices with their start and end apart: 14, of which 4 were waited for; matrix products, arithmetic and copies ran while one was open for 0% of the time, Pallas kernels for 26%

profile of v7, /device:TPU:0, one launch (start us, length us, event | category | flops | bytes accessed | tf_op | source)
XLA Modules:
  0.0 30.3 jit_solution(6134977171937583938)
XLA Ops:
  0.6 1.4 %load.1 = (f32[15,2,3072]{2,1,0:T(2,128)S(1)}, f32[15,2,3072]{2,1,0:T(2,128)S(1)}, f32[4,3072]{1,0:T(4,128)S(1)}, bf16[96,288]{1,0:T(8,128)(2,1)S(1)}, bf16[288,...) custom-call(f32[1,16,4,3072]{3,2,1,0:T(4,128)} %state.1, ...), custom_call_target="tpu_custom_call" | custom-call | bytes 3241344 | tf_op jit(solution)/shard_map/load/pallas_call | solution.py:409
  2.0 3.4 %collective-permute-start.1 = (f32[15,2,3072]{2,1,0:T(2,128)S(1)}, f32[15,2,3072]{2,1,0:T(2,128)S(1)}, u32[]{:S(2)}, u32[]{:S(2)}) collective-permute-start(f32[15,2,3072]{2,1,0:T(2,128)S(1)} %get-tuple-element.51.x2), channel_id=1, source_target_pairs={{0,7},{1,2},{2,1},{3,4},{4,3},{5,6},{6,5},{7,0},{8,15},{9,10},{10,... | collective-permute-start | bytes 1105928 | tf_op jit(solution)/shard_map/ppermute | solution.py:484
  5.4 0.8 %remap.1 = (f32[2304,128]{1,0:T(8,128)S(1)}, f32[96,128]{1,0:T(8,128)S(1)}, f32[96,128]{1,0:T(8,128)S(1)}, f32[96,128]{1,0:T(8,128)S(1)}) custom-call(f32[1,4,3072]{2,1,0:T(4,128)S(1)} %get-tuple-element.53.coupling, bf16[1,288,8,128]{3,2,1,0:T(8,128)(2,1)S(1)} %get-tuple-element.54.weights, bf16[96,288]{1,0:T(8,128)(2,1)S(1)} %get-tuple-element.55.pick, ...), custom_call_target="tpu_custom_call" | custom-call | bytes 2353152 | tf_op jit(solution)/shard_map/remap/pallas_call | solution.py:409
  6.2 3.7 %collective-permute-start.2 = (f32[96,128]{1,0:T(8,128)S(1)}, f32[96,128]{1,0:T(8,128)S(1)}, u32[]{:S(2)}, u32[]{:S(2)}) collective-permute-start(f32[96,128]{1,0:T(8,128)S(1)} %get-tuple-element.64), channel_id=1, source_target_pairs={{0,24},{1,25},{2,26},{3,27},{4,28},{5,29},{6,30},{7,31},{8,9},{9,8... | collective-permute-start | bytes 147464 | tf_op jit(solution)/shard_map/ppermute | solution.py:486
  9.9 0.0 collective-permute-start.3
  9.9 0.5 %collective-permute-start.4 = (f32[96,128]{1,0:T(8,128)S(1)}, f32[96,128]{1,0:T(8,128)S(1)}, u32[]{:S(2)}, u32[]{:S(2)}) collective-permute-start(f32[96,128]{1,0:T(8,128)S(1)} %get-tuple-element.66), channel_id=1, source_target_pairs={{0,1},{1,0},{2,3},{3,2},{4,5},{5,4},{6,7},{7,6},{8,9},{9,8},{10,11... | collective-permute-start | bytes 147464 | tf_op jit(solution)/shard_map/ppermute | solution.py:486
  10.4 1.0 %sort.1 = (f32[8,288,128]{2,1,0:T(8,128)S(1)}, bf16[288,96]{1,0:T(8,128)(2,1)S(1)}, s32[1,4,3072]{2,1,0:T(4,128)S(1)}, s32[1,4,3072]{2,1,0:T(4,128)S(1)}, f32[4,...) custom-call(s32[1,288]{1,0:T(1,128)S(1)} %get-tuple-element.52.targets, ...), custom_call_target="tpu_custom_call" | custom-call | bytes 2727616 | tf_op jit(solution)/shard_map/sort/pallas_call | solution.py:409
  11.4 1.4 %start.1 = (f32[2,16,3072]{2,1,0:T(8,128)S(1)}, f32[2,16,3072]{2,1,0:T(8,128)S(1)}, f32[2,16,3072]{2,1,0:T(8,128)S(1)}, f32[2,16,3072]{2,1,0:T(8,128)S(1)}, f32[4,3072]{1,0:T(4,128)S(1)}) custom-call(f32[15,2,3072]{2,1,0:T(2,128)S(1)} %get-tuple-element.50.x1, f32[15,2,3072]{2,1,0:T(2,128)S(1)} %get-tuple-element.51.x2, ...), custom_call_target="tpu_custom_call" | custom-call | bytes 2458048 | tf_op jit(solution)/shard_map/start/pallas_call | solution.py:409
  12.8 0.0 collective-permute-done.4.refs_2_
  12.9 0.8 %collective-permute-start.5 = (f32[4,3072]{1,0:T(4,128)S(1)}, f32[4,3072]{1,0:T(4,128)S(1)}, u32[]{:S(2)}, u32[]{:S(2)}) collective-permute-start(f32[4,3072]{1,0:T(4,128)S(1)} %get-tuple-element.70.after.ns), channel_id=1, source_target_pairs={{0,7},{1,2},{2,1},{3,4},{4,3},{5,6},{6,5},{7,0},{8,15},{9,10},{10,... | collective-permute-start | bytes 147464 | tf_op jit(solution)/shard_map/ppermute | solution.py:513
  13.6 0.4 %collective-permute-start.6 = (f32[4,3072]{1,0:T(4,128)S(1)}, f32[4,3072]{1,0:T(4,128)S(1)}, u32[]{:S(2)}, u32[]{:S(2)}) collective-permute-start(f32[4,3072]{1,0:T(4,128)S(1)} %get-tuple-element.70.after.ns), channel_id=1, source_target_pairs={{0,1},{1,0},{2,3},{3,2},{4,5},{5,4},{6,7},{7,6},{8,9},{9,8},{10,11... | collective-permute-start | bytes 147464 | tf_op jit(solution)/shard_map/ppermute | solution.py:512
  14.0 0.0 collective-permute-done.1.y
  14.0 0.6 %outer.2 = (f32[17,2,3072]{2,1,0:T(2,128)S(1)}, f32[2,3072]{1,0:T(2,128)S(1)}, f32[4,3072]{1,0:T(4,128)S(1)}) custom-call(f32[2,16,3072]{2,1,0:T(8,128)S(1)} %get-tuple-element.63.base, f32[15,2,3072]{2,1,0:T(2,128)S(1)} %collective-permute-done.1.y, f32[4,3072]{1,0:T(4,128)S(1)} %get-tuple-element.70.after.ns, f32[3,16,1]{2,1,0:T(8,128)S(1)} %get-tuple-element.58.coef, ...), custom_call_target="tpu_custom_call" | custom-call | flops 4000000000 | bytes 1407168 | tf_op jit(solution)/shard_map/outer/pallas_call | solution.py:409
  14.6 2.3 %collective-permute-start.7 = (f32[17,2,3072]{2,1,0:T(2,128)S(1)}, f32[17,2,3072]{2,1,0:T(2,128)S(1)}, u32[]{:S(2)}, u32[]{:S(2)}) collective-permute-start(f32[17,2,3072]{2,1,0:T(2,128)S(1)} %get-tuple-element.74.part2), channel_id=1, source_target_pairs={{0,7},{1,2},{2,1},{3,4},{4,3},{5,6},{6,5},{7,0},{8,15},{9,10},{10,... | collective-permute-start | bytes 1253384 | tf_op jit(solution)/shard_map/ppermute | solution.py:484
  16.9 0.0 collective-permute-done.y
  16.9 0.5 %inner.2 = (f32[17,2,3072]{2,1,0:T(2,128)S(1)}, f32[2,3072]{1,0:T(2,128)S(1)}) custom-call(f32[2,16,3072]{2,1,0:T(8,128)S(1)} %get-tuple-element.62.base, f32[15,2,3072]{2,1,0:T(2,128)S(1)} %collective-permute-done.y, f32[2,3072]{1,0:T(2,128)S(1)} %get-tuple-element.72.after.part02, f32[3,16,1]{2,1,0:T(8,128)S(1)} %get-tuple-element.58.coef, ...), custom_call_target="tpu_custom_call" | custom-call | bytes 1333440 | tf_op jit(solution)/shard_map/inner/pallas_call | solution.py:409
  17.4 0.2 collective-permute-done.5.e2
  17.6 0.7 %hand.1 = (f32[4,3072]{1,0:T(4,128)S(1)}, f32[96,128]{1,0:T(8,128)S(1)}, f32[96,128]{1,0:T(8,128)S(1)}, f32[96,128]{1,0:T(8,128)S(1)}) custom-call(f32[4,3072]{1,0:T(4,128)S(1)} %get-tuple-element.78.own, f32[4,3072]{1,0:T(4,128)S(1)} %collective-permute-done.5.e2, f32[4,3072]{1,0:T(4,128)S(1)} %collective-permute-done.6.e1, ...), custom_call_target="tpu_custom_call" | custom-call | flops 20000000000 | bytes 1775808 | tf_op jit(solution)/shard_map/hand/pallas_call | solution.py:409
  18.3 3.5 %collective-permute-start.10 = (f32[96,128]{1,0:T(8,128)S(1)}, f32[96,128]{1,0:T(8,128)S(1)}, u32[]{:S(2)}, u32[]{:S(2)}) collective-permute-start(f32[96,128]{1,0:T(8,128)S(1)} %get-tuple-element.85), channel_id=1, source_target_pairs={{0,24},{1,25},{2,26},{3,27},{4,28},{5,29},{6,30},{7,31},{8,9},{9,8... | collective-permute-start | bytes 147464 | tf_op jit(solution)/shard_map/ppermute | solution.py:486
  21.8 0.0 collective-permute-start.8
  21.8 0.5 %collective-permute-start.9 = (f32[96,128]{1,0:T(8,128)S(1)}, f32[96,128]{1,0:T(8,128)S(1)}, u32[]{:S(2)}, u32[]{:S(2)}) collective-permute-start(f32[96,128]{1,0:T(8,128)S(1)} %get-tuple-element.84), channel_id=1, source_target_pairs={{0,1},{1,0},{2,3},{3,2},{4,5},{5,4},{6,7},{7,6},{8,9},{9,8},{10,11... | collective-permute-start | bytes 147464 | tf_op jit(solution)/shard_map/ppermute | solution.py:486
  22.3 0.0 collective-permute-start.13
  22.3 1.5 %evolve.1 = (f32[2,16,3072]{2,1,0:T(8,128)S(1)}, f32[2,16,3072]{2,1,0:T(8,128)S(1)}, f32[8,3072]{1,0:T(8,128)S(1)}) custom-call(f32[17,2,3072]{2,1,0:T(2,128)S(1)} %get-tuple-element.73.part1, f32[17,2,3072]{2,1,0:T(2,128)S(1)} %get-tuple-element.74.part2, f32[2,16,3072]{2,1,0:T(8,128)S(1)} %get-tuple-element.75.gain1, ...), custom_call_target="tpu_custom_call" | custom-call | bytes 2654400 | tf_op jit(solution)/shard_map/evolve/pallas_call | solution.py:409
  23.8 0.9 %collective-permute-done.10.refs_2_ = f32[96,128]{1,0:T(8,128)S(1)} collective-permute-done((f32[96,128]{1,0:T(8,128)S(1)}, f32[96,128]{1,0:T(8,128)S(1)}, u32[]{:S(2)}, u32[]{:S(2)}) %collective-permute-start.10) | collective-permute-done | bytes 49184 | tf_op jit(solution)/shard_map/ppermute | solution.py:486
  24.7 0.0 collective-permute-done.8.refs_0_
  24.7 0.1 surface.3
  24.8 0.6 %collective-permute-start.11 = (f32[2,3072]{1,0:T(2,128)S(1)}, f32[2,3072]{1,0:T(2,128)S(1)}, u32[]{:S(2)}, u32[]{:S(2)}) collective-permute-start(f32[2,3072]{1,0:T(2,128)S(1)} %get-tuple-element.90), channel_id=1, source_target_pairs={{0,7},{1,2},{2,1},{3,4},{4,3},{5,6},{6,5},{7,0},{8,15},{9,10},{10,... | collective-permute-start | bytes 73736 | tf_op jit(solution)/shard_map/ppermute | solution.py:513
  25.3 1.7 %collective-permute-done.7.y = f32[17,2,3072]{2,1,0:T(2,128)S(1)} collective-permute-done((f32[17,2,3072]{2,1,0:T(2,128)S(1)}, f32[17,2,3072]{2,1,0:T(2,128)S(1)}, u32[]{:S(2)}, u32[]{:S(2)}) %collective-permute-start.7) | collective-permute-done | bytes 417824 | tf_op jit(solution)/shard_map/ppermute | solution.py:484
  27.0 0.7 %outer.3 = (f32[2,16,3072]{2,1,0:T(8,128)S(1)}, f32[2,3072]{1,0:T(2,128)S(1)}, f32[4,3072]{1,0:T(4,128)S(1)}) custom-call(f32[2,16,3072]{2,1,0:T(8,128)S(1)} %get-tuple-element.77.base, f32[17,2,3072]{2,1,0:T(2,128)S(1)} %collective-permute-done.7.y, f32[4,3072]{1,0:T(4,128)S(1)} %get-tuple-element.87.after, f32[3,16,1]{2,1,0:T(8,128)S(1)} %get-tuple-element.58.coef, ...), custom_call_target="tpu_custom_call" | custom-call | flops 4000000000 | bytes 1530304 | tf_op jit(solution)/shard_map/outer/pallas_call | solution.py:409
  27.7 0.6 %inner.3 = (f32[2,16,3072]{2,1,0:T(8,128)S(1)}, f32[2,3072]{1,0:T(2,128)S(1)}) custom-call(f32[2,16,3072]{2,1,0:T(8,128)S(1)} %get-tuple-element.92.base, f32[17,2,3072]{2,1,0:T(2,128)S(1)} %collective-permute-done.13.y, f32[2,3072]{1,0:T(2,128)S(1)} %get-tuple-element.93.after.part02, f32[3,16,1]{2,1,0:T(8,128)S(1)} %get-tuple-element.58.coef, ...), custom_call_target="tpu_custom_call" | custom-call | bytes 1456576 | tf_op jit(solution)/shard_map/inner/pallas_call | solution.py:409
  28.3 0.7 %collective-permute-done.11.e2 = f32[2,3072]{1,0:T(2,128)S(1)} collective-permute-done((f32[2,3072]{1,0:T(2,128)S(1)}, f32[2,3072]{1,0:T(2,128)S(1)}, u32[]{:S(2)}, u32[]{:S(2)}) %collective-permute-start.11) | collective-permute-done | bytes 24608 | tf_op jit(solution)/shard_map/ppermute | solution.py:513
  29.1 1.3 %close.1 = (f32[1,16,4,3072]{3,2,1,0:T(4,128)}, f32[1,4,3072]{2,1,0:T(4,128)}) custom-call(f32[4,3072]{1,0:T(4,128)S(1)} %get-tuple-element.89.own, f32[2,3072]{1,0:T(2,128)S(1)} %collective-permute-done.11.e2, f32[2,3072]{1,0:T(2,128)S(1)} %collective-permute-done.12.e1, f32[3,16,1]{2,1,0:T(8,128)S(1)} %get-tuple-element.58.coef, ...), custom_call_target="tpu_custom_call" | custom-call | bytes 2703552 | tf_op jit(solution)/shard_map/close/pallas_call | solution.py:409
  (9 shorter events, 0.1 us)
Async XLA Ops:
  2.0 11.9 %collective-permute-start.1 = (f32[15,2,3072]{2,1,0:T(2,128)S(1)}, f32[15,2,3072]{2,1,0:T(2,128)S(1)}, u32[]{:S(2)}, u32[]{:S(2)}) collective-permute-start(f32[15,2,3072]{2,1,0:T(2,128)S(1)} %get-tuple-element.51.x2), channel_id=1, source_target_pairs={{0,7},{1,2},{2,1},{3,4},{4,3},{5,6},{6,5},{7,0},{8,15},{9,10},{10,... | collective-permute-start | bytes 1105928 | tf_op jit(solution)/shard_map/ppermute | solution.py:484
  6.2 6.6 %collective-permute-start.2 = (f32[96,128]{1,0:T(8,128)S(1)}, f32[96,128]{1,0:T(8,128)S(1)}, u32[]{:S(2)}, u32[]{:S(2)}) collective-permute-start(f32[96,128]{1,0:T(8,128)S(1)} %get-tuple-element.64), channel_id=1, source_target_pairs={{0,24},{1,25},{2,26},{3,27},{4,28},{5,29},{6,30},{7,31},{8,9},{9,8... | collective-permute-start | bytes 147464 | tf_op jit(solution)/shard_map/ppermute | solution.py:486
  9.9 2.9 %collective-permute-start.3 = (f32[96,128]{1,0:T(8,128)S(1)}, f32[96,128]{1,0:T(8,128)S(1)}, u32[]{:S(2)}, u32[]{:S(2)}) collective-permute-start(f32[96,128]{1,0:T(8,128)S(1)} %get-tuple-element.65), channel_id=1, source_target_pairs={{0,1},{1,0},{2,3},{3,2},{4,5},{5,4},{6,7},{7,6},{8,24},{9,25},{10,... | collective-permute-start | bytes 147464 | tf_op jit(solution)/shard_map/ppermute | solution.py:486
  9.9 2.9 %collective-permute-start.4 = (f32[96,128]{1,0:T(8,128)S(1)}, f32[96,128]{1,0:T(8,128)S(1)}, u32[]{:S(2)}, u32[]{:S(2)}) collective-permute-start(f32[96,128]{1,0:T(8,128)S(1)} %get-tuple-element.66), channel_id=1, source_target_pairs={{0,1},{1,0},{2,3},{3,2},{4,5},{5,4},{6,7},{7,6},{8,9},{9,8},{10,11... | collective-permute-start | bytes 147464 | tf_op jit(solution)/shard_map/ppermute | solution.py:486
  10.4 6.5 %collective-permute-start = (f32[15,2,3072]{2,1,0:T(2,128)S(1)}, f32[15,2,3072]{2,1,0:T(2,128)S(1)}, u32[]{:S(2)}, u32[]{:S(2)}) collective-permute-start(f32[15,2,3072]{2,1,0:T(2,128)S(1)} %get-tuple-element.50.x1), channel_id=1, source_target_pairs={{0,1},{1,0},{2,3},{3,2},{4,5},{5,4},{6,7},{7,6},{8,9},{9,8},{10,11... | collective-permute-start | bytes 1105928 | tf_op jit(solution)/shard_map/ppermute | solution.py:483
  12.9 4.7 %collective-permute-start.5 = (f32[4,3072]{1,0:T(4,128)S(1)}, f32[4,3072]{1,0:T(4,128)S(1)}, u32[]{:S(2)}, u32[]{:S(2)}) collective-permute-start(f32[4,3072]{1,0:T(4,128)S(1)} %get-tuple-element.70.after.ns), channel_id=1, source_target_pairs={{0,7},{1,2},{2,1},{3,4},{4,3},{5,6},{6,5},{7,0},{8,15},{9,10},{10,... | collective-permute-start | bytes 147464 | tf_op jit(solution)/shard_map/ppermute | solution.py:513
  13.6 4.0 %collective-permute-start.6 = (f32[4,3072]{1,0:T(4,128)S(1)}, f32[4,3072]{1,0:T(4,128)S(1)}, u32[]{:S(2)}, u32[]{:S(2)}) collective-permute-start(f32[4,3072]{1,0:T(4,128)S(1)} %get-tuple-element.70.after.ns), channel_id=1, source_target_pairs={{0,1},{1,0},{2,3},{3,2},{4,5},{5,4},{6,7},{7,6},{8,9},{9,8},{10,11... | collective-permute-start | bytes 147464 | tf_op jit(solution)/shard_map/ppermute | solution.py:512
  14.6 12.5 %collective-permute-start.7 = (f32[17,2,3072]{2,1,0:T(2,128)S(1)}, f32[17,2,3072]{2,1,0:T(2,128)S(1)}, u32[]{:S(2)}, u32[]{:S(2)}) collective-permute-start(f32[17,2,3072]{2,1,0:T(2,128)S(1)} %get-tuple-element.74.part2), channel_id=1, source_target_pairs={{0,7},{1,2},{2,1},{3,4},{4,3},{5,6},{6,5},{7,0},{8,15},{9,10},{10,... | collective-permute-start | bytes 1253384 | tf_op jit(solution)/shard_map/ppermute | solution.py:484
  18.3 6.4 %collective-permute-start.10 = (f32[96,128]{1,0:T(8,128)S(1)}, f32[96,128]{1,0:T(8,128)S(1)}, u32[]{:S(2)}, u32[]{:S(2)}) collective-permute-start(f32[96,128]{1,0:T(8,128)S(1)} %get-tuple-element.85), channel_id=1, source_target_pairs={{0,24},{1,25},{2,26},{3,27},{4,28},{5,29},{6,30},{7,31},{8,9},{9,8... | collective-permute-start | bytes 147464 | tf_op jit(solution)/shard_map/ppermute | solution.py:486
  21.8 2.9 %collective-permute-start.8 = (f32[96,128]{1,0:T(8,128)S(1)}, f32[96,128]{1,0:T(8,128)S(1)}, u32[]{:S(2)}, u32[]{:S(2)}) collective-permute-start(f32[96,128]{1,0:T(8,128)S(1)} %get-tuple-element.83), channel_id=1, source_target_pairs={{0,1},{1,0},{2,3},{3,2},{4,5},{5,4},{6,7},{7,6},{8,24},{9,25},{10,... | collective-permute-start | bytes 147464 | tf_op jit(solution)/shard_map/ppermute | solution.py:486
  21.8 2.9 %collective-permute-start.9 = (f32[96,128]{1,0:T(8,128)S(1)}, f32[96,128]{1,0:T(8,128)S(1)}, u32[]{:S(2)}, u32[]{:S(2)}) collective-permute-start(f32[96,128]{1,0:T(8,128)S(1)} %get-tuple-element.84), channel_id=1, source_target_pairs={{0,1},{1,0},{2,3},{3,2},{4,5},{5,4},{6,7},{7,6},{8,9},{9,8},{10,11... | collective-permute-start | bytes 147464 | tf_op jit(solution)/shard_map/ppermute | solution.py:486
  22.3 5.4 %collective-permute-start.13 = (f32[17,2,3072]{2,1,0:T(2,128)S(1)}, f32[17,2,3072]{2,1,0:T(2,128)S(1)}, u32[]{:S(2)}, u32[]{:S(2)}) collective-permute-start(f32[17,2,3072]{2,1,0:T(2,128)S(1)} %get-tuple-element.73.part1), channel_id=1, source_target_pairs={{0,1},{1,0},{2,3},{3,2},{4,5},{5,4},{6,7},{7,6},{8,9},{9,8},{10,11... | collective-permute-start | bytes 1253384 | tf_op jit(solution)/shard_map/ppermute | solution.py:483
  24.8 4.3 %collective-permute-start.11 = (f32[2,3072]{1,0:T(2,128)S(1)}, f32[2,3072]{1,0:T(2,128)S(1)}, u32[]{:S(2)}, u32[]{:S(2)}) collective-permute-start(f32[2,3072]{1,0:T(2,128)S(1)} %get-tuple-element.90), channel_id=1, source_target_pairs={{0,7},{1,2},{2,1},{3,4},{4,3},{5,6},{6,5},{7,0},{8,15},{9,10},{10,... | collective-permute-start | bytes 73736 | tf_op jit(solution)/shard_map/ppermute | solution.py:513
  25.3 3.7 %collective-permute-start.12 = (f32[2,3072]{1,0:T(2,128)S(1)}, f32[2,3072]{1,0:T(2,128)S(1)}, u32[]{:S(2)}, u32[]{:S(2)}) collective-permute-start(f32[2,3072]{1,0:T(2,128)S(1)} %get-tuple-element.91), channel_id=1, source_target_pairs={{0,1},{1,0},{2,3},{3,2},{4,5},{5,4},{6,7},{7,6},{8,9},{9,8},{10,11... | collective-permute-start | bytes 73736 | tf_op jit(solution)/shard_map/ppermute | solution.py:512

commit v8 on v7

--- a/solution.py
+++ b/solution.py
@@ -59,10 +59,13 @@
     per_row = width // block
     for c in range(per_row):
         blk_ref[pl.ds(c, rows, stride=per_row), :] = handed[:, c * block : (c + 1) * block]
-    picked = picked_by(blk_ref[...].astype(BF16))
-    total = weight(0) * picked
+    blocks = blk_ref[...].astype(BF16)
+    even = blocks.astype(F32)
+    turned = [blocks] + [pltpu.roll(even, block - j, 1).astype(BF16) for j in range(1, BAND)]
+    picked = picked_by(jnp.concatenate(turned, axis=1))
+    total = weight(0) * picked[:, :block]
     for j in range(1, BAND):
-        total = total + weight(j) * pltpu.roll(picked, block - j, 1)
+        total = total + weight(j) * picked[:, j * block : (j + 1) * block]
     return total
 
 

time: 30.5 us -> 30.4 us (level)
  transfers between devices with their start and end apart: 14 -> 14, of which waited for: 4 -> 4; matrix products, arithmetic and copies ran while one was open for 0% -> 0% of each run, Pallas kernels for 26% -> 25%
where the time goes in v8:
time: 30.4 us; the launch traced here: 30.2 us
  starting transfers between devices  15.8 us (52%)
  Pallas kernels  10.3 us (34%)
  waiting for transfers between devices  3.33 us (11%)
  between operations  0.76 us (2%)
    pallas_call x13, Pallas kernels, call(): pl.pallas_call(kernel, name=name, out_shape=outs, in_specs=in_specs or [V...  10.3 us
    ppermute x6, starting transfers between devices, on_device(): lax.ppermute(value, ('comp', 'tile'), partner_pairs(groups, tiles, member))  8.28 us
    ppermute x2, starting transfers between devices, on_device(): y2 = lax.ppermute(x2, 'tile', outer_pairs(tiles))  5.8 us
    ppermute x2, waiting for transfers between devices, on_device(): y2 = lax.ppermute(x2, 'tile', outer_pairs(tiles))  1.66 us
    ppermute x2, starting transfers between devices, on_device(): e2 = lax.ppermute(d2, 'tile', outer_pairs(tiles))  1.39 us
    ppermute x2, waiting for transfers between devices, on_device(): e2 = lax.ppermute(d2, 'tile', outer_pairs(tiles))  0.85 us
    ppermute x6, waiting for transfers between devices, on_device(): lax.ppermute(value, ('comp', 'tile'), partner_pairs(groups, tiles, member))  0.81 us
  transfers between devices with their start and end apart: 14, of which 4 were waited for; matrix products, arithmetic and copies ran while one was open for 0% of the time, Pallas kernels for 25%

profile of v8, /device:TPU:0, one launch (start us, length us, event | category | flops | bytes accessed | tf_op | source)
XLA Modules:
  0.0 30.2 jit_solution(11351276121510893592)
XLA Ops:
  0.6 1.4 %load.1 = (f32[15,2,3072]{2,1,0:T(2,128)S(1)}, f32[15,2,3072]{2,1,0:T(2,128)S(1)}, f32[4,3072]{1,0:T(4,128)S(1)}, bf16[96,288]{1,0:T(8,128)(2,1)S(1)}, bf16[288,...) custom-call(f32[1,16,4,3072]{3,2,1,0:T(4,128)} %state.1, ...), custom_call_target="tpu_custom_call" | custom-call | bytes 3241344 | tf_op jit(solution)/shard_map/load/pallas_call | solution.py:412
  2.0 3.4 %collective-permute-start.1 = (f32[15,2,3072]{2,1,0:T(2,128)S(1)}, f32[15,2,3072]{2,1,0:T(2,128)S(1)}, u32[]{:S(2)}, u32[]{:S(2)}) collective-permute-start(f32[15,2,3072]{2,1,0:T(2,128)S(1)} %get-tuple-element.51.x2), channel_id=1, source_target_pairs={{0,7},{1,2},{2,1},{3,4},{4,3},{5,6},{6,5},{7,0},{8,15},{9,10},{10,... | collective-permute-start | bytes 1105928 | tf_op jit(solution)/shard_map/ppermute | solution.py:487
  5.4 0.7 %remap.1 = (f32[2304,128]{1,0:T(8,128)S(1)}, f32[96,128]{1,0:T(8,128)S(1)}, f32[96,128]{1,0:T(8,128)S(1)}, f32[96,128]{1,0:T(8,128)S(1)}) custom-call(f32[1,4,3072]{2,1,0:T(4,128)S(1)} %get-tuple-element.53.coupling, bf16[1,288,8,128]{3,2,1,0:T(8,128)(2,1)S(1)} %get-tuple-element.54.weights, bf16[96,288]{1,0:T(8,128)(2,1)S(1)} %get-tuple-element.55.pick, ...), custom_call_target="tpu_custom_call" | custom-call | bytes 2353152 | tf_op jit(solution)/shard_map/remap/pallas_call | solution.py:412
  6.1 3.7 %collective-permute-start.2 = (f32[96,128]{1,0:T(8,128)S(1)}, f32[96,128]{1,0:T(8,128)S(1)}, u32[]{:S(2)}, u32[]{:S(2)}) collective-permute-start(f32[96,128]{1,0:T(8,128)S(1)} %get-tuple-element.64), channel_id=1, source_target_pairs={{0,24},{1,25},{2,26},{3,27},{4,28},{5,29},{6,30},{7,31},{8,9},{9,8... | collective-permute-start | bytes 147464 | tf_op jit(solution)/shard_map/ppermute | solution.py:489
  9.8 0.5 %collective-permute-start.4 = (f32[96,128]{1,0:T(8,128)S(1)}, f32[96,128]{1,0:T(8,128)S(1)}, u32[]{:S(2)}, u32[]{:S(2)}) collective-permute-start(f32[96,128]{1,0:T(8,128)S(1)} %get-tuple-element.66), channel_id=1, source_target_pairs={{0,1},{1,0},{2,3},{3,2},{4,5},{5,4},{6,7},{7,6},{8,9},{9,8},{10,11... | collective-permute-start | bytes 147464 | tf_op jit(solution)/shard_map/ppermute | solution.py:489
  10.3 0.0 collective-permute-start
  10.3 1.0 %sort.1 = (f32[8,288,128]{2,1,0:T(8,128)S(1)}, bf16[288,96]{1,0:T(8,128)(2,1)S(1)}, s32[1,4,3072]{2,1,0:T(4,128)S(1)}, s32[1,4,3072]{2,1,0:T(4,128)S(1)}, f32[4,...) custom-call(s32[1,288]{1,0:T(1,128)S(1)} %get-tuple-element.52.targets, ...), custom_call_target="tpu_custom_call" | custom-call | bytes 2727616 | tf_op jit(solution)/shard_map/sort/pallas_call | solution.py:412
  11.3 1.4 %start.1 = (f32[2,16,3072]{2,1,0:T(8,128)S(1)}, f32[2,16,3072]{2,1,0:T(8,128)S(1)}, f32[2,16,3072]{2,1,0:T(8,128)S(1)}, f32[2,16,3072]{2,1,0:T(8,128)S(1)}, f32[4,3072]{1,0:T(4,128)S(1)}) custom-call(f32[15,2,3072]{2,1,0:T(2,128)S(1)} %get-tuple-element.50.x1, f32[15,2,3072]{2,1,0:T(2,128)S(1)} %get-tuple-element.51.x2, ...), custom_call_target="tpu_custom_call" | custom-call | bytes 2458048 | tf_op jit(solution)/shard_map/start/pallas_call | solution.py:412
  12.7 0.0 collective-permute-done.2.refs_0_
  12.7 0.0 collective-permute-done.3.refs_1_
  12.8 0.8 %collective-permute-start.5 = (f32[4,3072]{1,0:T(4,128)S(1)}, f32[4,3072]{1,0:T(4,128)S(1)}, u32[]{:S(2)}, u32[]{:S(2)}) collective-permute-start(f32[4,3072]{1,0:T(4,128)S(1)} %get-tuple-element.70.after.ns), channel_id=1, source_target_pairs={{0,7},{1,2},{2,1},{3,4},{4,3},{5,6},{6,5},{7,0},{8,15},{9,10},{10,... | collective-permute-start | bytes 147464 | tf_op jit(solution)/shard_map/ppermute | solution.py:516
  13.5 0.4 %collective-permute-start.6 = (f32[4,3072]{1,0:T(4,128)S(1)}, f32[4,3072]{1,0:T(4,128)S(1)}, u32[]{:S(2)}, u32[]{:S(2)}) collective-permute-start(f32[4,3072]{1,0:T(4,128)S(1)} %get-tuple-element.70.after.ns), channel_id=1, source_target_pairs={{0,1},{1,0},{2,3},{3,2},{4,5},{5,4},{6,7},{7,6},{8,9},{9,8},{10,11... | collective-permute-start | bytes 147464 | tf_op jit(solution)/shard_map/ppermute | solution.py:515
  13.9 0.6 %outer.2 = (f32[17,2,3072]{2,1,0:T(2,128)S(1)}, f32[2,3072]{1,0:T(2,128)S(1)}, f32[4,3072]{1,0:T(4,128)S(1)}) custom-call(f32[2,16,3072]{2,1,0:T(8,128)S(1)} %get-tuple-element.63.base, f32[15,2,3072]{2,1,0:T(2,128)S(1)} %collective-permute-done.1.y, f32[4,3072]{1,0:T(4,128)S(1)} %get-tuple-element.70.after.ns, f32[3,16,1]{2,1,0:T(8,128)S(1)} %get-tuple-element.58.coef, ...), custom_call_target="tpu_custom_call" | custom-call | flops 4000000000 | bytes 1407168 | tf_op jit(solution)/shard_map/outer/pallas_call | solution.py:412
  14.5 2.4 %collective-permute-start.7 = (f32[17,2,3072]{2,1,0:T(2,128)S(1)}, f32[17,2,3072]{2,1,0:T(2,128)S(1)}, u32[]{:S(2)}, u32[]{:S(2)}) collective-permute-start(f32[17,2,3072]{2,1,0:T(2,128)S(1)} %get-tuple-element.74.part2), channel_id=1, source_target_pairs={{0,7},{1,2},{2,1},{3,4},{4,3},{5,6},{6,5},{7,0},{8,15},{9,10},{10,... | collective-permute-start | bytes 1253384 | tf_op jit(solution)/shard_map/ppermute | solution.py:487
  16.9 0.0 collective-permute-done.y
  16.9 0.5 %inner.2 = (f32[17,2,3072]{2,1,0:T(2,128)S(1)}, f32[2,3072]{1,0:T(2,128)S(1)}) custom-call(f32[2,16,3072]{2,1,0:T(8,128)S(1)} %get-tuple-element.62.base, f32[15,2,3072]{2,1,0:T(2,128)S(1)} %collective-permute-done.y, f32[2,3072]{1,0:T(2,128)S(1)} %get-tuple-element.72.after.part02, f32[3,16,1]{2,1,0:T(8,128)S(1)} %get-tuple-element.58.coef, ...), custom_call_target="tpu_custom_call" | custom-call | bytes 1333440 | tf_op jit(solution)/shard_map/inner/pallas_call | solution.py:412
  17.4 0.1 collective-permute-done.5.e2
  17.5 0.0 collective-permute-done.6.e1
  17.5 0.6 %hand.1 = (f32[4,3072]{1,0:T(4,128)S(1)}, f32[96,128]{1,0:T(8,128)S(1)}, f32[96,128]{1,0:T(8,128)S(1)}, f32[96,128]{1,0:T(8,128)S(1)}) custom-call(f32[4,3072]{1,0:T(4,128)S(1)} %get-tuple-element.78.own, f32[4,3072]{1,0:T(4,128)S(1)} %collective-permute-done.5.e2, f32[4,3072]{1,0:T(4,128)S(1)} %collective-permute-done.6.e1, ...), custom_call_target="tpu_custom_call" | custom-call | flops 20000000000 | bytes 1775808 | tf_op jit(solution)/shard_map/hand/pallas_call | solution.py:412
  18.1 3.6 %collective-permute-start.10 = (f32[96,128]{1,0:T(8,128)S(1)}, f32[96,128]{1,0:T(8,128)S(1)}, u32[]{:S(2)}, u32[]{:S(2)}) collective-permute-start(f32[96,128]{1,0:T(8,128)S(1)} %get-tuple-element.85), channel_id=1, source_target_pairs={{0,24},{1,25},{2,26},{3,27},{4,28},{5,29},{6,30},{7,31},{8,9},{9,8... | collective-permute-start | bytes 147464 | tf_op jit(solution)/shard_map/ppermute | solution.py:489
  21.7 0.0 collective-permute-start.8
  21.7 0.5 %collective-permute-start.9 = (f32[96,128]{1,0:T(8,128)S(1)}, f32[96,128]{1,0:T(8,128)S(1)}, u32[]{:S(2)}, u32[]{:S(2)}) collective-permute-start(f32[96,128]{1,0:T(8,128)S(1)} %get-tuple-element.84), channel_id=1, source_target_pairs={{0,1},{1,0},{2,3},{3,2},{4,5},{5,4},{6,7},{7,6},{8,9},{9,8},{10,11... | collective-permute-start | bytes 147464 | tf_op jit(solution)/shard_map/ppermute | solution.py:489
  22.2 0.0 collective-permute-start.13
  22.2 1.5 %evolve.1 = (f32[2,16,3072]{2,1,0:T(8,128)S(1)}, f32[2,16,3072]{2,1,0:T(8,128)S(1)}, f32[8,3072]{1,0:T(8,128)S(1)}) custom-call(f32[17,2,3072]{2,1,0:T(2,128)S(1)} %get-tuple-element.73.part1, f32[17,2,3072]{2,1,0:T(2,128)S(1)} %get-tuple-element.74.part2, f32[2,16,3072]{2,1,0:T(8,128)S(1)} %get-tuple-element.75.gain1, ...), custom_call_target="tpu_custom_call" | custom-call | bytes 2654400 | tf_op jit(solution)/shard_map/evolve/pallas_call | solution.py:412
  23.7 0.8 %collective-permute-done.10.refs_2_ = f32[96,128]{1,0:T(8,128)S(1)} collective-permute-done((f32[96,128]{1,0:T(8,128)S(1)}, f32[96,128]{1,0:T(8,128)S(1)}, u32[]{:S(2)}, u32[]{:S(2)}) %collective-permute-start.10) | collective-permute-done | bytes 49184 | tf_op jit(solution)/shard_map/ppermute | solution.py:489
  24.5 0.1 surface.3
  24.6 0.6 %collective-permute-start.11 = (f32[2,3072]{1,0:T(2,128)S(1)}, f32[2,3072]{1,0:T(2,128)S(1)}, u32[]{:S(2)}, u32[]{:S(2)}) collective-permute-start(f32[2,3072]{1,0:T(2,128)S(1)} %get-tuple-element.90), channel_id=1, source_target_pairs={{0,7},{1,2},{2,1},{3,4},{4,3},{5,6},{6,5},{7,0},{8,15},{9,10},{10,... | collective-permute-start | bytes 73736 | tf_op jit(solution)/shard_map/ppermute | solution.py:516
  25.2 1.7 %collective-permute-done.7.y = f32[17,2,3072]{2,1,0:T(2,128)S(1)} collective-permute-done((f32[17,2,3072]{2,1,0:T(2,128)S(1)}, f32[17,2,3072]{2,1,0:T(2,128)S(1)}, u32[]{:S(2)}, u32[]{:S(2)}) %collective-permute-start.7) | collective-permute-done | bytes 417824 | tf_op jit(solution)/shard_map/ppermute | solution.py:487
  26.9 0.7 %outer.3 = (f32[2,16,3072]{2,1,0:T(8,128)S(1)}, f32[2,3072]{1,0:T(2,128)S(1)}, f32[4,3072]{1,0:T(4,128)S(1)}) custom-call(f32[2,16,3072]{2,1,0:T(8,128)S(1)} %get-tuple-element.77.base, f32[17,2,3072]{2,1,0:T(2,128)S(1)} %collective-permute-done.7.y, f32[4,3072]{1,0:T(4,128)S(1)} %get-tuple-element.87.after, f32[3,16,1]{2,1,0:T(8,128)S(1)} %get-tuple-element.58.coef, ...), custom_call_target="tpu_custom_call" | custom-call | flops 4000000000 | bytes 1530304 | tf_op jit(solution)/shard_map/outer/pallas_call | solution.py:412
  27.6 0.6 %inner.3 = (f32[2,16,3072]{2,1,0:T(8,128)S(1)}, f32[2,3072]{1,0:T(2,128)S(1)}) custom-call(f32[2,16,3072]{2,1,0:T(8,128)S(1)} %get-tuple-element.92.base, f32[17,2,3072]{2,1,0:T(2,128)S(1)} %collective-permute-done.13.y, f32[2,3072]{1,0:T(2,128)S(1)} %get-tuple-element.93.after.part02, f32[3,16,1]{2,1,0:T(8,128)S(1)} %get-tuple-element.58.coef, ...), custom_call_target="tpu_custom_call" | custom-call | bytes 1456576 | tf_op jit(solution)/shard_map/inner/pallas_call | solution.py:412
  28.2 0.7 %collective-permute-done.11.e2 = f32[2,3072]{1,0:T(2,128)S(1)} collective-permute-done((f32[2,3072]{1,0:T(2,128)S(1)}, f32[2,3072]{1,0:T(2,128)S(1)}, u32[]{:S(2)}, u32[]{:S(2)}) %collective-permute-start.11) | collective-permute-done | bytes 24608 | tf_op jit(solution)/shard_map/ppermute | solution.py:516
  29.0 1.3 %close.1 = (f32[1,16,4,3072]{3,2,1,0:T(4,128)}, f32[1,4,3072]{2,1,0:T(4,128)}) custom-call(f32[4,3072]{1,0:T(4,128)S(1)} %get-tuple-element.89.own, f32[2,3072]{1,0:T(2,128)S(1)} %collective-permute-done.11.e2, f32[2,3072]{1,0:T(2,128)S(1)} %collective-permute-done.12.e1, f32[3,16,1]{2,1,0:T(8,128)S(1)} %get-tuple-element.58.coef, ...), custom_call_target="tpu_custom_call" | custom-call | bytes 2703552 | tf_op jit(solution)/shard_map/close/pallas_call | solution.py:412
  (9 shorter events, 0.1 us)
Async XLA Ops:
  2.0 11.9 %collective-permute-start.1 = (f32[15,2,3072]{2,1,0:T(2,128)S(1)}, f32[15,2,3072]{2,1,0:T(2,128)S(1)}, u32[]{:S(2)}, u32[]{:S(2)}) collective-permute-start(f32[15,2,3072]{2,1,0:T(2,128)S(1)} %get-tuple-element.51.x2), channel_id=1, source_target_pairs={{0,7},{1,2},{2,1},{3,4},{4,3},{5,6},{6,5},{7,0},{8,15},{9,10},{10,... | collective-permute-start | bytes 1105928 | tf_op jit(solution)/shard_map/ppermute | solution.py:487
  6.1 6.6 %collective-permute-start.2 = (f32[96,128]{1,0:T(8,128)S(1)}, f32[96,128]{1,0:T(8,128)S(1)}, u32[]{:S(2)}, u32[]{:S(2)}) collective-permute-start(f32[96,128]{1,0:T(8,128)S(1)} %get-tuple-element.64), channel_id=1, source_target_pairs={{0,24},{1,25},{2,26},{3,27},{4,28},{5,29},{6,30},{7,31},{8,9},{9,8... | collective-permute-start | bytes 147464 | tf_op jit(solution)/shard_map/ppermute | solution.py:489
  9.8 2.9 %collective-permute-start.3 = (f32[96,128]{1,0:T(8,128)S(1)}, f32[96,128]{1,0:T(8,128)S(1)}, u32[]{:S(2)}, u32[]{:S(2)}) collective-permute-start(f32[96,128]{1,0:T(8,128)S(1)} %get-tuple-element.65), channel_id=1, source_target_pairs={{0,1},{1,0},{2,3},{3,2},{4,5},{5,4},{6,7},{7,6},{8,24},{9,25},{10,... | collective-permute-start | bytes 147464 | tf_op jit(solution)/shard_map/ppermute | solution.py:489
  9.8 2.9 %collective-permute-start.4 = (f32[96,128]{1,0:T(8,128)S(1)}, f32[96,128]{1,0:T(8,128)S(1)}, u32[]{:S(2)}, u32[]{:S(2)}) collective-permute-start(f32[96,128]{1,0:T(8,128)S(1)} %get-tuple-element.66), channel_id=1, source_target_pairs={{0,1},{1,0},{2,3},{3,2},{4,5},{5,4},{6,7},{7,6},{8,9},{9,8},{10,11... | collective-permute-start | bytes 147464 | tf_op jit(solution)/shard_map/ppermute | solution.py:489
  10.3 6.6 %collective-permute-start = (f32[15,2,3072]{2,1,0:T(2,128)S(1)}, f32[15,2,3072]{2,1,0:T(2,128)S(1)}, u32[]{:S(2)}, u32[]{:S(2)}) collective-permute-start(f32[15,2,3072]{2,1,0:T(2,128)S(1)} %get-tuple-element.50.x1), channel_id=1, source_target_pairs={{0,1},{1,0},{2,3},{3,2},{4,5},{5,4},{6,7},{7,6},{8,9},{9,8},{10,11... | collective-permute-start | bytes 1105928 | tf_op jit(solution)/shard_map/ppermute | solution.py:486
  12.8 4.7 %collective-permute-start.5 = (f32[4,3072]{1,0:T(4,128)S(1)}, f32[4,3072]{1,0:T(4,128)S(1)}, u32[]{:S(2)}, u32[]{:S(2)}) collective-permute-start(f32[4,3072]{1,0:T(4,128)S(1)} %get-tuple-element.70.after.ns), channel_id=1, source_target_pairs={{0,7},{1,2},{2,1},{3,4},{4,3},{5,6},{6,5},{7,0},{8,15},{9,10},{10,... | collective-permute-start | bytes 147464 | tf_op jit(solution)/shard_map/ppermute | solution.py:516
  13.5 4.0 %collective-permute-start.6 = (f32[4,3072]{1,0:T(4,128)S(1)}, f32[4,3072]{1,0:T(4,128)S(1)}, u32[]{:S(2)}, u32[]{:S(2)}) collective-permute-start(f32[4,3072]{1,0:T(4,128)S(1)} %get-tuple-element.70.after.ns), channel_id=1, source_target_pairs={{0,1},{1,0},{2,3},{3,2},{4,5},{5,4},{6,7},{7,6},{8,9},{9,8},{10,11... | collective-permute-start | bytes 147464 | tf_op jit(solution)/shard_map/ppermute | solution.py:515
  14.5 12.4 %collective-permute-start.7 = (f32[17,2,3072]{2,1,0:T(2,128)S(1)}, f32[17,2,3072]{2,1,0:T(2,128)S(1)}, u32[]{:S(2)}, u32[]{:S(2)}) collective-permute-start(f32[17,2,3072]{2,1,0:T(2,128)S(1)} %get-tuple-element.74.part2), channel_id=1, source_target_pairs={{0,7},{1,2},{2,1},{3,4},{4,3},{5,6},{6,5},{7,0},{8,15},{9,10},{10,... | collective-permute-start | bytes 1253384 | tf_op jit(solution)/shard_map/ppermute | solution.py:487
  18.1 6.4 %collective-permute-start.10 = (f32[96,128]{1,0:T(8,128)S(1)}, f32[96,128]{1,0:T(8,128)S(1)}, u32[]{:S(2)}, u32[]{:S(2)}) collective-permute-start(f32[96,128]{1,0:T(8,128)S(1)} %get-tuple-element.85), channel_id=1, source_target_pairs={{0,24},{1,25},{2,26},{3,27},{4,28},{5,29},{6,30},{7,31},{8,9},{9,8... | collective-permute-start | bytes 147464 | tf_op jit(solution)/shard_map/ppermute | solution.py:489
  21.7 2.8 %collective-permute-start.8 = (f32[96,128]{1,0:T(8,128)S(1)}, f32[96,128]{1,0:T(8,128)S(1)}, u32[]{:S(2)}, u32[]{:S(2)}) collective-permute-start(f32[96,128]{1,0:T(8,128)S(1)} %get-tuple-element.83), channel_id=1, source_target_pairs={{0,1},{1,0},{2,3},{3,2},{4,5},{5,4},{6,7},{7,6},{8,24},{9,25},{10,... | collective-permute-start | bytes 147464 | tf_op jit(solution)/shard_map/ppermute | solution.py:489
  21.7 2.8 %collective-permute-start.9 = (f32[96,128]{1,0:T(8,128)S(1)}, f32[96,128]{1,0:T(8,128)S(1)}, u32[]{:S(2)}, u32[]{:S(2)}) collective-permute-start(f32[96,128]{1,0:T(8,128)S(1)} %get-tuple-element.84), channel_id=1, source_target_pairs={{0,1},{1,0},{2,3},{3,2},{4,5},{5,4},{6,7},{7,6},{8,9},{9,8},{10,11... | collective-permute-start | bytes 147464 | tf_op jit(solution)/shard_map/ppermute | solution.py:489
  22.2 5.3 %collective-permute-start.13 = (f32[17,2,3072]{2,1,0:T(2,128)S(1)}, f32[17,2,3072]{2,1,0:T(2,128)S(1)}, u32[]{:S(2)}, u32[]{:S(2)}) collective-permute-start(f32[17,2,3072]{2,1,0:T(2,128)S(1)} %get-tuple-element.73.part1), channel_id=1, source_target_pairs={{0,1},{1,0},{2,3},{3,2},{4,5},{5,4},{6,7},{7,6},{8,9},{9,8},{10,11... | collective-permute-start | bytes 1253384 | tf_op jit(solution)/shard_map/ppermute | solution.py:486
  24.6 4.4 %collective-permute-start.11 = (f32[2,3072]{1,0:T(2,128)S(1)}, f32[2,3072]{1,0:T(2,128)S(1)}, u32[]{:S(2)}, u32[]{:S(2)}) collective-permute-start(f32[2,3072]{1,0:T(2,128)S(1)} %get-tuple-element.90), channel_id=1, source_target_pairs={{0,7},{1,2},{2,1},{3,4},{4,3},{5,6},{6,5},{7,0},{8,15},{9,10},{10,... | collective-permute-start | bytes 73736 | tf_op jit(solution)/shard_map/ppermute | solution.py:516
  25.2 3.7 %collective-permute-start.12 = (f32[2,3072]{1,0:T(2,128)S(1)}, f32[2,3072]{1,0:T(2,128)S(1)}, u32[]{:S(2)}, u32[]{:S(2)}) collective-permute-start(f32[2,3072]{1,0:T(2,128)S(1)} %get-tuple-element.91), channel_id=1, source_target_pairs={{0,1},{1,0},{2,3},{3,2},{4,5},{5,4},{6,7},{7,6},{8,9},{9,8},{10,11... | collective-permute-start | bytes 73736 | tf_op jit(solution)/shard_map/ppermute | solution.py:515

commit v9 on v8

--- a/solution.py
+++ b/solution.py
@@ -55,11 +55,11 @@
 
 def products(handed, picked_by, weight, blk_ref):
     rows, width = handed.shape
-    count, block = blk_ref.shape
+    block = blk_ref.shape[1]
     per_row = width // block
     for c in range(per_row):
         blk_ref[pl.ds(c, rows, stride=per_row), :] = handed[:, c * block : (c + 1) * block]
-    blocks = blk_ref[...].astype(BF16)
+    blocks = blk_ref[: rows * per_row, :].astype(BF16)
     even = blocks.astype(F32)
     turned = [blocks] + [pltpu.roll(even, block - j, 1).astype(BF16) for j in range(1, BAND)]
     picked = picked_by(jnp.concatenate(turned, axis=1))
@@ -212,7 +212,7 @@
     total = recs[0][...]
     for rec in recs[1:]:
         total = total + rec[...]
-    blk[...] = total
+    blk[: total.shape[0], :] = total
     received = jnp.concatenate(
         [blk[pl.ds(c, rows, stride=per_row), :] for c in range(per_row)], axis=1
     )
@@ -369,7 +369,7 @@
         lambda j: wide[j],
         blk,
     )
-    count = blk.shape[0]
+    count = outs[0].shape[0]
     thirds = [contrib[n * count : (n + 1) * count] for n in range(MEMBERS)]
     member = lax.rem(lax.axis_index("comp"), MEMBERS)
     for n, (out, third) in enumerate(zip(outs, thirds)):
@@ -445,7 +445,7 @@
 
     halves = [shape((half, fields, width), F32)] * 2
     payloads = [shape((count, block), F32)] * MEMBERS
-    blocks = pltpu.VMEM((count, block), F32)
+    blocks = pltpu.VMEM((max(SUBLANES // rows, 1) * count, block), F32)
     line, pair = shape((rows, width), F32), shape((half, width), F32)
     far = lambda args: [pltpu.with_memory_space_constraint(a, pltpu.HBM) for a in args]
     like = lambda args: [shape(a.shape, a.dtype) for a in args]

time: 30.4 us -> 30.4 us (level)
  no operation moved by 1% of the time
where the time goes in v9:
time: 30.4 us; the launch traced here: 30.2 us
  starting transfers between devices  15.8 us (52%)
  Pallas kernels  10.3 us (34%)
  waiting for transfers between devices  3.33 us (11%)
  between operations  0.76 us (2%)
    pallas_call x13, Pallas kernels, call(): pl.pallas_call(kernel, name=name, out_shape=outs, in_specs=in_specs or [V...  10.3 us
    ppermute x6, starting transfers between devices, on_device(): lax.ppermute(value, ('comp', 'tile'), partner_pairs(groups, tiles, member))  8.28 us
    ppermute x2, starting transfers between devices, on_device(): y2 = lax.ppermute(x2, 'tile', outer_pairs(tiles))  5.8 us
    ppermute x2, waiting for transfers between devices, on_device(): y2 = lax.ppermute(x2, 'tile', outer_pairs(tiles))  1.66 us
    ppermute x2, starting transfers between devices, on_device(): e2 = lax.ppermute(d2, 'tile', outer_pairs(tiles))  1.39 us
    ppermute x2, waiting for transfers between devices, on_device(): e2 = lax.ppermute(d2, 'tile', outer_pairs(tiles))  0.85 us
    ppermute x6, waiting for transfers between devices, on_device(): lax.ppermute(value, ('comp', 'tile'), partner_pairs(groups, tiles, member))  0.81 us
  transfers between devices with their start and end apart: 14, of which 4 were waited for; matrix products, arithmetic and copies ran while one was open for 0% of the time, Pallas kernels for 25%

profile of v9, /device:TPU:0, one launch (start us, length us, event | category | flops | bytes accessed | tf_op | source)
XLA Modules:
  0.0 30.2 jit_solution(18086875585955484093)
XLA Ops:
  0.6 1.4 %load.1 = (f32[15,2,3072]{2,1,0:T(2,128)S(1)}, f32[15,2,3072]{2,1,0:T(2,128)S(1)}, f32[4,3072]{1,0:T(4,128)S(1)}, bf16[96,288]{1,0:T(8,128)(2,1)S(1)}, bf16[288,...) custom-call(f32[1,16,4,3072]{3,2,1,0:T(4,128)} %state.1, ...), custom_call_target="tpu_custom_call" | custom-call | bytes 3241344 | tf_op jit(solution)/shard_map/load/pallas_call | solution.py:412
  2.0 3.4 %collective-permute-start.1 = (f32[15,2,3072]{2,1,0:T(2,128)S(1)}, f32[15,2,3072]{2,1,0:T(2,128)S(1)}, u32[]{:S(2)}, u32[]{:S(2)}) collective-permute-start(f32[15,2,3072]{2,1,0:T(2,128)S(1)} %get-tuple-element.51.x2), channel_id=1, source_target_pairs={{0,7},{1,2},{2,1},{3,4},{4,3},{5,6},{6,5},{7,0},{8,15},{9,10},{10,... | collective-permute-start | bytes 1105928 | tf_op jit(solution)/shard_map/ppermute | solution.py:487
  5.4 0.7 %remap.1 = (f32[2304,128]{1,0:T(8,128)S(1)}, f32[96,128]{1,0:T(8,128)S(1)}, f32[96,128]{1,0:T(8,128)S(1)}, f32[96,128]{1,0:T(8,128)S(1)}) custom-call(f32[1,4,3072]{2,1,0:T(4,128)S(1)} %get-tuple-element.53.coupling, bf16[1,288,8,128]{3,2,1,0:T(8,128)(2,1)S(1)} %get-tuple-element.54.weights, bf16[96,288]{1,0:T(8,128)(2,1)S(1)} %get-tuple-element.55.pick, ...), custom_call_target="tpu_custom_call" | custom-call | bytes 2353152 | tf_op jit(solution)/shard_map/remap/pallas_call | solution.py:412
  6.1 3.7 %collective-permute-start.2 = (f32[96,128]{1,0:T(8,128)S(1)}, f32[96,128]{1,0:T(8,128)S(1)}, u32[]{:S(2)}, u32[]{:S(2)}) collective-permute-start(f32[96,128]{1,0:T(8,128)S(1)} %get-tuple-element.64), channel_id=1, source_target_pairs={{0,24},{1,25},{2,26},{3,27},{4,28},{5,29},{6,30},{7,31},{8,9},{9,8... | collective-permute-start | bytes 147464 | tf_op jit(solution)/shard_map/ppermute | solution.py:489
  9.8 0.5 %collective-permute-start.4 = (f32[96,128]{1,0:T(8,128)S(1)}, f32[96,128]{1,0:T(8,128)S(1)}, u32[]{:S(2)}, u32[]{:S(2)}) collective-permute-start(f32[96,128]{1,0:T(8,128)S(1)} %get-tuple-element.66), channel_id=1, source_target_pairs={{0,1},{1,0},{2,3},{3,2},{4,5},{5,4},{6,7},{7,6},{8,9},{9,8},{10,11... | collective-permute-start | bytes 147464 | tf_op jit(solution)/shard_map/ppermute | solution.py:489
  10.3 0.0 collective-permute-start
  10.3 1.0 %sort.1 = (f32[8,288,128]{2,1,0:T(8,128)S(1)}, bf16[288,96]{1,0:T(8,128)(2,1)S(1)}, s32[1,4,3072]{2,1,0:T(4,128)S(1)}, s32[1,4,3072]{2,1,0:T(4,128)S(1)}, f32[4,...) custom-call(s32[1,288]{1,0:T(1,128)S(1)} %get-tuple-element.52.targets, ...), custom_call_target="tpu_custom_call" | custom-call | bytes 2727616 | tf_op jit(solution)/shard_map/sort/pallas_call | solution.py:412
  11.3 1.4 %start.1 = (f32[2,16,3072]{2,1,0:T(8,128)S(1)}, f32[2,16,3072]{2,1,0:T(8,128)S(1)}, f32[2,16,3072]{2,1,0:T(8,128)S(1)}, f32[2,16,3072]{2,1,0:T(8,128)S(1)}, f32[4,3072]{1,0:T(4,128)S(1)}) custom-call(f32[15,2,3072]{2,1,0:T(2,128)S(1)} %get-tuple-element.50.x1, f32[15,2,3072]{2,1,0:T(2,128)S(1)} %get-tuple-element.51.x2, ...), custom_call_target="tpu_custom_call" | custom-call | bytes 2458048 | tf_op jit(solution)/shard_map/start/pallas_call | solution.py:412
  12.7 0.0 collective-permute-done.2.refs_0_
  12.7 0.0 collective-permute-done.3.refs_1_
  12.8 0.8 %collective-permute-start.5 = (f32[4,3072]{1,0:T(4,128)S(1)}, f32[4,3072]{1,0:T(4,128)S(1)}, u32[]{:S(2)}, u32[]{:S(2)}) collective-permute-start(f32[4,3072]{1,0:T(4,128)S(1)} %get-tuple-element.70.after.ns), channel_id=1, source_target_pairs={{0,7},{1,2},{2,1},{3,4},{4,3},{5,6},{6,5},{7,0},{8,15},{9,10},{10,... | collective-permute-start | bytes 147464 | tf_op jit(solution)/shard_map/ppermute | solution.py:516
  13.5 0.4 %collective-permute-start.6 = (f32[4,3072]{1,0:T(4,128)S(1)}, f32[4,3072]{1,0:T(4,128)S(1)}, u32[]{:S(2)}, u32[]{:S(2)}) collective-permute-start(f32[4,3072]{1,0:T(4,128)S(1)} %get-tuple-element.70.after.ns), channel_id=1, source_target_pairs={{0,1},{1,0},{2,3},{3,2},{4,5},{5,4},{6,7},{7,6},{8,9},{9,8},{10,11... | collective-permute-start | bytes 147464 | tf_op jit(solution)/shard_map/ppermute | solution.py:515
  13.9 0.6 %outer.2 = (f32[17,2,3072]{2,1,0:T(2,128)S(1)}, f32[2,3072]{1,0:T(2,128)S(1)}, f32[4,3072]{1,0:T(4,128)S(1)}) custom-call(f32[2,16,3072]{2,1,0:T(8,128)S(1)} %get-tuple-element.63.base, f32[15,2,3072]{2,1,0:T(2,128)S(1)} %collective-permute-done.1.y, f32[4,3072]{1,0:T(4,128)S(1)} %get-tuple-element.70.after.ns, f32[3,16,1]{2,1,0:T(8,128)S(1)} %get-tuple-element.58.coef, ...), custom_call_target="tpu_custom_call" | custom-call | flops 4000000000 | bytes 1407168 | tf_op jit(solution)/shard_map/outer/pallas_call | solution.py:412
  14.5 2.4 %collective-permute-start.7 = (f32[17,2,3072]{2,1,0:T(2,128)S(1)}, f32[17,2,3072]{2,1,0:T(2,128)S(1)}, u32[]{:S(2)}, u32[]{:S(2)}) collective-permute-start(f32[17,2,3072]{2,1,0:T(2,128)S(1)} %get-tuple-element.74.part2), channel_id=1, source_target_pairs={{0,7},{1,2},{2,1},{3,4},{4,3},{5,6},{6,5},{7,0},{8,15},{9,10},{10,... | collective-permute-start | bytes 1253384 | tf_op jit(solution)/shard_map/ppermute | solution.py:487
  16.9 0.0 collective-permute-done.y
  16.9 0.5 %inner.2 = (f32[17,2,3072]{2,1,0:T(2,128)S(1)}, f32[2,3072]{1,0:T(2,128)S(1)}) custom-call(f32[2,16,3072]{2,1,0:T(8,128)S(1)} %get-tuple-element.62.base, f32[15,2,3072]{2,1,0:T(2,128)S(1)} %collective-permute-done.y, f32[2,3072]{1,0:T(2,128)S(1)} %get-tuple-element.72.after.part02, f32[3,16,1]{2,1,0:T(8,128)S(1)} %get-tuple-element.58.coef, ...), custom_call_target="tpu_custom_call" | custom-call | bytes 1333440 | tf_op jit(solution)/shard_map/inner/pallas_call | solution.py:412
  17.4 0.1 collective-permute-done.5.e2
  17.5 0.0 collective-permute-done.6.e1
  17.5 0.6 %hand.1 = (f32[4,3072]{1,0:T(4,128)S(1)}, f32[96,128]{1,0:T(8,128)S(1)}, f32[96,128]{1,0:T(8,128)S(1)}, f32[96,128]{1,0:T(8,128)S(1)}) custom-call(f32[4,3072]{1,0:T(4,128)S(1)} %get-tuple-element.78.own, f32[4,3072]{1,0:T(4,128)S(1)} %collective-permute-done.5.e2, f32[4,3072]{1,0:T(4,128)S(1)} %collective-permute-done.6.e1, ...), custom_call_target="tpu_custom_call" | custom-call | flops 20000000000 | bytes 1775808 | tf_op jit(solution)/shard_map/hand/pallas_call | solution.py:412
  18.1 3.6 %collective-permute-start.10 = (f32[96,128]{1,0:T(8,128)S(1)}, f32[96,128]{1,0:T(8,128)S(1)}, u32[]{:S(2)}, u32[]{:S(2)}) collective-permute-start(f32[96,128]{1,0:T(8,128)S(1)} %get-tuple-element.85), channel_id=1, source_target_pairs={{0,24},{1,25},{2,26},{3,27},{4,28},{5,29},{6,30},{7,31},{8,9},{9,8... | collective-permute-start | bytes 147464 | tf_op jit(solution)/shard_map/ppermute | solution.py:489
  21.7 0.0 collective-permute-start.8
  21.7 0.5 %collective-permute-start.9 = (f32[96,128]{1,0:T(8,128)S(1)}, f32[96,128]{1,0:T(8,128)S(1)}, u32[]{:S(2)}, u32[]{:S(2)}) collective-permute-start(f32[96,128]{1,0:T(8,128)S(1)} %get-tuple-element.84), channel_id=1, source_target_pairs={{0,1},{1,0},{2,3},{3,2},{4,5},{5,4},{6,7},{7,6},{8,9},{9,8},{10,11... | collective-permute-start | bytes 147464 | tf_op jit(solution)/shard_map/ppermute | solution.py:489
  22.2 0.0 collective-permute-start.13
  22.2 1.5 %evolve.1 = (f32[2,16,3072]{2,1,0:T(8,128)S(1)}, f32[2,16,3072]{2,1,0:T(8,128)S(1)}, f32[8,3072]{1,0:T(8,128)S(1)}) custom-call(f32[17,2,3072]{2,1,0:T(2,128)S(1)} %get-tuple-element.73.part1, f32[17,2,3072]{2,1,0:T(2,128)S(1)} %get-tuple-element.74.part2, f32[2,16,3072]{2,1,0:T(8,128)S(1)} %get-tuple-element.75.gain1, ...), custom_call_target="tpu_custom_call" | custom-call | bytes 2654400 | tf_op jit(solution)/shard_map/evolve/pallas_call | solution.py:412
  23.7 0.8 %collective-permute-done.10.refs_2_ = f32[96,128]{1,0:T(8,128)S(1)} collective-permute-done((f32[96,128]{1,0:T(8,128)S(1)}, f32[96,128]{1,0:T(8,128)S(1)}, u32[]{:S(2)}, u32[]{:S(2)}) %collective-permute-start.10) | collective-permute-done | bytes 49184 | tf_op jit(solution)/shard_map/ppermute | solution.py:489
  24.5 0.1 surface.3
  24.6 0.6 %collective-permute-start.11 = (f32[2,3072]{1,0:T(2,128)S(1)}, f32[2,3072]{1,0:T(2,128)S(1)}, u32[]{:S(2)}, u32[]{:S(2)}) collective-permute-start(f32[2,3072]{1,0:T(2,128)S(1)} %get-tuple-element.90), channel_id=1, source_target_pairs={{0,7},{1,2},{2,1},{3,4},{4,3},{5,6},{6,5},{7,0},{8,15},{9,10},{10,... | collective-permute-start | bytes 73736 | tf_op jit(solution)/shard_map/ppermute | solution.py:516
  25.2 1.7 %collective-permute-done.7.y = f32[17,2,3072]{2,1,0:T(2,128)S(1)} collective-permute-done((f32[17,2,3072]{2,1,0:T(2,128)S(1)}, f32[17,2,3072]{2,1,0:T(2,128)S(1)}, u32[]{:S(2)}, u32[]{:S(2)}) %collective-permute-start.7) | collective-permute-done | bytes 417824 | tf_op jit(solution)/shard_map/ppermute | solution.py:487
  26.9 0.7 %outer.3 = (f32[2,16,3072]{2,1,0:T(8,128)S(1)}, f32[2,3072]{1,0:T(2,128)S(1)}, f32[4,3072]{1,0:T(4,128)S(1)}) custom-call(f32[2,16,3072]{2,1,0:T(8,128)S(1)} %get-tuple-element.77.base, f32[17,2,3072]{2,1,0:T(2,128)S(1)} %collective-permute-done.7.y, f32[4,3072]{1,0:T(4,128)S(1)} %get-tuple-element.87.after, f32[3,16,1]{2,1,0:T(8,128)S(1)} %get-tuple-element.58.coef, ...), custom_call_target="tpu_custom_call" | custom-call | flops 4000000000 | bytes 1530304 | tf_op jit(solution)/shard_map/outer/pallas_call | solution.py:412
  27.6 0.6 %inner.3 = (f32[2,16,3072]{2,1,0:T(8,128)S(1)}, f32[2,3072]{1,0:T(2,128)S(1)}) custom-call(f32[2,16,3072]{2,1,0:T(8,128)S(1)} %get-tuple-element.92.base, f32[17,2,3072]{2,1,0:T(2,128)S(1)} %collective-permute-done.13.y, f32[2,3072]{1,0:T(2,128)S(1)} %get-tuple-element.93.after.part02, f32[3,16,1]{2,1,0:T(8,128)S(1)} %get-tuple-element.58.coef, ...), custom_call_target="tpu_custom_call" | custom-call | bytes 1456576 | tf_op jit(solution)/shard_map/inner/pallas_call | solution.py:412
  28.2 0.7 %collective-permute-done.11.e2 = f32[2,3072]{1,0:T(2,128)S(1)} collective-permute-done((f32[2,3072]{1,0:T(2,128)S(1)}, f32[2,3072]{1,0:T(2,128)S(1)}, u32[]{:S(2)}, u32[]{:S(2)}) %collective-permute-start.11) | collective-permute-done | bytes 24608 | tf_op jit(solution)/shard_map/ppermute | solution.py:516
  29.0 1.3 %close.1 = (f32[1,16,4,3072]{3,2,1,0:T(4,128)}, f32[1,4,3072]{2,1,0:T(4,128)}) custom-call(f32[4,3072]{1,0:T(4,128)S(1)} %get-tuple-element.89.own, f32[2,3072]{1,0:T(2,128)S(1)} %collective-permute-done.11.e2, f32[2,3072]{1,0:T(2,128)S(1)} %collective-permute-done.12.e1, f32[3,16,1]{2,1,0:T(8,128)S(1)} %get-tuple-element.58.coef, ...), custom_call_target="tpu_custom_call" | custom-call | bytes 2703552 | tf_op jit(solution)/shard_map/close/pallas_call | solution.py:412
  (9 shorter events, 0.1 us)
Async XLA Ops:
  2.0 11.9 %collective-permute-start.1 = (f32[15,2,3072]{2,1,0:T(2,128)S(1)}, f32[15,2,3072]{2,1,0:T(2,128)S(1)}, u32[]{:S(2)}, u32[]{:S(2)}) collective-permute-start(f32[15,2,3072]{2,1,0:T(2,128)S(1)} %get-tuple-element.51.x2), channel_id=1, source_target_pairs={{0,7},{1,2},{2,1},{3,4},{4,3},{5,6},{6,5},{7,0},{8,15},{9,10},{10,... | collective-permute-start | bytes 1105928 | tf_op jit(solution)/shard_map/ppermute | solution.py:487
  6.1 6.6 %collective-permute-start.2 = (f32[96,128]{1,0:T(8,128)S(1)}, f32[96,128]{1,0:T(8,128)S(1)}, u32[]{:S(2)}, u32[]{:S(2)}) collective-permute-start(f32[96,128]{1,0:T(8,128)S(1)} %get-tuple-element.64), channel_id=1, source_target_pairs={{0,24},{1,25},{2,26},{3,27},{4,28},{5,29},{6,30},{7,31},{8,9},{9,8... | collective-permute-start | bytes 147464 | tf_op jit(solution)/shard_map/ppermute | solution.py:489
  9.8 2.9 %collective-permute-start.3 = (f32[96,128]{1,0:T(8,128)S(1)}, f32[96,128]{1,0:T(8,128)S(1)}, u32[]{:S(2)}, u32[]{:S(2)}) collective-permute-start(f32[96,128]{1,0:T(8,128)S(1)} %get-tuple-element.65), channel_id=1, source_target_pairs={{0,1},{1,0},{2,3},{3,2},{4,5},{5,4},{6,7},{7,6},{8,24},{9,25},{10,... | collective-permute-start | bytes 147464 | tf_op jit(solution)/shard_map/ppermute | solution.py:489
  9.8 2.9 %collective-permute-start.4 = (f32[96,128]{1,0:T(8,128)S(1)}, f32[96,128]{1,0:T(8,128)S(1)}, u32[]{:S(2)}, u32[]{:S(2)}) collective-permute-start(f32[96,128]{1,0:T(8,128)S(1)} %get-tuple-element.66), channel_id=1, source_target_pairs={{0,1},{1,0},{2,3},{3,2},{4,5},{5,4},{6,7},{7,6},{8,9},{9,8},{10,11... | collective-permute-start | bytes 147464 | tf_op jit(solution)/shard_map/ppermute | solution.py:489
  10.3 6.6 %collective-permute-start = (f32[15,2,3072]{2,1,0:T(2,128)S(1)}, f32[15,2,3072]{2,1,0:T(2,128)S(1)}, u32[]{:S(2)}, u32[]{:S(2)}) collective-permute-start(f32[15,2,3072]{2,1,0:T(2,128)S(1)} %get-tuple-element.50.x1), channel_id=1, source_target_pairs={{0,1},{1,0},{2,3},{3,2},{4,5},{5,4},{6,7},{7,6},{8,9},{9,8},{10,11... | collective-permute-start | bytes 1105928 | tf_op jit(solution)/shard_map/ppermute | solution.py:486
  12.8 4.7 %collective-permute-start.5 = (f32[4,3072]{1,0:T(4,128)S(1)}, f32[4,3072]{1,0:T(4,128)S(1)}, u32[]{:S(2)}, u32[]{:S(2)}) collective-permute-start(f32[4,3072]{1,0:T(4,128)S(1)} %get-tuple-element.70.after.ns), channel_id=1, source_target_pairs={{0,7},{1,2},{2,1},{3,4},{4,3},{5,6},{6,5},{7,0},{8,15},{9,10},{10,... | collective-permute-start | bytes 147464 | tf_op jit(solution)/shard_map/ppermute | solution.py:516
  13.5 4.0 %collective-permute-start.6 = (f32[4,3072]{1,0:T(4,128)S(1)}, f32[4,3072]{1,0:T(4,128)S(1)}, u32[]{:S(2)}, u32[]{:S(2)}) collective-permute-start(f32[4,3072]{1,0:T(4,128)S(1)} %get-tuple-element.70.after.ns), channel_id=1, source_target_pairs={{0,1},{1,0},{2,3},{3,2},{4,5},{5,4},{6,7},{7,6},{8,9},{9,8},{10,11... | collective-permute-start | bytes 147464 | tf_op jit(solution)/shard_map/ppermute | solution.py:515
  14.5 12.4 %collective-permute-start.7 = (f32[17,2,3072]{2,1,0:T(2,128)S(1)}, f32[17,2,3072]{2,1,0:T(2,128)S(1)}, u32[]{:S(2)}, u32[]{:S(2)}) collective-permute-start(f32[17,2,3072]{2,1,0:T(2,128)S(1)} %get-tuple-element.74.part2), channel_id=1, source_target_pairs={{0,7},{1,2},{2,1},{3,4},{4,3},{5,6},{6,5},{7,0},{8,15},{9,10},{10,... | collective-permute-start | bytes 1253384 | tf_op jit(solution)/shard_map/ppermute | solution.py:487
  18.1 6.4 %collective-permute-start.10 = (f32[96,128]{1,0:T(8,128)S(1)}, f32[96,128]{1,0:T(8,128)S(1)}, u32[]{:S(2)}, u32[]{:S(2)}) collective-permute-start(f32[96,128]{1,0:T(8,128)S(1)} %get-tuple-element.85), channel_id=1, source_target_pairs={{0,24},{1,25},{2,26},{3,27},{4,28},{5,29},{6,30},{7,31},{8,9},{9,8... | collective-permute-start | bytes 147464 | tf_op jit(solution)/shard_map/ppermute | solution.py:489
  21.7 2.8 %collective-permute-start.8 = (f32[96,128]{1,0:T(8,128)S(1)}, f32[96,128]{1,0:T(8,128)S(1)}, u32[]{:S(2)}, u32[]{:S(2)}) collective-permute-start(f32[96,128]{1,0:T(8,128)S(1)} %get-tuple-element.83), channel_id=1, source_target_pairs={{0,1},{1,0},{2,3},{3,2},{4,5},{5,4},{6,7},{7,6},{8,24},{9,25},{10,... | collective-permute-start | bytes 147464 | tf_op jit(solution)/shard_map/ppermute | solution.py:489
  21.7 2.8 %collective-permute-start.9 = (f32[96,128]{1,0:T(8,128)S(1)}, f32[96,128]{1,0:T(8,128)S(1)}, u32[]{:S(2)}, u32[]{:S(2)}) collective-permute-start(f32[96,128]{1,0:T(8,128)S(1)} %get-tuple-element.84), channel_id=1, source_target_pairs={{0,1},{1,0},{2,3},{3,2},{4,5},{5,4},{6,7},{7,6},{8,9},{9,8},{10,11... | collective-permute-start | bytes 147464 | tf_op jit(solution)/shard_map/ppermute | solution.py:489
  22.2 5.3 %collective-permute-start.13 = (f32[17,2,3072]{2,1,0:T(2,128)S(1)}, f32[17,2,3072]{2,1,0:T(2,128)S(1)}, u32[]{:S(2)}, u32[]{:S(2)}) collective-permute-start(f32[17,2,3072]{2,1,0:T(2,128)S(1)} %get-tuple-element.73.part1), channel_id=1, source_target_pairs={{0,1},{1,0},{2,3},{3,2},{4,5},{5,4},{6,7},{7,6},{8,9},{9,8},{10,11... | collective-permute-start | bytes 1253384 | tf_op jit(solution)/shard_map/ppermute | solution.py:486
  24.6 4.4 %collective-permute-start.11 = (f32[2,3072]{1,0:T(2,128)S(1)}, f32[2,3072]{1,0:T(2,128)S(1)}, u32[]{:S(2)}, u32[]{:S(2)}) collective-permute-start(f32[2,3072]{1,0:T(2,128)S(1)} %get-tuple-element.90), channel_id=1, source_target_pairs={{0,7},{1,2},{2,1},{3,4},{4,3},{5,6},{6,5},{7,0},{8,15},{9,10},{10,... | collective-permute-start | bytes 73736 | tf_op jit(solution)/shard_map/ppermute | solution.py:516
  25.2 3.7 %collective-permute-start.12 = (f32[2,3072]{1,0:T(2,128)S(1)}, f32[2,3072]{1,0:T(2,128)S(1)}, u32[]{:S(2)}, u32[]{:S(2)}) collective-permute-start(f32[2,3072]{1,0:T(2,128)S(1)} %get-tuple-element.91), channel_id=1, source_target_pairs={{0,1},{1,0},{2,3},{3,2},{4,5},{5,4},{6,7},{7,6},{8,9},{9,8},{10,11... | collective-permute-start | bytes 73736 | tf_op jit(solution)/shard_map/ppermute | solution.py:515

commit v10 on v9

--- a/solution.py
+++ b/solution.py
@@ -387,7 +387,7 @@
     half, fields, width = gain1.shape
     top_field = lax.broadcasted_iota(jnp.int32, (SUBLANES, width), 0) == 0
     line1, line2 = halves_of([squashed[r : r + 1, :] for r in range(2 * half)])
-    for h in range(0, fields, SUBLANES):
+    for h in reversed(range(0, fields, SUBLANES)):
         some = slice(h, h + SUBLANES)
         for i in range(half):
             inner = part1[i, some] + gain1[i, some] * line1[i]

time: 30.4 us -> 30.4 us (level)
  no operation moved by 1% of the time
where the time goes in v10:
time: 30.4 us; the launch traced here: 30.2 us
  starting transfers between devices  15.8 us (52%)
  Pallas kernels  10.3 us (34%)
  waiting for transfers between devices  3.33 us (11%)
  between operations  0.76 us (2%)
    pallas_call x13, Pallas kernels, call(): pl.pallas_call(kernel, name=name, out_shape=outs, in_specs=in_specs or [V...  10.3 us
    ppermute x6, starting transfers between devices, on_device(): lax.ppermute(value, ('comp', 'tile'), partner_pairs(groups, tiles, member))  8.28 us
    ppermute x2, starting transfers between devices, on_device(): y2 = lax.ppermute(x2, 'tile', outer_pairs(tiles))  5.8 us
    ppermute x2, waiting for transfers between devices, on_device(): y2 = lax.ppermute(x2, 'tile', outer_pairs(tiles))  1.66 us
    ppermute x2, starting transfers between devices, on_device(): e2 = lax.ppermute(d2, 'tile', outer_pairs(tiles))  1.39 us
    ppermute x2, waiting for transfers between devices, on_device(): e2 = lax.ppermute(d2, 'tile', outer_pairs(tiles))  0.85 us
    ppermute x6, waiting for transfers between devices, on_device(): lax.ppermute(value, ('comp', 'tile'), partner_pairs(groups, tiles, member))  0.81 us
  transfers between devices with their start and end apart: 14, of which 4 were waited for; matrix products, arithmetic and copies ran while one was open for 0% of the time, Pallas kernels for 25%

profile of v10, /device:TPU:0, one launch (start us, length us, event | category | flops | bytes accessed | tf_op | source)
XLA Modules:
  0.0 30.2 jit_solution(16052953935766962891)
XLA Ops:
  0.6 1.4 %load.1 = (f32[15,2,3072]{2,1,0:T(2,128)S(1)}, f32[15,2,3072]{2,1,0:T(2,128)S(1)}, f32[4,3072]{1,0:T(4,128)S(1)}, bf16[96,288]{1,0:T(8,128)(2,1)S(1)}, bf16[288,...) custom-call(f32[1,16,4,3072]{3,2,1,0:T(4,128)} %state.1, ...), custom_call_target="tpu_custom_call" | custom-call | bytes 3241344 | tf_op jit(solution)/shard_map/load/pallas_call | solution.py:412
  2.0 3.4 %collective-permute-start.1 = (f32[15,2,3072]{2,1,0:T(2,128)S(1)}, f32[15,2,3072]{2,1,0:T(2,128)S(1)}, u32[]{:S(2)}, u32[]{:S(2)}) collective-permute-start(f32[15,2,3072]{2,1,0:T(2,128)S(1)} %get-tuple-element.51.x2), channel_id=1, source_target_pairs={{0,7},{1,2},{2,1},{3,4},{4,3},{5,6},{6,5},{7,0},{8,15},{9,10},{10,... | collective-permute-start | bytes 1105928 | tf_op jit(solution)/shard_map/ppermute | solution.py:487
  5.4 0.7 %remap.1 = (f32[2304,128]{1,0:T(8,128)S(1)}, f32[96,128]{1,0:T(8,128)S(1)}, f32[96,128]{1,0:T(8,128)S(1)}, f32[96,128]{1,0:T(8,128)S(1)}) custom-call(f32[1,4,3072]{2,1,0:T(4,128)S(1)} %get-tuple-element.53.coupling, bf16[1,288,8,128]{3,2,1,0:T(8,128)(2,1)S(1)} %get-tuple-element.54.weights, bf16[96,288]{1,0:T(8,128)(2,1)S(1)} %get-tuple-element.55.pick, ...), custom_call_target="tpu_custom_call" | custom-call | bytes 2353152 | tf_op jit(solution)/shard_map/remap/pallas_call | solution.py:412
  6.1 3.7 %collective-permute-start.2 = (f32[96,128]{1,0:T(8,128)S(1)}, f32[96,128]{1,0:T(8,128)S(1)}, u32[]{:S(2)}, u32[]{:S(2)}) collective-permute-start(f32[96,128]{1,0:T(8,128)S(1)} %get-tuple-element.64), channel_id=1, source_target_pairs={{0,24},{1,25},{2,26},{3,27},{4,28},{5,29},{6,30},{7,31},{8,9},{9,8... | collective-permute-start | bytes 147464 | tf_op jit(solution)/shard_map/ppermute | solution.py:489
  9.8 0.5 %collective-permute-start.4 = (f32[96,128]{1,0:T(8,128)S(1)}, f32[96,128]{1,0:T(8,128)S(1)}, u32[]{:S(2)}, u32[]{:S(2)}) collective-permute-start(f32[96,128]{1,0:T(8,128)S(1)} %get-tuple-element.66), channel_id=1, source_target_pairs={{0,1},{1,0},{2,3},{3,2},{4,5},{5,4},{6,7},{7,6},{8,9},{9,8},{10,11... | collective-permute-start | bytes 147464 | tf_op jit(solution)/shard_map/ppermute | solution.py:489
  10.3 0.0 collective-permute-start
  10.3 1.0 %sort.1 = (f32[8,288,128]{2,1,0:T(8,128)S(1)}, bf16[288,96]{1,0:T(8,128)(2,1)S(1)}, s32[1,4,3072]{2,1,0:T(4,128)S(1)}, s32[1,4,3072]{2,1,0:T(4,128)S(1)}, f32[4,...) custom-call(s32[1,288]{1,0:T(1,128)S(1)} %get-tuple-element.52.targets, ...), custom_call_target="tpu_custom_call" | custom-call | bytes 2727616 | tf_op jit(solution)/shard_map/sort/pallas_call | solution.py:412
  11.3 1.4 %start.1 = (f32[2,16,3072]{2,1,0:T(8,128)S(1)}, f32[2,16,3072]{2,1,0:T(8,128)S(1)}, f32[2,16,3072]{2,1,0:T(8,128)S(1)}, f32[2,16,3072]{2,1,0:T(8,128)S(1)}, f32[4,3072]{1,0:T(4,128)S(1)}) custom-call(f32[15,2,3072]{2,1,0:T(2,128)S(1)} %get-tuple-element.50.x1, f32[15,2,3072]{2,1,0:T(2,128)S(1)} %get-tuple-element.51.x2, ...), custom_call_target="tpu_custom_call" | custom-call | bytes 2458048 | tf_op jit(solution)/shard_map/start/pallas_call | solution.py:412
  12.7 0.0 collective-permute-done.2.refs_0_
  12.7 0.0 collective-permute-done.3.refs_1_
  12.8 0.8 %collective-permute-start.5 = (f32[4,3072]{1,0:T(4,128)S(1)}, f32[4,3072]{1,0:T(4,128)S(1)}, u32[]{:S(2)}, u32[]{:S(2)}) collective-permute-start(f32[4,3072]{1,0:T(4,128)S(1)} %get-tuple-element.70.after.ns), channel_id=1, source_target_pairs={{0,7},{1,2},{2,1},{3,4},{4,3},{5,6},{6,5},{7,0},{8,15},{9,10},{10,... | collective-permute-start | bytes 147464 | tf_op jit(solution)/shard_map/ppermute | solution.py:516
  13.5 0.4 %collective-permute-start.6 = (f32[4,3072]{1,0:T(4,128)S(1)}, f32[4,3072]{1,0:T(4,128)S(1)}, u32[]{:S(2)}, u32[]{:S(2)}) collective-permute-start(f32[4,3072]{1,0:T(4,128)S(1)} %get-tuple-element.70.after.ns), channel_id=1, source_target_pairs={{0,1},{1,0},{2,3},{3,2},{4,5},{5,4},{6,7},{7,6},{8,9},{9,8},{10,11... | collective-permute-start | bytes 147464 | tf_op jit(solution)/shard_map/ppermute | solution.py:515
  13.9 0.6 %outer.2 = (f32[17,2,3072]{2,1,0:T(2,128)S(1)}, f32[2,3072]{1,0:T(2,128)S(1)}, f32[4,3072]{1,0:T(4,128)S(1)}) custom-call(f32[2,16,3072]{2,1,0:T(8,128)S(1)} %get-tuple-element.63.base, f32[15,2,3072]{2,1,0:T(2,128)S(1)} %collective-permute-done.1.y, f32[4,3072]{1,0:T(4,128)S(1)} %get-tuple-element.70.after.ns, f32[3,16,1]{2,1,0:T(8,128)S(1)} %get-tuple-element.58.coef, ...), custom_call_target="tpu_custom_call" | custom-call | flops 4000000000 | bytes 1407168 | tf_op jit(solution)/shard_map/outer/pallas_call | solution.py:412
  14.5 2.4 %collective-permute-start.7 = (f32[17,2,3072]{2,1,0:T(2,128)S(1)}, f32[17,2,3072]{2,1,0:T(2,128)S(1)}, u32[]{:S(2)}, u32[]{:S(2)}) collective-permute-start(f32[17,2,3072]{2,1,0:T(2,128)S(1)} %get-tuple-element.74.part2), channel_id=1, source_target_pairs={{0,7},{1,2},{2,1},{3,4},{4,3},{5,6},{6,5},{7,0},{8,15},{9,10},{10,... | collective-permute-start | bytes 1253384 | tf_op jit(solution)/shard_map/ppermute | solution.py:487
  16.9 0.0 collective-permute-done.y
  16.9 0.5 %inner.2 = (f32[17,2,3072]{2,1,0:T(2,128)S(1)}, f32[2,3072]{1,0:T(2,128)S(1)}) custom-call(f32[2,16,3072]{2,1,0:T(8,128)S(1)} %get-tuple-element.62.base, f32[15,2,3072]{2,1,0:T(2,128)S(1)} %collective-permute-done.y, f32[2,3072]{1,0:T(2,128)S(1)} %get-tuple-element.72.after.part02, f32[3,16,1]{2,1,0:T(8,128)S(1)} %get-tuple-element.58.coef, ...), custom_call_target="tpu_custom_call" | custom-call | bytes 1333440 | tf_op jit(solution)/shard_map/inner/pallas_call | solution.py:412
  17.4 0.1 collective-permute-done.5.e2
  17.5 0.0 collective-permute-done.6.e1
  17.5 0.6 %hand.1 = (f32[4,3072]{1,0:T(4,128)S(1)}, f32[96,128]{1,0:T(8,128)S(1)}, f32[96,128]{1,0:T(8,128)S(1)}, f32[96,128]{1,0:T(8,128)S(1)}) custom-call(f32[4,3072]{1,0:T(4,128)S(1)} %get-tuple-element.78.own, f32[4,3072]{1,0:T(4,128)S(1)} %collective-permute-done.5.e2, f32[4,3072]{1,0:T(4,128)S(1)} %collective-permute-done.6.e1, ...), custom_call_target="tpu_custom_call" | custom-call | flops 20000000000 | bytes 1775808 | tf_op jit(solution)/shard_map/hand/pallas_call | solution.py:412
  18.1 3.6 %collective-permute-start.10 = (f32[96,128]{1,0:T(8,128)S(1)}, f32[96,128]{1,0:T(8,128)S(1)}, u32[]{:S(2)}, u32[]{:S(2)}) collective-permute-start(f32[96,128]{1,0:T(8,128)S(1)} %get-tuple-element.85), channel_id=1, source_target_pairs={{0,24},{1,25},{2,26},{3,27},{4,28},{5,29},{6,30},{7,31},{8,9},{9,8... | collective-permute-start | bytes 147464 | tf_op jit(solution)/shard_map/ppermute | solution.py:489
  21.7 0.0 collective-permute-start.8
  21.7 0.5 %collective-permute-start.9 = (f32[96,128]{1,0:T(8,128)S(1)}, f32[96,128]{1,0:T(8,128)S(1)}, u32[]{:S(2)}, u32[]{:S(2)}) collective-permute-start(f32[96,128]{1,0:T(8,128)S(1)} %get-tuple-element.84), channel_id=1, source_target_pairs={{0,1},{1,0},{2,3},{3,2},{4,5},{5,4},{6,7},{7,6},{8,9},{9,8},{10,11... | collective-permute-start | bytes 147464 | tf_op jit(solution)/shard_map/ppermute | solution.py:489
  22.2 0.0 collective-permute-start.13
  22.2 1.5 %evolve.1 = (f32[2,16,3072]{2,1,0:T(8,128)S(1)}, f32[2,16,3072]{2,1,0:T(8,128)S(1)}, f32[8,3072]{1,0:T(8,128)S(1)}) custom-call(f32[17,2,3072]{2,1,0:T(2,128)S(1)} %get-tuple-element.73.part1, f32[17,2,3072]{2,1,0:T(2,128)S(1)} %get-tuple-element.74.part2, f32[2,16,3072]{2,1,0:T(8,128)S(1)} %get-tuple-element.75.gain1, ...), custom_call_target="tpu_custom_call" | custom-call | bytes 2654400 | tf_op jit(solution)/shard_map/evolve/pallas_call | solution.py:412
  23.7 0.8 %collective-permute-done.10.refs_2_ = f32[96,128]{1,0:T(8,128)S(1)} collective-permute-done((f32[96,128]{1,0:T(8,128)S(1)}, f32[96,128]{1,0:T(8,128)S(1)}, u32[]{:S(2)}, u32[]{:S(2)}) %collective-permute-start.10) | collective-permute-done | bytes 49184 | tf_op jit(solution)/shard_map/ppermute | solution.py:489
  24.5 0.1 surface.3
  24.6 0.6 %collective-permute-start.11 = (f32[2,3072]{1,0:T(2,128)S(1)}, f32[2,3072]{1,0:T(2,128)S(1)}, u32[]{:S(2)}, u32[]{:S(2)}) collective-permute-start(f32[2,3072]{1,0:T(2,128)S(1)} %get-tuple-element.90), channel_id=1, source_target_pairs={{0,7},{1,2},{2,1},{3,4},{4,3},{5,6},{6,5},{7,0},{8,15},{9,10},{10,... | collective-permute-start | bytes 73736 | tf_op jit(solution)/shard_map/ppermute | solution.py:516
  25.2 1.7 %collective-permute-done.7.y = f32[17,2,3072]{2,1,0:T(2,128)S(1)} collective-permute-done((f32[17,2,3072]{2,1,0:T(2,128)S(1)}, f32[17,2,3072]{2,1,0:T(2,128)S(1)}, u32[]{:S(2)}, u32[]{:S(2)}) %collective-permute-start.7) | collective-permute-done | bytes 417824 | tf_op jit(solution)/shard_map/ppermute | solution.py:487
  26.9 0.7 %outer.3 = (f32[2,16,3072]{2,1,0:T(8,128)S(1)}, f32[2,3072]{1,0:T(2,128)S(1)}, f32[4,3072]{1,0:T(4,128)S(1)}) custom-call(f32[2,16,3072]{2,1,0:T(8,128)S(1)} %get-tuple-element.77.base, f32[17,2,3072]{2,1,0:T(2,128)S(1)} %collective-permute-done.7.y, f32[4,3072]{1,0:T(4,128)S(1)} %get-tuple-element.87.after, f32[3,16,1]{2,1,0:T(8,128)S(1)} %get-tuple-element.58.coef, ...), custom_call_target="tpu_custom_call" | custom-call | flops 4000000000 | bytes 1530304 | tf_op jit(solution)/shard_map/outer/pallas_call | solution.py:412
  27.6 0.6 %inner.3 = (f32[2,16,3072]{2,1,0:T(8,128)S(1)}, f32[2,3072]{1,0:T(2,128)S(1)}) custom-call(f32[2,16,3072]{2,1,0:T(8,128)S(1)} %get-tuple-element.92.base, f32[17,2,3072]{2,1,0:T(2,128)S(1)} %collective-permute-done.13.y, f32[2,3072]{1,0:T(2,128)S(1)} %get-tuple-element.93.after.part02, f32[3,16,1]{2,1,0:T(8,128)S(1)} %get-tuple-element.58.coef, ...), custom_call_target="tpu_custom_call" | custom-call | bytes 1456576 | tf_op jit(solution)/shard_map/inner/pallas_call | solution.py:412
  28.2 0.7 %collective-permute-done.11.e2 = f32[2,3072]{1,0:T(2,128)S(1)} collective-permute-done((f32[2,3072]{1,0:T(2,128)S(1)}, f32[2,3072]{1,0:T(2,128)S(1)}, u32[]{:S(2)}, u32[]{:S(2)}) %collective-permute-start.11) | collective-permute-done | bytes 24608 | tf_op jit(solution)/shard_map/ppermute | solution.py:516
  29.0 1.3 %close.1 = (f32[1,16,4,3072]{3,2,1,0:T(4,128)}, f32[1,4,3072]{2,1,0:T(4,128)}) custom-call(f32[4,3072]{1,0:T(4,128)S(1)} %get-tuple-element.89.own, f32[2,3072]{1,0:T(2,128)S(1)} %collective-permute-done.11.e2, f32[2,3072]{1,0:T(2,128)S(1)} %collective-permute-done.12.e1, f32[3,16,1]{2,1,0:T(8,128)S(1)} %get-tuple-element.58.coef, ...), custom_call_target="tpu_custom_call" | custom-call | bytes 2703552 | tf_op jit(solution)/shard_map/close/pallas_call | solution.py:412
  (9 shorter events, 0.1 us)
Async XLA Ops:
  2.0 11.9 %collective-permute-start.1 = (f32[15,2,3072]{2,1,0:T(2,128)S(1)}, f32[15,2,3072]{2,1,0:T(2,128)S(1)}, u32[]{:S(2)}, u32[]{:S(2)}) collective-permute-start(f32[15,2,3072]{2,1,0:T(2,128)S(1)} %get-tuple-element.51.x2), channel_id=1, source_target_pairs={{0,7},{1,2},{2,1},{3,4},{4,3},{5,6},{6,5},{7,0},{8,15},{9,10},{10,... | collective-permute-start | bytes 1105928 | tf_op jit(solution)/shard_map/ppermute | solution.py:487
  6.1 6.6 %collective-permute-start.2 = (f32[96,128]{1,0:T(8,128)S(1)}, f32[96,128]{1,0:T(8,128)S(1)}, u32[]{:S(2)}, u32[]{:S(2)}) collective-permute-start(f32[96,128]{1,0:T(8,128)S(1)} %get-tuple-element.64), channel_id=1, source_target_pairs={{0,24},{1,25},{2,26},{3,27},{4,28},{5,29},{6,30},{7,31},{8,9},{9,8... | collective-permute-start | bytes 147464 | tf_op jit(solution)/shard_map/ppermute | solution.py:489
  9.8 2.9 %collective-permute-start.3 = (f32[96,128]{1,0:T(8,128)S(1)}, f32[96,128]{1,0:T(8,128)S(1)}, u32[]{:S(2)}, u32[]{:S(2)}) collective-permute-start(f32[96,128]{1,0:T(8,128)S(1)} %get-tuple-element.65), channel_id=1, source_target_pairs={{0,1},{1,0},{2,3},{3,2},{4,5},{5,4},{6,7},{7,6},{8,24},{9,25},{10,... | collective-permute-start | bytes 147464 | tf_op jit(solution)/shard_map/ppermute | solution.py:489
  9.8 2.9 %collective-permute-start.4 = (f32[96,128]{1,0:T(8,128)S(1)}, f32[96,128]{1,0:T(8,128)S(1)}, u32[]{:S(2)}, u32[]{:S(2)}) collective-permute-start(f32[96,128]{1,0:T(8,128)S(1)} %get-tuple-element.66), channel_id=1, source_target_pairs={{0,1},{1,0},{2,3},{3,2},{4,5},{5,4},{6,7},{7,6},{8,9},{9,8},{10,11... | collective-permute-start | bytes 147464 | tf_op jit(solution)/shard_map/ppermute | solution.py:489
  10.3 6.6 %collective-permute-start = (f32[15,2,3072]{2,1,0:T(2,128)S(1)}, f32[15,2,3072]{2,1,0:T(2,128)S(1)}, u32[]{:S(2)}, u32[]{:S(2)}) collective-permute-start(f32[15,2,3072]{2,1,0:T(2,128)S(1)} %get-tuple-element.50.x1), channel_id=1, source_target_pairs={{0,1},{1,0},{2,3},{3,2},{4,5},{5,4},{6,7},{7,6},{8,9},{9,8},{10,11... | collective-permute-start | bytes 1105928 | tf_op jit(solution)/shard_map/ppermute | solution.py:486
  12.8 4.7 %collective-permute-start.5 = (f32[4,3072]{1,0:T(4,128)S(1)}, f32[4,3072]{1,0:T(4,128)S(1)}, u32[]{:S(2)}, u32[]{:S(2)}) collective-permute-start(f32[4,3072]{1,0:T(4,128)S(1)} %get-tuple-element.70.after.ns), channel_id=1, source_target_pairs={{0,7},{1,2},{2,1},{3,4},{4,3},{5,6},{6,5},{7,0},{8,15},{9,10},{10,... | collective-permute-start | bytes 147464 | tf_op jit(solution)/shard_map/ppermute | solution.py:516
  13.5 4.0 %collective-permute-start.6 = (f32[4,3072]{1,0:T(4,128)S(1)}, f32[4,3072]{1,0:T(4,128)S(1)}, u32[]{:S(2)}, u32[]{:S(2)}) collective-permute-start(f32[4,3072]{1,0:T(4,128)S(1)} %get-tuple-element.70.after.ns), channel_id=1, source_target_pairs={{0,1},{1,0},{2,3},{3,2},{4,5},{5,4},{6,7},{7,6},{8,9},{9,8},{10,11... | collective-permute-start | bytes 147464 | tf_op jit(solution)/shard_map/ppermute | solution.py:515
  14.5 12.4 %collective-permute-start.7 = (f32[17,2,3072]{2,1,0:T(2,128)S(1)}, f32[17,2,3072]{2,1,0:T(2,128)S(1)}, u32[]{:S(2)}, u32[]{:S(2)}) collective-permute-start(f32[17,2,3072]{2,1,0:T(2,128)S(1)} %get-tuple-element.74.part2), channel_id=1, source_target_pairs={{0,7},{1,2},{2,1},{3,4},{4,3},{5,6},{6,5},{7,0},{8,15},{9,10},{10,... | collective-permute-start | bytes 1253384 | tf_op jit(solution)/shard_map/ppermute | solution.py:487
  18.1 6.4 %collective-permute-start.10 = (f32[96,128]{1,0:T(8,128)S(1)}, f32[96,128]{1,0:T(8,128)S(1)}, u32[]{:S(2)}, u32[]{:S(2)}) collective-permute-start(f32[96,128]{1,0:T(8,128)S(1)} %get-tuple-element.85), channel_id=1, source_target_pairs={{0,24},{1,25},{2,26},{3,27},{4,28},{5,29},{6,30},{7,31},{8,9},{9,8... | collective-permute-start | bytes 147464 | tf_op jit(solution)/shard_map/ppermute | solution.py:489
  21.7 2.8 %collective-permute-start.8 = (f32[96,128]{1,0:T(8,128)S(1)}, f32[96,128]{1,0:T(8,128)S(1)}, u32[]{:S(2)}, u32[]{:S(2)}) collective-permute-start(f32[96,128]{1,0:T(8,128)S(1)} %get-tuple-element.83), channel_id=1, source_target_pairs={{0,1},{1,0},{2,3},{3,2},{4,5},{5,4},{6,7},{7,6},{8,24},{9,25},{10,... | collective-permute-start | bytes 147464 | tf_op jit(solution)/shard_map/ppermute | solution.py:489
  21.7 2.8 %collective-permute-start.9 = (f32[96,128]{1,0:T(8,128)S(1)}, f32[96,128]{1,0:T(8,128)S(1)}, u32[]{:S(2)}, u32[]{:S(2)}) collective-permute-start(f32[96,128]{1,0:T(8,128)S(1)} %get-tuple-element.84), channel_id=1, source_target_pairs={{0,1},{1,0},{2,3},{3,2},{4,5},{5,4},{6,7},{7,6},{8,9},{9,8},{10,11... | collective-permute-start | bytes 147464 | tf_op jit(solution)/shard_map/ppermute | solution.py:489
  22.2 5.3 %collective-permute-start.13 = (f32[17,2,3072]{2,1,0:T(2,128)S(1)}, f32[17,2,3072]{2,1,0:T(2,128)S(1)}, u32[]{:S(2)}, u32[]{:S(2)}) collective-permute-start(f32[17,2,3072]{2,1,0:T(2,128)S(1)} %get-tuple-element.73.part1), channel_id=1, source_target_pairs={{0,1},{1,0},{2,3},{3,2},{4,5},{5,4},{6,7},{7,6},{8,9},{9,8},{10,11... | collective-permute-start | bytes 1253384 | tf_op jit(solution)/shard_map/ppermute | solution.py:486
  24.6 4.4 %collective-permute-start.11 = (f32[2,3072]{1,0:T(2,128)S(1)}, f32[2,3072]{1,0:T(2,128)S(1)}, u32[]{:S(2)}, u32[]{:S(2)}) collective-permute-start(f32[2,3072]{1,0:T(2,128)S(1)} %get-tuple-element.90), channel_id=1, source_target_pairs={{0,7},{1,2},{2,1},{3,4},{4,3},{5,6},{6,5},{7,0},{8,15},{9,10},{10,... | collective-permute-start | bytes 73736 | tf_op jit(solution)/shard_map/ppermute | solution.py:516
  25.2 3.7 %collective-permute-start.12 = (f32[2,3072]{1,0:T(2,128)S(1)}, f32[2,3072]{1,0:T(2,128)S(1)}, u32[]{:S(2)}, u32[]{:S(2)}) collective-permute-start(f32[2,3072]{1,0:T(2,128)S(1)} %get-tuple-element.91), channel_id=1, source_target_pairs={{0,1},{1,0},{2,3},{3,2},{4,5},{5,4},{6,7},{7,6},{8,9},{9,8},{10,11... | collective-permute-start | bytes 73736 | tf_op jit(solution)/shard_map/ppermute | solution.py:515

commit v11 on v9

--- a/solution.py
+++ b/solution.py
@@ -112,16 +112,16 @@
     x1, x2, surface, pick, chosen, targets_v, coupling_v, weights_v, state_v, sources_v, sems = refs
     copies = copy_all(
         (
-            (state, state_v),
             (sources, sources_v),
             (targets, targets_v),
+            (state, state_v),
             (coupling, coupling_v),
             (weights, weights_v),
         ),
         sems,
     )
+    copies[0].wait()
     copies[1].wait()
-    copies[2].wait()
     count, margins = pick.shape
     slot = lax.broadcasted_iota(jnp.int32, (count, margins), 0)
     pick[...] = (slot == sources_v[...]).astype(F32).astype(BF16)
@@ -132,7 +132,7 @@
         partner = jnp.where(me < air_count, ocean, MEMBERS * (me - air_count) + n)
         hit = (targets_v[...] == slot + partner * count).astype(F32).astype(BF16)
         chosen[n * count : (n + 1) * count] = jnp.concatenate([hit, hit], axis=1)
-    copies[0].wait()
+    copies[2].wait()
     for ref, half in zip((x1, x2), halves_of([state_v[0, 1:, r, :] for r in range(state_v.shape[2])])):
         for i, value in enumerate(half):
             ref[:, i, :] = value

time: 30.4 us -> 30.4 us (level)
  no operation moved by 1% of the time
where the time goes in v11:
time: 30.4 us; the launch traced here: 30.2 us
  starting transfers between devices  15.8 us (52%)
  Pallas kernels  10.3 us (34%)
  waiting for transfers between devices  3.33 us (11%)
  between operations  0.76 us (2%)
    pallas_call x13, Pallas kernels, call(): pl.pallas_call(kernel, name=name, out_shape=outs, in_specs=in_specs or [V...  10.3 us
    ppermute x6, starting transfers between devices, on_device(): lax.ppermute(value, ('comp', 'tile'), partner_pairs(groups, tiles, member))  8.28 us
    ppermute x2, starting transfers between devices, on_device(): y2 = lax.ppermute(x2, 'tile', outer_pairs(tiles))  5.8 us
    ppermute x2, waiting for transfers between devices, on_device(): y2 = lax.ppermute(x2, 'tile', outer_pairs(tiles))  1.66 us
    ppermute x2, starting transfers between devices, on_device(): e2 = lax.ppermute(d2, 'tile', outer_pairs(tiles))  1.39 us
    ppermute x2, waiting for transfers between devices, on_device(): e2 = lax.ppermute(d2, 'tile', outer_pairs(tiles))  0.85 us
    ppermute x6, waiting for transfers between devices, on_device(): lax.ppermute(value, ('comp', 'tile'), partner_pairs(groups, tiles, member))  0.81 us
  transfers between devices with their start and end apart: 14, of which 4 were waited for; matrix products, arithmetic and copies ran while one was open for 0% of the time, Pallas kernels for 25%

profile of v11, /device:TPU:0, one launch (start us, length us, event | category | flops | bytes accessed | tf_op | source)
XLA Modules:
  0.0 30.2 jit_solution(13388802817901562470)
XLA Ops:
  0.6 1.4 %load.1 = (f32[15,2,3072]{2,1,0:T(2,128)S(1)}, f32[15,2,3072]{2,1,0:T(2,128)S(1)}, f32[4,3072]{1,0:T(4,128)S(1)}, bf16[96,288]{1,0:T(8,128)(2,1)S(1)}, bf16[288,...) custom-call(f32[1,16,4,3072]{3,2,1,0:T(4,128)} %state.1, ...), custom_call_target="tpu_custom_call" | custom-call | bytes 3241344 | tf_op jit(solution)/shard_map/load/pallas_call | solution.py:412
  2.0 3.4 %collective-permute-start.1 = (f32[15,2,3072]{2,1,0:T(2,128)S(1)}, f32[15,2,3072]{2,1,0:T(2,128)S(1)}, u32[]{:S(2)}, u32[]{:S(2)}) collective-permute-start(f32[15,2,3072]{2,1,0:T(2,128)S(1)} %get-tuple-element.51.x2), channel_id=1, source_target_pairs={{0,7},{1,2},{2,1},{3,4},{4,3},{5,6},{6,5},{7,0},{8,15},{9,10},{10,... | collective-permute-start | bytes 1105928 | tf_op jit(solution)/shard_map/ppermute | solution.py:487
  5.4 0.7 %remap.1 = (f32[2304,128]{1,0:T(8,128)S(1)}, f32[96,128]{1,0:T(8,128)S(1)}, f32[96,128]{1,0:T(8,128)S(1)}, f32[96,128]{1,0:T(8,128)S(1)}) custom-call(f32[1,4,3072]{2,1,0:T(4,128)S(1)} %get-tuple-element.53.coupling, bf16[1,288,8,128]{3,2,1,0:T(8,128)(2,1)S(1)} %get-tuple-element.54.weights, bf16[96,288]{1,0:T(8,128)(2,1)S(1)} %get-tuple-element.55.pick, ...), custom_call_target="tpu_custom_call" | custom-call | bytes 2353152 | tf_op jit(solution)/shard_map/remap/pallas_call | solution.py:412
  6.1 3.7 %collective-permute-start.2 = (f32[96,128]{1,0:T(8,128)S(1)}, f32[96,128]{1,0:T(8,128)S(1)}, u32[]{:S(2)}, u32[]{:S(2)}) collective-permute-start(f32[96,128]{1,0:T(8,128)S(1)} %get-tuple-element.64), channel_id=1, source_target_pairs={{0,24},{1,25},{2,26},{3,27},{4,28},{5,29},{6,30},{7,31},{8,9},{9,8... | collective-permute-start | bytes 147464 | tf_op jit(solution)/shard_map/ppermute | solution.py:489
  9.8 0.5 %collective-permute-start.4 = (f32[96,128]{1,0:T(8,128)S(1)}, f32[96,128]{1,0:T(8,128)S(1)}, u32[]{:S(2)}, u32[]{:S(2)}) collective-permute-start(f32[96,128]{1,0:T(8,128)S(1)} %get-tuple-element.66), channel_id=1, source_target_pairs={{0,1},{1,0},{2,3},{3,2},{4,5},{5,4},{6,7},{7,6},{8,9},{9,8},{10,11... | collective-permute-start | bytes 147464 | tf_op jit(solution)/shard_map/ppermute | solution.py:489
  10.3 0.0 collective-permute-start
  10.3 1.0 %sort.1 = (f32[8,288,128]{2,1,0:T(8,128)S(1)}, bf16[288,96]{1,0:T(8,128)(2,1)S(1)}, s32[1,4,3072]{2,1,0:T(4,128)S(1)}, s32[1,4,3072]{2,1,0:T(4,128)S(1)}, f32[4,...) custom-call(s32[1,288]{1,0:T(1,128)S(1)} %get-tuple-element.52.targets, ...), custom_call_target="tpu_custom_call" | custom-call | bytes 2727616 | tf_op jit(solution)/shard_map/sort/pallas_call | solution.py:412
  11.3 1.4 %start.1 = (f32[2,16,3072]{2,1,0:T(8,128)S(1)}, f32[2,16,3072]{2,1,0:T(8,128)S(1)}, f32[2,16,3072]{2,1,0:T(8,128)S(1)}, f32[2,16,3072]{2,1,0:T(8,128)S(1)}, f32[4,3072]{1,0:T(4,128)S(1)}) custom-call(f32[15,2,3072]{2,1,0:T(2,128)S(1)} %get-tuple-element.50.x1, f32[15,2,3072]{2,1,0:T(2,128)S(1)} %get-tuple-element.51.x2, ...), custom_call_target="tpu_custom_call" | custom-call | bytes 2458048 | tf_op jit(solution)/shard_map/start/pallas_call | solution.py:412
  12.7 0.0 collective-permute-done.2.refs_0_
  12.7 0.0 collective-permute-done.3.refs_1_
  12.8 0.8 %collective-permute-start.5 = (f32[4,3072]{1,0:T(4,128)S(1)}, f32[4,3072]{1,0:T(4,128)S(1)}, u32[]{:S(2)}, u32[]{:S(2)}) collective-permute-start(f32[4,3072]{1,0:T(4,128)S(1)} %get-tuple-element.70.after.ns), channel_id=1, source_target_pairs={{0,7},{1,2},{2,1},{3,4},{4,3},{5,6},{6,5},{7,0},{8,15},{9,10},{10,... | collective-permute-start | bytes 147464 | tf_op jit(solution)/shard_map/ppermute | solution.py:516
  13.5 0.4 %collective-permute-start.6 = (f32[4,3072]{1,0:T(4,128)S(1)}, f32[4,3072]{1,0:T(4,128)S(1)}, u32[]{:S(2)}, u32[]{:S(2)}) collective-permute-start(f32[4,3072]{1,0:T(4,128)S(1)} %get-tuple-element.70.after.ns), channel_id=1, source_target_pairs={{0,1},{1,0},{2,3},{3,2},{4,5},{5,4},{6,7},{7,6},{8,9},{9,8},{10,11... | collective-permute-start | bytes 147464 | tf_op jit(solution)/shard_map/ppermute | solution.py:515
  13.9 0.6 %outer.2 = (f32[17,2,3072]{2,1,0:T(2,128)S(1)}, f32[2,3072]{1,0:T(2,128)S(1)}, f32[4,3072]{1,0:T(4,128)S(1)}) custom-call(f32[2,16,3072]{2,1,0:T(8,128)S(1)} %get-tuple-element.63.base, f32[15,2,3072]{2,1,0:T(2,128)S(1)} %collective-permute-done.1.y, f32[4,3072]{1,0:T(4,128)S(1)} %get-tuple-element.70.after.ns, f32[3,16,1]{2,1,0:T(8,128)S(1)} %get-tuple-element.58.coef, ...), custom_call_target="tpu_custom_call" | custom-call | flops 4000000000 | bytes 1407168 | tf_op jit(solution)/shard_map/outer/pallas_call | solution.py:412
  14.5 2.4 %collective-permute-start.7 = (f32[17,2,3072]{2,1,0:T(2,128)S(1)}, f32[17,2,3072]{2,1,0:T(2,128)S(1)}, u32[]{:S(2)}, u32[]{:S(2)}) collective-permute-start(f32[17,2,3072]{2,1,0:T(2,128)S(1)} %get-tuple-element.74.part2), channel_id=1, source_target_pairs={{0,7},{1,2},{2,1},{3,4},{4,3},{5,6},{6,5},{7,0},{8,15},{9,10},{10,... | collective-permute-start | bytes 1253384 | tf_op jit(solution)/shard_map/ppermute | solution.py:487
  16.9 0.0 collective-permute-done.y
  16.9 0.5 %inner.2 = (f32[17,2,3072]{2,1,0:T(2,128)S(1)}, f32[2,3072]{1,0:T(2,128)S(1)}) custom-call(f32[2,16,3072]{2,1,0:T(8,128)S(1)} %get-tuple-element.62.base, f32[15,2,3072]{2,1,0:T(2,128)S(1)} %collective-permute-done.y, f32[2,3072]{1,0:T(2,128)S(1)} %get-tuple-element.72.after.part02, f32[3,16,1]{2,1,0:T(8,128)S(1)} %get-tuple-element.58.coef, ...), custom_call_target="tpu_custom_call" | custom-call | bytes 1333440 | tf_op jit(solution)/shard_map/inner/pallas_call | solution.py:412
  17.4 0.1 collective-permute-done.5.e2
  17.5 0.0 collective-permute-done.6.e1
  17.5 0.6 %hand.1 = (f32[4,3072]{1,0:T(4,128)S(1)}, f32[96,128]{1,0:T(8,128)S(1)}, f32[96,128]{1,0:T(8,128)S(1)}, f32[96,128]{1,0:T(8,128)S(1)}) custom-call(f32[4,3072]{1,0:T(4,128)S(1)} %get-tuple-element.78.own, f32[4,3072]{1,0:T(4,128)S(1)} %collective-permute-done.5.e2, f32[4,3072]{1,0:T(4,128)S(1)} %collective-permute-done.6.e1, ...), custom_call_target="tpu_custom_call" | custom-call | flops 20000000000 | bytes 1775808 | tf_op jit(solution)/shard_map/hand/pallas_call | solution.py:412
  18.1 3.6 %collective-permute-start.10 = (f32[96,128]{1,0:T(8,128)S(1)}, f32[96,128]{1,0:T(8,128)S(1)}, u32[]{:S(2)}, u32[]{:S(2)}) collective-permute-start(f32[96,128]{1,0:T(8,128)S(1)} %get-tuple-element.85), channel_id=1, source_target_pairs={{0,24},{1,25},{2,26},{3,27},{4,28},{5,29},{6,30},{7,31},{8,9},{9,8... | collective-permute-start | bytes 147464 | tf_op jit(solution)/shard_map/ppermute | solution.py:489
  21.7 0.0 collective-permute-start.8
  21.7 0.5 %collective-permute-start.9 = (f32[96,128]{1,0:T(8,128)S(1)}, f32[96,128]{1,0:T(8,128)S(1)}, u32[]{:S(2)}, u32[]{:S(2)}) collective-permute-start(f32[96,128]{1,0:T(8,128)S(1)} %get-tuple-element.84), channel_id=1, source_target_pairs={{0,1},{1,0},{2,3},{3,2},{4,5},{5,4},{6,7},{7,6},{8,9},{9,8},{10,11... | collective-permute-start | bytes 147464 | tf_op jit(solution)/shard_map/ppermute | solution.py:489
  22.2 0.0 collective-permute-start.13
  22.2 1.5 %evolve.1 = (f32[2,16,3072]{2,1,0:T(8,128)S(1)}, f32[2,16,3072]{2,1,0:T(8,128)S(1)}, f32[8,3072]{1,0:T(8,128)S(1)}) custom-call(f32[17,2,3072]{2,1,0:T(2,128)S(1)} %get-tuple-element.73.part1, f32[17,2,3072]{2,1,0:T(2,128)S(1)} %get-tuple-element.74.part2, f32[2,16,3072]{2,1,0:T(8,128)S(1)} %get-tuple-element.75.gain1, ...), custom_call_target="tpu_custom_call" | custom-call | bytes 2654400 | tf_op jit(solution)/shard_map/evolve/pallas_call | solution.py:412
  23.7 0.8 %collective-permute-done.10.refs_2_ = f32[96,128]{1,0:T(8,128)S(1)} collective-permute-done((f32[96,128]{1,0:T(8,128)S(1)}, f32[96,128]{1,0:T(8,128)S(1)}, u32[]{:S(2)}, u32[]{:S(2)}) %collective-permute-start.10) | collective-permute-done | bytes 49184 | tf_op jit(solution)/shard_map/ppermute | solution.py:489
  24.5 0.1 surface.3
  24.6 0.6 %collective-permute-start.11 = (f32[2,3072]{1,0:T(2,128)S(1)}, f32[2,3072]{1,0:T(2,128)S(1)}, u32[]{:S(2)}, u32[]{:S(2)}) collective-permute-start(f32[2,3072]{1,0:T(2,128)S(1)} %get-tuple-element.90), channel_id=1, source_target_pairs={{0,7},{1,2},{2,1},{3,4},{4,3},{5,6},{6,5},{7,0},{8,15},{9,10},{10,... | collective-permute-start | bytes 73736 | tf_op jit(solution)/shard_map/ppermute | solution.py:516
  25.2 1.7 %collective-permute-done.7.y = f32[17,2,3072]{2,1,0:T(2,128)S(1)} collective-permute-done((f32[17,2,3072]{2,1,0:T(2,128)S(1)}, f32[17,2,3072]{2,1,0:T(2,128)S(1)}, u32[]{:S(2)}, u32[]{:S(2)}) %collective-permute-start.7) | collective-permute-done | bytes 417824 | tf_op jit(solution)/shard_map/ppermute | solution.py:487
  26.9 0.7 %outer.3 = (f32[2,16,3072]{2,1,0:T(8,128)S(1)}, f32[2,3072]{1,0:T(2,128)S(1)}, f32[4,3072]{1,0:T(4,128)S(1)}) custom-call(f32[2,16,3072]{2,1,0:T(8,128)S(1)} %get-tuple-element.77.base, f32[17,2,3072]{2,1,0:T(2,128)S(1)} %collective-permute-done.7.y, f32[4,3072]{1,0:T(4,128)S(1)} %get-tuple-element.87.after, f32[3,16,1]{2,1,0:T(8,128)S(1)} %get-tuple-element.58.coef, ...), custom_call_target="tpu_custom_call" | custom-call | flops 4000000000 | bytes 1530304 | tf_op jit(solution)/shard_map/outer/pallas_call | solution.py:412
  27.6 0.6 %inner.3 = (f32[2,16,3072]{2,1,0:T(8,128)S(1)}, f32[2,3072]{1,0:T(2,128)S(1)}) custom-call(f32[2,16,3072]{2,1,0:T(8,128)S(1)} %get-tuple-element.92.base, f32[17,2,3072]{2,1,0:T(2,128)S(1)} %collective-permute-done.13.y, f32[2,3072]{1,0:T(2,128)S(1)} %get-tuple-element.93.after.part02, f32[3,16,1]{2,1,0:T(8,128)S(1)} %get-tuple-element.58.coef, ...), custom_call_target="tpu_custom_call" | custom-call | bytes 1456576 | tf_op jit(solution)/shard_map/inner/pallas_call | solution.py:412
  28.2 0.7 %collective-permute-done.11.e2 = f32[2,3072]{1,0:T(2,128)S(1)} collective-permute-done((f32[2,3072]{1,0:T(2,128)S(1)}, f32[2,3072]{1,0:T(2,128)S(1)}, u32[]{:S(2)}, u32[]{:S(2)}) %collective-permute-start.11) | collective-permute-done | bytes 24608 | tf_op jit(solution)/shard_map/ppermute | solution.py:516
  29.0 1.3 %close.1 = (f32[1,16,4,3072]{3,2,1,0:T(4,128)}, f32[1,4,3072]{2,1,0:T(4,128)}) custom-call(f32[4,3072]{1,0:T(4,128)S(1)} %get-tuple-element.89.own, f32[2,3072]{1,0:T(2,128)S(1)} %collective-permute-done.11.e2, f32[2,3072]{1,0:T(2,128)S(1)} %collective-permute-done.12.e1, f32[3,16,1]{2,1,0:T(8,128)S(1)} %get-tuple-element.58.coef, ...), custom_call_target="tpu_custom_call" | custom-call | bytes 2703552 | tf_op jit(solution)/shard_map/close/pallas_call | solution.py:412
  (9 shorter events, 0.1 us)
Async XLA Ops:
  2.0 11.9 %collective-permute-start.1 = (f32[15,2,3072]{2,1,0:T(2,128)S(1)}, f32[15,2,3072]{2,1,0:T(2,128)S(1)}, u32[]{:S(2)}, u32[]{:S(2)}) collective-permute-start(f32[15,2,3072]{2,1,0:T(2,128)S(1)} %get-tuple-element.51.x2), channel_id=1, source_target_pairs={{0,7},{1,2},{2,1},{3,4},{4,3},{5,6},{6,5},{7,0},{8,15},{9,10},{10,... | collective-permute-start | bytes 1105928 | tf_op jit(solution)/shard_map/ppermute | solution.py:487
  6.1 6.6 %collective-permute-start.2 = (f32[96,128]{1,0:T(8,128)S(1)}, f32[96,128]{1,0:T(8,128)S(1)}, u32[]{:S(2)}, u32[]{:S(2)}) collective-permute-start(f32[96,128]{1,0:T(8,128)S(1)} %get-tuple-element.64), channel_id=1, source_target_pairs={{0,24},{1,25},{2,26},{3,27},{4,28},{5,29},{6,30},{7,31},{8,9},{9,8... | collective-permute-start | bytes 147464 | tf_op jit(solution)/shard_map/ppermute | solution.py:489
  9.8 2.9 %collective-permute-start.3 = (f32[96,128]{1,0:T(8,128)S(1)}, f32[96,128]{1,0:T(8,128)S(1)}, u32[]{:S(2)}, u32[]{:S(2)}) collective-permute-start(f32[96,128]{1,0:T(8,128)S(1)} %get-tuple-element.65), channel_id=1, source_target_pairs={{0,1},{1,0},{2,3},{3,2},{4,5},{5,4},{6,7},{7,6},{8,24},{9,25},{10,... | collective-permute-start | bytes 147464 | tf_op jit(solution)/shard_map/ppermute | solution.py:489
  9.8 2.9 %collective-permute-start.4 = (f32[96,128]{1,0:T(8,128)S(1)}, f32[96,128]{1,0:T(8,128)S(1)}, u32[]{:S(2)}, u32[]{:S(2)}) collective-permute-start(f32[96,128]{1,0:T(8,128)S(1)} %get-tuple-element.66), channel_id=1, source_target_pairs={{0,1},{1,0},{2,3},{3,2},{4,5},{5,4},{6,7},{7,6},{8,9},{9,8},{10,11... | collective-permute-start | bytes 147464 | tf_op jit(solution)/shard_map/ppermute | solution.py:489
  10.3 6.6 %collective-permute-start = (f32[15,2,3072]{2,1,0:T(2,128)S(1)}, f32[15,2,3072]{2,1,0:T(2,128)S(1)}, u32[]{:S(2)}, u32[]{:S(2)}) collective-permute-start(f32[15,2,3072]{2,1,0:T(2,128)S(1)} %get-tuple-element.50.x1), channel_id=1, source_target_pairs={{0,1},{1,0},{2,3},{3,2},{4,5},{5,4},{6,7},{7,6},{8,9},{9,8},{10,11... | collective-permute-start | bytes 1105928 | tf_op jit(solution)/shard_map/ppermute | solution.py:486
  12.8 4.7 %collective-permute-start.5 = (f32[4,3072]{1,0:T(4,128)S(1)}, f32[4,3072]{1,0:T(4,128)S(1)}, u32[]{:S(2)}, u32[]{:S(2)}) collective-permute-start(f32[4,3072]{1,0:T(4,128)S(1)} %get-tuple-element.70.after.ns), channel_id=1, source_target_pairs={{0,7},{1,2},{2,1},{3,4},{4,3},{5,6},{6,5},{7,0},{8,15},{9,10},{10,... | collective-permute-start | bytes 147464 | tf_op jit(solution)/shard_map/ppermute | solution.py:516
  13.5 4.0 %collective-permute-start.6 = (f32[4,3072]{1,0:T(4,128)S(1)}, f32[4,3072]{1,0:T(4,128)S(1)}, u32[]{:S(2)}, u32[]{:S(2)}) collective-permute-start(f32[4,3072]{1,0:T(4,128)S(1)} %get-tuple-element.70.after.ns), channel_id=1, source_target_pairs={{0,1},{1,0},{2,3},{3,2},{4,5},{5,4},{6,7},{7,6},{8,9},{9,8},{10,11... | collective-permute-start | bytes 147464 | tf_op jit(solution)/shard_map/ppermute | solution.py:515
  14.5 12.4 %collective-permute-start.7 = (f32[17,2,3072]{2,1,0:T(2,128)S(1)}, f32[17,2,3072]{2,1,0:T(2,128)S(1)}, u32[]{:S(2)}, u32[]{:S(2)}) collective-permute-start(f32[17,2,3072]{2,1,0:T(2,128)S(1)} %get-tuple-element.74.part2), channel_id=1, source_target_pairs={{0,7},{1,2},{2,1},{3,4},{4,3},{5,6},{6,5},{7,0},{8,15},{9,10},{10,... | collective-permute-start | bytes 1253384 | tf_op jit(solution)/shard_map/ppermute | solution.py:487
  18.1 6.4 %collective-permute-start.10 = (f32[96,128]{1,0:T(8,128)S(1)}, f32[96,128]{1,0:T(8,128)S(1)}, u32[]{:S(2)}, u32[]{:S(2)}) collective-permute-start(f32[96,128]{1,0:T(8,128)S(1)} %get-tuple-element.85), channel_id=1, source_target_pairs={{0,24},{1,25},{2,26},{3,27},{4,28},{5,29},{6,30},{7,31},{8,9},{9,8... | collective-permute-start | bytes 147464 | tf_op jit(solution)/shard_map/ppermute | solution.py:489
  21.7 2.8 %collective-permute-start.8 = (f32[96,128]{1,0:T(8,128)S(1)}, f32[96,128]{1,0:T(8,128)S(1)}, u32[]{:S(2)}, u32[]{:S(2)}) collective-permute-start(f32[96,128]{1,0:T(8,128)S(1)} %get-tuple-element.83), channel_id=1, source_target_pairs={{0,1},{1,0},{2,3},{3,2},{4,5},{5,4},{6,7},{7,6},{8,24},{9,25},{10,... | collective-permute-start | bytes 147464 | tf_op jit(solution)/shard_map/ppermute | solution.py:489
  21.7 2.8 %collective-permute-start.9 = (f32[96,128]{1,0:T(8,128)S(1)}, f32[96,128]{1,0:T(8,128)S(1)}, u32[]{:S(2)}, u32[]{:S(2)}) collective-permute-start(f32[96,128]{1,0:T(8,128)S(1)} %get-tuple-element.84), channel_id=1, source_target_pairs={{0,1},{1,0},{2,3},{3,2},{4,5},{5,4},{6,7},{7,6},{8,9},{9,8},{10,11... | collective-permute-start | bytes 147464 | tf_op jit(solution)/shard_map/ppermute | solution.py:489
  22.2 5.3 %collective-permute-start.13 = (f32[17,2,3072]{2,1,0:T(2,128)S(1)}, f32[17,2,3072]{2,1,0:T(2,128)S(1)}, u32[]{:S(2)}, u32[]{:S(2)}) collective-permute-start(f32[17,2,3072]{2,1,0:T(2,128)S(1)} %get-tuple-element.73.part1), channel_id=1, source_target_pairs={{0,1},{1,0},{2,3},{3,2},{4,5},{5,4},{6,7},{7,6},{8,9},{9,8},{10,11... | collective-permute-start | bytes 1253384 | tf_op jit(solution)/shard_map/ppermute | solution.py:486
  24.6 4.4 %collective-permute-start.11 = (f32[2,3072]{1,0:T(2,128)S(1)}, f32[2,3072]{1,0:T(2,128)S(1)}, u32[]{:S(2)}, u32[]{:S(2)}) collective-permute-start(f32[2,3072]{1,0:T(2,128)S(1)} %get-tuple-element.90), channel_id=1, source_target_pairs={{0,7},{1,2},{2,1},{3,4},{4,3},{5,6},{6,5},{7,0},{8,15},{9,10},{10,... | collective-permute-start | bytes 73736 | tf_op jit(solution)/shard_map/ppermute | solution.py:516
  25.2 3.7 %collective-permute-start.12 = (f32[2,3072]{1,0:T(2,128)S(1)}, f32[2,3072]{1,0:T(2,128)S(1)}, u32[]{:S(2)}, u32[]{:S(2)}) collective-permute-start(f32[2,3072]{1,0:T(2,128)S(1)} %get-tuple-element.91), channel_id=1, source_target_pairs={{0,1},{1,0},{2,3},{3,2},{4,5},{5,4},{6,7},{7,6},{8,9},{9,8},{10,11... | collective-permute-start | bytes 73736 | tf_op jit(solution)/shard_map/ppermute | solution.py:515
